TPU v7x, 32 devices: a whole 2x2x4 slice. The times are simulated.
32 devices in a mesh: dp: 4 (over x, core), expert: 8 (over z, y).
Axes of the slice: x: 2, y: 2, z: 4, core: 2. Of those that a mesh axis runs over, the one named last changes fastest.
Arguments:
- points: float32 [16384], P(('dp', 'expert')), may hold values from -6 to 6
- experts: int32 [16384, 2], P(('dp', 'expert')), may hold values from 0 to 7, all different within a row; in each aligned block of 512 rows (0 to 511, 512 to 1023, ...) at most 256 rows name the same one
- lengths: int32 [32, 3], P(('dp', 'expert')), may hold values from 1 to 320, 512 in all within a row
- domains: int32 [32, 3], P(('dp', 'expert')), may hold values from 0 to 8, as said below
- domain_weights: float32 [9], replicated, may hold values from 0.5 to 2
- vectors: float32 [5, 384], P(None, 'expert'), may hold values from -4 to 4, as said below
- attend_input: float32 [384, 1152], P('expert'), may hold values from -0.3125 to 0.3125
- attend_output: float32 [384, 384], P('expert'), may hold values from -0.875 to 0.875
- router: float32 [384, 9], P('expert'), may hold values from -0.3125 to 0.3125
- shared_input: float32 [384, 3072], P('expert'), may hold values from -0.3125 to 0.3125
- shared_output: float32 [1536, 384], P('expert'), may hold values from -0.3125 to 0.3125
- horizon: float32 [384, 105], P('expert'), may hold values from -0.3125 to 0.3125
- expert_input: float32 [2, 384, 6144], P(None, None, 'expert'), may hold values from -0.3125 to 0.3125
- expert_output: float32 [6144, 384], P('expert'), may hold values from -0.625 to 0.625
- mean_vectors: float32 [5, 384], P(None, 'expert'), may hold values from -5.340576e-05 to 5.340576e-05
- mean_attend_input: float32 [384, 1152], P('expert'), may hold values from -4.7683716e-06 to 4.7683716e-06
- mean_attend_output: float32 [384, 384], P('expert'), may hold values from -4.7683716e-06 to 4.7683716e-06
- mean_router: float32 [384, 9], P('expert'), may hold values from -4.7683716e-06 to 4.7683716e-06
- mean_shared_input: float32 [384, 3072], P('expert'), may hold values from -4.7683716e-06 to 4.7683716e-06
- mean_shared_output: float32 [1536, 384], P('expert'), may hold values from -4.7683716e-06 to 4.7683716e-06
- mean_horizon: float32 [384, 105], P('expert'), may hold values from -4.7683716e-06 to 4.7683716e-06
- mean_expert_input: float32 [2, 384, 6144], P(None, None, 'expert'), may hold values from -4.7683716e-06 to 4.7683716e-06
- mean_expert_output: float32 [6144, 384], P('expert'), may hold values from -4.7683716e-06 to 4.7683716e-06
- square_vectors: float32 [5, 384], P(None, 'expert'), may hold values from 1.0650773e-11 to 4.260309e-11
- square_attend_input: float32 [384, 1152], P('expert'), may hold values from 1.06507725e-13 to 4.260309e-13
- square_attend_output: float32 [384, 384], P('expert'), may hold values from 1.06507725e-13 to 4.260309e-13
- square_router: float32 [384, 9], P('expert'), may hold values from 1.06507725e-13 to 4.260309e-13
- square_shared_input: float32 [384, 3072], P('expert'), may hold values from 1.06507725e-13 to 4.260309e-13
- square_shared_output: float32 [1536, 384], P('expert'), may hold values from 1.06507725e-13 to 4.260309e-13
- square_horizon: float32 [384, 105], P('expert'), may hold values from 1.06507725e-13 to 4.260309e-13
- square_expert_input: float32 [2, 384, 6144], P(None, None, 'expert'), may hold values from 1.06507725e-13 to 4.260309e-13
- square_expert_output: float32 [6144, 384], P('expert'), may hold values from 1.06507725e-13 to 4.260309e-13
Outputs:
- vectors_next: float32 [5, 384], P(None, 'expert')
- vectors_mean: float32 [5, 384], P(None, 'expert')
- vectors_square: float32 [5, 384], P(None, 'expert')
- attend_input_next: float32 [384, 1152], P('expert')
- attend_input_mean: float32 [384, 1152], P('expert')
- attend_input_square: float32 [384, 1152], P('expert')
- attend_output_next: float32 [384, 384], P('expert')
- attend_output_mean: float32 [384, 384], P('expert')
- attend_output_square: float32 [384, 384], P('expert')
- router_next: float32 [384, 9], P('expert')
- router_mean: float32 [384, 9], P('expert')
- router_square: float32 [384, 9], P('expert')
- shared_input_next: float32 [384, 3072], P('expert')
- shared_input_mean: float32 [384, 3072], P('expert')
- shared_input_square: float32 [384, 3072], P('expert')
- shared_output_next: float32 [1536, 384], P('expert')
- shared_output_mean: float32 [1536, 384], P('expert')
- shared_output_square: float32 [1536, 384], P('expert')
- horizon_next: float32 [384, 105], P('expert')
- horizon_mean: float32 [384, 105], P('expert')
- horizon_square: float32 [384, 105], P('expert')
- expert_input_next: float32 [2, 384, 6144], P(None, None, 'expert')
- expert_input_mean: float32 [2, 384, 6144], P(None, None, 'expert')
- expert_input_square: float32 [2, 384, 6144], P(None, None, 'expert')
- expert_output_next: float32 [6144, 384], P('expert')
- expert_output_mean: float32 [6144, 384], P('expert')
- expert_output_square: float32 [6144, 384], P('expert')
- domain_totals: float32 [2, 9], replicated
- grad_norm: float32 [1], replicated
- trust_norms: float32 [9, 2], replicated
Inputs may be any that keep to these rules, and one draw needn't show every extreme that they name: Each point names two different experts. Among the points of one device no expert is named more than 256 times, and in every draw some expert is named exactly 256 times by the points of some device. Each row lists the lengths of one device's series in order; it sums to 512 and its largest entry is exactly 320. `domains`: in every draw one domain, neither the first nor the last, names no series. The first two rows are the embedding vectors, the last three are norm gains, all positive.
All inputs are finite; a program needn't handle non-finite values.
Results may differ from a plain program's by a relative error of at most 0.0006.
The roundings to bfloat16 on the way count: a program that leaves them out, or rounds other values in their place, can miss the bound.
Values may be sent and summed in bfloat16 or wider, within the bound.
No kernel may reach another device: no remote copies, remote signals or barrier semaphores. Data moves between devices by JAX's collectives and lax.ppermute only.
A program may use at most 192 MiB of HBM per device.

v0:
```python
import jax
import jax.numpy as jnp
import numpy as np
from jax import lax
from jax.sharding import PartitionSpec as P

D = 384
HEADS = 12
HD = 32
FFS = 1536
EXPERTS = 8
DOMAINS = 9
STEP = 10
CAP = 256


HORIZONS = (1, 8, 32, 64)
REACH = 64
KINK_THRESHOLD = 2.0
EPS_NORM = 1e-06
CLIP = 0.01
BETA_ONE = 0.9
BETA_TWO = 0.99
EPS_ADAM = 1e-08
DECAY = 0.01
RATE = 0.3


def ahead_table():
    return np.concatenate([np.arange(horizon_len) for horizon_len in HORIZONS]).astype(np.int32)


def sigmoid_linear(inputs):
    return inputs * jax.nn.sigmoid(inputs)


def gated_unit(gate_in, lift_in):
    return sigmoid_linear(gate_in) * lift_in


def rms_norm(inputs, weight_gain):
    return (
        inputs
        * lax.rsqrt(jnp.mean(inputs * inputs, axis=-1, keepdims=True) + EPS_NORM)
        * weight_gain
    )


def rope_tables(position):
    half_width = HD // 2
    frequency = jnp.exp(-jnp.log(10000.0) * jnp.arange(half_width, dtype=jnp.float32) / half_width)
    angles = position.astype(jnp.float32)[:, None] * frequency[None, :]
    return (jnp.cos(angles)[:, None, :], jnp.sin(angles)[:, None, :])


def rotate(inputs, cosine, sine):
    half_width = inputs.shape[-1] // 2
    first_half = inputs[..., :half_width]
    second_half = inputs[..., half_width:]
    return jnp.concatenate(
        [first_half * cosine - second_half * sine, second_half * cosine + first_half * sine], -1
    )


def layout(samples, series_lengths, series_domains):
    amount = samples.shape[0]
    places = jnp.arange(amount, dtype=jnp.int32)
    finish = jnp.cumsum(series_lengths)
    anchor = finish - series_lengths
    series = jnp.sum((places[:, None] >= finish[None, :]).astype(jnp.int32), 1)
    member = series[:, None] == jnp.arange(series_lengths.shape[0], dtype=jnp.int32)[None, :]
    begin_at = jnp.sum(jnp.where(member, anchor[None, :], 0), 1)
    finish_at = jnp.sum(jnp.where(member, finish[None, :], 0), 1)
    domain_of = jnp.sum(jnp.where(member, series_domains[None, :], 0), 1)
    ahead_steps = jnp.asarray(ahead_table())
    reached = places[:, None] + 1 + ahead_steps[None, :]
    valid_mask = (reached < finish_at[:, None]).astype(jnp.float32)
    padded = jnp.concatenate([samples, jnp.zeros((REACH + 1,), samples.dtype)])
    future = jnp.stack([padded[1 + offset : 1 + offset + amount] for offset in range(REACH)], 1)
    observed_future = future[:, ahead_table()]
    return (series, places - begin_at, domain_of, valid_mask, observed_future)


def shards(
    points,
    experts,
    lengths,
    domains,
    domain_weights,
    vectors,
    attend_input,
    attend_output,
    router,
    shared_input,
    shared_output,
    horizon,
    expert_input,
    expert_output,
    mean_vectors,
    mean_attend_input,
    mean_attend_output,
    mean_router,
    mean_shared_input,
    mean_shared_output,
    mean_horizon,
    mean_expert_input,
    mean_expert_output,
    square_vectors,
    square_attend_input,
    square_attend_output,
    square_router,
    square_shared_input,
    square_shared_output,
    square_horizon,
    square_expert_input,
    square_expert_output,
):
    coarse_float_kind = jnp.bfloat16
    fine_float_kind = jnp.float32
    vec_low, input_low, output_low, router_low, shin_low, shout_low, readout_bfloat = (
        lax.all_gather(vectors.astype(coarse_float_kind), "expert", axis=1, tiled=True),
        lax.all_gather(attend_input.astype(coarse_float_kind), "expert", axis=0, tiled=True),
        lax.all_gather(attend_output.astype(coarse_float_kind), "expert", axis=0, tiled=True),
        lax.all_gather(router.astype(coarse_float_kind), "expert", axis=0, tiled=True),
        lax.all_gather(shared_input.astype(coarse_float_kind), "expert", axis=0, tiled=True),
        lax.all_gather(shared_output.astype(coarse_float_kind), "expert", axis=0, tiled=True),
        lax.all_gather(horizon.astype(coarse_float_kind), "expert", axis=0, tiled=True),
    )
    gain_rows = vec_low.astype(fine_float_kind)
    amount = points.shape[0]
    series, position, domain_of, valid_mask, observed_future = layout(
        points, lengths[0], domains[0]
    )
    cosine, sine = rope_tables(position)

    def front(gain_gate, gain_value, gain_norm):
        embedded = sigmoid_linear(points[:, None] * gain_gate) * (points[:, None] * gain_value)
        return (embedded, rms_norm(embedded, gain_norm))

    (embedded, first_norm), front_back = jax.vjp(front, gain_rows[0], gain_rows[1], gain_rows[2])
    first_low = first_norm.astype(coarse_float_kind)
    projected = jnp.dot(first_low, input_low, preferred_element_type=fine_float_kind)

    def turn(flat_rows):
        pieces = flat_rows.reshape(amount, 3, HEADS, HD)
        return (
            rotate(pieces[:, 0], cosine, sine),
            rotate(pieces[:, 1], cosine, sine),
            pieces[:, 2],
        )

    (queries, key_rows, value_rows), turn_back = jax.vjp(turn, projected)
    queries = queries.astype(coarse_float_kind)
    key_rows = key_rows.astype(coarse_float_kind)
    value_rows = value_rows.astype(coarse_float_kind)
    places = jnp.arange(amount)
    allowed = ((series[:, None] == series[None, :]) & (places[None, :] <= places[:, None]))[None]

    def score_block():
        raw_scores = jnp.einsum(
            "qhd,khd->hqk", queries, key_rows, preferred_element_type=fine_float_kind
        ) * HD ** (-0.5)
        return jnp.where(allowed, raw_scores, -1e30)

    scores = score_block()
    row_top = jnp.max(scores, -1, keepdims=True)
    exponent = jnp.exp(scores - row_top)
    row_total = jnp.sum(exponent, -1, keepdims=True)
    log_total = row_top + jnp.log(row_total)
    attention = (exponent / row_total).astype(coarse_float_kind)
    mixed = (
        jnp.einsum("hqk,khd->qhd", attention, value_rows, preferred_element_type=fine_float_kind)
        .reshape(amount, D)
        .astype(coarse_float_kind)
    )
    after_attend = embedded + jnp.dot(mixed, output_low, preferred_element_type=fine_float_kind)
    second_norm, second_back = jax.vjp(rms_norm, after_attend, gain_rows[3])
    second_low = second_norm.astype(coarse_float_kind)
    logits = jnp.dot(second_low, router_low, preferred_element_type=fine_float_kind)
    chosen = (experts[:, :, None] == jnp.arange(EXPERTS)[None, None, :]).astype(fine_float_kind)

    def gating(logit_rows):
        expert_logits = logit_rows[:, :EXPERTS]
        expert_exp = jnp.exp(expert_logits - jnp.max(expert_logits, -1, keepdims=True))
        probs_all = expert_exp / jnp.sum(expert_exp, -1, keepdims=True)
        return (
            jnp.sum(chosen * probs_all[:, None, :], -1),
            jax.nn.sigmoid(logit_rows[:, EXPERTS:]),
        )

    (gate_values, shared_gate), gating_back = jax.vjp(gating, logits)
    shared_both = jnp.dot(second_low, shin_low, preferred_element_type=fine_float_kind)
    shared_hidden, shared_back = jax.vjp(gated_unit, shared_both[:, :FFS], shared_both[:, FFS:])
    shared_low = shared_hidden.astype(coarse_float_kind)
    shared = jnp.dot(shared_low, shout_low, preferred_element_type=fine_float_kind)
    expert_devices = lax.axis_size("expert")
    group_size = expert_devices // EXPERTS
    flat_routes = experts.reshape(-1)
    expert_hot = (flat_routes[:, None] == jnp.arange(EXPERTS)[None, :]).astype(jnp.int32)
    ranked = jnp.sum((jnp.cumsum(expert_hot, 0) - expert_hot) * expert_hot, 1)
    slot_index = flat_routes * CAP + ranked

    def slot_buffer(rows_out):
        row_width = rows_out.shape[-1]
        return jnp.zeros((EXPERTS * CAP, row_width), rows_out.dtype).at[slot_index].set(rows_out)

    def send_out(rows_out):
        buffer = slot_buffer(rows_out).reshape(EXPERTS, CAP, rows_out.shape[-1])
        return jnp.repeat(buffer, group_size, 0)

    def bring_back(returned):
        summed = jnp.sum(returned.reshape(EXPERTS, group_size, CAP, returned.shape[-1]), 1)
        return summed.reshape(EXPERTS * CAP, -1)[slot_index].reshape(amount, 2, -1)

    gate_up_low = expert_input.astype(coarse_float_kind)
    down_low = expert_output.astype(coarse_float_kind)
    arrived = lax.all_to_all(
        send_out(jnp.repeat(second_low, 2, 0)), "expert", split_axis=0, concat_axis=0, tiled=True
    ).reshape(-1, D)
    expert_gate = jnp.dot(arrived, gate_up_low[0], preferred_element_type=fine_float_kind)
    expert_lift = jnp.dot(arrived, gate_up_low[1], preferred_element_type=fine_float_kind)
    expert_hidden = gated_unit(expert_gate, expert_lift).astype(coarse_float_kind)
    expert_rows = jnp.dot(expert_hidden, down_low, preferred_element_type=fine_float_kind)
    picked = bring_back(
        lax.all_to_all(
            expert_rows.reshape(expert_devices, -1, D),
            "expert",
            split_axis=0,
            concat_axis=0,
            tiled=True,
        )
    )
    after_mixer = after_attend + shared_gate * shared + jnp.sum(gate_values[:, :, None] * picked, 1)
    final_layer_scaling, third_back = jax.vjp(rms_norm, after_mixer, gain_rows[4])
    final_layer_bfloat = final_layer_scaling.astype(coarse_float_kind)
    predicted_series = jnp.dot(
        final_layer_bfloat, readout_bfloat, preferred_element_type=fine_float_kind
    )
    domain_onehot_rows = (domain_of[:, None] == jnp.arange(DOMAINS)[None, :]).astype(
        fine_float_kind
    )

    def smooth_absolute_sample_costs(prediction_source):
        prediction_residual = prediction_source - observed_future
        absolute_size = jnp.abs(prediction_residual)
        return jnp.sum(
            jnp.where(
                absolute_size <= KINK_THRESHOLD,
                0.5 * prediction_residual * prediction_residual,
                KINK_THRESHOLD * (absolute_size - 0.5 * KINK_THRESHOLD),
            )
            * valid_mask,
            -1,
        )

    sample_penalty, smooth_absolute_backward = jax.vjp(
        smooth_absolute_sample_costs, predicted_series
    )
    local_counts = jnp.sum(domain_onehot_rows * jnp.sum(valid_mask, -1)[:, None], 0)
    local_sums = jnp.sum(domain_onehot_rows * sample_penalty[:, None], 0)
    counts, domain_sums = lax.psum((local_counts, local_sums), ("dp", "expert"))
    domain_weighting = domain_weights / jnp.maximum(counts, 1.0)
    (prediction_slope,) = smooth_absolute_backward(
        jnp.sum(domain_onehot_rows * domain_weighting[None, :], 1)
    )
    prediction_bfloat = prediction_slope.astype(coarse_float_kind)
    head_gradient = jnp.dot(
        final_layer_bfloat.T, prediction_bfloat, preferred_element_type=fine_float_kind
    )
    grad_mixer, grad_gain_three = third_back(
        jnp.dot(prediction_bfloat, readout_bfloat.T, preferred_element_type=fine_float_kind)
    )
    grad_shared_low = (shared_gate * grad_mixer).astype(coarse_float_kind)
    grad_shared_gate = jnp.sum(grad_mixer * shared, -1, keepdims=True)
    grad_gates = jnp.sum(grad_mixer[:, None, :] * picked, -1)
    grad_picked = (gate_values[:, :, None] * grad_mixer[:, None, :]).astype(coarse_float_kind)
    received = lax.all_to_all(
        send_out(grad_picked.reshape(-1, D)), "expert", split_axis=0, concat_axis=0, tiled=True
    ).reshape(-1, D)
    grad_hidden = jnp.dot(received, down_low.T, preferred_element_type=fine_float_kind)
    grad_expert_out = jnp.dot(expert_hidden.T, received, preferred_element_type=fine_float_kind)
    gate_again, lift_again = (expert_gate, expert_lift)
    unused_hidden, expert_back = jax.vjp(gated_unit, gate_again, lift_again)
    grad_gate, grad_lift = expert_back(grad_hidden)
    grad_gate = grad_gate.astype(coarse_float_kind)
    grad_lift = grad_lift.astype(coarse_float_kind)
    grad_expert_in = jnp.stack(
        [
            jnp.dot(arrived.T, grad_gate, preferred_element_type=fine_float_kind),
            jnp.dot(arrived.T, grad_lift, preferred_element_type=fine_float_kind),
        ]
    )
    grad_rows = jnp.dot(
        grad_gate, gate_up_low[0].T, preferred_element_type=fine_float_kind
    ) + jnp.dot(grad_lift, gate_up_low[1].T, preferred_element_type=fine_float_kind)
    grad_routed = bring_back(
        lax.all_to_all(
            grad_rows.reshape(expert_devices, -1, D).astype(jnp.bfloat16),
            "expert",
            split_axis=0,
            concat_axis=0,
            tiled=True,
        ).astype(jnp.float32)
    )
    grad_second = jnp.sum(grad_routed, 1)
    grad_shared_hidden = jnp.dot(
        grad_shared_low, shout_low.T, preferred_element_type=fine_float_kind
    )
    grad_shout = jnp.dot(shared_low.T, grad_shared_low, preferred_element_type=fine_float_kind)
    grad_shared_gatein, grad_shared_lift = shared_back(grad_shared_hidden)
    grad_shared_both = jnp.concatenate([grad_shared_gatein, grad_shared_lift], 1).astype(
        coarse_float_kind
    )
    grad_shin = jnp.dot(second_low.T, grad_shared_both, preferred_element_type=fine_float_kind)
    grad_second = grad_second + jnp.dot(
        grad_shared_both, shin_low.T, preferred_element_type=fine_float_kind
    )
    (grad_logits,) = gating_back((grad_gates, grad_shared_gate))
    grad_logits = grad_logits.astype(coarse_float_kind)
    grad_router = jnp.dot(second_low.T, grad_logits, preferred_element_type=fine_float_kind)
    grad_second = grad_second + jnp.dot(
        grad_logits, router_low.T, preferred_element_type=fine_float_kind
    )
    grad_attend_norm, grad_gain_two = second_back(grad_second)
    grad_attend = grad_mixer + grad_attend_norm
    grad_attend_low = grad_attend.astype(coarse_float_kind)
    grad_output = jnp.dot(mixed.T, grad_attend_low, preferred_element_type=fine_float_kind)
    grad_mixed = (
        jnp.dot(grad_attend_low, output_low.T, preferred_element_type=fine_float_kind)
        .astype(coarse_float_kind)
        .reshape(amount, HEADS, HD)
    )
    attention_again = jnp.exp(score_block() - log_total)
    grad_values = jnp.einsum(
        "hqk,qhd->khd",
        attention_again.astype(coarse_float_kind),
        grad_mixed,
        preferred_element_type=fine_float_kind,
    )
    grad_probs = jnp.einsum(
        "qhd,khd->hqk", grad_mixed, value_rows, preferred_element_type=fine_float_kind
    )
    grad_scores = (
        attention_again * (grad_probs - jnp.sum(grad_probs * attention_again, -1, keepdims=True))
    ).astype(coarse_float_kind)
    grad_queries = jnp.einsum(
        "hqk,khd->qhd", grad_scores, key_rows, preferred_element_type=fine_float_kind
    ) * HD ** (-0.5)
    grad_keys = jnp.einsum(
        "hqk,qhd->khd", grad_scores, queries, preferred_element_type=fine_float_kind
    ) * HD ** (-0.5)
    (grad_projected,) = turn_back((grad_queries, grad_keys, grad_values))
    grad_projected = grad_projected.astype(coarse_float_kind)
    grad_input = jnp.dot(first_low.T, grad_projected, preferred_element_type=fine_float_kind)
    grad_first = jnp.dot(grad_projected, input_low.T, preferred_element_type=fine_float_kind)
    grad_gain_gate, grad_gain_value, grad_gain_one = front_back((grad_attend, grad_first))
    grad_vectors = jnp.stack(
        [grad_gain_gate, grad_gain_value, grad_gain_one, grad_gain_two, grad_gain_three]
    )
    summed = lax.psum(
        (
            grad_vectors,
            grad_input,
            grad_output,
            grad_router,
            grad_shin,
            grad_shout,
            head_gradient,
            grad_expert_in,
            grad_expert_out,
        ),
        "dp",
    )
    shares = (
        lax.psum_scatter(summed[0], "expert", scatter_dimension=1, tiled=True),
        lax.psum_scatter(summed[1], "expert", scatter_dimension=0, tiled=True),
        lax.psum_scatter(summed[2], "expert", scatter_dimension=0, tiled=True),
        lax.psum_scatter(summed[3], "expert", scatter_dimension=0, tiled=True),
        lax.psum_scatter(summed[4], "expert", scatter_dimension=0, tiled=True),
        lax.psum_scatter(summed[5], "expert", scatter_dimension=0, tiled=True),
        lax.psum_scatter(summed[6], "expert", scatter_dimension=0, tiled=True),
    )
    gradients = tuple(shares) + (summed[7], summed[8])
    masters = (
        vectors,
        attend_input,
        attend_output,
        router,
        shared_input,
        shared_output,
        horizon,
        expert_input,
        expert_output,
    )
    first_moments = (
        mean_vectors,
        mean_attend_input,
        mean_attend_output,
        mean_router,
        mean_shared_input,
        mean_shared_output,
        mean_horizon,
        mean_expert_input,
        mean_expert_output,
    )
    second_moments = (
        square_vectors,
        square_attend_input,
        square_attend_output,
        square_router,
        square_shared_input,
        square_shared_output,
        square_horizon,
        square_expert_input,
        square_expert_output,
    )
    local_square = jnp.sum(jnp.stack([jnp.sum(gradient * gradient) for gradient in gradients]))
    grad_norm = jnp.sqrt(lax.psum(local_square, "expert"))
    factor = jnp.minimum(1.0, CLIP / grad_norm)
    moments_new = []
    directions = []
    for master, gradient, moment_one, moment_two in zip(
        masters, gradients, first_moments, second_moments
    ):
        clipped = gradient * factor
        moment_new = BETA_ONE * moment_one + (1.0 - BETA_ONE) * clipped
        square_new = BETA_TWO * moment_two + (1.0 - BETA_TWO) * clipped * clipped
        directions.append(
            moment_new
            / (1.0 - BETA_ONE**STEP)
            / (jnp.sqrt(square_new / (1.0 - BETA_TWO**STEP)) + EPS_ADAM)
            + DECAY * master
        )
        moments_new.append((moment_new, square_new))
    weight_square = jnp.stack([jnp.sum(master * master) for master in masters])
    update_square = jnp.stack([jnp.sum(direction * direction) for direction in directions])
    weight_square, update_square = lax.psum((weight_square, update_square), "expert")
    weight_norm = jnp.sqrt(weight_square)
    update_norm = jnp.sqrt(update_square)
    results = []
    for position_index in range(9):
        ratio = weight_norm[position_index] / update_norm[position_index]
        results.append(masters[position_index] - RATE * ratio * directions[position_index])
        results.append(moments_new[position_index][0])
        results.append(moments_new[position_index][1])
    results.append(jnp.stack([domain_sums, counts]))
    results.append(grad_norm.reshape(1))
    results.append(jnp.stack([weight_norm, update_norm], 1))
    return tuple(results)


def solution(mesh):
    placed = (
        P(("dp", "expert")),
        P(("dp", "expert"), None),
        P(("dp", "expert"), None),
        P(("dp", "expert"), None),
        P(),
        P(None, "expert"),
        P("expert", None),
        P("expert", None),
        P("expert", None),
        P("expert", None),
        P("expert", None),
        P("expert", None),
        P(None, None, "expert"),
        P("expert", None),
        P(None, "expert"),
        P("expert", None),
        P("expert", None),
        P("expert", None),
        P("expert", None),
        P("expert", None),
        P("expert", None),
        P(None, None, "expert"),
        P("expert", None),
        P(None, "expert"),
        P("expert", None),
        P("expert", None),
        P("expert", None),
        P("expert", None),
        P("expert", None),
        P("expert", None),
        P(None, None, "expert"),
        P("expert", None),
    )
    return jax.shard_map(
        shards,
        mesh=mesh,
        in_specs=placed,
        out_specs=(
            P(None, "expert"),
            P(None, "expert"),
            P(None, "expert"),
            P("expert", None),
            P("expert", None),
            P("expert", None),
            P("expert", None),
            P("expert", None),
            P("expert", None),
            P("expert", None),
            P("expert", None),
            P("expert", None),
            P("expert", None),
            P("expert", None),
            P("expert", None),
            P("expert", None),
            P("expert", None),
            P("expert", None),
            P("expert", None),
            P("expert", None),
            P("expert", None),
            P(None, None, "expert"),
            P(None, None, "expert"),
            P(None, None, "expert"),
            P("expert", None),
            P("expert", None),
            P("expert", None),
            P(),
            P(),
            P(),
        ),
        check_vma=False,
    )
```

profile of v0, /device:TPU:0, one launch (start us, length us, event | category | flops | bytes accessed | tf_op | source)
XLA Modules:
  0.0 1269.8 jit_solution(3001777658648310082)
XLA Ops:
  12.9 27.8 %all-gather = bf16[8,48,5]{1,2,0:T(8,128)(2,1)S(1)} all-gather(bf16[1,48,5]{1,2,0:T(8,128)(2,1)S(1)} %convert_bitcast_fusion.1), channel_id=1, replica_groups=mesh['dp'=4,'expert'=8] {'expert'}, dimensions={0}, use_global_device_ids=true | all-gather | bytes 4320 | tf_op jit(solution)/shard_map/all_gather | solution.py:121
  44.3 30.9 %all_gather.23 = bf16[384,384]{1,0:T(8,128)(2,1)S(1)} all-gather(bf16[48,384]{1,0:T(8,128)(2,1)S(1)} %convert_element_type.144), channel_id=1, replica_groups=mesh['dp'=4,'expert'=8] {'expert'}, dimensions={0}, use_global_device_ids=true | all-gather | bytes 331776 | tf_op jit(solution)/shard_map/all_gather | solution.py:123
  78.3 32.3 %all_gather.22 = bf16[384,1152]{1,0:T(8,128)(2,1)S(1)} all-gather(bf16[48,1152]{1,0:T(8,128)(2,1)S(1)} %convert_element_type.136), channel_id=1, replica_groups=mesh['dp'=4,'expert'=8] {'expert'}, dimensions={0}, use_global_device_ids=true | all-gather | bytes 995328 | tf_op jit(solution)/shard_map/all_gather | solution.py:122
  120.2 3.6 fusion.24
  126.7 6.3 scatter_custom_fusion
  133.0 4.4 all-to-all-start
  139.4 31.1 %all-to-all-done = bf16[8,256,384]{2,1,0:T(8,128)(2,1)} async-done(((bf16[8,256,384]{2,1,0:T(8,128)(2,1)}), bf16[8,256,384]{2,1,0:T(8,128)(2,1)}, u32[]{:S(2)}, u32[]{:S(2)}) %all-to-all-start) | async-done | bytes 1572896 | tf_op jit(solution)/shard_map/all_to_all | solution.py:217
  174.0 7.4 multiply_convert_fusion.2
  181.5 3.5 fusion.50
  185.0 11.0 all-to-all-start.1
  199.0 84.0 %all-gather.1 = bf16[8,48,9]{1,2,0:T(8,128)(2,1)S(1)} all-gather(bf16[1,48,9]{1,2,0:T(8,128)(2,1)S(1)} %convert_bitcast_fusion), channel_id=1, replica_groups=mesh['dp'=4,'expert'=8] {'expert'}, dimensions={0}, use_global_device_ids=true | all-gather | bytes 7776 | tf_op jit(solution)/shard_map/all_gather | solution.py:124
  294.0 6.0 stack.374
  302.8 30.7 %all_gather.27 = bf16[384,105]{1,0:T(8,128)(2,1)S(1)} all-gather(bf16[48,105]{1,0:T(8,128)(2,1)} %convert_element_type.156), channel_id=1, replica_groups=mesh['dp'=4,'expert'=8] {'expert'}, dimensions={0}, use_global_device_ids=true | all-gather | bytes 90720 | tf_op jit(solution)/shard_map/all_gather | solution.py:127
  335.1 3.6 fusion.123
  343.4 4.8 gather_fusion
  350.4 4.0 multiply_reduce_fusion.5
  356.7 3.5 multiply_reduce_fusion.17
  363.0 40.0 %psum.99 = f32[9]{0:T(128)S(1)} all-reduce(f32[9]{0:T(128)} %select_reduce_fusion.3), channel_id=1, replica_groups=mesh['dp'=4,'expert'=8] {'dp','expert'}, use_global_device_ids=true, to_apply=%region_30.31 | all-reduce | flops 9 | bytes 72 | tf_op jit(solution)/shard_map/psum | solution.py:261
  415.8 7.3 scatter_custom_fusion.1
  423.1 6.1 all-to-all-start.2
  429.2 35.6 %all-to-all-done.2 = bf16[8,256,384]{2,1,0:T(8,128)(2,1)} async-done(((bf16[8,256,384]{2,1,0:T(8,128)(2,1)}), bf16[8,256,384]{2,1,0:T(8,128)(2,1)}, u32[]{:S(2)}, u32[]{:S(2)}) %all-to-all-start.2) | async-done | bytes 1572896 | tf_op jit(solution)/shard_map/all_to_all | solution.py:277
  464.9 7.8 multiply_convert_fusion.1
  478.4 4.4 all-to-all-start.3
  483.4 3.6 fusion.73
  489.3 5.5 fusion.13
  494.8 42.8 %all-to-all-done.3 = bf16[8,256,384]{2,1,0:T(8,128)(2,1)} async-done(((bf16[8,256,384]{2,1,0:T(8,128)(2,1)}), bf16[8,256,384]{2,1,0:T(8,128)(2,1)}, u32[]{:S(2)}, u32[]{:S(2)}) %all-to-all-start.3) | async-done | bytes 1572896 | tf_op jit(solution)/shard_map/all_to_all | solution.py:297
  539.3 4.8 gather_fusion.2
  548.5 4.1 fusion.23
  555.7 11.1 multiply_reduce_fusion
  568.7 7.1 multiply_convert_fusion
  579.5 6.1 fusion.18
  589.1 5.0 fusion.16
  600.6 3.9 convolution_bitcast_fusion
  610.2 4.2 fusion.124
  614.4 25.6 %reduce-scatter.14.cloned.1.call-done = f32[48,384]{1,0:T(8,128)} async-done(((f32[384,384]{1,0:T(8,128)}), f32[48,384]{1,0:T(8,128)}) %reduce-scatter.14.cloned.1.call-update) | async-done | bytes 73744 | tf_op jit(solution)/shard_map/reduce_scatter | solution.py:377
  640.0 69.5 %reduce-scatter.12.cloned.1.call-done = f32[48,1152]{1,0:T(8,128)} async-done(((f32[384,1152]{1,0:T(8,128)}), f32[48,1152]{1,0:T(8,128)}) %reduce-scatter.12.cloned.1.call-update) | async-done | bytes 221200 | tf_op jit(solution)/shard_map/reduce_scatter | solution.py:376
  709.6 97.7 %reduce-scatter.16.cloned.1.call-done = f32[48,3072]{1,0:T(8,128)} async-done(((f32[384,3072]{1,0:T(8,128)}), f32[48,3072]{1,0:T(8,128)}) %reduce-scatter.16.cloned.1.call-update) | async-done | bytes 589840 | tf_op jit(solution)/shard_map/reduce_scatter | solution.py:379
  807.3 64.7 %reduce-scatter.24.cloned.1.call-done = f32[48,9]{1,0:T(8,128)} async-done(((f32[384,9]{1,0:T(8,128)}), f32[48,9]{1,0:T(8,128)}) %reduce-scatter.24.cloned.1.call-update) | async-done | bytes 1744
  872.9 63.2 %reduce-scatter.22.cloned.1.call-done = f32[48,5]{1,0:T(8,128)} async-done(((f32[384,5]{1,0:T(8,128)}), f32[48,5]{1,0:T(8,128)}) %reduce-scatter.22.cloned.1.call-update) | async-done | bytes 976
  936.9 63.3 %reduce-scatter.20.cloned.1.call-done = f32[48,105]{1,0:T(8,128)} async-done(((f32[384,105]{1,0:T(8,128)}), f32[48,105]{1,0:T(8,128)}) %reduce-scatter.20.cloned.1.call-update) | async-done | bytes 20176 | tf_op jit(solution)/shard_map/reduce_scatter | solution.py:381
  1000.2 10.5 all-reduce.11
  1012.5 85.4 %all-reduce.15.cloned.1.call-done = (f32[48,1152]{1,0:T(8,128)}, f32[48,384]{1,0:T(8,128)}, f32[48,3072]{1,0:T(8,128)}, f32[192,384]{1,0:T(8,128)}, f32[2,384,768]{2,1,0:T(8,128)}, /*index=5*/f32[768,384]{1,0:T(8,128)}) async-done(((f32[48,1152]{1,0:T(8,128)}, f32[48,384]{1,0:T(8,128)}, f32[48,3072]{1,0:T(8,128)}, f32[192,384]{1,0:T(8,128)}, f32[2,384,768]{2,1,0:T(8,128)}, /*index=5*/f32[768,384]{1,0:T(8,128)}), ...) | async-done | bytes 4718608 | tf_op jit(solution)/shard_map/psum | solution.py:360
  1111.8 39.7 %psum.111 = f32[1,9]{1,0:T(1,128)} all-reduce(f32[1,9]{1,0:T(1,128)} %bitcast.332), channel_id=1, replica_groups=mesh['dp'=4,'expert'=8] {'dp','expert'}, use_global_device_ids=true, to_apply=%region_87.88 | all-reduce | flops 9 | bytes 72 | tf_op jit(solution)/shard_map/psum | solution.py:261
  1151.5 22.0 %psum.109 = f32[]{:T(128)} all-reduce(f32[]{:T(128)S(6)} %reduce_sum.679), channel_id=1, replica_groups=mesh['dp'=4,'expert'=8] {'expert'}, use_global_device_ids=true, to_apply=%region_74.75 | all-reduce | flops 1 | bytes 8 | tf_op jit(solution)/shard_map/psum | solution.py:418
  1194.1 4.7 multiply_reduce_fusion.1
  1198.8 6.4 stack.388
  1205.2 6.1 stack.309
  1212.5 17.8 %all-reduce.10 = (f32[9]{0:T(128)}, f32[9]{0:T(128)}) all-reduce(f32[9]{0:T(128)} %stack.309, f32[9]{0:T(128)} %stack.388), channel_id=1, replica_groups=mesh['dp'=4,'expert'=8] {'expert'}, use_global_device_ids=true, to_apply=%region_9.10 | all-reduce | flops 18 | bytes 144 | tf_op jit(solution)/shard_map/psum | solution.py:437
  (435 shorter events, 162.9 us)
Async XLA Ops:
  7.2 103.5 %copy-start.81 = (f32[512]{0:T(512)S(1)}, f32[512]{0:T(512)}, u32[]{:S(2)}) copy-start(f32[512]{0:T(512)} %param.35) | copy-start | bytes 6148
  11.6 106.6 %copy-start.24 = (pred[512,512]{0,1:T(8,128)(4,1)}, pred[512,512]{0,1:T(8,128)(4,1)S(1)}, u32[]{:S(2)}) copy-start(pred[512,512]{0,1:T(8,128)(4,1)S(1)} %fusion.26) | copy-start | bytes 786436
  41.4 70.4 %copy-start.100 = (f32[384]{0:T(512)}, f32[384]{0:T(512)S(1)}, u32[]{:S(2)}) copy-start(f32[384]{0:T(512)S(1)} %get-tuple-element.54) | copy-start | bytes 4612
  41.4 82.5 %copy-start.102 = (f32[384]{0:T(512)}, f32[384]{0:T(512)S(1)}, u32[]{:S(2)}) copy-start(f32[384]{0:T(512)S(1)} %get-tuple-element.55) | copy-start | bytes 4612
  41.4 82.5 %copy-start.104 = (f32[384]{0:T(512)}, f32[384]{0:T(512)S(1)}, u32[]{:S(2)}) copy-start(f32[384]{0:T(512)S(1)} %get-tuple-element.56) | copy-start | bytes 4612
  41.4 83.3 %copy-start.89 = (f32[384]{0:T(512)}, f32[384]{0:T(512)S(1)}, u32[]{:S(2)}) copy-start(f32[384]{0:T(512)S(1)} %get-tuple-element.53) | copy-start | bytes 4612
  42.5 32.7 %copy-start.110 = (f32[512]{0:T(512)}, f32[512]{0:T(512)S(1)}, u32[]{:S(2)}) copy-start(f32[512]{0:T(512)S(1)} %multiply_reduce_fusion.19) | copy-start | bytes 6148
  42.5 69.3 %copy-start.106 = (f32[512]{0:T(512)}, f32[512]{0:T(512)S(1)}, u32[]{:S(2)}) copy-start(f32[512]{0:T(512)S(1)} %fusion.89) | copy-start | bytes 6148
  75.2 48.7 %copy-start.46 = (bf16[384,384]{1,0:T(8,128)(2,1)}, bf16[384,384]{1,0:T(8,128)(2,1)S(1)}, u32[]{:S(2)}) copy-start(bf16[384,384]{1,0:T(8,128)(2,1)S(1)} %all_gather.23) | copy-start | bytes 884740
  125.7 158.7 %copy-start.5 = (bf16[512,384]{0,1:T(8,128)(2,1)}, bf16[512,384]{0,1:T(8,128)(2,1)S(1)}, u32[]{:S(2)}) copy-start(bf16[512,384]{0,1:T(8,128)(2,1)S(1)} %multiply_convert_fusion.9) | copy-start | bytes 1179652
  126.7 10.8 copy-start.16
  133.0 37.5 %all-to-all-start = ((bf16[8,256,384]{2,1,0:T(8,128)(2,1)}), bf16[8,256,384]{2,1,0:T(8,128)(2,1)}, u32[]{:S(2)}, u32[]{:S(2)}) async-start(bf16[8,256,384]{2,1,0:T(8,128)(2,1)} %bitcast.241), calls=%async_computation | async-start | bytes 3145728 | tf_op jit(solution)/shard_map/all_to_all | solution.py:217
  137.5 197.6 %all-gather.5.cloned.1.call-start = ((), (), s32[]{:S(2)}) async-start(), calls=%async_computation.11 | async-start | bytes 2654208 | tf_op jit(solution)/shard_map/all_gather | solution.py:125
  185.0 14.0 %copy-start.78 = (f32[48,9]{0,1:T(8,128)S(1)}, f32[48,9]{0,1:T(8,128)}, u32[]{:S(2)}) copy-start(f32[48,9]{0,1:T(8,128)} %param.43) | copy-start | bytes 5188
  185.0 158.4 %all-to-all-start.1 = ((f32[8,256,384]{2,1,0:T(8,128)}), f32[8,256,384]{2,1,0:T(8,128)S(1)}, u32[]{:S(2)}, u32[]{:S(2)}) async-start(f32[8,256,384]{2,1,0:T(8,128)} %bitcast.243), calls=%async_computation.1 | async-start | bytes 6291456 | tf_op jit(solution)/shard_map/all_to_all | solution.py:225
  195.9 160.8 %all-gather.7.cloned.1.call-start = ((), (), s32[]{:S(2)}) async-start(), calls=%async_computation.12 | async-start | bytes 1327104 | tf_op jit(solution)/shard_map/all_gather | solution.py:126
  284.6 9.4 copy-start.83
  333.6 26.7 %copy-start.116 = (s32[512]{0:T(512)}, s32[512]{0:T(512)S(1)}, u32[]{:S(2)}) copy-start(s32[512]{0:T(512)S(1)} %iota_add_fusion) | copy-start | bytes 6148
  334.3 9.1 copy-start.86
  335.0 148.3 %copy-start.93 = (f32[512,1]{0,1:T(1,128)}, f32[512,1]{0,1:T(1,128)S(1)}, u32[]{:S(2)}) copy-start(f32[512,1]{0,1:T(1,128)S(1)} %fusion.88) | copy-start | bytes 6148
  360.3 47.2 %copy-start.108 = (f32[512]{0:T(512)}, f32[512]{0:T(512)S(1)}, u32[]{:S(2)}) copy-start(f32[512]{0:T(512)S(1)} %fusion.91) | copy-start | bytes 6148
  423.1 41.7 %all-to-all-start.2 = ((bf16[8,256,384]{2,1,0:T(8,128)(2,1)}), bf16[8,256,384]{2,1,0:T(8,128)(2,1)}, u32[]{:S(2)}, u32[]{:S(2)}) async-start(bf16[8,256,384]{2,1,0:T(8,128)(2,1)} %bitcast.242), calls=%async_computation.2 | async-start | bytes 3145728 | tf_op jit(solution)/shard_map/all_to_all | solution.py:277
  464.9 7.8 copy-start.33
  478.4 59.2 %all-to-all-start.3 = ((bf16[8,256,384]{2,1,0:T(8,128)(2,1)}), bf16[8,256,384]{2,1,0:T(8,128)(2,1)}, u32[]{:S(2)}, u32[]{:S(2)}) async-start(bf16[8,256,384]{2,1,0:T(8,128)(2,1)} %bitcast.247), calls=%async_computation.3 | async-start | bytes 3145728 | tf_op jit(solution)/shard_map/all_to_all | solution.py:297
  482.9 131.6 %reduce-scatter.18.cloned.1.call-start = ((), (), s32[]{:S(2)}) async-start(), calls=%async_computation.16 | async-start | bytes 2654208 | tf_op jit(solution)/shard_map/reduce_scatter | solution.py:380
  487.0 153.1 %reduce-scatter.14.cloned.1.call-start = ((), (), s32[]{:S(2)}) async-start(), calls=%async_computation.14 | async-start | bytes 663552 | tf_op jit(solution)/shard_map/reduce_scatter | solution.py:377
  494.8 44.5 %copy-start.87 = (s32[1024]{0:T(1024)S(1)}, s32[1024]{0:T(1024)}, u32[]{:S(2)}) copy-start(s32[1024]{0:T(1024)} %copy-done.86) | copy-start | bytes 12292
  555.7 11.1 slice-start
  555.7 11.3 slice-start.1
  555.7 13.1 %slice-start.2 = ((s8[12582912]{0:T(1024)(128)(4,1)}), s8[4194304]{0:T(1024)(128)(4,1)S(1)}, s32[]{:S(2)}) async-start(s8[12582912]{0:T(1024)(128)(4,1)} %bitcast.238), calls=%async_computation.23 | async-start | bytes 8388608
  578.9 130.7 %reduce-scatter.12.cloned.1.call-start = ((), (), s32[]{:S(2)}) async-start(), calls=%async_computation.13 | async-start | bytes 1990656 | tf_op jit(solution)/shard_map/reduce_scatter | solution.py:376
  589.0 218.3 %reduce-scatter.16.cloned.1.call-start = ((), (), s32[]{:S(2)}) async-start(), calls=%async_computation.15 | async-start | bytes 5308416 | tf_op jit(solution)/shard_map/reduce_scatter | solution.py:379
  594.1 278.0 %reduce-scatter.24.cloned.1.call-start = ((), (), s32[]{:S(2)}) async-start(), calls=%async_computation.19 | async-start | bytes 221184
  595.2 340.9 %reduce-scatter.22.cloned.1.call-start = ((), (), s32[]{:S(2)}) async-start(), calls=%async_computation.18 | async-start | bytes 221184
  599.3 400.8 %reduce-scatter.20.cloned.1.call-start = ((), (), s32[]{:S(2)}) async-start(), calls=%async_computation.17 | async-start | bytes 221184 | tf_op jit(solution)/shard_map/reduce_scatter | solution.py:381
  600.6 497.3 %all-reduce.15.cloned.1.call-start = ((), (), s32[]{:S(2)}) async-start(), calls=%async_computation.20 | async-start | bytes 9437184 | tf_op jit(solution)/shard_map/psum | solution.py:360
  1097.9 76.3 %copy-start.85 = (f32[5,48]{1,0:T(8,128)S(1)}, f32[5,48]{1,0:T(8,128)}, u32[]{:S(2)}) copy-start(f32[5,48]{1,0:T(8,128)} %param.40) | copy-start | bytes 2884
  1098.0 78.2 %copy-start.79 = (f32[48,9]{0,1:T(8,128)S(1)}, f32[48,9]{0,1:T(8,128)}, u32[]{:S(2)}) copy-start(f32[48,9]{0,1:T(8,128)} %param.43) | copy-start | bytes 5188
  1098.0 82.2 %copy-start.60 = (f32[48,384]{1,0:T(8,128)S(1)}, f32[48,384]{1,0:T(8,128)}, u32[]{:S(2)}) copy-start(f32[48,384]{1,0:T(8,128)} %param.42) | copy-start | bytes 221188
  1100.2 82.2 %copy-start.41 = (f32[48,1152]{1,0:T(8,128)S(1)}, f32[48,1152]{1,0:T(8,128)}, u32[]{:S(2)}) copy-start(f32[48,1152]{1,0:T(8,128)} %param.41) | copy-start | bytes 663556
  1100.2 84.9 %copy-start.34 = (f32[192,384]{1,0:T(8,128)S(1)}, f32[192,384]{1,0:T(8,128)}, u32[]{:S(2)}) copy-start(f32[192,384]{1,0:T(8,128)} %param.45) | copy-start | bytes 884740
  1100.3 87.7 %copy-start.62 = (f32[48,3072]{1,0:T(8,128)S(1)}, f32[48,3072]{1,0:T(8,128)}, u32[]{:S(2)}) copy-start(f32[48,3072]{1,0:T(8,128)} %param.62) | copy-start | bytes 1769476
  1103.2 84.8 %copy-start.61 = (f32[48,3072]{1,0:T(8,128)S(1)}, f32[48,3072]{1,0:T(8,128)}, u32[]{:S(2)}) copy-start(f32[48,3072]{1,0:T(8,128)} %param.53) | copy-start | bytes 1769476
  1103.9 84.1 %copy-start.17 = (f32[48,3072]{1,0:T(8,128)S(1)}, f32[48,3072]{1,0:T(8,128)}, u32[]{:S(2)}) copy-start(f32[48,3072]{1,0:T(8,128)} %param.44) | copy-start | bytes 1769476
  1178.1 12.0 copy-start.49
  1194.1 51.3 %copy-start.97 = (f32[5,48]{1,0:T(8,128)S(1)}, f32[5,48]{1,0:T(8,128)}, u32[]{:S(2)}) copy-start(f32[5,48]{1,0:T(8,128)} %get-tuple-element.95) | copy-start | bytes 2884
  1230.3 24.7 %copy-start.36 = (f32[48,3072]{1,0:T(8,128)S(1)}, f32[48,3072]{1,0:T(8,128)}, u32[]{:S(2)}) copy-start(f32[48,3072]{1,0:T(8,128)} %get-tuple-element.87) | copy-start | bytes 1769476
  1230.3 24.7 %copy-start.37 = (f32[48,3072]{1,0:T(8,128)S(1)}, f32[48,3072]{1,0:T(8,128)}, u32[]{:S(2)}) copy-start(f32[48,3072]{1,0:T(8,128)} %get-tuple-element.88) | copy-start | bytes 1769476
  (94 other events, 324.6 us)
Sparse Core Ops, SparseCore 0:
  141.1 83.3 all-gather.4
  226.7 45.0 all-gather.6
  487.8 86.7 reduce-scatter.17
  579.0 60.9 reduce-scatter.13
  644.3 65.2 reduce-scatter.11
  713.1 94.1 reduce-scatter.15
  811.1 60.8 reduce-scatter.23
  875.9 60.1 reduce-scatter.21
  939.9 60.2 reduce-scatter.19
  1003.9 93.9 all-reduce.14
where the time goes:
time: 1280 us; the launch traced here: 1270 us
  waiting for transfers between devices  579 us (45%)
  blocking collectives  336 us (26%)
  other arithmetic  103 us (8%)
  matrix products  102 us (8%)
  local copies, waits for them, and re-layouts  87 us (7%)
  between operations  35.6 us (3%)
  starting transfers between devices  26.9 us (2%)
    unnamed x12, waiting for transfers between devices  128 us
    reduce_scatter x1, waiting for transfers between devices, shards(): lax.psum_scatter(summed[4], 'expert', scatter_dimension=0, tiled=True)  97.7 us
    psum x1, waiting for transfers between devices, shards(): lax.psum((grad_vectors, grad_input, grad_output, grad_router, grad_shin,...  85.4 us
    all_gather x1, blocking collectives, shards(): lax.all_gather(router.astype(coarse_float_kind), 'expert', axis=0, tiled=...  84 us
    psum x2, blocking collectives, shards(): counts, domain_sums = lax.psum((local_counts, local_sums), ('dp', 'expert'))  79.8 us
    reduce_scatter x1, waiting for transfers between devices, shards(): lax.psum_scatter(summed[1], 'expert', scatter_dimension=0, tiled=True)  69.5 us
    reduce_scatter x1, waiting for transfers between devices, shards(): lax.psum_scatter(summed[6], 'expert', scatter_dimension=0, tiled=True)  63.3 us
    all_to_all x1, waiting for transfers between devices, shards(): lax.all_to_all(grad_rows.reshape(expert_devices, -1, D).astype(jnp.bfloat...  42.8 us
  transfers between devices with their start and end apart: 14, of which 10 were waited for; matrix products, arithmetic and copies ran while one was open for 11% of the time, Pallas kernels for 0%

commit v1 on v0

--- a/solution.py
+++ b/solution.py
@@ -79,6 +79,71 @@
     future = jnp.stack([padded[1 + offset : 1 + offset + amount] for offset in range(REACH)], 1)
     observed_future = future[:, ahead_table()]
     return (series, places - begin_at, domain_of, valid_mask, observed_future)
+
+
+def flip(value, axis_name, bit):
+    count = lax.axis_size(axis_name)
+    return lax.ppermute(value, axis_name, [(i, i ^ bit) for i in range(count)])
+
+
+def bits_of(axis_name):
+    count = lax.axis_size(axis_name)
+    return [1 << i for i in range(count.bit_length() - 1)]
+
+
+def sum_small(value, axes):
+    for axis_name in axes:
+        for bit in bits_of(axis_name):
+            value = value + flip(value, axis_name, bit)
+    return value
+
+
+def halves(value, axis, take_high):
+    size = value.shape[axis] // 2
+    low = lax.slice_in_dim(value, 0, size, axis=axis)
+    high = lax.slice_in_dim(value, size, 2 * size, axis=axis)
+    return (jnp.where(take_high, high, low), jnp.where(take_high, low, high))
+
+
+def scatter_sum(value, axis, bits):
+    for bit in bits:
+        side = (lax.axis_index("dp") & bit) != 0
+        keep, give = halves(value, axis, side)
+        value = keep + flip(give, "dp", bit)
+    return value
+
+
+def join(value, axis, bits):
+    for bit in reversed(bits):
+        side = (lax.axis_index("dp") & bit) != 0
+        other = flip(value, "dp", bit)
+        value = jnp.concatenate(
+            [jnp.where(side, other, value), jnp.where(side, value, other)], axis
+        )
+    return value
+
+
+def spread(value):
+    count = lax.axis_size("expert")
+    return lax.all_to_all(
+        jnp.broadcast_to(value[None], (count, *value.shape)),
+        "expert",
+        split_axis=0,
+        concat_axis=0,
+        tiled=True,
+    )
+
+
+def gather_packed(value):
+    core = (lax.axis_index("dp") & 1) != 0
+    mine, unused = halves(value, 1, core)
+    return join(spread(mine), 2, [1])
+
+
+def expert_scatter(value):
+    return jnp.sum(
+        lax.all_to_all(value, "expert", split_axis=0, concat_axis=0, tiled=True), 0
+    )
 
 
 def shards(
@@ -117,15 +182,30 @@
 ):
     coarse_float_kind = jnp.bfloat16
     fine_float_kind = jnp.float32
-    vec_low, input_low, output_low, router_low, shin_low, shout_low, readout_bfloat = (
-        lax.all_gather(vectors.astype(coarse_float_kind), "expert", axis=1, tiled=True),
-        lax.all_gather(attend_input.astype(coarse_float_kind), "expert", axis=0, tiled=True),
-        lax.all_gather(attend_output.astype(coarse_float_kind), "expert", axis=0, tiled=True),
-        lax.all_gather(router.astype(coarse_float_kind), "expert", axis=0, tiled=True),
-        lax.all_gather(shared_input.astype(coarse_float_kind), "expert", axis=0, tiled=True),
-        lax.all_gather(shared_output.astype(coarse_float_kind), "expert", axis=0, tiled=True),
-        lax.all_gather(horizon.astype(coarse_float_kind), "expert", axis=0, tiled=True),
-    )
+    expert_count = lax.axis_size("expert")
+    dp_bits = bits_of("dp")
+    local_rows = attend_input.shape[0]
+    head_columns = horizon.shape[1]
+    small = jnp.concatenate([router, horizon, vectors.T], 1).astype(coarse_float_kind)
+    small_columns = small.shape[1]
+    small = jnp.pad(small, ((0, 0), (0, 128 - small_columns)))
+    first_pack = gather_packed(
+        jnp.concatenate(
+            [
+                attend_input.astype(coarse_float_kind),
+                small,
+                attend_output.astype(coarse_float_kind),
+            ],
+            1,
+        )
+    ).reshape(D, -1)
+    input_low = first_pack[:, : 3 * D]
+    router_low = first_pack[:, 3 * D : 3 * D + EXPERTS + 1]
+    readout_bfloat = first_pack[:, 3 * D + EXPERTS + 1 : 3 * D + EXPERTS + 1 + head_columns]
+    vec_low = first_pack[:, 3 * D + small_columns - 5 : 3 * D + small_columns].T
+    output_low = first_pack[:, 3 * D + 128 :]
+    shin_low = gather_packed(shared_input.astype(coarse_float_kind)).reshape(D, -1)
+    shout_low = gather_packed(shared_output.astype(coarse_float_kind)).reshape(FFS, D)
     gain_rows = vec_low.astype(fine_float_kind)
     amount = points.shape[0]
     series, position, domain_of, valid_mask, observed_future = layout(
@@ -200,12 +280,22 @@
     ranked = jnp.sum((jnp.cumsum(expert_hot, 0) - expert_hot) * expert_hot, 1)
     slot_index = flat_routes * CAP + ranked
 
-    def slot_buffer(rows_out):
-        row_width = rows_out.shape[-1]
-        return jnp.zeros((EXPERTS * CAP, row_width), rows_out.dtype).at[slot_index].set(rows_out)
-
-    def send_out(rows_out):
-        buffer = slot_buffer(rows_out).reshape(EXPERTS, CAP, rows_out.shape[-1])
+    slots = jnp.arange(EXPERTS * CAP)
+    slot_pairs = slot_index.reshape(amount, 2)
+    slot_hot = [
+        (slots[:, None] == slot_pairs[None, :, k]).astype(coarse_float_kind) for k in range(2)
+    ]
+
+    def to_slots(first_rows, second_rows):
+        if second_rows is None:
+            buffer = jnp.dot(
+                slot_hot[0] + slot_hot[1], first_rows, preferred_element_type=fine_float_kind
+            )
+        else:
+            buffer = jnp.dot(
+                slot_hot[0], first_rows, preferred_element_type=fine_float_kind
+            ) + jnp.dot(slot_hot[1], second_rows, preferred_element_type=fine_float_kind)
+        buffer = buffer.astype(coarse_float_kind).reshape(EXPERTS, CAP, -1)
         return jnp.repeat(buffer, group_size, 0)
 
     def bring_back(returned):
@@ -215,7 +305,7 @@
     gate_up_low = expert_input.astype(coarse_float_kind)
     down_low = expert_output.astype(coarse_float_kind)
     arrived = lax.all_to_all(
-        send_out(jnp.repeat(second_low, 2, 0)), "expert", split_axis=0, concat_axis=0, tiled=True
+        to_slots(second_low, None), "expert", split_axis=0, concat_axis=0, tiled=True
     ).reshape(-1, D)
     expert_gate = jnp.dot(arrived, gate_up_low[0], preferred_element_type=fine_float_kind)
     expert_lift = jnp.dot(arrived, gate_up_low[1], preferred_element_type=fine_float_kind)
@@ -258,7 +348,8 @@
     )
     local_counts = jnp.sum(domain_onehot_rows * jnp.sum(valid_mask, -1)[:, None], 0)
     local_sums = jnp.sum(domain_onehot_rows * sample_penalty[:, None], 0)
-    counts, domain_sums = lax.psum((local_counts, local_sums), ("dp", "expert"))
+    counts = sum_small(local_counts, ("dp", "expert"))
+    domain_sums = sum_small(local_sums, ("dp", "expert"))
     domain_weighting = domain_weights / jnp.maximum(counts, 1.0)
     (prediction_slope,) = smooth_absolute_backward(
         jnp.sum(domain_onehot_rows * domain_weighting[None, :], 1)
@@ -275,7 +366,7 @@
     grad_gates = jnp.sum(grad_mixer[:, None, :] * picked, -1)
     grad_picked = (gate_values[:, :, None] * grad_mixer[:, None, :]).astype(coarse_float_kind)
     received = lax.all_to_all(
-        send_out(grad_picked.reshape(-1, D)), "expert", split_axis=0, concat_axis=0, tiled=True
+        to_slots(grad_picked[:, 0], grad_picked[:, 1]), "expert", split_axis=0, concat_axis=0, tiled=True
     ).reshape(-1, D)
     grad_hidden = jnp.dot(received, down_low.T, preferred_element_type=fine_float_kind)
     grad_expert_out = jnp.dot(expert_hidden.T, received, preferred_element_type=fine_float_kind)
@@ -293,16 +384,28 @@
     grad_rows = jnp.dot(
         grad_gate, gate_up_low[0].T, preferred_element_type=fine_float_kind
     ) + jnp.dot(grad_lift, gate_up_low[1].T, preferred_element_type=fine_float_kind)
-    grad_routed = bring_back(
-        lax.all_to_all(
-            grad_rows.reshape(expert_devices, -1, D).astype(jnp.bfloat16),
-            "expert",
-            split_axis=0,
-            concat_axis=0,
-            tiled=True,
-        ).astype(jnp.float32)
-    )
-    grad_second = jnp.sum(grad_routed, 1)
+    routed_back = lax.all_to_all(
+        grad_rows.reshape(expert_devices, -1, D).astype(jnp.bfloat16),
+        "expert",
+        split_axis=0,
+        concat_axis=0,
+        tiled=True,
+    )
+    if group_size > 1:
+        routed_back = jnp.sum(
+            routed_back.reshape(EXPERTS, group_size, CAP, D).astype(fine_float_kind), 1
+        )
+        grad_second = jnp.dot(
+            (slot_hot[0] + slot_hot[1]).T.astype(fine_float_kind),
+            routed_back.reshape(-1, D),
+            precision=lax.Precision.HIGHEST,
+        )
+    else:
+        grad_second = jnp.dot(
+            (slot_hot[0] + slot_hot[1]).T,
+            routed_back.reshape(-1, D),
+            preferred_element_type=fine_float_kind,
+        )
     grad_shared_hidden = jnp.dot(
         grad_shared_low, shout_low.T, preferred_element_type=fine_float_kind
     )
@@ -357,30 +460,40 @@
     grad_vectors = jnp.stack(
         [grad_gain_gate, grad_gain_value, grad_gain_one, grad_gain_two, grad_gain_three]
     )
-    summed = lax.psum(
-        (
-            grad_vectors,
-            grad_input,
-            grad_output,
-            grad_router,
-            grad_shin,
-            grad_shout,
-            head_gradient,
-            grad_expert_in,
-            grad_expert_out,
-        ),
-        "dp",
-    )
-    shares = (
-        lax.psum_scatter(summed[0], "expert", scatter_dimension=1, tiled=True),
-        lax.psum_scatter(summed[1], "expert", scatter_dimension=0, tiled=True),
-        lax.psum_scatter(summed[2], "expert", scatter_dimension=0, tiled=True),
-        lax.psum_scatter(summed[3], "expert", scatter_dimension=0, tiled=True),
-        lax.psum_scatter(summed[4], "expert", scatter_dimension=0, tiled=True),
-        lax.psum_scatter(summed[5], "expert", scatter_dimension=0, tiled=True),
-        lax.psum_scatter(summed[6], "expert", scatter_dimension=0, tiled=True),
-    )
-    gradients = tuple(shares) + (summed[7], summed[8])
+    parts = scatter_sum(grad_expert_in.reshape(-1, grad_expert_in.shape[-1]), 0, dp_bits)
+    expert_in_total = join(parts, 0, dp_bits).reshape(grad_expert_in.shape)
+    expert_out_total = join(scatter_sum(grad_expert_out, 0, dp_bits), 0, dp_bits)
+    shin_total = join(
+        expert_scatter(scatter_sum(grad_shin.reshape(expert_count, local_rows, -1), 2, dp_bits)),
+        1,
+        dp_bits,
+    )
+    shout_total = join(
+        expert_scatter(scatter_sum(grad_shout.reshape(expert_count, -1, D), 1, dp_bits)),
+        0,
+        dp_bits,
+    )
+    small_gradient = jnp.concatenate([grad_router, head_gradient, grad_vectors.T], 1)
+    small_gradient = jnp.pad(small_gradient, ((0, 0), (0, 128 - small_columns)))
+    last_pack = jnp.concatenate([grad_input, small_gradient, grad_output], 1)
+    last_part = expert_scatter(
+        scatter_sum(last_pack.reshape(expert_count, local_rows, -1), 2, [1])
+    )
+    for bit in dp_bits[1:]:
+        last_part = last_part + flip(last_part, "dp", bit)
+    last_total = join(last_part, 1, [1])
+    edge = 3 * D + EXPERTS + 1
+    gradients = (
+        last_total[:, edge + head_columns : edge + head_columns + 5].T,
+        last_total[:, : 3 * D],
+        last_total[:, 3 * D + 128 :],
+        last_total[:, 3 * D : edge],
+        shin_total,
+        shout_total,
+        last_total[:, edge : edge + head_columns],
+        expert_in_total,
+        expert_out_total,
+    )
     masters = (
         vectors,
         attend_input,
@@ -415,7 +528,7 @@
         square_expert_output,
     )
     local_square = jnp.sum(jnp.stack([jnp.sum(gradient * gradient) for gradient in gradients]))
-    grad_norm = jnp.sqrt(lax.psum(local_square, "expert"))
+    grad_norm = jnp.sqrt(sum_small(local_square.reshape(1), ("expert",))[0])
     factor = jnp.minimum(1.0, CLIP / grad_norm)
     moments_new = []
     directions = []
@@ -434,7 +547,8 @@
         moments_new.append((moment_new, square_new))
     weight_square = jnp.stack([jnp.sum(master * master) for master in masters])
     update_square = jnp.stack([jnp.sum(direction * direction) for direction in directions])
-    weight_square, update_square = lax.psum((weight_square, update_square), "expert")
+    weight_square = sum_small(weight_square, ("expert",))
+    update_square = sum_small(update_square, ("expert",))
     weight_norm = jnp.sqrt(weight_square)
     update_norm = jnp.sqrt(update_square)
     results = []

time: 1280 us -> 610 us (0.48)
  waiting for transfers between devices: 579 us -> 177 us
  blocking collectives: 336 us -> 0 us
  starting transfers between devices: 26.9 us -> 98.5 us
  other arithmetic: 103 us -> 126 us
    reduce_scatter x5 -> x0, waiting for transfers between devices: 256 us -> none  [the longest x1 97.7 us: shards(): lax.psum_scatter(summed[4], 'expert', scatter_dimension=0, tiled=True)]
    all_gather x5 -> x0, blocking collectives: 206 us -> none  [the longest x1 84 us: shards(): lax.all_gather(router.astype(coarse_float_kind), 'expert', axis=0, tiled=...]
    psum x5 -> x0, blocking collectives: 130 us -> none  [the longest x2 79.8 us: shards(): counts, domain_sums = lax.psum((local_counts, local_sums), ('dp', 'expert'))]
    unnamed x12 -> x0, waiting for transfers between devices: 128 us -> none
    psum x1 -> x0, waiting for transfers between devices: 85.4 us -> none  [shards(): lax.psum((grad_vectors, grad_input, grad_output, grad_router, grad_shin,...]
    ppermute x0 -> x41, waiting for transfers between devices: none -> 75 us  [flip(): return lax.ppermute(value, axis_name, [(i, i ^ bit) for i in range(count)])]
    ppermute x0 -> x41, starting transfers between devices: none -> 46.3 us  [flip(): return lax.ppermute(value, axis_name, [(i, i ^ bit) for i in range(count)])]
    all_to_all x1, waiting for transfers between devices: 42.8 us -> 1.2 us  [shards(): lax.all_to_all(grad_rows.reshape(expert_devices, -1, D).astype(jnp.bfloat...]
  transfers between devices with their start and end apart: 14 -> 51, of which waited for: 10 -> 27; matrix products, arithmetic and copies ran while one was open for 11% -> 30% of each run, Pallas kernels for 0% -> 0%
where the time goes in v1:
time: 610 us; the launch traced here: 599 us
  waiting for transfers between devices  177 us (29%)
  other arithmetic  126 us (21%)
  starting transfers between devices  98.5 us (16%)
  matrix products  96.6 us (16%)
  local copies, waits for them, and re-layouts  77.3 us (13%)
  between operations  24.2 us (4%)
    ppermute x41, waiting for transfers between devices, flip(): return lax.ppermute(value, axis_name, [(i, i ^ bit) for i in range(count)])  75 us
    ppermute x41, starting transfers between devices, flip(): return lax.ppermute(value, axis_name, [(i, i ^ bit) for i in range(count)])  46.3 us
    all_to_all x1, waiting for transfers between devices, shards(): lax.all_to_all(expert_rows.reshape(expert_devices, -1, D), 'expert', spli...  39.1 us
    all_to_all x1, waiting for transfers between devices, shards(): lax.all_to_all(to_slots(second_low, None), 'expert', split_axis=0, concat...  37.2 us
    unnamed x370, local copies, waits for them, and re-layouts  36.5 us
    all_to_all x3, waiting for transfers between devices, spread(): lax.all_to_all(jnp.broadcast_to(value[None], (count, *value.shape)), 'exp...  24.8 us
    reduce_sum x9, other arithmetic, shards(): jnp.sum(direction * direction)  24.6 us
    all_to_all x3, starting transfers between devices, expert_scatter(): lax.all_to_all(value, 'expert', split_axis=0, concat_axis=0, tiled=True)  17.2 us
  transfers between devices with their start and end apart: 51, of which 27 were waited for; matrix products, arithmetic and copies ran while one was open for 30% of the time, Pallas kernels for 0%

profile of v1, /device:TPU:0, one launch (start us, length us, event | category | flops | bytes accessed | tf_op | source)
XLA Modules:
  0.0 599.5 jit_solution(10481843376052739950)
XLA Ops:
  7.0 7.3 %all-to-all-start = ((bf16[8,48,832]{2,1,0:T(8,128)(2,1)}), bf16[8,48,832]{2,1,0:T(8,128)(2,1)S(1)}, u32[]{:S(2)}, u32[]{:S(2)}) async-start(bf16[8,48,832]{2,1,0:T(8,128)(2,1)} %broadcast_in_dim.74), calls=%async_computation | async-start | bytes 1376256 | tf_op jit(solution)/shard_map/all_to_all | solution.py:128
  20.0 12.3 %all-to-all-done = bf16[8,48,832]{2,1,0:T(8,128)(2,1)S(1)} async-done(((bf16[8,48,832]{2,1,0:T(8,128)(2,1)}), bf16[8,48,832]{2,1,0:T(8,128)(2,1)S(1)}, u32[]{:S(2)}, u32[]{:S(2)}) %all-to-all-start) | async-done | bytes 639008 | tf_op jit(solution)/shard_map/all_to_all | solution.py:128
  33.2 3.8 all-to-all-start.2
  50.9 4.6 fusion.39
  61.4 6.3 %all-to-all-start.3 = ((bf16[8,256,384]{2,1,0:T(8,128)(2,1)}), bf16[8,256,384]{2,1,0:T(8,128)(2,1)}, u32[]{:S(2)}, u32[]{:S(2)}) async-start(bf16[8,256,384]{2,1,0:T(8,128)(2,1)} %bitcast.267), calls=%async_computation.3 | async-start | bytes 3145728 | tf_op jit(solution)/shard_map/all_to_all | solution.py:307
  67.7 37.2 %all-to-all-done.3 = bf16[8,256,384]{2,1,0:T(8,128)(2,1)} async-done(((bf16[8,256,384]{2,1,0:T(8,128)(2,1)}), bf16[8,256,384]{2,1,0:T(8,128)(2,1)}, u32[]{:S(2)}, u32[]{:S(2)}) %all-to-all-start.3) | async-done | bytes 1572896 | tf_op jit(solution)/shard_map/all_to_all | solution.py:307
  106.1 3.6 all-to-all-start.1
  109.9 3.6 fusion.56
  113.5 7.3 %multiply_convert_fusion.2 = (bf16[2048,768]{1,0:T(8,128)(2,1)S(1)}, f32[2048,768]{1,0:T(8,128)}) fusion(f32[2048,768]{1,0:T(8,128)S(1)} %fusion.56, bf16[2048,384]{1,0:T(8,128)(2,1)} %bitcast.27, bf16[2,384,768]{2,1,0:T(8,128)(2,1)S(1)} %convert_element_type.163), kind=kOutput, calls=%fused_computation.17 | convolution fusion | flops 1217396736 | bytes 17891328 | tf_op jit(solution)/shard_map/dot_general | solution.py:311
  122.6 3.5 fusion.63
  126.1 12.5 %all-to-all-done.1 = bf16[8,48,1536]{2,1,0:T(8,128)(2,1)S(1)} async-done(((bf16[8,48,1536]{2,1,0:T(8,128)(2,1)}), bf16[8,48,1536]{2,1,0:T(8,128)(2,1)S(1)}, u32[]{:S(2)}, u32[]{:S(2)}) %all-to-all-start.1) | async-done | bytes 1179680 | tf_op jit(solution)/shard_map/all_to_all | solution.py:128
  139.5 3.6 all-to-all-start.4
  154.9 3.1 stack.368
  175.0 39.1 %all-to-all-done.4 = f32[8,256,384]{2,1,0:T(8,128)S(1)} async-done(((f32[8,256,384]{2,1,0:T(8,128)}), f32[8,256,384]{2,1,0:T(8,128)S(1)}, u32[]{:S(2)}, u32[]{:S(2)}) %all-to-all-start.4) | async-done | bytes 3145760 | tf_op jit(solution)/shard_map/all_to_all | solution.py:315
  214.0 5.0 gather_fusion
  226.1 3.0 multiply_reduce_fusion.17
  239.0 3.5 collective-permute-done.9
  243.4 3.6 collective-permute-done.10
  251.3 3.7 fusion.17
  266.3 4.3 all-to-all-start.5
  270.6 3.3 fusion.30
  284.8 11.9 %collective-permute-done.37 = f32[9]{0:T(128)S(1)} collective-permute-done((f32[9]{0:T(128)S(1)}, f32[9]{0:T(128)S(1)}, u32[]{:S(2)}, u32[]{:S(2)}) %collective-permute-start.37) | collective-permute-done | bytes 68 | tf_op jit(solution)/shard_map/ppermute | solution.py:86
  309.8 6.1 %all-to-all-start.9 = ((f32[8,48,384]{2,1,0:T(8,128)}), f32[8,48,384]{2,1,0:T(8,128)}, u32[]{:S(2)}, u32[]{:S(2)}) async-start(f32[8,48,384]{2,1,0:T(8,128)} %select_add_fusion.7), calls=%async_computation.9 | async-start | bytes 1179648 | tf_op jit(solution)/shard_map/all_to_all | solution.py:145
  315.9 8.0 %multiply_convert_fusion.1 = (bf16[2048,768]{1,0:T(8,128)(2,1)S(1)}, bf16[2048,768]{1,0:T(8,128)(2,1)S(1)}) fusion(f32[2048,768]{1,0:T(8,128)} %copy-done.15, f32[2048,768]{1,0:T(8,128)} %get-tuple-element.500, bf16[2048,384]{1,0:T(8,128)(2,1)} %bitcast.103, f32[768,384]{1,0:T(8,128)S(1)} %copy-done.33), kind=kOutput, calls=%fused_computation.16 | convolution fusion | flops 1230274560 | bytes 21626880 | tf_op jit(solution)/shard_map/dot_general | solution.py:371
  326.5 3.1 add_convert_fusion
  329.6 5.9 all-to-all-start.6
  335.6 3.9 select_add_fusion
  342.2 3.2 fusion.152
  350.3 4.7 broadcast_select_fusion.8
  357.6 8.7 %collective-permute-done.15 = f32[8,48,768]{2,1,0:T(8,128)} collective-permute-done((f32[8,48,768]{2,1,0:T(8,128)}, f32[8,48,768]{2,1,0:T(8,128)}, u32[]{:S(2)}, u32[]{:S(2)}) %collective-permute-start.15) | collective-permute-done | bytes 1179680 | tf_op jit(solution)/shard_map/ppermute | solution.py:86
  370.1 5.0 all-to-all-start.8
  378.0 3.4 fusion.38
  384.0 3.1 fusion.33
  387.1 7.8 %multiply_reduce_fusion = (f32[12,512]{1,0:T(8,128)S(1)}, f32[12,512,512]{1,2,0:T(8,128)}) fusion(f32[12,512]{1,0:T(8,128)S(1)} %copy-done.101, f32[12,512,512]{1,2,0:T(8,128)S(1)} %bitcast.237, pred[512,512]{0,1:T(8,128)(4,1)S(1)} %copy-done.39, bf16[512,12,32]{0,2,1:T(8,128)(2,1)S(1)} %bitcast.269, f32[512,3,12,32]{0,3,2,1:T(8,128)} %bitcast.264), kind=kOutput, calls=%fused_computation.3 | convolution fusion | flops 217049088 | bytes 26263552 | tf_op jit(solution)/shard_map/qhd,khd->hqk/dot_general | solution.py:443
  394.9 7.0 %multiply_convert_fusion = bf16[12,512,512]{1,2,0:T(8,128)(2,1)S(1)} fusion(f32[12,512,512]{1,2,0:T(8,128)} %get-tuple-element.506, f32[12,512]{1,0:T(8,128)S(1)} %get-tuple-element.505, f32[12,512]{1,0:T(8,128)S(1)} %copy-done.101, f32[12,512,512]{1,2,0:T(8,128)S(1)} %bitcast.237, pred[512,512]{0,1:T(8,128)(4,1)S(1)} %copy-done.39), kind=kLoop, calls=%fused_computation.2 | loop fusion | flops 18874368 | bytes 31768576 | tf_op jit(solution)/shard_map/convert_element_type | solution.py:448
  422.2 6.1 %all-to-all-start.7 = ((f32[8,48,832]{2,1,0:T(8,128)}), f32[8,48,832]{2,1,0:T(8,128)S(1)}, u32[]{:S(2)}, u32[]{:S(2)}) async-start(f32[8,48,832]{2,1,0:T(8,128)} %select_add_fusion.1), calls=%async_computation.7 | async-start | bytes 2752512 | tf_op jit(solution)/shard_map/all_to_all | solution.py:145
  428.4 10.3 %collective-permute-done.27 = f32[192,384]{1,0:T(8,128)} collective-permute-done((f32[192,384]{1,0:T(8,128)}, f32[192,384]{1,0:T(8,128)}, u32[]{:S(2)}, u32[]{:S(2)}) %collective-permute-start.27) | collective-permute-done | bytes 294944 | tf_op jit(solution)/shard_map/ppermute | solution.py:86
  444.7 5.0 collective-permute-done.28
  453.5 8.4 %collective-permute-done.24 = f32[192,768]{1,0:T(8,128)S(1)} collective-permute-done((f32[192,768]{1,0:T(8,128)S(1)}, f32[192,768]{1,0:T(8,128)S(1)}, u32[]{:S(2)}, u32[]{:S(2)}) %collective-permute-start.24) | collective-permute-done | bytes 589856 | tf_op jit(solution)/shard_map/ppermute | solution.py:86
  471.6 8.5 %collective-permute-done.12 = f32[48,832]{0,1:T(8,128)S(1)} collective-permute-done((f32[48,832]{0,1:T(8,128)S(1)}, f32[48,832]{0,1:T(8,128)S(1)}, u32[]{:S(2)}, u32[]{:S(2)}) %collective-permute-start.12) | collective-permute-done | bytes 159776 | tf_op jit(solution)/shard_map/ppermute | solution.py:86
  494.0 3.4 collective-permute-start.30
  498.2 3.4 collective-permute-start.31
  502.5 4.3 collective-permute-start.32
  524.5 3.3 multiply_reduce_fusion.20
  527.9 4.5 multiply_reduce_fusion.6
  532.4 4.7 multiply_reduce_fusion.1
  537.1 6.4 %stack.303 = f32[9]{0:T(128)} concatenate(f32[1]{0:T(128)} %bitcast, f32[1]{0:T(128)} %bitcast.1, f32[1]{0:T(128)} %bitcast.2, f32[1]{0:T(128)} %bitcast.3, f32[1]{0:T(128)} %bitcast.4, f32[1]{0:T(128)} %bitcast.5, f32[1]{0:T(128)} %bitcast.6, f32[1]{0:T(128)} %bitcast.7, f32[1]{0:T(128)} %bitcast.8), dimensions={0} | concatenate | bytes 72 | tf_op jit(solution)/shard_map/stack | solution.py:548
  545.6 6.2 %stack.379 = f32[9]{0:T(128)} concatenate(f32[1]{0:T(128)} %bitcast.123, f32[1]{0:T(128)} %bitcast.124, f32[1]{0:T(128)} %bitcast.125, f32[1]{0:T(128)} %bitcast.126, f32[1]{0:T(128)} %bitcast.127, f32[1]{0:T(128)} %bitcast.128, f32[1]{0:T(128)} %bitcast.129, f32[1]{0:T(128)} %bitcast.131, f32[1]{0:T(128)} %bitcast.132), dimensions={0} | concatenate | bytes 72 | tf_op jit(solution)/shard_map/stack | solution.py:549
  (655 shorter events, 244.6 us)
Async XLA Ops:
  7.0 25.3 %all-to-all-start = ((bf16[8,48,832]{2,1,0:T(8,128)(2,1)}), bf16[8,48,832]{2,1,0:T(8,128)(2,1)S(1)}, u32[]{:S(2)}, u32[]{:S(2)}) async-start(bf16[8,48,832]{2,1,0:T(8,128)(2,1)} %broadcast_in_dim.74), calls=%async_computation | async-start | bytes 1376256 | tf_op jit(solution)/shard_map/all_to_all | solution.py:128
  33.2 27.3 %all-to-all-start.2 = ((bf16[8,192,192]{2,1,0:T(8,128)(2,1)}), bf16[8,192,192]{2,1,0:T(8,128)(2,1)S(1)}, u32[]{:S(2)}, u32[]{:S(2)}) async-start(bf16[8,192,192]{2,1,0:T(8,128)(2,1)} %broadcast_in_dim.81), calls=%async_computation.2 | async-start | bytes 1572864 | tf_op jit(solution)/shard_map/all_to_all | solution.py:128
  61.4 43.6 %all-to-all-start.3 = ((bf16[8,256,384]{2,1,0:T(8,128)(2,1)}), bf16[8,256,384]{2,1,0:T(8,128)(2,1)}, u32[]{:S(2)}, u32[]{:S(2)}) async-start(bf16[8,256,384]{2,1,0:T(8,128)(2,1)} %bitcast.267), calls=%async_computation.3 | async-start | bytes 3145728 | tf_op jit(solution)/shard_map/all_to_all | solution.py:307
  106.1 32.4 %all-to-all-start.1 = ((bf16[8,48,1536]{2,1,0:T(8,128)(2,1)}), bf16[8,48,1536]{2,1,0:T(8,128)(2,1)S(1)}, u32[]{:S(2)}, u32[]{:S(2)}) async-start(bf16[8,48,1536]{2,1,0:T(8,128)(2,1)} %broadcast_in_dim.80), calls=%async_computation.1 | async-start | bytes 2359296 | tf_op jit(solution)/shard_map/all_to_all | solution.py:128
  139.5 74.5 %all-to-all-start.4 = ((f32[8,256,384]{2,1,0:T(8,128)}), f32[8,256,384]{2,1,0:T(8,128)S(1)}, u32[]{:S(2)}, u32[]{:S(2)}) async-start(f32[8,256,384]{2,1,0:T(8,128)} %bitcast.252), calls=%async_computation.4 | async-start | bytes 6291456 | tf_op jit(solution)/shard_map/all_to_all | solution.py:315
  146.8 14.0 %collective-permute-start.5 = (bf16[8,192,192]{2,1,0:T(8,128)(2,1)}, bf16[8,192,192]{2,1,0:T(8,128)(2,1)}, u32[]{:S(2)}, u32[]{:S(2)}) collective-permute-start(bf16[8,192,192]{2,1,0:T(8,128)(2,1)} %copy-done.46), channel_id=1, source_target_pairs={{0,8},{8,0},{16,24},{24,16},{1,9},{9,1},{17,25},{25,17},{2,10},{10... | collective-permute-start | bytes 1769480 | tf_op jit(solution)/shard_map/ppermute | solution.py:86
  164.9 3.0 collective-permute-start.4
  231.9 3.5 collective-permute-start.7
  235.5 3.5 collective-permute-start.8
  239.0 3.5 collective-permute-start.9
  242.6 4.4 collective-permute-start.10
  258.3 25.3 %collective-permute-start.36 = (f32[9]{0:T(128)}, f32[9]{0:T(128)}, u32[]{:S(2)}, u32[]{:S(2)}) collective-permute-start(f32[9]{0:T(128)} %get-tuple-element.331), channel_id=1, source_target_pairs={{0,8},{8,0},{16,24},{24,16},{1,9},{9,1},{17,25},{25,17},{2,10},{10... | collective-permute-start | bytes 116 | tf_op jit(solution)/shard_map/ppermute | solution.py:86
  262.0 17.2 %collective-permute-start.18 = (f32[8,96,384]{2,1,0:T(8,128)}, f32[8,96,384]{2,1,0:T(8,128)}, u32[]{:S(2)}, u32[]{:S(2)}) collective-permute-start(f32[8,96,384]{2,1,0:T(8,128)} %slice_select_fusion.2), channel_id=1, source_target_pairs={{0,8},{8,0},{16,24},{24,16},{1,9},{9,1},{17,25},{25,17},{2,10},{10... | collective-permute-start | bytes 3538952 | tf_op jit(solution)/shard_map/ppermute | solution.py:86
  266.3 43.5 %all-to-all-start.5 = ((bf16[8,256,384]{2,1,0:T(8,128)(2,1)}), bf16[8,256,384]{2,1,0:T(8,128)(2,1)}, u32[]{:S(2)}, u32[]{:S(2)}) async-start(bf16[8,256,384]{2,1,0:T(8,128)(2,1)} %bitcast.265), calls=%async_computation.5 | async-start | bytes 3145728 | tf_op jit(solution)/shard_map/all_to_all | solution.py:368
  277.4 58.1 %collective-permute-start.14 = (f32[8,48,1536]{2,1,0:T(8,128)}, f32[8,48,1536]{2,1,0:T(8,128)}, u32[]{:S(2)}, u32[]{:S(2)}) collective-permute-start(f32[8,48,1536]{2,1,0:T(8,128)} %slice_select_fusion), channel_id=1, source_target_pairs={{0,8},{8,0},{16,24},{24,16},{1,9},{9,1},{17,25},{25,17},{2,10},{10... | collective-permute-start | bytes 7077896 | tf_op jit(solution)/shard_map/ppermute | solution.py:86
  280.9 28.0 %collective-permute-start.19 = (f32[8,48,384]{2,1,0:T(8,128)S(1)}, f32[8,48,384]{2,1,0:T(8,128)S(1)}, u32[]{:S(2)}, u32[]{:S(2)}) collective-permute-start(f32[8,48,384]{2,1,0:T(8,128)S(1)} %slice_select_fusion.6), channel_id=1, source_target_pairs={{0,16},{8,24},{16,0},{24,8},{1,17},{9,25},{17,1},{25,9},{2,18},{10... | collective-permute-start | bytes 1769480 | tf_op jit(solution)/shard_map/ppermute | solution.py:86
  284.3 12.4 %collective-permute-start.37 = (f32[9]{0:T(128)S(1)}, f32[9]{0:T(128)S(1)}, u32[]{:S(2)}, u32[]{:S(2)}) collective-permute-start(f32[9]{0:T(128)S(1)} %add.487), channel_id=1, source_target_pairs={{0,16},{8,24},{16,0},{24,8},{1,17},{9,25},{17,1},{25,9},{2,18},{10... | collective-permute-start | bytes 116 | tf_op jit(solution)/shard_map/ppermute | solution.py:86
  296.7 3.5 collective-permute-start.38
  300.3 3.5 collective-permute-start.39
  303.8 4.4 collective-permute-start.40
  309.8 19.8 %all-to-all-start.9 = ((f32[8,48,384]{2,1,0:T(8,128)}), f32[8,48,384]{2,1,0:T(8,128)}, u32[]{:S(2)}, u32[]{:S(2)}) async-start(f32[8,48,384]{2,1,0:T(8,128)} %select_add_fusion.7), calls=%async_computation.9 | async-start | bytes 1179648 | tf_op jit(solution)/shard_map/all_to_all | solution.py:145
  329.6 40.4 %all-to-all-start.6 = ((bf16[8,256,384]{2,1,0:T(8,128)(2,1)}), bf16[8,256,384]{2,1,0:T(8,128)(2,1)}, u32[]{:S(2)}, u32[]{:S(2)}) async-start(bf16[8,256,384]{2,1,0:T(8,128)(2,1)} %bitcast.266), calls=%async_computation.6 | async-start | bytes 3145728 | tf_op jit(solution)/shard_map/all_to_all | solution.py:387
  340.7 25.7 %collective-permute-start.15 = (f32[8,48,768]{2,1,0:T(8,128)}, f32[8,48,768]{2,1,0:T(8,128)}, u32[]{:S(2)}, u32[]{:S(2)}) collective-permute-start(f32[8,48,768]{2,1,0:T(8,128)} %slice_select_fusion.3), channel_id=1, source_target_pairs={{0,16},{8,24},{16,0},{24,8},{1,17},{9,25},{17,1},{25,9},{2,18},{10... | collective-permute-start | bytes 3538952 | tf_op jit(solution)/shard_map/ppermute | solution.py:86
  347.3 65.9 %collective-permute-start.26 = (f32[384,384]{1,0:T(8,128)}, f32[384,384]{1,0:T(8,128)}, u32[]{:S(2)}, u32[]{:S(2)}) collective-permute-start(f32[384,384]{1,0:T(8,128)} %slice_select_fusion.4), channel_id=1, source_target_pairs={{0,8},{8,0},{16,24},{24,16},{1,9},{9,1},{17,25},{25,17},{2,10},{10... | collective-permute-start | bytes 1769480 | tf_op jit(solution)/shard_map/ppermute | solution.py:86
  355.0 59.5 %collective-permute-start.22 = (f32[384,768]{1,0:T(8,128)}, f32[384,768]{1,0:T(8,128)}, u32[]{:S(2)}, u32[]{:S(2)}) collective-permute-start(f32[384,768]{1,0:T(8,128)} %get-tuple-element.508), channel_id=1, source_target_pairs={{0,8},{8,0},{16,24},{24,16},{1,9},{9,1},{17,25},{25,17},{2,10},{10... | collective-permute-start | bytes 3538952 | tf_op jit(solution)/shard_map/ppermute | solution.py:86
  356.5 56.2 %collective-permute-start.20 = (f32[48,384]{1,0:T(8,128)S(1)}, f32[48,384]{1,0:T(8,128)S(1)}, u32[]{:S(2)}, u32[]{:S(2)}) collective-permute-start(f32[48,384]{1,0:T(8,128)S(1)} %reduce_sum.690), channel_id=1, source_target_pairs={{0,16},{8,24},{16,0},{24,8},{1,17},{9,25},{17,1},{25,9},{2,18},{10... | collective-permute-start | bytes 221192 | tf_op jit(solution)/shard_map/ppermute | solution.py:86
  370.1 51.1 %all-to-all-start.8 = ((f32[8,48,768]{2,1,0:T(8,128)}), f32[8,48,768]{2,1,0:T(8,128)S(1)}, u32[]{:S(2)}, u32[]{:S(2)}) async-start(f32[8,48,768]{2,1,0:T(8,128)} %select_add_fusion.4), calls=%async_computation.8 | async-start | bytes 2359296 | tf_op jit(solution)/shard_map/all_to_all | solution.py:145
  412.5 7.2 %collective-permute-start.11 = (f32[8,48,832]{2,1,0:T(8,128)S(1)}, f32[8,48,832]{2,1,0:T(8,128)S(1)}, u32[]{:S(2)}, u32[]{:S(2)}) collective-permute-start(f32[8,48,832]{2,1,0:T(8,128)S(1)} %slice_select_fusion.1), channel_id=1, source_target_pairs={{0,8},{8,0},{16,24},{24,16},{1,9},{9,1},{17,25},{25,17},{2,10},{10... | collective-permute-start | bytes 3833864 | tf_op jit(solution)/shard_map/ppermute | solution.py:86
  412.7 30.4 %collective-permute-start.21 = (f32[96,384]{1,0:T(8,128)S(1)}, f32[96,384]{1,0:T(8,128)}, u32[]{:S(2)}, u32[]{:S(2)}) collective-permute-start(f32[96,384]{1,0:T(8,128)S(1)} %pad_maximum_fusion.25), channel_id=1, source_target_pairs={{0,8},{8,0},{16,24},{24,16},{1,9},{9,1},{17,25},{25,17},{2,10},{10... | collective-permute-start | bytes 442376 | tf_op jit(solution)/shard_map/ppermute | solution.py:86
  416.9 24.3 %collective-permute-start.23 = (f32[192,768]{1,0:T(8,128)}, f32[192,768]{1,0:T(8,128)}, u32[]{:S(2)}, u32[]{:S(2)}) collective-permute-start(f32[192,768]{1,0:T(8,128)} %slice_select_fusion.5), channel_id=1, source_target_pairs={{0,16},{8,24},{16,0},{24,8},{1,17},{9,25},{17,1},{25,9},{2,18},{10... | collective-permute-start | bytes 1769480 | tf_op jit(solution)/shard_map/ppermute | solution.py:86
  419.1 19.5 %collective-permute-start.27 = (f32[192,384]{1,0:T(8,128)}, f32[192,384]{1,0:T(8,128)}, u32[]{:S(2)}, u32[]{:S(2)}) collective-permute-start(f32[192,384]{1,0:T(8,128)} %slice_select_fusion.7), channel_id=1, source_target_pairs={{0,16},{8,24},{16,0},{24,8},{1,17},{9,25},{17,1},{25,9},{2,18},{10... | collective-permute-start | bytes 884744 | tf_op jit(solution)/shard_map/ppermute | solution.py:86
  422.2 45.7 %all-to-all-start.7 = ((f32[8,48,832]{2,1,0:T(8,128)}), f32[8,48,832]{2,1,0:T(8,128)S(1)}, u32[]{:S(2)}, u32[]{:S(2)}) async-start(f32[8,48,832]{2,1,0:T(8,128)} %select_add_fusion.1), calls=%async_computation.7 | async-start | bytes 2752512 | tf_op jit(solution)/shard_map/all_to_all | solution.py:145
  439.7 10.0 %collective-permute-start.28 = (f32[192,384]{1,0:T(8,128)S(1)}, f32[192,384]{1,0:T(8,128)S(1)}, u32[]{:S(2)}, u32[]{:S(2)}) collective-permute-start(f32[192,384]{1,0:T(8,128)S(1)} %select_add_fusion.8), channel_id=1, source_target_pairs={{0,16},{8,24},{16,0},{24,8},{1,17},{9,25},{17,1},{25,9},{2,18},{10... | collective-permute-start | bytes 884744 | tf_op jit(solution)/shard_map/ppermute | solution.py:86
  442.4 19.5 %collective-permute-start.24 = (f32[192,768]{1,0:T(8,128)S(1)}, f32[192,768]{1,0:T(8,128)S(1)}, u32[]{:S(2)}, u32[]{:S(2)}) collective-permute-start(f32[192,768]{1,0:T(8,128)S(1)} %select_add_fusion.6), channel_id=1, source_target_pairs={{0,16},{8,24},{16,0},{24,8},{1,17},{9,25},{17,1},{25,9},{2,18},{10... | collective-permute-start | bytes 1769480 | tf_op jit(solution)/shard_map/ppermute | solution.py:86
  450.6 14.3 %collective-permute-start.29 = (f32[384,384]{1,0:T(8,128)}, f32[384,384]{1,0:T(8,128)}, u32[]{:S(2)}, u32[]{:S(2)}) collective-permute-start(f32[384,384]{1,0:T(8,128)} %pad_maximum_fusion.13), channel_id=1, source_target_pairs={{0,8},{8,0},{16,24},{24,16},{1,9},{9,1},{17,25},{25,17},{2,10},{10... | collective-permute-start | bytes 1769480 | tf_op jit(solution)/shard_map/ppermute | solution.py:86
  452.0 12.3 %collective-permute-start.16 = (f32[48,768]{1,0:T(8,128)S(1)}, f32[48,768]{1,0:T(8,128)S(1)}, u32[]{:S(2)}, u32[]{:S(2)}) collective-permute-start(f32[48,768]{1,0:T(8,128)S(1)} %reduce_sum.687), channel_id=1, source_target_pairs={{0,16},{8,24},{16,0},{24,8},{1,17},{9,25},{17,1},{25,9},{2,18},{10... | collective-permute-start | bytes 442376 | tf_op jit(solution)/shard_map/ppermute | solution.py:86
  464.3 15.9 %collective-permute-start.25 = (f32[384,768]{1,0:T(8,128)}, f32[384,768]{1,0:T(8,128)}, u32[]{:S(2)}, u32[]{:S(2)}) collective-permute-start(f32[384,768]{1,0:T(8,128)} %pad_maximum_fusion.10), channel_id=1, source_target_pairs={{0,8},{8,0},{16,24},{24,16},{1,9},{9,1},{17,25},{25,17},{2,10},{10... | collective-permute-start | bytes 3538952 | tf_op jit(solution)/shard_map/ppermute | solution.py:86
  464.3 5.5 collective-permute-start.17
  468.2 11.8 %collective-permute-start.12 = (f32[48,832]{0,1:T(8,128)S(1)}, f32[48,832]{0,1:T(8,128)S(1)}, u32[]{:S(2)}, u32[]{:S(2)}) collective-permute-start(f32[48,832]{0,1:T(8,128)S(1)} %copy.474), channel_id=1, source_target_pairs={{0,16},{8,24},{16,0},{24,8},{1,17},{9,25},{17,1},{25,9},{2,18},{10... | collective-permute-start | bytes 479240 | tf_op jit(solution)/shard_map/ppermute | solution.py:86
  494.0 3.6 collective-permute-start.30
  498.2 3.6 collective-permute-start.31
  502.5 4.5 collective-permute-start.32
  543.5 8.3 %collective-permute-start = (f32[9]{0:T(128)}, f32[9]{0:T(128)}, u32[]{:S(2)}, u32[]{:S(2)}) collective-permute-start(f32[9]{0:T(128)} %stack.303), channel_id=1, source_target_pairs={{0,1},{1,0},{2,3},{3,2},{4,5},{5,4},{6,7},{7,6},{8,9},{9,8},{10,11... | collective-permute-start | bytes 116 | tf_op jit(solution)/shard_map/ppermute | solution.py:86
  551.8 3.7 collective-permute-start.33
  552.5 5.1 collective-permute-start.1
  556.1 3.8 collective-permute-start.34
  557.6 4.4 collective-permute-start.2
  560.0 4.4 collective-permute-start.35
  (181 other events, 1487.3 us)

commit v2 on v0

v2 whole, which is shorter than its diff:
```python
import functools

import jax
import jax.numpy as jnp
import numpy as np
from jax import lax
from jax.experimental import pallas as pl
from jax.experimental.pallas import tpu as pltpu
from jax.sharding import PartitionSpec as P

D = 384
HEADS = 12
HD = 32
FFS = 1536
EXPERTS = 8
DOMAINS = 9
STEP = 10
CAP = 256


HORIZONS = (1, 8, 32, 64)
REACH = 64
KINK_THRESHOLD = 2.0
EPS_NORM = 1e-06
CLIP = 0.01
BETA_ONE = 0.9
BETA_TWO = 0.99
EPS_ADAM = 1e-08
DECAY = 0.01
RATE = 0.3


def ahead_table():
    return np.concatenate([np.arange(horizon_len) for horizon_len in HORIZONS]).astype(np.int32)


def target_columns(samples):
    amount = samples.shape[0]
    padded = jnp.concatenate([samples, jnp.zeros((REACH + 1,), samples.dtype)])
    future = jnp.stack([padded[1 + offset : 1 + offset + amount] for offset in range(REACH)], 1)
    return future[:, ahead_table()]


ROW_BLOCK = 256
SMALL = 128
HORIZON_AT = EXPERTS + 1
VECTORS_AT = 120
SMALL_AT = 4 * D
COUNTS_AT = 125
CODE_ROWS = 16
VMEM = 56 * 1024 * 1024
F32 = jnp.float32
BF16 = jnp.bfloat16


def mm(left, right):
    return jnp.dot(left, right, preferred_element_type=F32)


def mm_nt(left, right):
    return lax.dot_general(left, right, (((1,), (1,)), ((), ())), preferred_element_type=F32)


def mm_tn(left, right):
    return lax.dot_general(left, right, (((0,), (0,)), ((), ())), preferred_element_type=F32)


def inverse_rms(rows):
    return lax.rsqrt(jnp.mean(rows * rows, axis=-1, keepdims=True) + EPS_NORM)


def rms_back(rows, inverse, gain, slope):
    gain_slope = jnp.sum(slope * rows * inverse, 0, keepdims=True)
    scaled = slope * gain
    return (
        inverse * scaled
        - rows * (inverse * inverse * inverse) * jnp.mean(rows * scaled, -1, keepdims=True),
        gain_slope,
    )


def lanes_of(shape):
    return lax.broadcasted_iota(jnp.int32, shape, len(shape) - 1)


def half_swap(rows):
    half_width = HD // 2
    lane = lanes_of(rows.shape)
    return jnp.where(
        lane % HD < half_width,
        pltpu.roll(rows, rows.shape[1] - half_width, 1),
        pltpu.roll(rows, half_width, 1),
    )


SLOT, SERIES_OF, FINISH, DOMAIN, CHOICE, VALUE, PLACE = 0, 2, 3, 4, 5, 7, 8


def tables_kernel(
    lengths, domains, frequency, points_row, experts_row, cosine, sine, columns_out, rows_out
):
    amount = points_row.shape[1]
    place = lax.broadcasted_iota(jnp.int32, (1, amount), 1)
    series = jnp.zeros((1, amount), jnp.int32)
    begin = jnp.zeros((1, amount), jnp.int32)
    finish = jnp.zeros((1, amount), jnp.int32)
    domain = jnp.zeros((1, amount), jnp.int32)
    start = jnp.int32(0)
    for index in range(lengths.shape[1]):
        stop = start + lengths[0, index]
        inside = (place >= start) & (place < stop)
        series = jnp.where(inside, index, series)
        begin = jnp.where(inside, start, begin)
        finish = jnp.where(inside, stop, finish)
        domain = jnp.where(inside, domains[0, index], domain)
        start = stop
    name = lax.broadcasted_iota(jnp.int32, (16, amount), 0)
    choices = [experts_row[k : k + 1, :] for k in range(2)]
    named = [(name == choice).astype(F32) for choice in choices]
    earlier = (
        lax.broadcasted_iota(jnp.int32, (amount, amount), 0)
        < lax.broadcasted_iota(jnp.int32, (amount, amount), 1)
    )
    before = mm((named[0] + named[1]).astype(BF16), earlier.astype(F32).astype(BF16))
    entries = []
    for k in range(2):
        rank = jnp.sum(named[k] * before, 0, keepdims=True)
        entries.append(choices[k].astype(F32) * CAP + rank)
    entries += [series, finish, domain, *choices, points_row[...], place - begin]
    row = lax.broadcasted_iota(jnp.int32, (128, amount), 0)
    table = jnp.zeros((128, amount), F32)
    for index, entry in enumerate(entries):
        table = jnp.where(row == index, entry.astype(F32), table)
    rows_out[...] = table[:8]
    columns = table.T
    columns_out[...] = columns
    angles = columns[:, PLACE : PLACE + 1] * frequency[...]
    cosine[...] = jnp.cos(angles)
    turned = jnp.sin(angles)
    sine[...] = jnp.where(lanes_of((amount, 128)) % HD < HD // 2, -turned, turned)


def allowed_block(table, rows_table, start, rows, keys):
    query = start + lax.broadcasted_iota(jnp.int32, (rows, keys), 0)
    key = lax.broadcasted_iota(jnp.int32, (rows, keys), 1)
    series_col = table[start : start + rows, SERIES_OF : SERIES_OF + 1]
    return (series_col == rows_table[SERIES_OF : SERIES_OF + 1, :keys]) & (key <= query)


def slot_rows_hot(slot_row, expert):
    slot = expert * CAP + lax.broadcasted_iota(jnp.int32, (CAP, slot_row.shape[1]), 0)
    return (slot_row.astype(jnp.int32) == slot).astype(F32).astype(BF16)


def slot_cols_hot(slot_col, expert):
    slot = expert * CAP + lax.broadcasted_iota(jnp.int32, (slot_col.shape[0], CAP), 1)
    return (slot_col.astype(jnp.int32) == slot).astype(F32).astype(BF16)


def pack_kernel(small_end, core, lengths, domains, ahead, input_w, output_w, router, horizon, vectors, out):
    rows = input_w.shape[0]

    def placed(count, at):
        row = lax.broadcasted_iota(jnp.int32, (count, SMALL), 0)
        return (row + at == lanes_of((count, SMALL))).astype(F32).astype(BF16)

    small = (
        mm_tn(router[...].astype(BF16), placed(HORIZON_AT, 0))
        + mm(horizon[...].astype(BF16), placed(small_end - HORIZON_AT, HORIZON_AT))
        + mm_tn(vectors[...].astype(BF16), placed(vectors.shape[0], VECTORS_AT))
    )
    row = lax.broadcasted_iota(jnp.int32, (rows, SMALL), 0)
    lane = lanes_of((rows, SMALL))
    counts = jnp.zeros((rows, SMALL), F32)
    for series in range(lengths.shape[1]):
        left = jnp.maximum(lengths[0, series] - 1 - ahead[...], 0).astype(F32)
        entries = jnp.sum(left, -1, keepdims=True)
        counts = counts + jnp.where(row == domains[0, series], entries, 0.0)
    high = jnp.floor(counts * (1.0 / 256.0))
    small = jnp.where(lane == COUNTS_AT, high, small)
    small = jnp.where(lane == COUNTS_AT + 1, counts - 256.0 * high, small)
    flat = jnp.concatenate([input_w[...], output_w[...]], 1)
    half = 2 * D
    mine = jnp.where(core[0] == 0, flat[:, :half], flat[:, half:]).astype(BF16)
    for target in range(out.shape[0]):
        out[target, :, :half] = mine
        out[target, :, half:] = small.astype(BF16)


def front_kernel(
    local_rows, core, mine, other, cosine, sine, known, slot_row,
    embedded_out, first_out, qkv_out, log_out, mixed_out, after_out, second_out, logits_out,
    slots_out, gains_out, pack, counts_out,
):
    amount = known.shape[0]
    half = 2 * D
    low = core[0] == 0
    pack[:, :half] = jnp.where(low, mine[:, :half], other[:, :half])
    pack[:, half:SMALL_AT] = jnp.where(low, other[:, :half], mine[:, :half])
    pack[:, SMALL_AT:] = mine[:, half:]
    table = mine[:, half:].astype(F32).T
    gains = table[VECTORS_AT : VECTORS_AT + 8]
    gains_out[...] = gains
    other_table = other[:, half:].astype(F32).T
    row = lax.broadcasted_iota(jnp.int32, (D, SMALL), 0)
    fold = (row % local_rows == lanes_of((D, SMALL))).astype(F32).astype(BF16)
    digits = mm(table[VECTORS_AT : VECTORS_AT + 8].astype(BF16), fold) + mm(
        other_table[VECTORS_AT : VECTORS_AT + 8].astype(BF16), fold
    )
    at = COUNTS_AT - VECTORS_AT
    counts_out[...] = digits[at : at + 1] * 256.0 + digits[at + 1 : at + 2]
    value = known[:, VALUE : VALUE + 1]
    gate = value * gains[0:1]
    embedded = gate * jax.nn.sigmoid(gate) * (value * gains[1:2])
    embedded_out[...] = embedded
    first = (embedded * inverse_rms(embedded) * gains[2:3]).astype(BF16)
    first_out[...] = first
    projected = mm(first, pack[:, : 3 * D])
    cos_rows, sin_rows = cosine[...], sine[...]
    for block in range(6):
        part = projected[:, block * 128 : (block + 1) * 128]
        part = part * cos_rows + half_swap(part) * sin_rows
        qkv_out[:, block * 128 : (block + 1) * 128] = part.astype(BF16)
    qkv_out[:, 2 * D :] = projected[:, 2 * D :].astype(BF16)
    lane = lanes_of((ROW_BLOCK, 128))
    for start in range(0, amount, ROW_BLOCK):
        keys = start + ROW_BLOCK
        allowed = allowed_block(known[...], slot_row[...], start, ROW_BLOCK, keys)
        log_rows = jnp.zeros((ROW_BLOCK, 128), F32)
        for group in range(D // 128):
            query = qkv_out[start : start + ROW_BLOCK, group * 128 : (group + 1) * 128]
            key = qkv_out[:keys, D + group * 128 : D + (group + 1) * 128]
            held = qkv_out[:keys, 2 * D + group * 128 : 2 * D + (group + 1) * 128]
            gathered = jnp.zeros((ROW_BLOCK, 128), F32)
            for head in range(128 // HD):
                own = lane // HD == head
                raw = mm_nt(jnp.where(own, query, jnp.zeros_like(query)), key) * HD ** (-0.5)
                raw = jnp.where(allowed, raw, -1e30)
                top = jnp.max(raw, -1, keepdims=True)
                exponent = jnp.exp(raw - top)
                total = jnp.sum(exponent, -1, keepdims=True)
                attention = (exponent * (1.0 / total)).astype(BF16)
                gathered = jnp.where(own, mm(attention, held), gathered)
                log_rows = jnp.where(
                    lane == group * (128 // HD) + head, top + jnp.log(total), log_rows
                )
            mixed_out[start : start + ROW_BLOCK, group * 128 : (group + 1) * 128] = (
                gathered.astype(BF16)
            )
        log_out[start : start + ROW_BLOCK, :] = log_rows
    after = embedded + mm(mixed_out[...], pack[:, 3 * D : 4 * D])
    after_out[...] = after
    second = (after * inverse_rms(after) * gains[3:4]).astype(BF16)
    second_out[...] = second
    logits_out[...] = mm(second, pack[:, SMALL_AT:])
    for expert in range(EXPERTS):
        hot = slot_rows_hot(slot_row[0:1, :], expert) + slot_rows_hot(slot_row[1:2, :], expert)
        slots_out[expert * CAP : (expert + 1) * CAP, :] = mm(hot, second).astype(BF16)


def shared_kernel(second, gate_w, lift_w, down_w, shared_out):
    gate = mm(second[...], gate_w[...])
    lift = mm(second[...], lift_w[...])
    hidden = (gate * jax.nn.sigmoid(gate) * lift).astype(BF16)
    part = mm(hidden, down_w[...])

    @pl.when(pl.program_id(0) == 0)
    def _():
        shared_out[...] = part

    @pl.when(pl.program_id(0) != 0)
    def _():
        shared_out[...] += part


def expert_kernel(rows, gate_up, down, rows_out):
    gate = mm(rows[...], gate_up[0])
    lift = mm(rows[...], gate_up[1])
    hidden = (gate * jax.nn.sigmoid(gate) * lift).astype(BF16)
    result = mm(hidden, down[...])
    if len(rows_out.shape) == 2:
        rows_out[...] = result
        return
    for source in range(rows_out.shape[0]):
        part = result[source * CAP : (source + 1) * CAP]
        top = jnp.max(jnp.abs(part), -1, keepdims=True)
        power = jnp.ceil(jnp.log2(jnp.maximum(top, 1e-30)))
        code = jnp.clip(jnp.round(part * jnp.exp2(15.0 - power)), -32767.0, 32767.0)
        rows_out[source, :CAP, :] = code.astype(jnp.int32).astype(jnp.int16)
        row = lax.broadcasted_iota(jnp.int32, (CAP, CAP), 0)
        column = lax.broadcasted_iota(jnp.int32, (CAP, CAP), 1)
        powers = jnp.sum(jnp.where(row == column, power, 0.0), 0, keepdims=True)
        powers = jnp.concatenate([powers, jnp.zeros((1, D - CAP), F32)], 1)
        rows_out[source, CAP:, :] = (
            jnp.broadcast_to(powers, (CODE_ROWS, D)).astype(jnp.int32).astype(jnp.int16)
        )


def unit_back(rows, slope, gate_w, lift_w, down_w):
    gate = mm(rows, gate_w)
    lift = mm(rows, lift_w)
    bent = jax.nn.sigmoid(gate)
    smooth = gate * bent
    hidden = (smooth * lift).astype(BF16)
    hidden_slope = mm_nt(slope, down_w)
    gate_slope = (hidden_slope * lift * (bent * (1.0 + gate * (1.0 - bent)))).astype(BF16)
    lift_slope = (hidden_slope * smooth).astype(BF16)
    return hidden, gate_slope, lift_slope


def expert_back_kernel(rows, slope, gate_up, down, rows_out, in_out, out_out):
    hidden, gate_slope, lift_slope = unit_back(
        rows[...], slope[...], gate_up[0], gate_up[1], down[...]
    )
    rows_out[...] = (mm_nt(gate_slope, gate_up[0]) + mm_nt(lift_slope, gate_up[1])).astype(BF16)

    @pl.when(pl.program_id(0) == 0)
    def _():
        in_out[...] = jnp.zeros_like(in_out)
        out_out[...] = jnp.zeros_like(out_out)

    in_out[0] += mm_tn(rows[...], gate_slope)
    in_out[1] += mm_tn(rows[...], lift_slope)
    out_out[...] += mm_tn(hidden, slope[...])


def shared_back_kernel(second, slope, gate_w, lift_w, down_w, second_out, in_out, out_out):
    hidden, gate_slope, lift_slope = unit_back(
        second[...], slope[...], gate_w[...], lift_w[...], down_w[...]
    )
    part = mm_nt(gate_slope, gate_w[...]) + mm_nt(lift_slope, lift_w[...])

    @pl.when(pl.program_id(0) == 0)
    def _():
        second_out[...] = part

    @pl.when(pl.program_id(0) != 0)
    def _():
        second_out[...] += part

    in_out[0] = mm_tn(second[...], gate_slope)
    in_out[1] = mm_tn(second[...], lift_slope)
    out_out[...] = mm_tn(hidden, slope[...])


def expert_back_split_kernel(
    core, rows, slope, gate_up, down, rows_out, in_keep, in_give, out_keep, out_give
):
    hidden, gate_slope, lift_slope = unit_back(
        rows[...], slope[...], gate_up[0], gate_up[1], down[...]
    )
    rows_out[...] = (mm_nt(gate_slope, gate_up[0]) + mm_nt(lift_slope, gate_up[1])).astype(BF16)

    @pl.when(pl.program_id(0) == 0)
    def _():
        for ref in (in_keep, in_give, out_keep, out_give):
            ref[...] = jnp.zeros_like(ref)

    half = hidden.shape[1] // 2
    low = core[0] == 0
    gate = mm_tn(rows[...], gate_slope)
    lift = mm_tn(rows[...], lift_slope)
    in_keep[...] += jnp.where(low, gate, lift)
    in_give[...] += jnp.where(low, lift, gate)
    first = mm_tn(hidden[:, :half], slope[...])
    last = mm_tn(hidden[:, half:], slope[...])
    out_keep[...] += jnp.where(low, first, last)
    out_give[...] += jnp.where(low, last, first)


def shared_back_split_kernel(
    sides, second, slope, gate_w, lift_w, down_w,
    second_out, in_keep, in_give, out_keep, out_give, out_ref,
):
    hidden, gate_slope, lift_slope = unit_back(
        second[...], slope[...], gate_w[...], lift_w[...], down_w[...]
    )
    part = mm_nt(gate_slope, gate_w[...]) + mm_nt(lift_slope, lift_w[...])

    @pl.when(pl.program_id(0) == 0)
    def _():
        second_out[...] = part

    @pl.when(pl.program_id(0) != 0)
    def _():
        second_out[...] += part

    core, cross = sides[0], sides[1]
    low = core == 0
    gate = mm_tn(second[...], gate_slope)
    lift = mm_tn(second[...], lift_slope)
    in_keep[0] = jnp.where(low, gate, lift)
    in_give[0] = jnp.where(low, lift, gate)
    out_ref[...] = mm_tn(hidden, slope[...])
    quarter = out_keep.shape[1] // 2
    for shard in range(2):
        for side in range(2):
            for ref, half in ((out_keep, core), (out_give, 1 - core)):
                piece = half * 2 + jnp.bitwise_xor(cross, side)
                start = pl.multiple_of(shard * 4 * quarter + piece * quarter, 8)
                ref[side, shard * quarter : (shard + 1) * quarter, :] = out_ref[
                    pl.ds(start, quarter), :
                ]


def fold_kernel(in_keep, in_other, out_keep, out_other, keep, give):
    wide = in_keep.shape[2]
    for side, ref in enumerate((keep, give)):
        ref[:, :wide] = in_keep[side] + in_other[side]
        ref[:, wide:] = out_keep[side] + out_other[side]


def middle_kernel(
    returned, known, slot_row, after, shared, logits, small, gains, target, ahead, weighting,
    mixer_out, shared_slope_out, slots_out, logits_slope_out, small_out, gain_out, sums_out,
):
    amount = after.shape[0]
    lane = lanes_of((amount, SMALL))
    table = known[...]
    integers = table[:, :8].astype(jnp.int32)
    chosen = [
        (lane == integers[:, CHOICE + k : CHOICE + k + 1]).astype(F32) for k in range(2)
    ]
    place = lax.broadcasted_iota(jnp.int32, (amount, SMALL), 0)
    usable = (place + 1 + ahead[...] < integers[:, FINISH : FINISH + 1]).astype(F32)
    logit = logits[...]
    routed = lane < EXPERTS
    top = jnp.max(jnp.where(routed, logit, -1e30), -1, keepdims=True)
    exponent = jnp.where(routed, jnp.exp(jnp.where(routed, logit - top, 0.0)), 0.0)
    probs = exponent / jnp.sum(exponent, -1, keepdims=True)
    gates = [jnp.sum(chosen[k] * probs, -1, keepdims=True) for k in range(2)]
    shared_gate = jax.nn.sigmoid(
        jnp.sum(jnp.where(lane == EXPERTS, logit, 0.0), -1, keepdims=True)
    )
    picked = [jnp.zeros((amount, D), F32), jnp.zeros((amount, D), F32)]
    for expert in range(EXPERTS):
        if len(returned.shape) == 2:
            rows = returned[expert * CAP : (expert + 1) * CAP, :]
            scale = 1.0
        else:
            rows = returned[expert, :CAP, :].astype(jnp.int32).astype(F32)
            powers = returned[expert, CAP:, :].astype(jnp.int32).astype(F32)
            scale = jnp.exp2(powers[0:1, :CAP] - 15.0)
        high = rows.astype(BF16)
        rest = (rows - high.astype(F32)).astype(BF16)
        for k in range(2):
            slot = expert * CAP + lax.broadcasted_iota(jnp.int32, (amount, CAP), 1)
            hot = jnp.where(integers[:, SLOT + k : SLOT + k + 1] == slot, scale, 0.0).astype(BF16)
            picked[k] = picked[k] + (mm(hot, high) + mm(hot, rest))
    mixer = (
        after[...] + shared_gate * shared[...] + (gates[0] * picked[0] + gates[1] * picked[1])
    )
    inverse = inverse_rms(mixer)
    gain = gains[4:5]
    third = (mixer * inverse * gain).astype(BF16)
    residue = mm(third, small[...]) - target[...]
    size = jnp.abs(residue)
    cost = (
        jnp.where(
            size <= KINK_THRESHOLD,
            0.5 * residue * residue,
            KINK_THRESHOLD * (size - 0.5 * KINK_THRESHOLD),
        )
        * usable
    )
    domain_hot = (lane == integers[:, DOMAIN : DOMAIN + 1]).astype(F32)
    sums_out[...] = jnp.sum(domain_hot * jnp.sum(cost, -1, keepdims=True), 0, keepdims=True)
    weight = jnp.sum(domain_hot * weighting[...], -1, keepdims=True)
    slope = (
        jnp.clip(residue, -KINK_THRESHOLD, KINK_THRESHOLD) * usable * weight
    ).astype(BF16)
    small_out[...] = mm_tn(third, slope)
    mixer_slope, gain_slope = rms_back(mixer, inverse, gain, mm_nt(slope, small[...]))
    gain_out[...] = gain_slope
    mixer_out[...] = mixer_slope
    shared_slope_out[...] = (shared_gate * mixer_slope).astype(BF16)
    gate_slope = jnp.sum(mixer_slope * shared[...], -1, keepdims=True)
    probs_slope = chosen[0] * jnp.sum(mixer_slope * picked[0], -1, keepdims=True) + chosen[
        1
    ] * jnp.sum(mixer_slope * picked[1], -1, keepdims=True)
    inner = jnp.sum(probs * probs_slope, -1, keepdims=True)
    logits_slope_out[...] = jnp.where(
        routed,
        probs * (probs_slope - inner),
        jnp.where(lane == EXPERTS, gate_slope * (shared_gate * (1.0 - shared_gate)), 0.0),
    ).astype(BF16)
    slopes = [(gates[k] * mixer_slope).astype(BF16) for k in range(2)]
    for expert in range(EXPERTS):
        slots_out[expert * CAP : (expert + 1) * CAP, :] = (
            mm(slot_rows_hot(slot_row[0:1, :], expert), slopes[0])
            + mm(slot_rows_hot(slot_row[1:2, :], expert), slopes[1])
        ).astype(BF16)


def attend_back_kernel(
    returned, known, second_slope, logits_slope, small, after, mixer_slope, gains, mixed, second,
    output_w, small_before,
    attend_out, mixed_out, output_out, gain_out, small_out,
):
    slope = second_slope[...] + mm_nt(logits_slope[...], small[...])
    for expert in range(EXPERTS):
        hot = slot_cols_hot(known[:, 0:1], expert) + slot_cols_hot(known[:, 1:2], expert)
        slope = slope + mm(hot, returned[expert * CAP : (expert + 1) * CAP, :])
    after_rows = after[...]
    part, gain_slope = rms_back(after_rows, inverse_rms(after_rows), gains[3:4], slope)
    gain_out[...] = gain_slope
    attend = mixer_slope[...] + part
    attend_out[...] = attend
    low = attend.astype(BF16)
    output_out[...] = mm_tn(mixed[...], low)
    mixed_out[...] = mm_nt(low, output_w[...]).astype(BF16)
    small_out[...] = small_before[...] + mm_tn(second[...], logits_slope[...])


def front_back_kernel(
    fast, core, mixed_slope, qkv, log_total, known, rows_table, cosine, sine, first, embedded,
    gains, input_w, attend_slope, small_before, gain_two, gain_three, output_before,
    keep_out, give_out,
    pack_out, query_acc, key_acc, held_acc, slope_ref,
):
    amount = first.shape[0]
    key_acc[...] = jnp.zeros_like(key_acc)
    held_acc[...] = jnp.zeros_like(held_acc)
    lane = lanes_of((ROW_BLOCK, 128))
    lane_all = lanes_of((amount, 128))
    for start in range(0, amount, ROW_BLOCK):
        keys = start + ROW_BLOCK
        here = slice(start, start + ROW_BLOCK)
        allowed = allowed_block(known[...], rows_table[...], start, ROW_BLOCK, keys)
        for group in range(D // 128):
            wide = slice(group * 128, (group + 1) * 128)
            query = qkv[here, group * 128 : (group + 1) * 128]
            key = qkv[:keys, D + group * 128 : D + (group + 1) * 128]
            held = qkv[:keys, 2 * D + group * 128 : 2 * D + (group + 1) * 128]
            out_slope = mixed_slope[here, wide]
            query_sum = jnp.zeros((ROW_BLOCK, 128), F32)
            key_sum = jnp.zeros((keys, 128), F32)
            held_sum = jnp.zeros((keys, 128), F32)
            for head in range(128 // HD):
                own = lane // HD == head
                own_query = jnp.where(own, query, jnp.zeros_like(query))
                own_slope = jnp.where(own, out_slope, jnp.zeros_like(out_slope))
                own_key = jnp.where(lane_all[:keys] // HD == head, key, jnp.zeros_like(key))
                at = group * (128 // HD) + head
                raw = mm_nt(own_query, key) * HD ** (-0.5)
                probs = jnp.exp(jnp.where(allowed, raw - log_total[here, at : at + 1], -1e30))
                held_sum = held_sum + mm_tn(probs.astype(BF16), own_slope)
                probs_slope = mm_nt(own_slope, held)
                inner = jnp.sum(probs_slope * probs, -1, keepdims=True)
                raw_slope = (probs * (probs_slope - inner)).astype(BF16)
                query_sum = query_sum + mm(raw_slope, own_key)
                key_sum = key_sum + mm_tn(raw_slope, own_query)
            query_acc[here, wide] = query_sum
            key_acc[:keys, wide] += key_sum
            held_acc[:keys, wide] += held_sum
    cos_rows, sin_rows = cosine[...], sine[...]
    for block in range(3):
        wide = slice(block * 128, (block + 1) * 128)
        for base, acc in ((0, query_acc), (D, key_acc)):
            part = acc[:, wide] * HD ** (-0.5)
            part = part * cos_rows + half_swap(part * sin_rows)
            slope_ref[:, base + block * 128 : base + (block + 1) * 128] = part.astype(BF16)
    slope_ref[:, 2 * D :] = held_acc[...].astype(BF16)
    projected_slope = slope_ref[...]
    pack_out[:, : 3 * D] = mm_tn(first[...], projected_slope)
    pack_out[:, 3 * D : SMALL_AT] = output_before[...]
    first_slope = mm_nt(projected_slope, input_w[...])
    rows = embedded[...]
    part, gain_one = rms_back(rows, inverse_rms(rows), gains[2:3], first_slope)
    slope = attend_slope[...] + part
    value = known[:, VALUE : VALUE + 1]
    gate = value * gains[0:1]
    bent = jax.nn.sigmoid(gate)
    gate_gradient = jnp.sum(
        slope * (value * gains[1:2]) * (bent * (1.0 + gate * (1.0 - bent))) * value,
        0,
        keepdims=True,
    )
    lift_gradient = jnp.sum(slope * (gate * bent) * value, 0, keepdims=True)
    row = lax.broadcasted_iota(jnp.int32, (128, D), 0)
    table = jnp.zeros((128, D), F32)
    for offset, piece in enumerate(
        (gate_gradient, lift_gradient, gain_one, gain_two[...], gain_three[...])
    ):
        table = jnp.where(row == VECTORS_AT + offset, piece, table)
    pack_out[:, SMALL_AT:] = small_before[...] + table.T
    if not fast:
        keep_out[...] = pack_out[...]
        give_out[...] = jnp.zeros_like(give_out)
        return
    shard = keep_out.shape[0] // EXPERTS
    for index in range(EXPERTS):
        here = slice(index * shard, (index + 1) * shard)
        base = 2 * shard * index
        keep_out[here, :] = pack_out[pl.ds(pl.multiple_of(base + core[0] * shard, 8), shard), :]
        give_out[here, :] = pack_out[
            pl.ds(pl.multiple_of(base + (1 - core[0]) * shard, 8), shard), :
        ]


def lamb_direction(master, gradient, mean, square, factor):
    clipped = gradient * factor
    mean_next = BETA_ONE * mean + (1.0 - BETA_ONE) * clipped
    square_next = BETA_TWO * square + (1.0 - BETA_TWO) * clipped * clipped
    direction = (
        mean_next
        / (1.0 - BETA_ONE**STEP)
        / (jnp.sqrt(square_next / (1.0 - BETA_TWO**STEP)) + EPS_ADAM)
        + DECAY * master
    )
    return mean_next, square_next, direction


def whole(array):
    shape = array.shape
    return pl.BlockSpec(shape, lambda *unused: (0,) * len(shape))


def params(**extra):
    return pltpu.CompilerParams(vmem_limit_bytes=VMEM, **extra)


def cost(flops, size):
    return pl.CostEstimate(
        flops=int(flops / 1000), bytes_accessed=int(size / 1000), transcendentals=0
    )


def columns(array, width, at):
    return (array, pl.BlockSpec((array.shape[0], width), lambda *unused: (0, at)))


def simple_call(kernel, outs, args, flops, scratch=()):
    pairs = [a if isinstance(a, tuple) else (a, whole(a)) for a in args]
    args = [a for a, spec in pairs]
    size = sum(a.size * a.dtype.itemsize for a in list(args) + list(outs))
    return pl.pallas_call(
        kernel,
        out_shape=outs,
        in_specs=[spec for a, spec in pairs],
        out_specs=[whole(a) for a in outs],
        scratch_shapes=list(scratch),
        grid=(1,),
        compiler_params=params(),
        cost_estimate=cost(flops, size),
    )(*args)


def out(shape, dtype=F32):
    return jax.ShapeDtypeStruct(shape, dtype)


def flip(value, axis_name, bit):
    count = lax.axis_size(axis_name)
    return lax.ppermute(value, axis_name, [(i, i ^ bit) for i in range(count)])


def bits_of(axis_name):
    count = lax.axis_size(axis_name)
    return [1 << i for i in range(count.bit_length() - 1)]


def sum_small(value, axes):
    for axis_name in axes:
        for bit in bits_of(axis_name):
            value = value + flip(value, axis_name, bit)
    return value


def halves(value, axis, take_high):
    size = value.shape[axis] // 2
    side = take_high.astype(jnp.int32)
    return (
        lax.dynamic_slice_in_dim(value, side * size, size, axis),
        lax.dynamic_slice_in_dim(value, (1 - side) * size, size, axis),
    )


def scatter_sum(value, axis, bits):
    for bit in bits:
        side = (lax.axis_index("dp") & bit) != 0
        keep, give = halves(value, axis, side)
        value = keep + flip(give, "dp", bit)
    return value


def join(value, axis, bits):
    for bit in reversed(bits):
        side = (lax.axis_index("dp") & bit) != 0
        other = flip(value, "dp", bit)
        value = jnp.concatenate(
            [jnp.where(side, other, value), jnp.where(side, value, other)], axis
        )
    return value


def ready(value, *others):
    return lax.optimization_barrier((value, *others))[0]


def exchange(value):
    return lax.all_to_all(value, "expert", split_axis=0, concat_axis=0, tiled=True)


def spread(value):
    count = lax.axis_size("expert")
    return exchange(jnp.broadcast_to(value[None], (count, *value.shape)))


def expert_scatter(value):
    return jnp.sum(exchange(value), 0)


def squares_kernel(weights, sums, *refs):
    total = jnp.zeros((1, 1), F32)
    for weight, ref in zip(weights, refs[:-1]):
        piece = ref[...]
        part = jnp.sum(jnp.sum(piece * piece, -1, keepdims=True), 0, keepdims=True)
        total = total + part * weight
    refs[-1][0:1, :] = jnp.broadcast_to(total, (1, 128))
    refs[-1][1:2, :] = sums[...]


def sum_all(value):
    while value.ndim > 2:
        value = jnp.sum(value, 0)
    return jnp.sum(jnp.sum(value, 0, keepdims=True), -1, keepdims=True)


TILED = (4, 7, 8)


def tile_spec(index, shape, steps):
    if index == 7:
        return pl.BlockSpec((2, D // steps, shape[2]), lambda i: (0, i, 0))
    if index == 8:
        return pl.BlockSpec((shape[0] // steps, D), lambda i: (i, 0))
    if index == 4 and len(shape) == 3:
        half = steps // 2
        return pl.BlockSpec((1, shape[1], shape[2] // half), lambda i: (i // half, 0, i % half))
    if index == 4:
        return pl.BlockSpec((shape[0], shape[1] // steps), lambda i: (0, i))
    return pl.BlockSpec(shape, lambda i: (0,) * len(shape))


def tile_specs(arrays, steps):
    return [tile_spec(index, array.shape, steps) for index, array in enumerate(arrays)]


def prepare_kernel(count, *refs):
    masters = refs[:count]
    gate_up_low, down_low, totals = refs[count:]
    step = pl.program_id(0)
    gate_up_low[...] = masters[7][...].astype(BF16)
    down_low[...] = masters[8][...].astype(BF16)

    @pl.when(step == 0)
    def _():
        totals[...] = jnp.zeros_like(totals)

    def add(index):
        master = masters[index][...]
        totals[index : index + 1, :] += jnp.broadcast_to(sum_all(master * master), (1, 128))

    for index in TILED:
        add(index)

    @pl.when(step == 0)
    def _():
        for index in range(count):
            if index not in TILED:
                add(index)


def picked_piece(pieces, index, part):
    value = part(pieces[0])
    for other in range(1, len(pieces)):
        value = jnp.where(index == other, part(pieces[other]), value)
    return value


def moments_kernel(fast, count, small_end, sides, square_ref, *refs):
    masters, means, squares = (refs[k * count : (k + 1) * count] for k in range(3))
    results = refs[-3 * count - 1 :]
    pieces = refs[3 * count : -3 * count - 1]
    totals = results[-1]
    factor = jnp.minimum(1.0, CLIP / jnp.sqrt(square_ref[0:1, 0:1]))
    step = pl.program_id(0)

    @pl.when(step == 0)
    def _():
        totals[...] = jnp.zeros_like(totals)

    def last_rows(start, stop):
        if not fast:
            return pieces[0][:, start:stop]
        mine, other = pieces[0][:, start:stop], pieces[1][:, start:stop]
        low = sides[0] == 0
        return jnp.concatenate([jnp.where(low, mine, other), jnp.where(low, other, mine)], 0)

    def gradient_of(index):
        if index in (0, 3):
            table = last_rows(SMALL_AT, SMALL_AT + SMALL).T
            return table[VECTORS_AT : VECTORS_AT + 5] if index == 0 else table[:HORIZON_AT]
        if index == 6:
            return last_rows(SMALL_AT, SMALL_AT + SMALL)[:, HORIZON_AT:small_end]
        if index == 1:
            return last_rows(0, 3 * D)
        if index == 2:
            return last_rows(3 * D, SMALL_AT)
        if not fast:
            return pieces[{4: 1, 5: 2, 7: 3, 8: 4}[index]][...]
        low = sides[0] == 0
        me = sides[0] * 2 + sides[1]
        shared = pieces[2:6]
        wide = 2 * FFS // 4
        if index == 4:
            at = pl.multiple_of((step % 2) * (wide // 2), 128)
            return picked_piece(
                shared,
                jnp.bitwise_xor(step // 2, me),
                lambda ref: ref[:, pl.ds(at, wide // 2)],
            )
        if index == 5:
            return jnp.concatenate(
                [
                    picked_piece(shared, jnp.bitwise_xor(piece, me), lambda ref: ref[:, wide:])
                    for piece in range(4)
                ],
                0,
            )
        if index == 7:
            mine, other = pieces[6][...], pieces[7][...]
            return jnp.stack([jnp.where(low, mine, other), jnp.where(low, other, mine)])
        return jnp.where(step // 4 == sides[0], pieces[8][...], pieces[9][...])

    def update(index):
        gradient = gradient_of(index)
        if index == 4 and gradient.ndim == 3:
            gradient = gradient[0]
        scale = factor.reshape(1, 1, 1) if gradient.ndim == 3 else factor
        mean_next, square_next, direction = lamb_direction(
            masters[index][...], gradient, means[index][...], squares[index][...], scale
        )
        results[index][...] = direction
        results[count + index][...] = mean_next
        results[2 * count + index][...] = square_next
        totals[index : index + 1, :] += jnp.broadcast_to(sum_all(direction * direction), (1, 128))

    for index in TILED:
        update(index)
    for index in range(count):
        if index not in TILED:
            pl.when(step == min(index, 7))(functools.partial(update, index))


def step_kernel(count, totals, master_totals, *refs):
    masters, directions = refs[:count], refs[count : 2 * count]
    results = refs[2 * count :]
    step = pl.program_id(0)

    def update(index):
        ratio = jnp.sqrt(master_totals[index : index + 1, 0:1]) / jnp.sqrt(
            totals[index : index + 1, 0:1]
        )
        ratio = RATE * ratio
        if len(masters[index].shape) == 3:
            ratio = ratio.reshape(1, 1, 1)
        results[index][...] = masters[index][...] - ratio * directions[index][...]

    for index in TILED:
        update(index)
    for index in range(count):
        if index not in TILED:
            pl.when(step == min(index, 7))(functools.partial(update, index))


def shards(
    points,
    experts,
    lengths,
    domains,
    domain_weights,
    vectors,
    attend_input,
    attend_output,
    router,
    shared_input,
    shared_output,
    horizon,
    expert_input,
    expert_output,
    mean_vectors,
    mean_attend_input,
    mean_attend_output,
    mean_router,
    mean_shared_input,
    mean_shared_output,
    mean_horizon,
    mean_expert_input,
    mean_expert_output,
    square_vectors,
    square_attend_input,
    square_attend_output,
    square_router,
    square_shared_input,
    square_shared_output,
    square_horizon,
    square_expert_input,
    square_expert_output,
):
    expert_count = lax.axis_size("expert")
    group_size = expert_count // EXPERTS
    dp_count = lax.axis_size("dp")
    dp_bits = bits_of("dp")
    amount = points.shape[0]
    local_rows = attend_input.shape[0]
    head_columns = horizon.shape[1]
    hidden_local = expert_output.shape[0]
    small_end = HORIZON_AT + head_columns
    fast = group_size == 1 and dp_count == 4 and local_rows % 16 == 0
    core = lax.axis_index("dp") & 1
    sides = jnp.stack([core, lax.axis_index("dp") >> 1]).astype(jnp.int32)
    in_smem = pl.BlockSpec(memory_space=pltpu.SMEM)
    in_vmem = pl.BlockSpec(memory_space=pltpu.VMEM)
    ahead_row = jnp.pad(
        jnp.asarray(ahead_table())[None], ((0, 0), (0, SMALL - head_columns)), constant_values=1 << 20
    )
    packed = pl.pallas_call(
        functools.partial(pack_kernel, small_end),
        out_shape=out((expert_count, local_rows, 2 * D + SMALL), BF16),
        in_specs=[*[in_smem] * 3, *[in_vmem] * 6],
        out_specs=in_vmem,
        compiler_params=params(),
        cost_estimate=cost(1e6, 1e6),
    )(sides, lengths, domains, ahead_row, attend_input, attend_output, router.T, horizon, vectors)
    gathered = exchange(packed)

    def state(group):
        return tuple(a.T if index == 3 else a for index, a in enumerate(group))

    masters = state(
        (
            vectors, attend_input, attend_output, router, shared_input, shared_output, horizon,
            expert_input, expert_output,
        )
    )
    first_moments = state(
        (
            mean_vectors, mean_attend_input, mean_attend_output, mean_router, mean_shared_input,
            mean_shared_output, mean_horizon, mean_expert_input, mean_expert_output,
        )
    )
    second_moments = state(
        (
            square_vectors, square_attend_input, square_attend_output, square_router,
            square_shared_input, square_shared_output, square_horizon, square_expert_input,
            square_expert_output,
        )
    )
    count = len(masters)
    steps = 8
    gate_up_low, down_low, master_squares = pl.pallas_call(
        functools.partial(prepare_kernel, count),
        out_shape=[
            out(expert_input.shape, BF16), out(expert_output.shape, BF16), out((16, 128)),
        ],
        grid=(steps,),
        in_specs=tile_specs(masters, steps),
        out_specs=[
            tile_spec(7, expert_input.shape, steps),
            tile_spec(8, expert_output.shape, steps),
            whole(out((16, 128))),
        ],
        compiler_params=params(),
        cost_estimate=cost(3e6, 7e6),
    )(*masters)
    frequency = jnp.exp(-jnp.log(10000.0) * jnp.arange(HD // 2, dtype=F32) / (HD // 2))
    cosine, sine, known, rows_table = pl.pallas_call(
        tables_kernel,
        out_shape=[out((amount, 128)), out((amount, 128)), out((amount, 128)), out((8, amount))],
        in_specs=[*[in_smem] * 2, *[in_vmem] * 3],
        out_specs=[in_vmem] * 4,
        compiler_params=params(),
        cost_estimate=cost(1e6, 1e6),
    )(
        lengths,
        domains,
        jnp.tile(frequency, 128 // (HD // 2))[None],
        points.reshape(1, amount),
        experts.T,
    )
    folds = FFS // D
    shared_piece = jnp.concatenate(
        [
            shared_input,
            shared_output.reshape(folds, local_rows, D).swapaxes(0, 1).reshape(local_rows, -1),
        ],
        1,
    ).astype(BF16)
    for bit in dp_bits:
        shared_piece, unused = halves(shared_piece, 1, (lax.axis_index("dp") & bit) != 0)
    gathered = ready(
        gathered, known, gate_up_low, down_low, master_squares, shared_piece
    ).reshape(D, -1)
    gathered_other = flip(gathered, "dp", 1)
    shared_pieces = spread(ready(shared_piece, gathered))
    (
        embedded, first, qkv, log_total, mixed, after, second, logits, slots, gains, pack,
        counts_half,
    ) = simple_call(
        functools.partial(front_kernel, local_rows),
        [
            out((amount, D)), out((amount, D), BF16), out((amount, 3 * D), BF16),
            out((amount, 128)), out((amount, D), BF16), out((amount, D)),
            out((amount, D), BF16), out((amount, SMALL)), out((EXPERTS * CAP, D), BF16),
            out((8, D)), out((D, SMALL_AT + SMALL), BF16), out((1, SMALL)),
        ],
        [(sides, in_smem), gathered, gathered_other, cosine, sine, known, rows_table],
        8e9,
    )

    def to_devices(rows):
        rows = rows.reshape(EXPERTS, CAP, D)
        return exchange(jnp.repeat(rows, group_size, 0)).reshape(-1, D)

    def to_points(rows):
        rows = exchange(rows.reshape(expert_count, CAP, D))
        if group_size > 1:
            kind = rows.dtype
            rows = rows.reshape(EXPERTS, group_size, CAP, D).astype(F32)
            rows = jnp.sum(rows, 1).astype(kind)
        return rows.reshape(-1, D)

    arrived = to_devices(ready(slots, shared_pieces))
    first_bit = dp_bits[-1]
    shared_pieces = ready(shared_pieces, slots)
    shared_other = flip(shared_pieces, "dp", first_bit)
    arrived = ready(arrived, shared_other)
    block = 512
    total_rows = arrived.shape[0]
    coded = group_size == 1
    sources = block // CAP
    expert_rows = pl.pallas_call(
        expert_kernel,
        out_shape=(
            out((EXPERTS, CAP + CODE_ROWS, D), jnp.int16) if coded else out((total_rows, D))
        ),
        grid=(total_rows // block,),
        in_specs=[
            pl.BlockSpec((block, D), lambda i: (i, 0)), whole(gate_up_low), whole(down_low),
        ],
        out_specs=(
            pl.BlockSpec((sources, CAP + CODE_ROWS, D), lambda i: (i, 0, 0))
            if coded
            else pl.BlockSpec((block, D), lambda i: (i, 0))
        ),
        compiler_params=params(),
        cost_estimate=cost(total_rows * D * 3 * hidden_local * 2, 7e6),
    )(arrived, gate_up_low, down_low)
    returned = exchange(expert_rows) if coded else to_points(expert_rows)
    shared_pieces = ready(shared_pieces, expert_rows)
    side = (lax.axis_index("dp") & first_bit) != 0
    shared_pack = jnp.concatenate(
        [
            jnp.where(side, shared_other, shared_pieces),
            jnp.where(side, shared_pieces, shared_other),
        ],
        2,
    )
    shared_pack = join(shared_pack, 2, dp_bits[:-1])
    shin_low = shared_pack[:, :, : 2 * FFS].reshape(D, -1)
    shout_low = (
        shared_pack[:, :, 2 * FFS :]
        .reshape(expert_count, local_rows, folds, D)
        .swapaxes(1, 2)
        .reshape(FFS, D)
    )
    chunk = 512
    chunks = FFS // chunk
    shared = pl.pallas_call(
        shared_kernel,
        out_shape=out((amount, D)),
        grid=(chunks,),
        in_specs=[
            whole(second),
            pl.BlockSpec((D, chunk), lambda i: (0, i)),
            pl.BlockSpec((D, chunk), lambda i: (0, i + chunks)),
            pl.BlockSpec((chunk, D), lambda i: (i, 0)),
        ],
        out_specs=pl.BlockSpec((amount, D), lambda i: (0, 0)),
        compiler_params=params(),
        cost_estimate=cost(amount * D * 3 * FFS * 2, 5e6),
    )(second, shin_low, shin_low, shout_low)
    counts = ready(counts_half, expert_rows)
    for bit in dp_bits[1:]:
        counts = counts + flip(counts, "dp", bit)
    weighting = jnp.pad(domain_weights, (0, SMALL - DOMAINS))[None] / jnp.maximum(counts, 1.0)
    side_pad = ((0, 0), (HORIZON_AT, SMALL - small_end))
    target = jnp.pad(target_columns(points), side_pad)
    ahead_small = jnp.pad(
        jnp.asarray(ahead_table())[None], ((0, 0), side_pad[1]), constant_values=1 << 20
    )
    small_low = columns(pack, SMALL, SMALL_AT // SMALL)
    (
        mixer_slope, shared_slope, slope_slots, logits_slope, small_head, gain_three, local_sums,
    ) = simple_call(
        middle_kernel,
        [
            out((amount, D)), out((amount, D), BF16), out((EXPERTS * CAP, D), BF16),
            out((amount, SMALL), BF16), out((D, SMALL)), out((1, D)), out((1, SMALL)),
        ],
        [
            returned, known, rows_table, after, shared, logits, small_low, gains, target,
            ahead_small, weighting,
        ],
        7e9,
    )
    received = to_devices(slope_slots)
    chunk = D
    chunks = FFS // chunk
    back_in = [
        pl.BlockSpec((amount, D), lambda i, *unused: (0, 0)),
        pl.BlockSpec((amount, D), lambda i, *unused: (0, 0)),
        pl.BlockSpec((D, chunk), lambda i, *unused: (0, i)),
        pl.BlockSpec((D, chunk), lambda i, *unused: (0, i + chunks)),
        pl.BlockSpec((chunk, D), lambda i, *unused: (i, 0)),
    ]
    second_spec = pl.BlockSpec((amount, D), lambda i, *unused: (0, 0))
    back_args = (second, shared_slope, shin_low, shin_low, shout_low)
    back_cost = cost(amount * D * 8 * FFS * 2, 14e6)
    if fast:
        in_spec = pl.BlockSpec(
            (1, D, chunk), lambda i, sides: (jnp.bitwise_xor(i // 2, sides[1]), 0, i % 2)
        )
        out_spec = pl.BlockSpec((2, D // chunks, D), lambda i, sides: (0, i, 0))
        shared_second_slope, in_keep, in_give, out_keep, out_give = pl.pallas_call(
            shared_back_split_kernel,
            out_shape=[
                out((amount, D)), out((2, D, FFS // 2)), out((2, D, FFS // 2)), out((2, D, D)),
                out((2, D, D)),
            ],
            grid_spec=pltpu.PrefetchScalarGridSpec(
                num_scalar_prefetch=1,
                grid=(chunks,),
                in_specs=back_in,
                out_specs=[second_spec, in_spec, in_spec, out_spec, out_spec],
                scratch_shapes=[pltpu.VMEM((chunk, D), F32)],
            ),
            compiler_params=params(),
            cost_estimate=back_cost,
        )(sides, *back_args)
    else:
        shared_second_slope, grad_shin, grad_shout = pl.pallas_call(
            shared_back_kernel,
            out_shape=[out((amount, D)), out((2, D, FFS)), out((FFS, D))],
            grid=(chunks,),
            in_specs=back_in,
            out_specs=[
                second_spec,
                pl.BlockSpec((2, D, chunk), lambda i: (0, 0, i)),
                pl.BlockSpec((chunk, D), lambda i: (i, 0)),
            ],
            compiler_params=params(),
            cost_estimate=back_cost,
        )(*back_args)
    received = ready(received, shared_second_slope)
    row_spec = pl.BlockSpec((block, D), lambda i: (i, 0))
    expert_cost = cost(total_rows * D * 8 * hidden_local * 2, 10e6)
    weight_specs = [whole(gate_up_low), whole(down_low)]
    if fast:
        half_shapes = [out((D, hidden_local))] * 2 + [out((hidden_local // 2, D))] * 2
        grad_rows, expert_in, expert_in_give, expert_out, expert_out_give = pl.pallas_call(
            expert_back_split_kernel,
            out_shape=[out((total_rows, D), BF16), *half_shapes],
            grid=(total_rows // block,),
            in_specs=[in_smem, row_spec, row_spec, *weight_specs],
            out_specs=[row_spec, *[whole(a) for a in half_shapes]],
            compiler_params=params(),
            cost_estimate=expert_cost,
        )(sides, arrived, received, gate_up_low, down_low)
    else:
        grad_rows, grad_expert_in, grad_expert_out = pl.pallas_call(
            expert_back_kernel,
            out_shape=[
                out((total_rows, D), BF16), out((2, D, hidden_local)), out((hidden_local, D)),
            ],
            grid=(total_rows // block,),
            in_specs=[row_spec, row_spec, *weight_specs],
            out_specs=[
                row_spec,
                pl.BlockSpec((2, D, hidden_local), lambda i: (0, 0, 0)),
                pl.BlockSpec((hidden_local, D), lambda i: (0, 0)),
            ],
            compiler_params=params(),
            cost_estimate=expert_cost,
        )(arrived, received, gate_up_low, down_low)
    routed_back = to_points(grad_rows)
    if fast:
        in_other, out_other = flip(in_give, "dp", 1), flip(out_give, "dp", 1)
        fold_in = pl.BlockSpec((2, D // 4, FFS // 2), lambda i: (0, i, 0))
        fold_out = pl.BlockSpec((2, D // 4, D), lambda i: (0, i, 0))
        wide = FFS // 2 + D
        fold_to = pl.BlockSpec((D // 4, wide), lambda i: (i, 0))
        shared_keep, shared_give = pl.pallas_call(
            fold_kernel,
            out_shape=[out((D, wide)), out((D, wide))],
            grid=(4,),
            in_specs=[fold_in, fold_in, fold_out, fold_out],
            out_specs=[fold_to, fold_to],
            compiler_params=params(),
            cost_estimate=cost(2e6, 10e6),
        )(in_keep, in_other, out_keep, out_other)
        shared_other = flip(shared_give, "dp", 2)
        expert_in = expert_in + flip(expert_in_give, "dp", 1)
        expert_out = expert_out + flip(expert_out_give, "dp", 1)
        sums = local_sums + flip(local_sums, "dp", 2)
        routed_back = ready(routed_back, shared_other, expert_in, expert_out, sums)
    attend_slope, mixed_slope, grad_output, gain_two, small_routed = simple_call(
        attend_back_kernel,
        [
            out((amount, D)), out((amount, D), BF16), out((D, D)), out((1, D)), out((D, SMALL)),
        ],
        [
            routed_back, known, shared_second_slope, logits_slope, small_low, after,
            mixer_slope, gains, mixed, second, columns(pack, D, 3), small_head,
        ],
        2e9,
    )
    shard_rows = D // 2 if fast else D
    pack_columns = SMALL_AT + SMALL
    last_keep, last_give = simple_call(
        functools.partial(front_back_kernel, fast),
        [out((shard_rows, pack_columns)), out((shard_rows if fast else 8, pack_columns))],
        [
            (sides, in_smem), mixed_slope, qkv, log_total, known, rows_table, cosine, sine, first,
            embedded, gains, columns(pack, 3 * D, 0), attend_slope, small_routed, gain_two,
            gain_three, grad_output,
        ],
        16e9,
        [
            pltpu.VMEM((D, pack_columns), F32),
            pltpu.VMEM((amount, D), F32),
            pltpu.VMEM((amount, D), F32),
            pltpu.VMEM((amount, D), F32),
            pltpu.VMEM((amount, 3 * D), BF16),
        ],
    )

    if fast:
        shared_sum = (shared_keep + shared_other).reshape(expert_count, local_rows, wide)
        shared_sum = expert_scatter(ready(shared_sum, mixed_slope))
        expert_in = ready(expert_in, mixed_slope)
        expert_out = ready(expert_out, mixed_slope)
        expert_in_other = flip(expert_in, "dp", 2)
        expert_out_other = flip(expert_out, "dp", 2)
        last_part = last_keep + flip(last_give, "dp", 1)
        last_part = ready(last_part, shared_sum, expert_in_other, expert_out_other)
        last_part = expert_scatter(last_part.reshape(expert_count, local_rows // 2, -1))
        last_part = last_part + flip(last_part, "dp", 2)
        expert_in = expert_in + expert_in_other
        expert_out = expert_out + expert_out_other
        shared_cross = flip(shared_sum, "dp", 2)
        square_pieces = [expert_in, expert_out, shared_sum, shared_cross, last_part]
        weights = (1.0,) * 5
        square_bits = [1]
        pieces = [
            last_part, flip(last_part, "dp", 1), shared_sum, shared_cross,
            flip(shared_sum, "dp", 1), flip(shared_cross, "dp", 1), expert_in,
            flip(expert_in, "dp", 1), expert_out, flip(expert_out, "dp", 1),
        ]
        tile_in = pl.BlockSpec((D // steps, hidden_local), lambda i: (i, 0))
        half_steps = steps // 2
        tile_out = pl.BlockSpec((hidden_local // steps, D), lambda i: (i % half_steps, 0))
        piece_specs = [*[whole(a) for a in pieces[:6]], tile_in, tile_in, tile_out, tile_out]
    else:
        sums = local_sums
        shin_part = scatter_sum(grad_shin, 0, [1])[0].reshape(expert_count, local_rows, FFS)
        shin_part = expert_scatter(scatter_sum(shin_part, 2, dp_bits[1:]))
        shout_part = scatter_sum(grad_shout.reshape(expert_count, -1, D), 1, dp_bits)
        shout_part = expert_scatter(shout_part)
        expert_in_part = scatter_sum(grad_expert_in.reshape(-1, hidden_local), 0, dp_bits)
        expert_out_part = scatter_sum(grad_expert_out, 0, dp_bits)
        last_part = expert_scatter(last_keep.reshape(expert_count, local_rows, -1))
        for bit in dp_bits:
            last_part = last_part + flip(last_part, "dp", bit)
        square_pieces = [expert_in_part, expert_out_part, shin_part, shout_part, last_part]
        weights = (1.0, 1.0, 1.0, 1.0, 1.0 / dp_count)
        square_bits = dp_bits
        pieces = [
            last_part,
            join(join(shin_part, 1, dp_bits[1:])[None], 0, [1]),
            join(shout_part, 0, dp_bits),
            join(expert_in_part, 0, dp_bits).reshape(expert_input.shape),
            join(expert_out_part, 0, dp_bits),
        ]
        piece_specs = [
            whole(last_part),
            *[tile_spec(i, a.shape, steps) for i, a in zip((4, 5, 7, 8), pieces[1:])],
        ]
    (both_sums,) = simple_call(
        functools.partial(squares_kernel, weights), [out((2, 128))], [sums, *square_pieces], 3e6
    )
    for bit in square_bits:
        both_sums = both_sums + flip(both_sums, "dp", bit)
    both_sums = sum_small(both_sums, ("expert",))
    domain_sums = both_sums[1, :DOMAINS]
    grad_norm = jnp.sqrt(both_sums[0, 0:1])
    shapes = [out(a.shape) for a in masters]
    state_specs = tile_specs(masters, steps)
    updates = pl.pallas_call(
        functools.partial(moments_kernel, fast, count, small_end),
        out_shape=[*shapes, *shapes, *shapes, out((16, 128))],
        grid=(steps,),
        in_specs=[
            in_smem, whole(both_sums), *state_specs, *state_specs, *state_specs, *piece_specs,
        ],
        out_specs=[*state_specs, *state_specs, *state_specs, whole(out((16, 128)))],
        compiler_params=params(),
        cost_estimate=cost(3e7, 34e6),
    )(sides, both_sums, *masters, *first_moments, *second_moments, *pieces)
    directions = updates[:count]
    all_totals = sum_small(
        jnp.concatenate([updates[-1][:count], master_squares[:count]], 0), ("expert",)
    )
    totals, master_totals = all_totals[:count], all_totals[count:]
    next_masters = pl.pallas_call(
        functools.partial(step_kernel, count),
        out_shape=shapes,
        grid=(steps,),
        in_specs=[whole(totals), whole(master_totals), *state_specs, *state_specs],
        out_specs=state_specs,
        compiler_params=params(),
        cost_estimate=cost(3e6, 15e6),
    )(totals, master_totals, *masters, *directions)
    results = []
    for index in range(count):
        for group in (next_masters, updates[count : 2 * count], updates[2 * count : 3 * count]):
            results.append(group[index].T if index == 3 else group[index])
    norms = jnp.sqrt(all_totals[:, 0])
    results.append(jnp.stack([domain_sums, counts[0, :DOMAINS]]))
    results.append(grad_norm)
    results.append(jnp.stack([norms[count:], norms[:count]], 1))
    return tuple(results)


def solution(mesh):
    placed = (
        P(("dp", "expert")),
        P(("dp", "expert"), None),
        P(("dp", "expert"), None),
        P(("dp", "expert"), None),
        P(),
        P(None, "expert"),
        P("expert", None),
        P("expert", None),
        P("expert", None),
        P("expert", None),
        P("expert", None),
        P("expert", None),
        P(None, None, "expert"),
        P("expert", None),
        P(None, "expert"),
        P("expert", None),
        P("expert", None),
        P("expert", None),
        P("expert", None),
        P("expert", None),
        P("expert", None),
        P(None, None, "expert"),
        P("expert", None),
        P(None, "expert"),
        P("expert", None),
        P("expert", None),
        P("expert", None),
        P("expert", None),
        P("expert", None),
        P("expert", None),
        P(None, None, "expert"),
        P("expert", None),
    )
    return jax.shard_map(
        shards,
        mesh=mesh,
        in_specs=placed,
        out_specs=(
            P(None, "expert"),
            P(None, "expert"),
            P(None, "expert"),
            P("expert", None),
            P("expert", None),
            P("expert", None),
            P("expert", None),
            P("expert", None),
            P("expert", None),
            P("expert", None),
            P("expert", None),
            P("expert", None),
            P("expert", None),
            P("expert", None),
            P("expert", None),
            P("expert", None),
            P("expert", None),
            P("expert", None),
            P("expert", None),
            P("expert", None),
            P("expert", None),
            P(None, None, "expert"),
            P(None, None, "expert"),
            P(None, None, "expert"),
            P("expert", None),
            P("expert", None),
            P("expert", None),
            P(),
            P(),
            P(),
        ),
        check_vma=False,
    )
```

time: 1280 us -> 460 us (0.36)
  waiting for transfers between devices: 579 us -> 214 us
  blocking collectives: 336 us -> 0 us
  Pallas kernels: 0 us -> 143 us
  matrix products: 102 us -> 0 us
  other arithmetic: 103 us -> 22.8 us
  local copies, waits for them, and re-layouts: 87 us -> 17.8 us
  between operations: 35.6 us -> 3.29 us
  starting transfers between devices: 26.9 us -> 55.3 us
    reduce_scatter x5 -> x0, waiting for transfers between devices: 256 us -> none  [the longest x1 97.7 us: shards(): lax.psum_scatter(summed[4], 'expert', scatter_dimension=0, tiled=True)]
    all_gather x5 -> x0, blocking collectives: 206 us -> none  [the longest x1 84 us: shards(): lax.all_gather(router.astype(coarse_float_kind), 'expert', axis=0, tiled=...]
    pallas_call x0 -> x15, Pallas kernels: none -> 143 us  [the longest x5 52.8 us: simple_call(): pl.pallas_call(kernel, out_shape=outs, in_specs=[spec for a, spec in pair...]
    psum x5 -> x0, blocking collectives: 130 us -> none  [the longest x2 79.8 us: shards(): counts, domain_sums = lax.psum((local_counts, local_sums), ('dp', 'expert'))]
    unnamed x12 -> x0, waiting for transfers between devices: 128 us -> none
    ppermute x0 -> x27, waiting for transfers between devices: none -> 103 us  [flip(): return lax.ppermute(value, axis_name, [(i, i ^ bit) for i in range(count)])]
    dot_general x32 -> x0, matrix products: 101 us -> none  [the longest x1 11.1 us: shards(): jnp.einsum('qhd,khd->hqk', grad_mixed, value_rows, preferred_element_type...]
    psum x1 -> x0, waiting for transfers between devices: 85.4 us -> none  [shards(): lax.psum((grad_vectors, grad_input, grad_output, grad_router, grad_shin,...]
  transfers between devices with their start and end apart: 14 -> 35, of which waited for: 10 -> 21; matrix products, arithmetic and copies ran while one was open for 11% -> 6% of each run, Pallas kernels for 0% -> 20%
where the time goes in v2:
time: 460 us; the launch traced here: 456 us
  waiting for transfers between devices  214 us (47%)
  Pallas kernels  143 us (31%)
  starting transfers between devices  55.3 us (12%)
  other arithmetic  22.8 us (5%)
  local copies, waits for them, and re-layouts  17.8 us (4%)
    all_to_all x8, waiting for transfers between devices, exchange(): lax.all_to_all(value, 'expert', split_axis=0, concat_axis=0, tiled=True)  111 us
    ppermute x27, waiting for transfers between devices, flip(): return lax.ppermute(value, axis_name, [(i, i ^ bit) for i in range(count)])  103 us
    pallas_call x5, Pallas kernels, simple_call(): pl.pallas_call(kernel, out_shape=outs, in_specs=[spec for a, spec in pair...  52.8 us
    all_to_all x8, starting transfers between devices, exchange(): lax.all_to_all(value, 'expert', split_axis=0, concat_axis=0, tiled=True)  39.2 us
    pallas_call x1, Pallas kernels, shards(): pl.pallas_call(expert_back_split_kernel, out_shape=[out((total_rows, D),...  19.2 us
    pallas_call x1, Pallas kernels, shards(): pl.pallas_call(functools.partial(moments_kernel, fast, count, small_end),...  17.2 us
    ppermute x27, starting transfers between devices, flip(): return lax.ppermute(value, axis_name, [(i, i ^ bit) for i in range(count)])  16.1 us
    pallas_call x1, Pallas kernels, shards(): pl.pallas_call(shared_back_split_kernel, out_shape=[out((amount, D)), out...  13.3 us
  transfers between devices with their start and end apart: 35, of which 21 were waited for; matrix products, arithmetic and copies ran while one was open for 6% of the time, Pallas kernels for 20%

profile of v2, /device:TPU:0, one launch (start us, length us, event | category | flops | bytes accessed | tf_op | source)
XLA Modules:
  0.0 456.2 jit_solution(17769346752132565233)
XLA Ops:
  1.3 2.1 shard_map.571
  3.4 7.3 %all-to-all-start = ((bf16[8,48,896]{2,1,0:T(8,128)(2,1)}), bf16[8,48,896]{2,1,0:T(8,128)(2,1)S(1)}, u32[]{:S(2)}, u32[]{:S(2)}) async-start(bf16[8,48,896]{2,1,0:T(8,128)(2,1)} %shard_map.571), calls=%async_computation | async-start | bytes 1376256 | tf_op jit(solution)/shard_map/all_to_all | solution.py:702
  11.2 3.0 shard_map.572
  14.2 7.0 %shard_map.573 = (bf16[2,384,768]{2,1,0:T(8,128)(2,1)}, bf16[768,384]{1,0:T(8,128)(2,1)}, f32[16,128]{1,0:T(8,128)}) custom-call(f32[5,48]{1,0:T(8,128)} %refs_0_.5, f32[48,1152]{1,0:T(8,128)} %refs_1_.5, f32[48,384]{1,0:T(8,128)} %refs_2_.5, f32[9,48]{1,0:T(8,128)} %bitcast.119, f32[48,3072]{1,0:T(8,128)} %refs_4_.5, f32[192,384]{1,0:T(8,128)} %refs_5_.5, ...), custom_call_target="tpu_custom_call" | custom-call | flops 3000 | bytes 7000 | tf_op jit(solution)/shard_map/pallas_call | solution.py:963
  21.5 7.1 %all-to-all-done = bf16[8,48,896]{2,1,0:T(8,128)(2,1)S(1)} async-done(((bf16[8,48,896]{2,1,0:T(8,128)(2,1)}), bf16[8,48,896]{2,1,0:T(8,128)(2,1)S(1)}, u32[]{:S(2)}, u32[]{:S(2)}) %all-to-all-start) | async-done | bytes 688160 | tf_op jit(solution)/shard_map/all_to_all | solution.py:702
  29.7 4.0 all-to-all-start.1
  33.7 2.1 collective-permute-done.other
  36.7 14.7 %shard_map.574 = (f32[512,384]{1,0:T(8,128)}, bf16[512,384]{1,0:T(8,128)(2,1)}, bf16[512,1152]{1,0:T(8,128)(2,1)}, f32[512,128]{1,0:T(8,128)}, bf16[512,384]{1,0...) custom-call(s32[2]{0:T(128)} %pad_add_fusion.core.sides, ...), custom_call_target="tpu_custom_call" | custom-call | flops 8000000 | bytes 9499 | tf_op jit(solution)/shard_map/pallas_call | solution.py:637
  51.5 4.6 %all-to-all-done.1 = bf16[8,48,1152]{2,1,0:T(8,128)(2,1)S(1)} async-done(((bf16[8,48,1152]{2,1,0:T(8,128)(2,1)}), bf16[8,48,1152]{2,1,0:T(8,128)(2,1)S(1)}, u32[]{:S(2)}, u32[]{:S(2)}) %all-to-all-start.1) | async-done | bytes 884768 | tf_op jit(solution)/shard_map/all_to_all | solution.py:702
  56.1 3.6 all-to-all-start.2
  61.2 19.7 %collective-permute-done.1 = bf16[8,48,1152]{2,1,0:T(8,128)(2,1)S(1)} collective-permute-done((bf16[8,48,1152]{2,1,0:T(8,128)(2,1)S(1)}, bf16[8,48,1152]{2,1,0:T(8,128)(2,1)S(1)}, u32[]{:S(2)}, u32[]{:S(2)}) %collective-permute-start.1) | collective-permute-done | bytes 884768 | tf_op jit(solution)/shard_map/ppermute | solution.py:655
  80.9 15.9 %all-to-all-done.2 = bf16[8,256,384]{2,1,0:T(8,128)(2,1)S(1)} async-done(((bf16[8,256,384]{2,1,0:T(8,128)(2,1)}), bf16[8,256,384]{2,1,0:T(8,128)(2,1)S(1)}, u32[]{:S(2)}, u32[]{:S(2)}) %all-to-all-start.2) | async-done | bytes 1572896 | tf_op jit(solution)/shard_map/all_to_all | solution.py:702
  98.0 8.5 %shard_map.575 = s16[8,272,384]{2,1,0:T(8,128)(2,1)} custom-call(bf16[2048,384]{1,0:T(8,128)(2,1)} %bitcast.102, bf16[2,384,768]{2,1,0:T(8,128)(2,1)} %get-tuple-element.126.gate_up, bf16[768,384]{1,0:T(8,128)(2,1)} %get-tuple-element.127.down), custom_call_target="tpu_custom_call" | custom-call | flops 3623878 | bytes 7000 | tf_op jit(solution)/shard_map/pallas_call | solution.py:1044
  108.0 5.0 %all-to-all-start.3 = ((s16[8,272,384]{2,1,0:T(8,128)(2,1)}), s16[8,272,384]{2,1,0:T(8,128)(2,1)}, u32[]{:S(2)}, u32[]{:S(2)}) async-start(s16[8,272,384]{2,1,0:T(8,128)(2,1)} %shard_map.575), calls=%async_computation.3 | async-start | bytes 3342336 | tf_op jit(solution)/shard_map/all_to_all | solution.py:702
  117.6 3.3 broadcast_select_fusion.1
  122.0 2.5 reshape.119
  126.4 1.7 pad_maximum_fusion
  128.1 5.7 %shard_map.576.shared = f32[512,384]{1,0:T(8,128)} custom-call(bf16[512,384]{1,0:T(8,128)(2,1)} %get-tuple-element.139.second, bf16[384,3072]{1,0:T(8,128)(2,1)} %bitcast.98, bf16[384,3072]{1,0:T(8,128)(2,1)} %bitcast.99, bf16[1536,384]{1,0:T(8,128)(2,1)} %bitcast.104), custom_call_target="tpu_custom_call" | custom-call | flops 1811939 | bytes 5000 | tf_op jit(solution)/shard_map/pallas_call | solution.py:1081
  133.8 19.1 %all-to-all-done.3.returned = s16[8,272,384]{2,1,0:T(8,128)(2,1)} async-done(((s16[8,272,384]{2,1,0:T(8,128)(2,1)}), s16[8,272,384]{2,1,0:T(8,128)(2,1)}, u32[]{:S(2)}, u32[]{:S(2)}) %all-to-all-start.3) | async-done | bytes 1671200 | tf_op jit(solution)/shard_map/all_to_all | solution.py:702
  152.9 11.4 %shard_map.577 = (f32[512,384]{1,0:T(8,128)}, bf16[512,384]{1,0:T(8,128)(2,1)}, bf16[2048,384]{1,0:T(8,128)(2,1)}, bf16[512,128]{1,0:T(8,128)(2,1)}, f32[384,128...) custom-call(s16[8,272,384]{2,1,0:T(8,128)(2,1)} %all-to-all-done.3.returned, f32[512,128]{1,0:T(8,128)} %get-tuple-element.125.known, ...), custom_call_target="tpu_custom_call" | custom-call | flops 7000000 | bytes 8420 | tf_op jit(solution)/shard_map/pallas_call | solution.py:637
  164.3 3.8 all-to-all-start.4
  168.2 13.3 %shard_map.578 = (f32[512,384]{1,0:T(8,128)}, f32[2,384,768]{2,1,0:T(8,128)}, f32[2,384,768]{2,1,0:T(8,128)}, f32[2,384,384]{2,1,0:T(8,128)}, f32[2,384,384]{2,1,0:T(8,128)}) custom-call(s32[2]{0:T(128)} %pad_add_fusion.core.sides, bf16[512,384]{1,0:T(8,128)(2,1)} %get-tuple-element.139.second, bf16[512,384]{1,0:T(8,128)(2,1)} %get-tuple-element.148.slope, ...), custom_call_target="tpu_custom_call" | custom-call | flops 4831838 | bytes 14000 | tf_op jit(solution)/shard_map/pallas_call | solution.py:1137
  182.0 23.3 %all-to-all-done.4 = bf16[8,256,384]{2,1,0:T(8,128)(2,1)S(1)} async-done(((bf16[8,256,384]{2,1,0:T(8,128)(2,1)}), bf16[8,256,384]{2,1,0:T(8,128)(2,1)S(1)}, u32[]{:S(2)}, u32[]{:S(2)}) %all-to-all-start.4) | async-done | bytes 1572896 | tf_op jit(solution)/shard_map/all_to_all | solution.py:702
  206.5 19.2 %shard_map.579 = (bf16[2048,384]{1,0:T(8,128)(2,1)}, f32[384,768]{1,0:T(8,128)}, f32[384,768]{1,0:T(8,128)}, f32[384,384]{1,0:T(8,128)}, f32[384,384]{1,0:T(8,128)}) custom-call(s32[2]{0:T(128)} %pad_add_fusion.core.sides, bf16[2048,384]{1,0:T(8,128)(2,1)} %bitcast.103, bf16[2048,384]{1,0:T(8,128)(2,1)} %bitcast.106, ...), custom_call_target="tpu_custom_call" | custom-call | flops 9663676 | bytes 10000 | tf_op jit(solution)/shard_map/pallas_call | solution.py:1173
  225.6 3.6 all-to-all-start.5
  229.3 5.4 %shard_map.580 = (f32[384,1152]{1,0:T(8,128)}, f32[384,1152]{1,0:T(8,128)}) custom-call(f32[2,384,768]{2,1,0:T(8,128)} %get-tuple-element.154.in_keep, f32[2,384,768]{2,1,0:T(8,128)} %collective-permute-done.6.in_other, f32[2,384,384]{2,1,0:T(8,128)} %get-tuple-element.156.out_keep, f32[2,384,384]{2,1,0:T(8,128)} %collective-permute-done.7.out_other), custom_call_target="tpu_custom_call" | custom-call | flops 2000 | bytes 10000 | tf_op jit(solution)/shard_map/pallas_call | solution.py:1205
  237.3 38.0 %collective-permute-done.4 = f32[1,128]{1,0:T(1,128)S(1)} collective-permute-done((f32[1,128]{1,0:T(1,128)S(1)}, f32[1,128]{1,0:T(1,128)S(1)}, u32[]{:S(2)}, u32[]{:S(2)}) %collective-permute-start.4) | collective-permute-done | bytes 544 | tf_op jit(solution)/shard_map/ppermute | solution.py:655
  276.1 1.9 copy-done.13
  280.5 5.8 %shard_map.581 = (f32[512,384]{1,0:T(8,128)}, bf16[512,384]{1,0:T(8,128)(2,1)}, f32[384,384]{1,0:T(8,128)}, f32[1,384]{1,0:T(1,128)}, f32[384,128]{1,0:T(8,128)}) custom-call(bf16[2048,384]{1,0:T(8,128)(2,1)} %bitcast.107, f32[512,128]{1,0:T(8,128)} %get-tuple-element.125.known, f32[512,384]{1,0:T(8,128)} %get-tuple-element.149.second_slope, ...), custom_call_target="tpu_custom_call" | custom-call | flops 2000000 | bytes 9844 | tf_op jit(solution)/shard_map/pallas_call | solution.py:637
  286.4 5.9 %all-to-all-start.6 = ((f32[8,48,1152]{2,1,0:T(8,128)}), f32[8,48,1152]{2,1,0:T(8,128)S(1)}, u32[]{:S(2)}, u32[]{:S(2)}) async-start(f32[8,48,1152]{2,1,0:T(8,128)} %bitcast.83), calls=%async_computation.6 | async-start | bytes 3538944 | tf_op jit(solution)/shard_map/all_to_all | solution.py:702
  292.3 18.3 %shard_map.582 = (f32[192,1664]{1,0:T(8,128)}, f32[192,1664]{1,0:T(8,128)}) custom-call(s32[2]{0:T(128)} %pad_add_fusion.core.sides, bf16[512,384]{1,0:T(8,128)(2,1)} %get-tuple-element.166.mixed_slope, bf16[512,1152]{1,0:T(8,128)(2,1)} %get-tuple-element.171.qkv, f32[512,128]{1,0:T(8,128)} %get-tuple-element.172.log_total, ...), custom_call_target="tpu_custom_call" | custom-call | flops 16000000 | bytes 9239 | tf_op jit(solution)/shard_map/pallas_call | solution.py:637
  313.8 2.5 add.77
  316.3 15.8 %all-to-all-done.6 = f32[8,48,1152]{2,1,0:T(8,128)S(1)} async-done(((f32[8,48,1152]{2,1,0:T(8,128)}), f32[8,48,1152]{2,1,0:T(8,128)S(1)}, u32[]{:S(2)}, u32[]{:S(2)}) %all-to-all-start.6) | async-done | bytes 1769504 | tf_op jit(solution)/shard_map/all_to_all | solution.py:702
  332.9 18.9 %collective-permute-done.11 = f32[384,384]{1,0:T(8,128)} collective-permute-done((f32[384,384]{1,0:T(8,128)S(1)}, f32[384,384]{1,0:T(8,128)}, u32[]{:S(2)}, u32[]{:S(2)}) %collective-permute-start.11) | collective-permute-done | bytes 589856 | tf_op jit(solution)/shard_map/ppermute | solution.py:655
  351.8 6.0 %all-to-all-start.7 = ((f32[8,24,1664]{2,1,0:T(8,128)}), f32[8,24,1664]{2,1,0:T(8,128)S(1)}, u32[]{:S(2)}, u32[]{:S(2)}) async-start(f32[8,24,1664]{2,1,0:T(8,128)} %bitcast.108), calls=%async_computation.7 | async-start | bytes 2555904 | tf_op jit(solution)/shard_map/all_to_all | solution.py:702
  357.8 1.8 add.74.refs_0_.refs_33_
  363.0 25.3 %all-to-all-done.7 = f32[8,24,1664]{2,1,0:T(8,128)S(1)} async-done(((f32[8,24,1664]{2,1,0:T(8,128)}), f32[8,24,1664]{2,1,0:T(8,128)S(1)}, u32[]{:S(2)}, u32[]{:S(2)}) %all-to-all-start.7) | async-done | bytes 1277984 | tf_op jit(solution)/shard_map/all_to_all | solution.py:702
  391.0 3.5 collective-permute-done.14
  394.5 1.6 add.78.refs_4_.refs_27_
  396.2 2.4 shard_map.583
  402.1 2.2 collective-permute-done.16
  404.2 3.6 collective-permute-done.17
  408.4 3.9 collective-permute-done.18
  414.3 17.2 %shard_map.584 = (f32[5,48]{1,0:T(8,128)}, f32[48,1152]{1,0:T(8,128)}, f32[48,384]{1,0:T(8,128)}, f32[9,48]{1,0:T(8,128)}, f32[48,3072]{1,0:T(8,128)}, /*index=5...) custom-call(s32[2]{0:T(128)} %pad_add_fusion.core.sides, ...), custom_call_target="tpu_custom_call" | custom-call | flops 30000 | bytes 34000 | tf_op jit(solution)/shard_map/pallas_call | solution.py:1311
  433.6 2.3 collective-permute-done.24
  436.6 3.7 collective-permute-done.25
  442.7 2.2 collective-permute-done.26
  446.3 8.6 %shard_map.585 = (f32[5,48]{1,0:T(8,128)}, f32[48,1152]{1,0:T(8,128)}, f32[48,384]{1,0:T(8,128)}, f32[9,48]{1,0:T(8,128)}, f32[48,3072]{1,0:T(8,128)}, /*index=5...) custom-call(f32[9,128]{1,0:T(8,128)} %get-tuple-element.289.totals, ...), custom_call_target="tpu_custom_call" | custom-call | flops 3000 | bytes 15000 | tf_op jit(solution)/shard_map/pallas_call | solution.py:1327
  (152 shorter events, 44.6 us)
Async XLA Ops:
  3.4 25.3 %all-to-all-start = ((bf16[8,48,896]{2,1,0:T(8,128)(2,1)}), bf16[8,48,896]{2,1,0:T(8,128)(2,1)S(1)}, u32[]{:S(2)}, u32[]{:S(2)}) async-start(bf16[8,48,896]{2,1,0:T(8,128)(2,1)} %shard_map.571), calls=%async_computation | async-start | bytes 1376256 | tf_op jit(solution)/shard_map/all_to_all | solution.py:702
  14.2 7.0 %copy-start.8 = (f32[192,384]{1,0:T(8,128)S(1)}, f32[192,384]{1,0:T(8,128)}, u32[]{:S(2)}) copy-start(f32[192,384]{1,0:T(8,128)} %refs_5_.5) | copy-start | bytes 884740
  14.2 7.0 %copy-start.2 = (f32[48,3072]{1,0:T(8,128)S(1)}, f32[48,3072]{1,0:T(8,128)}, u32[]{:S(2)}) copy-start(f32[48,3072]{1,0:T(8,128)} %refs_4_.5) | copy-start | bytes 1769476
  28.6 7.3 %copy-start.9 = (bf16[8,48,896]{2,1,0:T(8,128)(2,1)}, bf16[8,48,896]{2,1,0:T(8,128)(2,1)S(1)}, u32[]{:S(2)}) copy-start(bf16[8,48,896]{2,1,0:T(8,128)(2,1)S(1)} %all-to-all-done) | copy-start | bytes 2064388
  29.7 26.3 %all-to-all-start.1 = ((bf16[8,48,1152]{2,1,0:T(8,128)(2,1)}), bf16[8,48,1152]{2,1,0:T(8,128)(2,1)S(1)}, u32[]{:S(2)}, u32[]{:S(2)}) async-start(bf16[8,48,1152]{2,1,0:T(8,128)(2,1)} %broadcast_in_dim.20), calls=%async_computation.1 | async-start | bytes 1769472 | tf_op jit(solution)/shard_map/all_to_all | solution.py:702
  33.7 2.2 collective-permute-start
  56.1 40.8 %all-to-all-start.2 = ((bf16[8,256,384]{2,1,0:T(8,128)(2,1)}), bf16[8,256,384]{2,1,0:T(8,128)(2,1)S(1)}, u32[]{:S(2)}, u32[]{:S(2)}) async-start(bf16[8,256,384]{2,1,0:T(8,128)(2,1)} %bitcast.114), calls=%async_computation.2 | async-start | bytes 3145728 | tf_op jit(solution)/shard_map/all_to_all | solution.py:702
  59.7 21.3 %collective-permute-start.1 = (bf16[8,48,1152]{2,1,0:T(8,128)(2,1)S(1)}, bf16[8,48,1152]{2,1,0:T(8,128)(2,1)S(1)}, u32[]{:S(2)}, u32[]{:S(2)}) collective-permute-start(bf16[8,48,1152]{2,1,0:T(8,128)(2,1)S(1)} %all-to-all-done.1), channel_id=1, source_target_pairs={{0,16},{8,24},{16,0},{24,8},{1,17},{9,25},{17,1},{25,9},{2,18},{10... | collective-permute-start | bytes 2654216 | tf_op jit(solution)/shard_map/ppermute | solution.py:655
  108.0 9.6 %collective-permute-start.2 = (bf16[8,48,2304]{2,1,0:T(8,128)(2,1)}, bf16[8,48,2304]{2,1,0:T(8,128)(2,1)}, u32[]{:S(2)}, u32[]{:S(2)}) collective-permute-start(bf16[8,48,2304]{2,1,0:T(8,128)(2,1)} %pad_maximum_fusion.1), channel_id=1, source_target_pairs={{0,8},{8,0},{16,24},{24,16},{1,9},{9,1},{17,25},{25,17},{2,10},{10... | collective-permute-start | bytes 5308424 | tf_op jit(solution)/shard_map/ppermute | solution.py:655
  108.0 44.9 %all-to-all-start.3 = ((s16[8,272,384]{2,1,0:T(8,128)(2,1)}), s16[8,272,384]{2,1,0:T(8,128)(2,1)}, u32[]{:S(2)}, u32[]{:S(2)}) async-start(s16[8,272,384]{2,1,0:T(8,128)(2,1)} %shard_map.575), calls=%async_computation.3 | async-start | bytes 3342336 | tf_op jit(solution)/shard_map/all_to_all | solution.py:702
  113.4 3.6 collective-permute-start.3
  164.3 41.0 %all-to-all-start.4 = ((bf16[8,256,384]{2,1,0:T(8,128)(2,1)}), bf16[8,256,384]{2,1,0:T(8,128)(2,1)S(1)}, u32[]{:S(2)}, u32[]{:S(2)}) async-start(bf16[8,256,384]{2,1,0:T(8,128)(2,1)} %bitcast.113), calls=%async_computation.4 | async-start | bytes 3145728 | tf_op jit(solution)/shard_map/all_to_all | solution.py:702
  181.5 47.8 %collective-permute-start.6 = (f32[2,384,768]{2,1,0:T(8,128)}, f32[2,384,768]{2,1,0:T(8,128)}, u32[]{:S(2)}, u32[]{:S(2)}) collective-permute-start(f32[2,384,768]{2,1,0:T(8,128)} %get-tuple-element.155), channel_id=1, source_target_pairs={{0,8},{8,0},{16,24},{24,16},{1,9},{9,1},{17,25},{25,17},{2,10},{10... | collective-permute-start | bytes 7077896 | tf_op jit(solution)/shard_map/ppermute | solution.py:655
  181.5 47.8 %collective-permute-start.7 = (f32[2,384,384]{2,1,0:T(8,128)}, f32[2,384,384]{2,1,0:T(8,128)}, u32[]{:S(2)}, u32[]{:S(2)}) collective-permute-start(f32[2,384,384]{2,1,0:T(8,128)} %get-tuple-element.157), channel_id=1, source_target_pairs={{0,8},{8,0},{16,24},{24,16},{1,9},{9,1},{17,25},{25,17},{2,10},{10... | collective-permute-start | bytes 3538952 | tf_op jit(solution)/shard_map/ppermute | solution.py:655
  225.6 53.7 %all-to-all-start.5 = ((bf16[8,256,384]{2,1,0:T(8,128)(2,1)}), bf16[8,256,384]{2,1,0:T(8,128)(2,1)S(1)}, u32[]{:S(2)}, u32[]{:S(2)}) async-start(bf16[8,256,384]{2,1,0:T(8,128)(2,1)} %bitcast.112), calls=%async_computation.5 | async-start | bytes 3145728 | tf_op jit(solution)/shard_map/all_to_all | solution.py:702
  229.3 7.4 %copy-start.30 = (f32[1,128]{1,0:T(1,128)S(1)}, f32[1,128]{1,0:T(1,128)}, u32[]{:S(2)}) copy-start(f32[1,128]{1,0:T(1,128)} %get-tuple-element.146) | copy-start | bytes 1540
  229.3 46.4 %copy-start.18 = (f32[384,384]{1,0:T(8,128)S(1)}, f32[384,384]{1,0:T(8,128)}, u32[]{:S(2)}) copy-start(f32[384,384]{1,0:T(8,128)} %get-tuple-element.159) | copy-start | bytes 1769476
  234.7 41.2 %copy-start.15 = (f32[384,768]{1,0:T(8,128)S(1)}, f32[384,768]{1,0:T(8,128)}, u32[]{:S(2)}) copy-start(f32[384,768]{1,0:T(8,128)} %get-tuple-element.151) | copy-start | bytes 3538948
  234.7 41.3 %collective-permute-start.8 = (f32[384,1152]{1,0:T(8,128)}, f32[384,1152]{1,0:T(8,128)S(1)}, u32[]{:S(2)}, u32[]{:S(2)}) collective-permute-start(f32[384,1152]{1,0:T(8,128)} %get-tuple-element.158), channel_id=1, source_target_pairs={{0,16},{8,24},{16,0},{24,8},{1,17},{9,25},{17,1},{25,9},{2,18},{10... | collective-permute-start | bytes 5308424 | tf_op jit(solution)/shard_map/ppermute | solution.py:655
  236.2 39.7 %collective-permute-start.5 = (f32[384,768]{1,0:T(8,128)S(1)}, f32[384,768]{1,0:T(8,128)S(1)}, u32[]{:S(2)}, u32[]{:S(2)}) collective-permute-start(f32[384,768]{1,0:T(8,128)S(1)} %copy-done.28), channel_id=1, source_target_pairs={{0,8},{8,0},{16,24},{24,16},{1,9},{9,1},{17,25},{25,17},{2,10},{10... | collective-permute-start | bytes 3538952 | tf_op jit(solution)/shard_map/ppermute | solution.py:655
  236.2 39.5 %collective-permute-start.9 = (f32[384,384]{1,0:T(8,128)S(1)}, f32[384,384]{1,0:T(8,128)S(1)}, u32[]{:S(2)}, u32[]{:S(2)}) collective-permute-start(f32[384,384]{1,0:T(8,128)S(1)} %copy-done.29), channel_id=1, source_target_pairs={{0,8},{8,0},{16,24},{24,16},{1,9},{9,1},{17,25},{25,17},{2,10},{10... | collective-permute-start | bytes 1769480 | tf_op jit(solution)/shard_map/ppermute | solution.py:655
  236.7 38.5 %collective-permute-start.4 = (f32[1,128]{1,0:T(1,128)S(1)}, f32[1,128]{1,0:T(1,128)S(1)}, u32[]{:S(2)}, u32[]{:S(2)}) collective-permute-start(f32[1,128]{1,0:T(1,128)S(1)} %copy-done.30), channel_id=1, source_target_pairs={{0,16},{8,24},{16,0},{24,8},{1,17},{9,25},{17,1},{25,9},{2,18},{10... | collective-permute-start | bytes 1544 | tf_op jit(solution)/shard_map/ppermute | solution.py:655
  275.9 36.4 %copy-start.10 = (f32[384,384]{1,0:T(8,128)}, f32[384,384]{1,0:T(8,128)S(1)}, u32[]{:S(2)}) copy-start(f32[384,384]{1,0:T(8,128)S(1)} %add.73) | copy-start | bytes 1769476
  276.0 34.6 %copy-start.7 = (f32[384,768]{1,0:T(8,128)}, f32[384,768]{1,0:T(8,128)S(1)}, u32[]{:S(2)}) copy-start(f32[384,768]{1,0:T(8,128)S(1)} %add.72) | copy-start | bytes 3538948
  286.4 45.8 %all-to-all-start.6 = ((f32[8,48,1152]{2,1,0:T(8,128)}), f32[8,48,1152]{2,1,0:T(8,128)S(1)}, u32[]{:S(2)}, u32[]{:S(2)}) async-start(f32[8,48,1152]{2,1,0:T(8,128)} %bitcast.83), calls=%async_computation.6 | async-start | bytes 3538944 | tf_op jit(solution)/shard_map/all_to_all | solution.py:702
  310.6 3.2 collective-permute-start.13
  310.7 41.1 %collective-permute-start.10 = (f32[384,768]{1,0:T(8,128)S(1)}, f32[384,768]{1,0:T(8,128)}, u32[]{:S(2)}, u32[]{:S(2)}) collective-permute-start(f32[384,768]{1,0:T(8,128)S(1)} %add.72), channel_id=1, source_target_pairs={{0,16},{8,24},{16,0},{24,8},{1,17},{9,25},{17,1},{25,9},{2,18},{10... | collective-permute-start | bytes 3538952 | tf_op jit(solution)/shard_map/ppermute | solution.py:655
  312.2 39.6 %collective-permute-start.11 = (f32[384,384]{1,0:T(8,128)S(1)}, f32[384,384]{1,0:T(8,128)}, u32[]{:S(2)}, u32[]{:S(2)}) collective-permute-start(f32[384,384]{1,0:T(8,128)S(1)} %add.73), channel_id=1, source_target_pairs={{0,16},{8,24},{16,0},{24,8},{1,17},{9,25},{17,1},{25,9},{2,18},{10... | collective-permute-start | bytes 1769480 | tf_op jit(solution)/shard_map/ppermute | solution.py:655
  351.8 36.5 %all-to-all-start.7 = ((f32[8,24,1664]{2,1,0:T(8,128)}), f32[8,24,1664]{2,1,0:T(8,128)S(1)}, u32[]{:S(2)}, u32[]{:S(2)}) async-start(f32[8,24,1664]{2,1,0:T(8,128)} %bitcast.108), calls=%async_computation.7 | async-start | bytes 2555904 | tf_op jit(solution)/shard_map/all_to_all | solution.py:702
  359.6 36.5 %copy-start.1 = (f32[384,768]{1,0:T(8,128)}, f32[384,768]{1,0:T(8,128)S(1)}, u32[]{:S(2)}) copy-start(f32[384,768]{1,0:T(8,128)S(1)} %add.74.refs_0_.refs_33_) | copy-start | bytes 3538948
  359.7 53.2 %collective-permute-start.22 = (f32[384,768]{1,0:T(8,128)S(1)}, f32[384,768]{1,0:T(8,128)}, u32[]{:S(2)}, u32[]{:S(2)}) collective-permute-start(f32[384,768]{1,0:T(8,128)S(1)} %add.74.refs_0_.refs_33_), channel_id=1, source_target_pairs={{0,8},{8,0},{16,24},{24,16},{1,9},{9,1},{17,25},{25,17},{2,10},{10... | collective-permute-start | bytes 3538952 | tf_op jit(solution)/shard_map/ppermute | solution.py:655
  361.3 34.8 %copy-start.6 = (f32[384,384]{1,0:T(8,128)}, f32[384,384]{1,0:T(8,128)S(1)}, u32[]{:S(2)}) copy-start(f32[384,384]{1,0:T(8,128)S(1)} %add.75.refs_1_.refs_35_) | copy-start | bytes 1769476
  361.3 51.5 %collective-permute-start.23 = (f32[384,384]{1,0:T(8,128)S(1)}, f32[384,384]{1,0:T(8,128)}, u32[]{:S(2)}, u32[]{:S(2)}) collective-permute-start(f32[384,384]{1,0:T(8,128)S(1)} %add.75.refs_1_.refs_35_), channel_id=1, source_target_pairs={{0,8},{8,0},{16,24},{24,16},{1,9},{9,1},{17,25},{25,17},{2,10},{10... | collective-permute-start | bytes 1769480 | tf_op jit(solution)/shard_map/ppermute | solution.py:655
  361.4 29.1 %collective-permute-start.12 = (f32[48,1152]{1,0:T(8,128)S(1)}, f32[48,1152]{1,0:T(8,128)S(1)}, u32[]{:S(2)}, u32[]{:S(2)}) collective-permute-start(f32[48,1152]{1,0:T(8,128)S(1)} %copy-done.12), channel_id=1, source_target_pairs={{0,16},{8,24},{16,0},{24,8},{1,17},{9,25},{17,1},{25,9},{2,18},{10... | collective-permute-start | bytes 663560 | tf_op jit(solution)/shard_map/ppermute | solution.py:655
  389.0 5.5 %collective-permute-start.14 = (f32[24,1664]{1,0:T(8,128)}, f32[24,1664]{1,0:T(8,128)S(1)}, u32[]{:S(2)}, u32[]{:S(2)}) collective-permute-start(f32[24,1664]{1,0:T(8,128)} %reduce_sum.19), channel_id=1, source_target_pairs={{0,16},{8,24},{16,0},{24,8},{1,17},{9,25},{17,1},{25,9},{2,18},{10... | collective-permute-start | bytes 479240 | tf_op jit(solution)/shard_map/ppermute | solution.py:655
  390.5 22.3 %collective-permute-start.20 = (f32[48,1152]{1,0:T(8,128)S(1)}, f32[48,1152]{1,0:T(8,128)S(1)}, u32[]{:S(2)}, u32[]{:S(2)}) collective-permute-start(f32[48,1152]{1,0:T(8,128)S(1)} %copy-done.12), channel_id=1, source_target_pairs={{0,8},{8,0},{16,24},{24,16},{1,9},{9,1},{17,25},{25,17},{2,10},{10... | collective-permute-start | bytes 663560 | tf_op jit(solution)/shard_map/ppermute | solution.py:655
  390.5 22.3 %collective-permute-start.21 = (f32[48,1152]{1,0:T(8,128)S(1)}, f32[48,1152]{1,0:T(8,128)S(1)}, u32[]{:S(2)}, u32[]{:S(2)}) collective-permute-start(f32[48,1152]{1,0:T(8,128)S(1)} %collective-permute-done.12.refs_3_.refs_30_), channel_id=1, source_target_pairs={{0,8},{8,0},{16,24},{24,16},{1,9},{9,1},{17,25},{25,17},{2,10},{10... | collective-permute-start | bytes 663560 | tf_op jit(solution)/shard_map/ppermute | solution.py:655
  396.2 16.1 %copy-start.14 = (f32[24,1664]{1,0:T(8,128)S(1)}, f32[24,1664]{1,0:T(8,128)}, u32[]{:S(2)}) copy-start(f32[24,1664]{1,0:T(8,128)} %add.78.refs_4_.refs_27_) | copy-start | bytes 479236
  398.6 1.4 collective-permute-start.15
  400.6 3.6 collective-permute-start.16
  404.2 3.6 collective-permute-start.17
  407.8 4.5 collective-permute-start.18
  412.3 1.4 collective-permute-start.19
  414.3 17.2 %copy-start.23 = (f32[16,128]{1,0:T(8,128)S(1)}, f32[16,128]{1,0:T(8,128)}, u32[]{:S(2)}) copy-start(f32[16,128]{1,0:T(8,128)} %get-tuple-element.128) | copy-start | bytes 24580
  414.3 22.3 %copy-start.24 = (f32[2,128]{1,0:T(2,128)S(1)}, f32[2,128]{1,0:T(2,128)}, u32[]{:S(2)}) copy-start(f32[2,128]{1,0:T(2,128)} %add.82.square_ref) | copy-start | bytes 3076
  432.2 3.7 collective-permute-start.24
  436.6 3.7 collective-permute-start.25
  440.3 4.6 %collective-permute-start.26 = (f32[18,128]{1,0:T(8,128)S(1)}, f32[18,128]{1,0:T(8,128)S(1)}, u32[]{:S(2)}, u32[]{:S(2)}) collective-permute-start(f32[18,128]{1,0:T(8,128)S(1)} %add.84), channel_id=1, source_target_pairs={{0,4},{1,5},{2,6},{3,7},{4,0},{5,1},{6,2},{7,3},{8,12},{9,13},{10,... | collective-permute-start | bytes 27656 | tf_op jit(solution)/shard_map/ppermute | solution.py:655
  (18 other events, 51.3 us)

commit v3 on v2

--- a/solution.py
+++ b/solution.py
@@ -403,11 +403,79 @@
                 ]
 
 
+def coded_tile(value):
+    top = jnp.max(jnp.abs(value), -1, keepdims=True)
+    power = jnp.ceil(jnp.log2(jnp.maximum(top, 1e-30)))
+    code = jnp.clip(jnp.round(value * jnp.exp2(15.0 - power)), -32767.0, 32767.0)
+    return code, power
+
+
+def encode(ref, tiles):
+    lane = lanes_of(tiles[0].shape)
+    powers = jnp.zeros(tiles[0].shape, F32)
+    for index, tile in enumerate(tiles):
+        code, power = coded_tile(tile)
+        ref[:, index * 128 : (index + 1) * 128] = code.astype(jnp.int32).astype(jnp.int16)
+        powers = jnp.where(lane == index, power, powers)
+    ref[:, len(tiles) * 128 :] = powers.astype(jnp.int32).astype(jnp.int16)
+
+
+def decode(ref):
+    count = ref.shape[-1] // 128 - 1
+    scale = jnp.exp2(ref[..., count * 128 :].astype(jnp.int32).astype(F32) - 15.0)
+    return [
+        ref[..., index * 128 : (index + 1) * 128].astype(jnp.int32).astype(F32)
+        * scale[..., index : index + 1]
+        for index in range(count)
+    ]
+
+
+def tiles_of(value):
+    return [value[:, at : at + 128] for at in range(0, value.shape[1], 128)]
+
+
 def fold_kernel(in_keep, in_other, out_keep, out_other, keep, give):
     wide = in_keep.shape[2]
-    for side, ref in enumerate((keep, give)):
-        ref[:, :wide] = in_keep[side] + in_other[side]
-        ref[:, wide:] = out_keep[side] + out_other[side]
+    keep[:, :wide] = in_keep[0] + in_other[0]
+    keep[:, wide:] = out_keep[0] + out_other[0]
+    encode(give, tiles_of(in_keep[1] + in_other[1]) + tiles_of(out_keep[1] + out_other[1]))
+
+
+def add_code_kernel(keep, other, code):
+    encode(code, [mine + theirs for mine, theirs in zip(tiles_of(keep[...]), decode(other))])
+
+
+def shard_sum_kernel(codes, total):
+    for index, tile in enumerate(decode(codes)):
+        total[:, index * 128 : (index + 1) * 128] = jnp.sum(tile, 0)
+
+
+def expert_code_kernel(in_keep, in_other, out_keep, out_other, code):
+    encode(code, tiles_of(in_keep[...] + in_other[...]) + tiles_of(out_keep[...] + out_other[...]))
+
+
+def expert_sum_kernel(mine, other, in_total, out_total):
+    split = in_total.shape[1] // 128
+    for index, (left, right) in enumerate(zip(decode(mine), decode(other))):
+        ref, at = (in_total, index) if index < split else (out_total, index - split)
+        ref[:, at * 128 : (at + 1) * 128] = left + right
+
+
+def last_code_kernel(core, keep, other, code):
+    tiles = tiles_of(keep[...] + other[...])
+    rough, power = coded_tile(tiles[5])
+    tiles[6] = jnp.where(core[0] == 1, tiles[5] - rough * jnp.exp2(power - 15.0), tiles[6])
+    encode(code, tiles)
+
+
+def last_sum_kernel(core, codes, total):
+    tiles = decode(codes)
+    high = core[0] == 1
+    fine = tiles[6]
+    tiles[5] = jnp.where(high, tiles[5] + fine, tiles[5])
+    tiles[6] = jnp.where(high, 0.0, fine)
+    for index, tile in enumerate(tiles):
+        total[:, index * 128 : (index + 1) * 128] = jnp.sum(tile, 0)
 
 
 def middle_kernel(
@@ -583,19 +651,15 @@
         (gate_gradient, lift_gradient, gain_one, gain_two[...], gain_three[...])
     ):
         table = jnp.where(row == VECTORS_AT + offset, piece, table)
-    pack_out[:, SMALL_AT:] = small_before[...] + table.T
+    pack_out[:, SMALL_AT : SMALL_AT + SMALL] = small_before[...] + table.T
     if not fast:
-        keep_out[...] = pack_out[...]
+        keep_out[...] = pack_out[:, : keep_out.shape[1]]
         give_out[...] = jnp.zeros_like(give_out)
         return
-    shard = keep_out.shape[0] // EXPERTS
-    for index in range(EXPERTS):
-        here = slice(index * shard, (index + 1) * shard)
-        base = 2 * shard * index
-        keep_out[here, :] = pack_out[pl.ds(pl.multiple_of(base + core[0] * shard, 8), shard), :]
-        give_out[here, :] = pack_out[
-            pl.ds(pl.multiple_of(base + (1 - core[0]) * shard, 8), shard), :
-        ]
+    pack_out[:, SMALL_AT + SMALL :] = jnp.zeros_like(pack_out[:, SMALL_AT + SMALL :])
+    half = keep_out.shape[1]
+    keep_out[...] = pack_out[:, pl.ds(pl.multiple_of(core[0] * half, 128), half)]
+    give_out[...] = pack_out[:, pl.ds(pl.multiple_of((1 - core[0]) * half, 128), half)]
 
 
 def lamb_direction(master, gradient, mean, square, factor):
@@ -616,8 +680,8 @@
     return pl.BlockSpec(shape, lambda *unused: (0,) * len(shape))
 
 
-def params(**extra):
-    return pltpu.CompilerParams(vmem_limit_bytes=VMEM, **extra)
+def params(limit=VMEM):
+    return pltpu.CompilerParams(vmem_limit_bytes=limit)
 
 
 def cost(flops, size):
@@ -794,9 +858,16 @@
     def last_rows(start, stop):
         if not fast:
             return pieces[0][:, start:stop]
-        mine, other = pieces[0][:, start:stop], pieces[1][:, start:stop]
         low = sides[0] == 0
-        return jnp.concatenate([jnp.where(low, mine, other), jnp.where(low, other, mine)], 0)
+        half = pieces[0].shape[1]
+        parts = []
+        for side in range(2):
+            begin, end = max(start, side * half), min(stop, (side + 1) * half)
+            if begin < end:
+                begin, end = begin - side * half, end - side * half
+                mine, other = pieces[0][:, begin:end], pieces[1][:, begin:end]
+                parts.append(jnp.where(low == (side == 0), mine, other))
+        return jnp.concatenate(parts, 1) if len(parts) > 1 else parts[0]
 
     def gradient_of(index):
         if index in (0, 3):
@@ -815,11 +886,8 @@
         shared = pieces[2:6]
         wide = 2 * FFS // 4
         if index == 4:
-            at = pl.multiple_of((step % 2) * (wide // 2), 128)
             return picked_piece(
-                shared,
-                jnp.bitwise_xor(step // 2, me),
-                lambda ref: ref[:, pl.ds(at, wide // 2)],
+                shared, jnp.bitwise_xor(step, me), lambda ref: ref[:, :wide]
             )
         if index == 5:
             return jnp.concatenate(
@@ -832,7 +900,7 @@
         if index == 7:
             mine, other = pieces[6][...], pieces[7][...]
             return jnp.stack([jnp.where(low, mine, other), jnp.where(low, other, mine)])
-        return jnp.where(step // 4 == sides[0], pieces[8][...], pieces[9][...])
+        return jnp.where(step // 2 == sides[0], pieces[8][...], pieces[9][...])
 
     def update(index):
         gradient = gradient_of(index)
@@ -851,7 +919,7 @@
         update(index)
     for index in range(count):
         if index not in TILED:
-            pl.when(step == min(index, 7))(functools.partial(update, index))
+            pl.when(step == min(index, 3))(functools.partial(update, index))
 
 
 def step_kernel(count, totals, master_totals, *refs):
@@ -872,7 +940,7 @@
         update(index)
     for index in range(count):
         if index not in TILED:
-            pl.when(step == min(index, 7))(functools.partial(update, index))
+            pl.when(step == min(index, 3))(functools.partial(update, index))
 
 
 def shards(
@@ -918,7 +986,9 @@
     head_columns = horizon.shape[1]
     hidden_local = expert_output.shape[0]
     small_end = HORIZON_AT + head_columns
-    fast = group_size == 1 and dp_count == 4 and local_rows % 16 == 0
+    fast = (
+        group_size == 1 and dp_count == 4 and local_rows % 16 == 0 and hidden_local == 2 * D
+    )
     core = lax.axis_index("dp") & 1
     sides = jnp.stack([core, lax.axis_index("dp") >> 1]).astype(jnp.int32)
     in_smem = pl.BlockSpec(memory_space=pltpu.SMEM)
@@ -959,7 +1029,7 @@
         )
     )
     count = len(masters)
-    steps = 8
+    steps = 4
     gate_up_low, down_low, master_squares = pl.pallas_call(
         functools.partial(prepare_kernel, count),
         out_shape=[
@@ -1164,7 +1234,26 @@
             compiler_params=params(),
             cost_estimate=back_cost,
         )(*back_args)
-    received = ready(received, shared_second_slope)
+    if fast:
+        in_other, out_other = flip(in_give, "dp", 1), flip(out_give, "dp", 1)
+        fold_in = pl.BlockSpec((2, D // 4, FFS // 2), lambda i: (0, i, 0))
+        fold_out = pl.BlockSpec((2, D // 4, D), lambda i: (0, i, 0))
+        wide = FFS // 2 + D
+        fold_to = pl.BlockSpec((D // 4, wide), lambda i: (i, 0))
+        code_to = pl.BlockSpec((D // 4, wide + 128), lambda i: (i, 0))
+        shared_keep, shared_give = pl.pallas_call(
+            fold_kernel,
+            out_shape=[out((D, wide)), out((D, wide + 128), jnp.int16)],
+            grid=(4,),
+            in_specs=[fold_in, fold_in, fold_out, fold_out],
+            out_specs=[fold_to, code_to],
+            compiler_params=params(),
+            cost_estimate=cost(2e6, 10e6),
+        )(in_keep, in_other, out_keep, out_other)
+        shared_other = flip(shared_give, "dp", 2)
+        received = ready(received, shared_second_slope, shared_give)
+    else:
+        received = ready(received, shared_second_slope)
     row_spec = pl.BlockSpec((block, D), lambda i: (i, 0))
     expert_cost = cost(total_rows * D * 8 * hidden_local * 2, 10e6)
     weight_specs = [whole(gate_up_low), whole(down_low)]
@@ -1197,25 +1286,31 @@
         )(arrived, received, gate_up_low, down_low)
     routed_back = to_points(grad_rows)
     if fast:
-        in_other, out_other = flip(in_give, "dp", 1), flip(out_give, "dp", 1)
-        fold_in = pl.BlockSpec((2, D // 4, FFS // 2), lambda i: (0, i, 0))
-        fold_out = pl.BlockSpec((2, D // 4, D), lambda i: (0, i, 0))
-        wide = FFS // 2 + D
-        fold_to = pl.BlockSpec((D // 4, wide), lambda i: (i, 0))
-        shared_keep, shared_give = pl.pallas_call(
-            fold_kernel,
-            out_shape=[out((D, wide)), out((D, wide))],
+        shared_code = pl.pallas_call(
+            add_code_kernel,
+            out_shape=out((D, wide + 128), jnp.int16),
             grid=(4,),
-            in_specs=[fold_in, fold_in, fold_out, fold_out],
-            out_specs=[fold_to, fold_to],
+            in_specs=[fold_to, code_to],
+            out_specs=code_to,
             compiler_params=params(),
-            cost_estimate=cost(2e6, 10e6),
-        )(in_keep, in_other, out_keep, out_other)
-        shared_other = flip(shared_give, "dp", 2)
-        expert_in = expert_in + flip(expert_in_give, "dp", 1)
-        expert_out = expert_out + flip(expert_out_give, "dp", 1)
+            cost_estimate=cost(2e6, 4e6),
+        )(shared_keep, shared_other)
+        expert_in_other = flip(expert_in_give, "dp", 1)
+        expert_out_other = flip(expert_out_give, "dp", 1)
+        sum_in = pl.BlockSpec((D // 4, hidden_local), lambda i: (i, 0))
+        sum_out = pl.BlockSpec((D // 4, D), lambda i: (i, 0))
+        expert_code = pl.pallas_call(
+            expert_code_kernel,
+            out_shape=out((D, wide + 128), jnp.int16),
+            grid=(4,),
+            in_specs=[sum_in, sum_in, sum_out, sum_out],
+            out_specs=code_to,
+            compiler_params=params(),
+            cost_estimate=cost(2e6, 8e6),
+        )(expert_in, expert_in_other, expert_out, expert_out_other)
         sums = local_sums + flip(local_sums, "dp", 2)
-        routed_back = ready(routed_back, shared_other, expert_in, expert_out, sums)
+        routed_plain = routed_back
+        routed_back = ready(routed_back, shared_code, expert_code, sums)
     attend_slope, mixed_slope, grad_output, gain_two, small_routed = simple_call(
         attend_back_kernel,
         [
@@ -1227,11 +1322,14 @@
         ],
         2e9,
     )
-    shard_rows = D // 2 if fast else D
     pack_columns = SMALL_AT + SMALL
+    half_columns = SMALL_AT // 2 + SMALL
     last_keep, last_give = simple_call(
         functools.partial(front_back_kernel, fast),
-        [out((shard_rows, pack_columns)), out((shard_rows if fast else 8, pack_columns))],
+        [
+            out((D, half_columns if fast else pack_columns)),
+            out((D, half_columns) if fast else (8, 128)),
+        ],
         [
             (sides, in_smem), mixed_slope, qkv, log_total, known, rows_table, cosine, sine, first,
             embedded, gains, columns(pack, 3 * D, 0), attend_slope, small_routed, gain_two,
@@ -1239,7 +1337,7 @@
         ],
         16e9,
         [
-            pltpu.VMEM((D, pack_columns), F32),
+            pltpu.VMEM((D, 2 * half_columns), F32),
             pltpu.VMEM((amount, D), F32),
             pltpu.VMEM((amount, D), F32),
             pltpu.VMEM((amount, D), F32),
@@ -1248,18 +1346,35 @@
     )
 
     if fast:
-        shared_sum = (shared_keep + shared_other).reshape(expert_count, local_rows, wide)
-        shared_sum = expert_scatter(ready(shared_sum, mixed_slope))
-        expert_in = ready(expert_in, mixed_slope)
-        expert_out = ready(expert_out, mixed_slope)
-        expert_in_other = flip(expert_in, "dp", 2)
-        expert_out_other = flip(expert_out, "dp", 2)
-        last_part = last_keep + flip(last_give, "dp", 1)
-        last_part = ready(last_part, shared_sum, expert_in_other, expert_out_other)
-        last_part = expert_scatter(last_part.reshape(expert_count, local_rows // 2, -1))
+        shared_code = ready(shared_code, routed_plain).reshape(expert_count, local_rows, -1)
+        (shared_sum,) = simple_call(
+            shard_sum_kernel, [out((local_rows, wide))], [exchange(shared_code)], 4e6
+        )
+        expert_code_other = flip(ready(expert_code, mixed_slope), "dp", 2)
+        last_give = ready(last_give, expert_code_other)
+        (last_code,) = simple_call(
+            last_code_kernel,
+            [out((D, half_columns + 128), jnp.int16)],
+            [(sides, in_smem), last_keep, flip(last_give, "dp", 1)],
+            4e6,
+        )
+        last_code = ready(last_code, shared_sum).reshape(expert_count, local_rows, -1)
+        (last_part,) = simple_call(
+            last_sum_kernel,
+            [out((local_rows, half_columns))],
+            [(sides, in_smem), exchange(last_code)],
+            4e6,
+        )
         last_part = last_part + flip(last_part, "dp", 2)
-        expert_in = expert_in + expert_in_other
-        expert_out = expert_out + expert_out_other
+        expert_in, expert_out = pl.pallas_call(
+            expert_sum_kernel,
+            out_shape=[out((D, hidden_local)), out((D, D))],
+            grid=(4,),
+            in_specs=[code_to, code_to],
+            out_specs=[sum_in, sum_out],
+            compiler_params=params(),
+            cost_estimate=cost(2e6, 8e6),
+        )(ready(expert_code, mixed_slope), expert_code_other)
         shared_cross = flip(shared_sum, "dp", 2)
         square_pieces = [expert_in, expert_out, shared_sum, shared_cross, last_part]
         weights = (1.0,) * 5

time: 460 us -> 408 us (0.89)
  waiting for transfers between devices: 214 us -> 155 us
  Pallas kernels: 143 us -> 159 us
  other arithmetic: 22.8 us -> 13.8 us
  starting transfers between devices: 55.3 us -> 49.8 us
  local copies, waits for them, and re-layouts: 17.8 us -> 22.7 us
    all_to_all x8, waiting for transfers between devices: 111 us -> 80.5 us  [exchange(): lax.all_to_all(value, 'expert', split_axis=0, concat_axis=0, tiled=True)]
    ppermute x27 -> x26, waiting for transfers between devices: 103 us -> 74.3 us  [flip(): return lax.ppermute(value, axis_name, [(i, i ^ bit) for i in range(count)])]
    pallas_call x1 -> x4, Pallas kernels: 5.37 us -> 18.2 us  [the longest x1 5.33 us: shards(): pl.pallas_call(fold_kernel, out_shape=[out((D, wide)), out((D, wide + 128...]
    pallas_call x5 -> x8, Pallas kernels: 52.8 us -> 60.9 us  [simple_call(): pl.pallas_call(kernel, out_shape=outs, in_specs=[spec for a, spec in pair...]
    add x6 -> x0, other arithmetic: 7.48 us -> none  [the longest x1 2.48 us: shards(): last_part = last_keep + flip(last_give, 'dp', 1)]
    unnamed x62 -> x70, local copies, waits for them, and re-layouts: 7.71 us -> 12.6 us
    ppermute x27 -> x26, starting transfers between devices: 16.1 us -> 14 us  [flip(): return lax.ppermute(value, axis_name, [(i, i ^ bit) for i in range(count)])]
  transfers between devices with their start and end apart: 35 -> 34, of which waited for: 21 -> 21; matrix products, arithmetic and copies ran while one was open for 6% -> 4% of each run, Pallas kernels for 20% -> 21%
where the time goes in v3:
time: 408 us; the launch traced here: 404 us
  Pallas kernels  159 us (39%)
  waiting for transfers between devices  155 us (38%)
  starting transfers between devices  49.8 us (12%)
  local copies, waits for them, and re-layouts  22.7 us (6%)
  other arithmetic  13.8 us (3%)
    all_to_all x8, waiting for transfers between devices, exchange(): lax.all_to_all(value, 'expert', split_axis=0, concat_axis=0, tiled=True)  80.5 us
    ppermute x26, waiting for transfers between devices, flip(): return lax.ppermute(value, axis_name, [(i, i ^ bit) for i in range(count)])  74.3 us
    pallas_call x8, Pallas kernels, simple_call(): pl.pallas_call(kernel, out_shape=outs, in_specs=[spec for a, spec in pair...  60.9 us
    all_to_all x8, starting transfers between devices, exchange(): lax.all_to_all(value, 'expert', split_axis=0, concat_axis=0, tiled=True)  35.9 us
    pallas_call x1, Pallas kernels, shards(): pl.pallas_call(expert_back_split_kernel, out_shape=[out((total_rows, D),...  19.2 us
    pallas_call x1, Pallas kernels, shards(): pl.pallas_call(functools.partial(moments_kernel, fast, count, small_end),...  16.9 us
    ppermute x26, starting transfers between devices, flip(): return lax.ppermute(value, axis_name, [(i, i ^ bit) for i in range(count)])  14 us
    pallas_call x1, Pallas kernels, shards(): pl.pallas_call(shared_back_split_kernel, out_shape=[out((amount, D)), out...  13.3 us
  transfers between devices with their start and end apart: 34, of which 21 were waited for; matrix products, arithmetic and copies ran while one was open for 4% of the time, Pallas kernels for 21%

profile of v3, /device:TPU:0, one launch (start us, length us, event | category | flops | bytes accessed | tf_op | source)
XLA Modules:
  0.0 403.8 jit_solution(7684753705690755319)
XLA Ops:
  3.4 7.3 %all-to-all-start = ((bf16[8,48,896]{2,1,0:T(8,128)(2,1)}), bf16[8,48,896]{2,1,0:T(8,128)(2,1)S(1)}, u32[]{:S(2)}, u32[]{:S(2)}) async-start(bf16[8,48,896]{2,1,0:T(8,128)(2,1)} %shard_map.571), calls=%async_computation | async-start | bytes 1376256 | tf_op jit(solution)/shard_map/all_to_all | solution.py:766
  11.2 3.0 shard_map.572
  14.2 4.9 %shard_map.573 = (bf16[2,384,768]{2,1,0:T(8,128)(2,1)}, bf16[768,384]{1,0:T(8,128)(2,1)}, f32[16,128]{1,0:T(8,128)}) custom-call(f32[5,48]{1,0:T(8,128)} %refs_0_.5, f32[48,1152]{1,0:T(8,128)} %refs_1_.5, f32[48,384]{1,0:T(8,128)} %refs_2_.5, f32[9,48]{1,0:T(8,128)} %bitcast.119, f32[48,3072]{1,0:T(8,128)} %refs_4_.5, f32[192,384]{1,0:T(8,128)} %refs_5_.5, ...), custom_call_target="tpu_custom_call" | custom-call | flops 3000 | bytes 7000 | tf_op jit(solution)/shard_map/pallas_call | solution.py:1033
  19.5 9.2 %all-to-all-done = bf16[8,48,896]{2,1,0:T(8,128)(2,1)S(1)} async-done(((bf16[8,48,896]{2,1,0:T(8,128)(2,1)}), bf16[8,48,896]{2,1,0:T(8,128)(2,1)S(1)}, u32[]{:S(2)}, u32[]{:S(2)}) %all-to-all-start) | async-done | bytes 688160 | tf_op jit(solution)/shard_map/all_to_all | solution.py:766
  29.7 4.0 all-to-all-start.1
  33.7 2.1 collective-permute-done.other
  36.7 14.7 %shard_map.574 = (f32[512,384]{1,0:T(8,128)}, bf16[512,384]{1,0:T(8,128)(2,1)}, bf16[512,1152]{1,0:T(8,128)(2,1)}, f32[512,128]{1,0:T(8,128)}, bf16[512,384]{1,0...) custom-call(s32[2]{0:T(128)} %pad_add_fusion.core.sides, ...), custom_call_target="tpu_custom_call" | custom-call | flops 8000000 | bytes 9499 | tf_op jit(solution)/shard_map/pallas_call | solution.py:701
  51.4 4.6 %all-to-all-done.1 = bf16[8,48,1152]{2,1,0:T(8,128)(2,1)S(1)} async-done(((bf16[8,48,1152]{2,1,0:T(8,128)(2,1)}), bf16[8,48,1152]{2,1,0:T(8,128)(2,1)S(1)}, u32[]{:S(2)}, u32[]{:S(2)}) %all-to-all-start.1) | async-done | bytes 884768 | tf_op jit(solution)/shard_map/all_to_all | solution.py:766
  56.0 3.6 all-to-all-start.2
  61.2 19.7 %collective-permute-done.1 = bf16[8,48,1152]{2,1,0:T(8,128)(2,1)S(1)} collective-permute-done((bf16[8,48,1152]{2,1,0:T(8,128)(2,1)S(1)}, bf16[8,48,1152]{2,1,0:T(8,128)(2,1)S(1)}, u32[]{:S(2)}, u32[]{:S(2)}) %collective-permute-start.1) | collective-permute-done | bytes 884768 | tf_op jit(solution)/shard_map/ppermute | solution.py:719
  80.9 15.9 %all-to-all-done.2 = bf16[8,256,384]{2,1,0:T(8,128)(2,1)S(1)} async-done(((bf16[8,256,384]{2,1,0:T(8,128)(2,1)}), bf16[8,256,384]{2,1,0:T(8,128)(2,1)S(1)}, u32[]{:S(2)}, u32[]{:S(2)}) %all-to-all-start.2) | async-done | bytes 1572896 | tf_op jit(solution)/shard_map/all_to_all | solution.py:766
  98.0 8.5 %shard_map.575 = s16[8,272,384]{2,1,0:T(8,128)(2,1)} custom-call(bf16[2048,384]{1,0:T(8,128)(2,1)} %bitcast.102, bf16[2,384,768]{2,1,0:T(8,128)(2,1)} %get-tuple-element.128.gate_up, bf16[768,384]{1,0:T(8,128)(2,1)} %get-tuple-element.129.down), custom_call_target="tpu_custom_call" | custom-call | flops 3623878 | bytes 7000 | tf_op jit(solution)/shard_map/pallas_call | solution.py:1114
  108.1 5.0 %all-to-all-start.3 = ((s16[8,272,384]{2,1,0:T(8,128)(2,1)}), s16[8,272,384]{2,1,0:T(8,128)(2,1)}, u32[]{:S(2)}, u32[]{:S(2)}) async-start(s16[8,272,384]{2,1,0:T(8,128)(2,1)} %shard_map.575), calls=%async_computation.3 | async-start | bytes 3342336 | tf_op jit(solution)/shard_map/all_to_all | solution.py:766
  117.6 3.3 broadcast_select_fusion.1
  122.0 2.5 reshape.119
  128.1 5.7 %shard_map.576.shared = f32[512,384]{1,0:T(8,128)} custom-call(bf16[512,384]{1,0:T(8,128)(2,1)} %get-tuple-element.141.second, bf16[384,3072]{1,0:T(8,128)(2,1)} %bitcast.98, bf16[384,3072]{1,0:T(8,128)(2,1)} %bitcast.99, bf16[1536,384]{1,0:T(8,128)(2,1)} %bitcast.104), custom_call_target="tpu_custom_call" | custom-call | flops 1811939 | bytes 5000 | tf_op jit(solution)/shard_map/pallas_call | solution.py:1151
  133.8 19.1 %all-to-all-done.3.returned = s16[8,272,384]{2,1,0:T(8,128)(2,1)} async-done(((s16[8,272,384]{2,1,0:T(8,128)(2,1)}), s16[8,272,384]{2,1,0:T(8,128)(2,1)}, u32[]{:S(2)}, u32[]{:S(2)}) %all-to-all-start.3) | async-done | bytes 1671200 | tf_op jit(solution)/shard_map/all_to_all | solution.py:766
  152.9 11.3 %shard_map.577 = (f32[512,384]{1,0:T(8,128)}, bf16[512,384]{1,0:T(8,128)(2,1)}, bf16[2048,384]{1,0:T(8,128)(2,1)}, bf16[512,128]{1,0:T(8,128)(2,1)}, f32[384,128...) custom-call(s16[8,272,384]{2,1,0:T(8,128)(2,1)} %all-to-all-done.3.returned, f32[512,128]{1,0:T(8,128)} %get-tuple-element.127.known, ...), custom_call_target="tpu_custom_call" | custom-call | flops 7000000 | bytes 8420 | tf_op jit(solution)/shard_map/pallas_call | solution.py:701
  164.3 3.8 all-to-all-start.4
  168.1 13.3 %shard_map.578 = (f32[512,384]{1,0:T(8,128)}, f32[2,384,768]{2,1,0:T(8,128)}, f32[2,384,768]{2,1,0:T(8,128)}, f32[2,384,384]{2,1,0:T(8,128)}, f32[2,384,384]{2,1,0:T(8,128)}) custom-call(s32[2]{0:T(128)} %pad_add_fusion.core.sides, bf16[512,384]{1,0:T(8,128)(2,1)} %get-tuple-element.141.second, bf16[512,384]{1,0:T(8,128)(2,1)} %get-tuple-element.150.slope, ...), custom_call_target="tpu_custom_call" | custom-call | flops 4831838 | bytes 14000 | tf_op jit(solution)/shard_map/pallas_call | solution.py:1207
  182.0 5.9 %collective-permute-done.6.out_other = f32[2,384,384]{2,1,0:T(8,128)S(1)} collective-permute-done((f32[2,384,384]{2,1,0:T(8,128)}, f32[2,384,384]{2,1,0:T(8,128)S(1)}, u32[]{:S(2)}, u32[]{:S(2)}) %collective-permute-start.6) | collective-permute-done | bytes 1179680 | tf_op jit(solution)/shard_map/ppermute | solution.py:719
  189.7 5.3 %shard_map.579 = (f32[384,1152]{1,0:T(8,128)}, s16[384,1280]{1,0:T(8,128)(2,1)}) custom-call(f32[2,384,768]{2,1,0:T(8,128)} %get-tuple-element.152.in_keep, f32[2,384,768]{2,1,0:T(8,128)} %copy-done.10, f32[2,384,384]{2,1,0:T(8,128)} %get-tuple-element.154.out_keep, f32[2,384,384]{2,1,0:T(8,128)} %copy-done.15), custom_call_target="tpu_custom_call" | custom-call | flops 2000 | bytes 10000 | tf_op jit(solution)/shard_map/pallas_call | solution.py:1244
  195.0 10.3 %all-to-all-done.4 = bf16[8,256,384]{2,1,0:T(8,128)(2,1)S(1)} async-done(((bf16[8,256,384]{2,1,0:T(8,128)(2,1)}), bf16[8,256,384]{2,1,0:T(8,128)(2,1)S(1)}, u32[]{:S(2)}, u32[]{:S(2)}) %all-to-all-start.4) | async-done | bytes 1572896 | tf_op jit(solution)/shard_map/all_to_all | solution.py:766
  206.4 19.2 %shard_map.580 = (bf16[2048,384]{1,0:T(8,128)(2,1)}, f32[384,768]{1,0:T(8,128)}, f32[384,768]{1,0:T(8,128)}, f32[384,384]{1,0:T(8,128)}, f32[384,384]{1,0:T(8,128)}) custom-call(s32[2]{0:T(128)} %pad_add_fusion.core.sides, bf16[2048,384]{1,0:T(8,128)(2,1)} %bitcast.103, bf16[2048,384]{1,0:T(8,128)(2,1)} %bitcast.106, ...), custom_call_target="tpu_custom_call" | custom-call | flops 9663676 | bytes 10000 | tf_op jit(solution)/shard_map/pallas_call | solution.py:1262
  225.6 3.8 all-to-all-start.5
  231.8 22.2 %collective-permute-done.4 = f32[1,128]{1,0:T(1,128)S(1)} collective-permute-done((f32[1,128]{1,0:T(1,128)S(1)}, f32[1,128]{1,0:T(1,128)S(1)}, u32[]{:S(2)}, u32[]{:S(2)}) %collective-permute-start.4) | collective-permute-done | bytes 544 | tf_op jit(solution)/shard_map/ppermute | solution.py:719
  255.4 4.4 %shard_map.582 = s16[384,1280]{1,0:T(8,128)(2,1)} custom-call(f32[384,1152]{1,0:T(8,128)} %get-tuple-element.163.keep, s16[384,1280]{1,0:T(8,128)(2,1)} %copy-done.17), custom_call_target="tpu_custom_call" | custom-call | flops 2000 | bytes 4000 | tf_op jit(solution)/shard_map/pallas_call | solution.py:1289
  261.0 4.2 %shard_map.581.mine = s16[384,1280]{1,0:T(8,128)(2,1)} custom-call(f32[384,768]{1,0:T(8,128)} %get-tuple-element.158.in_keep, f32[384,768]{1,0:T(8,128)} %copy-done.16, f32[384,384]{1,0:T(8,128)} %get-tuple-element.160.out_keep, f32[384,384]{1,0:T(8,128)} %copy-done.22), custom_call_target="tpu_custom_call" | custom-call | flops 2000 | bytes 8000 | tf_op jit(solution)/shard_map/pallas_call | solution.py:1302
  267.7 5.9 %shard_map.583 = (f32[512,384]{1,0:T(8,128)}, bf16[512,384]{1,0:T(8,128)(2,1)}, f32[384,384]{1,0:T(8,128)}, f32[1,384]{1,0:T(1,128)}, f32[384,128]{1,0:T(8,128)}) custom-call(bf16[2048,384]{1,0:T(8,128)(2,1)} %bitcast.107, f32[512,128]{1,0:T(8,128)} %get-tuple-element.127.known, f32[512,384]{1,0:T(8,128)} %get-tuple-element.151.second_slope, ...), custom_call_target="tpu_custom_call" | custom-call | flops 2000000 | bytes 9844 | tf_op jit(solution)/shard_map/pallas_call | solution.py:701
  275.2 4.7 %all-to-all-start.6 = ((s16[8,48,1280]{2,1,0:T(8,128)(2,1)}), s16[8,48,1280]{2,1,0:T(8,128)(2,1)S(1)}, u32[]{:S(2)}, u32[]{:S(2)}) async-start(s16[8,48,1280]{2,1,0:T(8,128)(2,1)} %bitcast.83), calls=%async_computation.6 | async-start | bytes 1966080 | tf_op jit(solution)/shard_map/all_to_all | solution.py:766
  280.0 18.4 %shard_map.586 = (f32[384,896]{1,0:T(8,128)}, f32[384,896]{1,0:T(8,128)}) custom-call(s32[2]{0:T(128)} %pad_add_fusion.core.sides, bf16[512,384]{1,0:T(8,128)(2,1)} %get-tuple-element.169.mixed_slope, bf16[512,1152]{1,0:T(8,128)(2,1)} %get-tuple-element.174.qkv, f32[512,128]{1,0:T(8,128)} %get-tuple-element.175.log_total, ...), custom_call_target="tpu_custom_call" | custom-call | flops 16000000 | bytes 9436 | tf_op jit(solution)/shard_map/pallas_call | solution.py:701
  298.5 5.3 %all-to-all-done.6.codes = s16[8,48,1280]{2,1,0:T(8,128)(2,1)S(1)} async-done(((s16[8,48,1280]{2,1,0:T(8,128)(2,1)}), s16[8,48,1280]{2,1,0:T(8,128)(2,1)S(1)}, u32[]{:S(2)}, u32[]{:S(2)}) %all-to-all-start.6) | async-done | bytes 983072 | tf_op jit(solution)/shard_map/all_to_all | solution.py:766
  304.8 2.4 shard_map.585.refs_2_.refs_29_
  308.3 3.3 shard_map.587
  311.6 3.7 all-to-all-start.7
  315.3 4.3 %shard_map.584 = (f32[384,768]{1,0:T(8,128)}, f32[384,384]{1,0:T(8,128)}) custom-call(s16[384,1280]{1,0:T(8,128)(2,1)} %shard_map.581.mine, s16[384,1280]{1,0:T(8,128)(2,1)} %copy-done.18), custom_call_target="tpu_custom_call" | custom-call | flops 2000 | bytes 8000 | tf_op jit(solution)/shard_map/pallas_call | solution.py:1369
  320.7 14.8 %all-to-all-done.7.codes = s16[8,48,1024]{2,1,0:T(8,128)(2,1)S(1)} async-done(((s16[8,48,1024]{2,1,0:T(8,128)(2,1)}), s16[8,48,1024]{2,1,0:T(8,128)(2,1)S(1)}, u32[]{:S(2)}, u32[]{:S(2)}) %all-to-all-start.7) | async-done | bytes 786464 | tf_op jit(solution)/shard_map/all_to_all | solution.py:766
  336.3 2.3 shard_map.588
  339.6 4.6 %collective-permute-done.13 = f32[48,896]{1,0:T(8,128)S(1)} collective-permute-done((f32[48,896]{1,0:T(8,128)}, f32[48,896]{1,0:T(8,128)S(1)}, u32[]{:S(2)}, u32[]{:S(2)}) %collective-permute-start.13) | collective-permute-done | bytes 172064 | tf_op jit(solution)/shard_map/ppermute | solution.py:719
  345.8 2.4 shard_map.589
  351.7 2.2 collective-permute-done.15
  354.2 3.2 collective-permute-done.16
  357.8 4.1 %collective-permute-done.17 = f32[2,128]{1,0:T(2,128)S(1)} collective-permute-done((f32[2,128]{1,0:T(2,128)S(1)}, f32[2,128]{1,0:T(2,128)S(1)}, u32[]{:S(2)}, u32[]{:S(2)}) %collective-permute-start.17) | collective-permute-done | bytes 1056 | tf_op jit(solution)/shard_map/ppermute | solution.py:719
  364.0 16.9 %shard_map.590 = (f32[5,48]{1,0:T(8,128)}, f32[48,1152]{1,0:T(8,128)}, f32[48,384]{1,0:T(8,128)}, f32[9,48]{1,0:T(8,128)}, f32[48,3072]{1,0:T(8,128)}, /*index=5...) custom-call(s32[2]{0:T(128)} %pad_add_fusion.core.sides, ...), custom_call_target="tpu_custom_call" | custom-call | flops 30000 | bytes 34000 | tf_op jit(solution)/shard_map/pallas_call | solution.py:1426
  383.0 2.3 collective-permute-done.23
  386.4 3.3 collective-permute-done.24
  391.9 2.5 collective-permute-done.25
  395.7 6.7 %shard_map.591 = (f32[5,48]{1,0:T(8,128)}, f32[48,1152]{1,0:T(8,128)}, f32[48,384]{1,0:T(8,128)}, f32[9,48]{1,0:T(8,128)}, f32[48,3072]{1,0:T(8,128)}, /*index=5...) custom-call(f32[9,128]{1,0:T(8,128)} %get-tuple-element.293.totals, ...), custom_call_target="tpu_custom_call" | custom-call | flops 3000 | bytes 15000 | tf_op jit(solution)/shard_map/pallas_call | solution.py:1442
  (156 shorter events, 50.3 us)
Async XLA Ops:
  3.4 25.3 %all-to-all-start = ((bf16[8,48,896]{2,1,0:T(8,128)(2,1)}), bf16[8,48,896]{2,1,0:T(8,128)(2,1)S(1)}, u32[]{:S(2)}, u32[]{:S(2)}) async-start(bf16[8,48,896]{2,1,0:T(8,128)(2,1)} %shard_map.571), calls=%async_computation | async-start | bytes 1376256 | tf_op jit(solution)/shard_map/all_to_all | solution.py:766
  14.2 5.0 %copy-start.1 = (f32[48,3072]{1,0:T(8,128)S(1)}, f32[48,3072]{1,0:T(8,128)}, u32[]{:S(2)}) copy-start(f32[48,3072]{1,0:T(8,128)} %refs_4_.5) | copy-start | bytes 1769476
  28.6 7.2 %copy-start.9 = (bf16[8,48,896]{2,1,0:T(8,128)(2,1)}, bf16[8,48,896]{2,1,0:T(8,128)(2,1)S(1)}, u32[]{:S(2)}) copy-start(bf16[8,48,896]{2,1,0:T(8,128)(2,1)S(1)} %all-to-all-done) | copy-start | bytes 2064388
  29.7 26.3 %all-to-all-start.1 = ((bf16[8,48,1152]{2,1,0:T(8,128)(2,1)}), bf16[8,48,1152]{2,1,0:T(8,128)(2,1)S(1)}, u32[]{:S(2)}, u32[]{:S(2)}) async-start(bf16[8,48,1152]{2,1,0:T(8,128)(2,1)} %broadcast_in_dim.20), calls=%async_computation.1 | async-start | bytes 1769472 | tf_op jit(solution)/shard_map/all_to_all | solution.py:766
  33.6 2.2 collective-permute-start
  56.0 40.8 %all-to-all-start.2 = ((bf16[8,256,384]{2,1,0:T(8,128)(2,1)}), bf16[8,256,384]{2,1,0:T(8,128)(2,1)S(1)}, u32[]{:S(2)}, u32[]{:S(2)}) async-start(bf16[8,256,384]{2,1,0:T(8,128)(2,1)} %bitcast.114), calls=%async_computation.2 | async-start | bytes 3145728 | tf_op jit(solution)/shard_map/all_to_all | solution.py:766
  59.6 21.3 %collective-permute-start.1 = (bf16[8,48,1152]{2,1,0:T(8,128)(2,1)S(1)}, bf16[8,48,1152]{2,1,0:T(8,128)(2,1)S(1)}, u32[]{:S(2)}, u32[]{:S(2)}) collective-permute-start(bf16[8,48,1152]{2,1,0:T(8,128)(2,1)S(1)} %all-to-all-done.1), channel_id=1, source_target_pairs={{0,16},{8,24},{16,0},{24,8},{1,17},{9,25},{17,1},{25,9},{2,18},{10... | collective-permute-start | bytes 2654216 | tf_op jit(solution)/shard_map/ppermute | solution.py:719
  108.0 5.0 %copy-start.31 = (s32[105]{0:T(128)S(1)}, s32[105]{0:T(128)}, u32[]{:S(2)}) copy-start(s32[105]{0:T(128)} %constant.65) | copy-start | bytes 1264
  108.0 5.0 %copy-start.26 = (f32[512]{0:T(512)S(1)}, f32[512]{0:T(512)}, u32[]{:S(2)}) copy-start(f32[512]{0:T(512)} %param.36) | copy-start | bytes 6148
  108.0 5.4 %copy-start.30 = (f32[1,128]{1,0:T(1,128)S(1)}, f32[1,128]{1,0:T(1,128)}, u32[]{:S(2)}) copy-start(f32[1,128]{1,0:T(1,128)} %get-tuple-element.147) | copy-start | bytes 1540
  108.0 9.5 %collective-permute-start.2 = (bf16[8,48,2304]{2,1,0:T(8,128)(2,1)}, bf16[8,48,2304]{2,1,0:T(8,128)(2,1)}, u32[]{:S(2)}, u32[]{:S(2)}) collective-permute-start(bf16[8,48,2304]{2,1,0:T(8,128)(2,1)} %pad_maximum_fusion.1), channel_id=1, source_target_pairs={{0,8},{8,0},{16,24},{24,16},{1,9},{9,1},{17,25},{25,17},{2,10},{10... | collective-permute-start | bytes 5308424 | tf_op jit(solution)/shard_map/ppermute | solution.py:719
  108.1 44.9 %all-to-all-start.3 = ((s16[8,272,384]{2,1,0:T(8,128)(2,1)}), s16[8,272,384]{2,1,0:T(8,128)(2,1)}, u32[]{:S(2)}, u32[]{:S(2)}) async-start(s16[8,272,384]{2,1,0:T(8,128)(2,1)} %shard_map.575), calls=%async_computation.3 | async-start | bytes 3342336 | tf_op jit(solution)/shard_map/all_to_all | solution.py:766
  113.4 3.6 collective-permute-start.3
  164.3 41.0 %all-to-all-start.4 = ((bf16[8,256,384]{2,1,0:T(8,128)(2,1)}), bf16[8,256,384]{2,1,0:T(8,128)(2,1)S(1)}, u32[]{:S(2)}, u32[]{:S(2)}) async-start(bf16[8,256,384]{2,1,0:T(8,128)(2,1)} %bitcast.113), calls=%async_computation.4 | async-start | bytes 3145728 | tf_op jit(solution)/shard_map/all_to_all | solution.py:766
  181.5 6.4 %collective-permute-start.5 = (f32[2,384,768]{2,1,0:T(8,128)}, f32[2,384,768]{2,1,0:T(8,128)S(1)}, u32[]{:S(2)}, u32[]{:S(2)}) collective-permute-start(f32[2,384,768]{2,1,0:T(8,128)} %get-tuple-element.153), channel_id=1, source_target_pairs={{0,8},{8,0},{16,24},{24,16},{1,9},{9,1},{17,25},{25,17},{2,10},{10... | collective-permute-start | bytes 7077896 | tf_op jit(solution)/shard_map/ppermute | solution.py:719
  181.5 6.4 %collective-permute-start.6 = (f32[2,384,384]{2,1,0:T(8,128)}, f32[2,384,384]{2,1,0:T(8,128)S(1)}, u32[]{:S(2)}, u32[]{:S(2)}) collective-permute-start(f32[2,384,384]{2,1,0:T(8,128)} %get-tuple-element.155), channel_id=1, source_target_pairs={{0,8},{8,0},{16,24},{24,16},{1,9},{9,1},{17,25},{25,17},{2,10},{10... | collective-permute-start | bytes 3538952 | tf_op jit(solution)/shard_map/ppermute | solution.py:719
  225.6 5.5 %copy-start.33 = (f32[384,384]{1,0:T(8,128)S(1)}, f32[384,384]{1,0:T(8,128)}, u32[]{:S(2)}) copy-start(f32[384,384]{1,0:T(8,128)} %get-tuple-element.161) | copy-start | bytes 1769476
  225.6 5.6 %copy-start.34 = (f32[1,128]{1,0:T(1,128)S(1)}, f32[1,128]{1,0:T(1,128)}, u32[]{:S(2)}) copy-start(f32[1,128]{1,0:T(1,128)} %get-tuple-element.148) | copy-start | bytes 1540
  225.6 41.0 %all-to-all-start.5 = ((bf16[8,256,384]{2,1,0:T(8,128)(2,1)}), bf16[8,256,384]{2,1,0:T(8,128)(2,1)S(1)}, u32[]{:S(2)}, u32[]{:S(2)}) async-start(bf16[8,256,384]{2,1,0:T(8,128)(2,1)} %bitcast.112), calls=%async_computation.5 | async-start | bytes 3145728 | tf_op jit(solution)/shard_map/all_to_all | solution.py:766
  229.4 30.4 %collective-permute-start.7 = (f32[384,768]{1,0:T(8,128)S(1)}, f32[384,768]{1,0:T(8,128)S(1)}, u32[]{:S(2)}, u32[]{:S(2)}) collective-permute-start(f32[384,768]{1,0:T(8,128)S(1)} %copy-done.32), channel_id=1, source_target_pairs={{0,8},{8,0},{16,24},{24,16},{1,9},{9,1},{17,25},{25,17},{2,10},{10... | collective-permute-start | bytes 3538952 | tf_op jit(solution)/shard_map/ppermute | solution.py:719
  229.5 25.0 %collective-permute-start.9 = (s16[384,1280]{1,0:T(8,128)(2,1)}, s16[384,1280]{1,0:T(8,128)(2,1)S(1)}, u32[]{:S(2)}, u32[]{:S(2)}) collective-permute-start(s16[384,1280]{1,0:T(8,128)(2,1)} %get-tuple-element.156), channel_id=1, source_target_pairs={{0,16},{8,24},{16,0},{24,8},{1,17},{9,25},{17,1},{25,9},{2,18},{10... | collective-permute-start | bytes 2949128 | tf_op jit(solution)/shard_map/ppermute | solution.py:719
  231.1 28.7 %collective-permute-start.8 = (f32[384,384]{1,0:T(8,128)S(1)}, f32[384,384]{1,0:T(8,128)S(1)}, u32[]{:S(2)}, u32[]{:S(2)}) collective-permute-start(f32[384,384]{1,0:T(8,128)S(1)} %copy-done.33), channel_id=1, source_target_pairs={{0,8},{8,0},{16,24},{24,16},{1,9},{9,1},{17,25},{25,17},{2,10},{10... | collective-permute-start | bytes 1769480 | tf_op jit(solution)/shard_map/ppermute | solution.py:719
  231.2 22.7 %collective-permute-start.4 = (f32[1,128]{1,0:T(1,128)S(1)}, f32[1,128]{1,0:T(1,128)S(1)}, u32[]{:S(2)}, u32[]{:S(2)}) collective-permute-start(f32[1,128]{1,0:T(1,128)S(1)} %copy-done.34), channel_id=1, source_target_pairs={{0,16},{8,24},{16,0},{24,8},{1,17},{9,25},{17,1},{25,9},{2,18},{10... | collective-permute-start | bytes 1544 | tf_op jit(solution)/shard_map/ppermute | solution.py:719
  267.7 5.9 %copy-start.6 = (s16[384,1280]{1,0:T(8,128)(2,1)S(1)}, s16[384,1280]{1,0:T(8,128)(2,1)}, u32[]{:S(2)}) copy-start(s16[384,1280]{1,0:T(8,128)(2,1)} %shard_map.581.mine) | copy-start | bytes 2949124
  273.7 24.7 %collective-permute-start.10 = (s16[384,1280]{1,0:T(8,128)(2,1)S(1)}, s16[384,1280]{1,0:T(8,128)(2,1)S(1)}, u32[]{:S(2)}, u32[]{:S(2)}) collective-permute-start(s16[384,1280]{1,0:T(8,128)(2,1)S(1)} %copy-done.6), channel_id=1, source_target_pairs={{0,16},{8,24},{16,0},{24,8},{1,17},{9,25},{17,1},{25,9},{2,18},{10... | collective-permute-start | bytes 2949128 | tf_op jit(solution)/shard_map/ppermute | solution.py:719
  275.2 28.6 %all-to-all-start.6 = ((s16[8,48,1280]{2,1,0:T(8,128)(2,1)}), s16[8,48,1280]{2,1,0:T(8,128)(2,1)S(1)}, u32[]{:S(2)}, u32[]{:S(2)}) async-start(s16[8,48,1280]{2,1,0:T(8,128)(2,1)} %bitcast.83), calls=%async_computation.6 | async-start | bytes 1966080 | tf_op jit(solution)/shard_map/all_to_all | solution.py:766
  298.4 16.9 %copy-start.18 = (s16[384,1280]{1,0:T(8,128)(2,1)}, s16[384,1280]{1,0:T(8,128)(2,1)S(1)}, u32[]{:S(2)}) copy-start(s16[384,1280]{1,0:T(8,128)(2,1)S(1)} %collective-permute-done.10.other) | copy-start | bytes 2949124
  298.4 8.8 %collective-permute-start.12 = (f32[384,896]{1,0:T(8,128)}, f32[384,896]{1,0:T(8,128)S(1)}, u32[]{:S(2)}, u32[]{:S(2)}) collective-permute-start(f32[384,896]{1,0:T(8,128)} %get-tuple-element.185), channel_id=1, source_target_pairs={{0,8},{8,0},{16,24},{24,16},{1,9},{9,1},{17,25},{25,17},{2,10},{10... | collective-permute-start | bytes 4128776 | tf_op jit(solution)/shard_map/ppermute | solution.py:719
  311.6 8.5 %copy-start.11 = (f32[48,1152]{1,0:T(8,128)S(1)}, f32[48,1152]{1,0:T(8,128)}, u32[]{:S(2)}) copy-start(f32[48,1152]{1,0:T(8,128)} %shard_map.585.refs_2_.refs_29_) | copy-start | bytes 663556
  311.6 23.8 %all-to-all-start.7 = ((s16[8,48,1024]{2,1,0:T(8,128)(2,1)}), s16[8,48,1024]{2,1,0:T(8,128)(2,1)S(1)}, u32[]{:S(2)}, u32[]{:S(2)}) async-start(s16[8,48,1024]{2,1,0:T(8,128)(2,1)} %bitcast.109), calls=%async_computation.7 | async-start | bytes 1572864 | tf_op jit(solution)/shard_map/all_to_all | solution.py:766
  319.6 42.9 %collective-permute-start.21 = (f32[384,768]{1,0:T(8,128)}, f32[384,768]{1,0:T(8,128)S(1)}, u32[]{:S(2)}, u32[]{:S(2)}) collective-permute-start(f32[384,768]{1,0:T(8,128)} %get-tuple-element.171.refs_0_.refs_33_), channel_id=1, source_target_pairs={{0,8},{8,0},{16,24},{24,16},{1,9},{9,1},{17,25},{25,17},{2,10},{10... | collective-permute-start | bytes 3538952 | tf_op jit(solution)/shard_map/ppermute | solution.py:719
  319.6 42.9 %collective-permute-start.22 = (f32[384,384]{1,0:T(8,128)}, f32[384,384]{1,0:T(8,128)S(1)}, u32[]{:S(2)}, u32[]{:S(2)}) collective-permute-start(f32[384,384]{1,0:T(8,128)} %get-tuple-element.172.refs_1_.refs_35_), channel_id=1, source_target_pairs={{0,8},{8,0},{16,24},{24,16},{1,9},{9,1},{17,25},{25,17},{2,10},{10... | collective-permute-start | bytes 1769480 | tf_op jit(solution)/shard_map/ppermute | solution.py:719
  320.1 19.0 %collective-permute-start.11 = (f32[48,1152]{1,0:T(8,128)S(1)}, f32[48,1152]{1,0:T(8,128)S(1)}, u32[]{:S(2)}, u32[]{:S(2)}) collective-permute-start(f32[48,1152]{1,0:T(8,128)S(1)} %copy-done.11), channel_id=1, source_target_pairs={{0,16},{8,24},{16,0},{24,8},{1,17},{9,25},{17,1},{25,9},{2,18},{10... | collective-permute-start | bytes 663560 | tf_op jit(solution)/shard_map/ppermute | solution.py:719
  338.6 5.6 %collective-permute-start.13 = (f32[48,896]{1,0:T(8,128)}, f32[48,896]{1,0:T(8,128)S(1)}, u32[]{:S(2)}, u32[]{:S(2)}) collective-permute-start(f32[48,896]{1,0:T(8,128)} %shard_map.588), channel_id=1, source_target_pairs={{0,16},{8,24},{16,0},{24,8},{1,17},{9,25},{17,1},{25,9},{2,18},{10... | collective-permute-start | bytes 516104 | tf_op jit(solution)/shard_map/ppermute | solution.py:719
  339.1 23.4 %collective-permute-start.19 = (f32[48,1152]{1,0:T(8,128)S(1)}, f32[48,1152]{1,0:T(8,128)S(1)}, u32[]{:S(2)}, u32[]{:S(2)}) collective-permute-start(f32[48,1152]{1,0:T(8,128)S(1)} %copy-done.11), channel_id=1, source_target_pairs={{0,8},{8,0},{16,24},{24,16},{1,9},{9,1},{17,25},{25,17},{2,10},{10... | collective-permute-start | bytes 663560 | tf_op jit(solution)/shard_map/ppermute | solution.py:719
  339.1 6.7 %copy-start.19 = (f32[48,1152]{1,0:T(8,128)}, f32[48,1152]{1,0:T(8,128)S(1)}, u32[]{:S(2)}) copy-start(f32[48,1152]{1,0:T(8,128)S(1)} %collective-permute-done.11.refs_3_.refs_30_) | copy-start | bytes 663556
  339.1 23.4 %collective-permute-start.20 = (f32[48,1152]{1,0:T(8,128)S(1)}, f32[48,1152]{1,0:T(8,128)S(1)}, u32[]{:S(2)}, u32[]{:S(2)}) collective-permute-start(f32[48,1152]{1,0:T(8,128)S(1)} %collective-permute-done.11.refs_3_.refs_30_), channel_id=1, source_target_pairs={{0,8},{8,0},{16,24},{24,16},{1,9},{9,1},{17,25},{25,17},{2,10},{10... | collective-permute-start | bytes 663560 | tf_op jit(solution)/shard_map/ppermute | solution.py:719
  345.8 16.1 %copy-start.12 = (f32[48,896]{1,0:T(8,128)S(1)}, f32[48,896]{1,0:T(8,128)}, u32[]{:S(2)}) copy-start(f32[48,896]{1,0:T(8,128)} %add.54.refs_4_.refs_27_) | copy-start | bytes 516100
  348.3 1.4 collective-permute-start.14
  350.3 3.6 collective-permute-start.15
  353.9 3.6 collective-permute-start.16
  357.4 4.5 %collective-permute-start.17 = (f32[2,128]{1,0:T(2,128)S(1)}, f32[2,128]{1,0:T(2,128)S(1)}, u32[]{:S(2)}, u32[]{:S(2)}) collective-permute-start(f32[2,128]{1,0:T(2,128)S(1)} %add.57), channel_id=1, source_target_pairs={{0,4},{1,5},{2,6},{3,7},{4,0},{5,1},{6,2},{7,3},{8,12},{9,13},{10,... | collective-permute-start | bytes 3080 | tf_op jit(solution)/shard_map/ppermute | solution.py:719
  361.9 1.4 collective-permute-start.18
  364.0 16.9 %copy-start.27 = (f32[16,128]{1,0:T(8,128)S(1)}, f32[16,128]{1,0:T(8,128)}, u32[]{:S(2)}) copy-start(f32[16,128]{1,0:T(8,128)} %get-tuple-element.130) | copy-start | bytes 24580
  364.0 22.4 %copy-start.28 = (f32[2,128]{1,0:T(2,128)S(1)}, f32[2,128]{1,0:T(2,128)}, u32[]{:S(2)}) copy-start(f32[2,128]{1,0:T(2,128)} %add.58.square_ref) | copy-start | bytes 3076
  381.6 3.7 collective-permute-start.23
  386.0 3.7 collective-permute-start.24
  389.7 4.6 %collective-permute-start.25 = (f32[18,128]{1,0:T(8,128)S(1)}, f32[18,128]{1,0:T(8,128)S(1)}, u32[]{:S(2)}, u32[]{:S(2)}) collective-permute-start(f32[18,128]{1,0:T(8,128)S(1)} %add.60), channel_id=1, source_target_pairs={{0,4},{1,5},{2,6},{3,7},{4,0},{5,1},{6,2},{7,3},{8,12},{9,13},{10,... | collective-permute-start | bytes 27656 | tf_op jit(solution)/shard_map/ppermute | solution.py:719
  (21 other events, 30.4 us)

commit v4 on v3

--- a/solution.py
+++ b/solution.py
@@ -147,6 +147,10 @@
     return (series_col == rows_table[SERIES_OF : SERIES_OF + 1, :keys]) & (key <= query)
 
 
+def slot_place(grouped, expert):
+    return (expert % 4) * 2 + expert // 4 if grouped else expert
+
+
 def slot_rows_hot(slot_row, expert):
     slot = expert * CAP + lax.broadcasted_iota(jnp.int32, (CAP, slot_row.shape[1]), 0)
     return (slot_row.astype(jnp.int32) == slot).astype(F32).astype(BF16)
@@ -187,18 +191,32 @@
         out[target, :, half:] = small.astype(BF16)
 
 
+def pair_kernel(sides, own, far, out):
+    low = sides[2] == 0
+    first = jnp.where(low, own[...], far[...])
+    second = jnp.where(low, far[...], own[...])
+    for target in range(out.shape[0]):
+        out[target, 0] = first
+        out[target, 1] = second
+
+
 def front_kernel(
-    local_rows, core, mine, other, cosine, sine, known, slot_row,
+    grouped, local_rows, core, mine, other, cosine, sine, known, slot_row,
     embedded_out, first_out, qkv_out, log_out, mixed_out, after_out, second_out, logits_out,
     slots_out, gains_out, pack, counts_out,
 ):
     amount = known.shape[0]
     half = 2 * D
     low = core[0] == 0
-    pack[:, :half] = jnp.where(low, mine[:, :half], other[:, :half])
-    pack[:, half:SMALL_AT] = jnp.where(low, other[:, :half], mine[:, :half])
-    pack[:, SMALL_AT:] = mine[:, half:]
-    table = mine[:, half:].astype(F32).T
+    for index in range(D // local_rows):
+        place = slot_place(grouped, index)
+        here = slice(index * local_rows, (index + 1) * local_rows)
+        there = slice(place * local_rows, (place + 1) * local_rows)
+        left, right = mine[there, :half], other[there, :half]
+        pack[here, :half] = jnp.where(low, left, right)
+        pack[here, half:SMALL_AT] = jnp.where(low, right, left)
+        pack[here, SMALL_AT:] = mine[there, half:]
+    table = pack[:, SMALL_AT:].astype(F32).T
     gains = table[VECTORS_AT : VECTORS_AT + 8]
     gains_out[...] = gains
     other_table = other[:, half:].astype(F32).T
@@ -255,7 +273,8 @@
     logits_out[...] = mm(second, pack[:, SMALL_AT:])
     for expert in range(EXPERTS):
         hot = slot_rows_hot(slot_row[0:1, :], expert) + slot_rows_hot(slot_row[1:2, :], expert)
-        slots_out[expert * CAP : (expert + 1) * CAP, :] = mm(hot, second).astype(BF16)
+        place = slot_place(grouped, expert)
+        slots_out[place * CAP : (place + 1) * CAP, :] = mm(hot, second).astype(BF16)
 
 
 def shared_kernel(second, gate_w, lift_w, down_w, shared_out):
@@ -273,27 +292,71 @@
         shared_out[...] += part
 
 
+def code_rows(part, ref):
+    top = jnp.max(jnp.abs(part), -1, keepdims=True)
+    power = jnp.ceil(jnp.log2(jnp.maximum(top, 1e-30)))
+    code = jnp.clip(jnp.round(part * jnp.exp2(15.0 - power)), -32767.0, 32767.0)
+    ref[:CAP, :] = code.astype(jnp.int32).astype(jnp.int16)
+    row = lax.broadcasted_iota(jnp.int32, (CAP, CAP), 0)
+    column = lax.broadcasted_iota(jnp.int32, (CAP, CAP), 1)
+    powers = jnp.sum(jnp.where(row == column, power, 0.0), 0, keepdims=True)
+    powers = jnp.concatenate([powers, jnp.zeros((1, D - CAP), F32)], 1)
+    ref[CAP:, :] = jnp.broadcast_to(powers, (CODE_ROWS, D)).astype(jnp.int32).astype(jnp.int16)
+
+
+def unit(rows, gate_up, down):
+    gate = mm(rows, gate_up[0])
+    lift = mm(rows, gate_up[1])
+    hidden = (gate * jax.nn.sigmoid(gate) * lift).astype(BF16)
+    return mm(hidden, down[...])
+
+
 def expert_kernel(rows, gate_up, down, rows_out):
-    gate = mm(rows[...], gate_up[0])
-    lift = mm(rows[...], gate_up[1])
-    hidden = (gate * jax.nn.sigmoid(gate) * lift).astype(BF16)
-    result = mm(hidden, down[...])
-    if len(rows_out.shape) == 2:
-        rows_out[...] = result
-        return
-    for source in range(rows_out.shape[0]):
-        part = result[source * CAP : (source + 1) * CAP]
-        top = jnp.max(jnp.abs(part), -1, keepdims=True)
-        power = jnp.ceil(jnp.log2(jnp.maximum(top, 1e-30)))
-        code = jnp.clip(jnp.round(part * jnp.exp2(15.0 - power)), -32767.0, 32767.0)
-        rows_out[source, :CAP, :] = code.astype(jnp.int32).astype(jnp.int16)
-        row = lax.broadcasted_iota(jnp.int32, (CAP, CAP), 0)
-        column = lax.broadcasted_iota(jnp.int32, (CAP, CAP), 1)
-        powers = jnp.sum(jnp.where(row == column, power, 0.0), 0, keepdims=True)
-        powers = jnp.concatenate([powers, jnp.zeros((1, D - CAP), F32)], 1)
-        rows_out[source, CAP:, :] = (
-            jnp.broadcast_to(powers, (CODE_ROWS, D)).astype(jnp.int32).astype(jnp.int16)
-        )
+    rows_out[...] = unit(rows[...], gate_up, down)
+
+
+def pair_expert_kernel(sides, rows, gate_up, down, gate_up_far, down_far, rows_out):
+    sources = rows.shape[0]
+    flat = rows[...].reshape(sources * CAP, D)
+
+    def serve(weights):
+        result = unit(flat, *weights)
+        for source in range(sources):
+            code_rows(result[source * CAP : (source + 1) * CAP], rows_out.at[source, 0])
+
+    pl.when(pl.program_id(0) == 0)(lambda: serve((gate_up, down)))
+    pl.when(pl.program_id(0) == 1)(lambda: serve((gate_up_far, down_far)))
+
+
+def far_weights_kernel(sides, *refs):
+    pieces, (gate_up, down) = refs[:4], refs[4:]
+    me = sides[0] * 2 + sides[1]
+    half, wide = pieces[0].shape[0], gate_up.shape[2]
+    for piece in range(4):
+        core, cross = piece // 2, piece % 2
+        value = picked_piece(pieces, jnp.bitwise_xor(piece, me), lambda ref: ref[...])
+        gate_up[core, cross * half : (cross + 1) * half, :] = value[:, :wide]
+        down[piece * half : (piece + 1) * half, :] = value[:, wide:]
+
+
+def shared_weights_kernel(local_rows, sides, *refs):
+    pieces, (both, down) = refs[:4], refs[4:]
+    me = sides[0] * 2 + sides[1]
+    wide = pieces[0].shape[1]
+    shard = down.shape[0] // (D // local_rows)
+    for piece in range(4):
+        value = picked_piece(pieces, jnp.bitwise_xor(piece, me), lambda ref: ref[...])
+        for index in range(D // local_rows):
+            place = slot_place(True, index)
+            rows = value[place * local_rows : (place + 1) * local_rows]
+            for at in range(0, wide, D):
+                column = piece * wide + at
+                part = rows[:, at : at + D]
+                if column < 2 * FFS:
+                    both[index * local_rows : (index + 1) * local_rows, column : column + D] = part
+                else:
+                    row = index * shard + (column - 2 * FFS) // D * local_rows
+                    down[row : row + local_rows, :] = part
 
 
 def unit_back(rows, slope, gate_w, lift_w, down_w):
@@ -344,33 +407,42 @@
 
 
 def expert_back_split_kernel(
-    core, rows, slope, gate_up, down, rows_out, in_keep, in_give, out_keep, out_give
+    sides, rows, slope, gate_up, down, gate_up_far, down_far,
+    rows_out, in_keep, in_give, out_keep, out_give,
 ):
-    hidden, gate_slope, lift_slope = unit_back(
-        rows[...], slope[...], gate_up[0], gate_up[1], down[...]
-    )
-    rows_out[...] = (mm_nt(gate_slope, gate_up[0]) + mm_nt(lift_slope, gate_up[1])).astype(BF16)
-
-    @pl.when(pl.program_id(0) == 0)
+    sources = rows.shape[0]
+    flat = rows[...].reshape(sources * CAP, D)
+    flat_slope = slope[...].reshape(sources * CAP, D)
+
+    @pl.when(pl.program_id(1) == 0)
     def _():
         for ref in (in_keep, in_give, out_keep, out_give):
             ref[...] = jnp.zeros_like(ref)
 
-    half = hidden.shape[1] // 2
-    low = core[0] == 0
-    gate = mm_tn(rows[...], gate_slope)
-    lift = mm_tn(rows[...], lift_slope)
-    in_keep[...] += jnp.where(low, gate, lift)
-    in_give[...] += jnp.where(low, lift, gate)
-    first = mm_tn(hidden[:, :half], slope[...])
-    last = mm_tn(hidden[:, half:], slope[...])
-    out_keep[...] += jnp.where(low, first, last)
-    out_give[...] += jnp.where(low, last, first)
+    def serve(gate_w, down_w):
+        hidden, gate_slope, lift_slope = unit_back(
+            flat, flat_slope, gate_w[0], gate_w[1], down_w[...]
+        )
+        result = (mm_nt(gate_slope, gate_w[0]) + mm_nt(lift_slope, gate_w[1])).astype(BF16)
+        rows_out[...] = result.reshape(rows_out.shape)
+        half = hidden.shape[1] // 2
+        low = sides[0] == 0
+        gate = mm_tn(flat, gate_slope)
+        lift = mm_tn(flat, lift_slope)
+        in_keep[0] += jnp.where(low, gate, lift)
+        in_give[0] += jnp.where(low, lift, gate)
+        first = mm_tn(hidden[:, :half], flat_slope)
+        last = mm_tn(hidden[:, half:], flat_slope)
+        out_keep[0] += jnp.where(low, first, last)
+        out_give[0] += jnp.where(low, last, first)
+
+    pl.when(pl.program_id(0) == 0)(lambda: serve(gate_up, down))
+    pl.when(pl.program_id(0) == 1)(lambda: serve(gate_up_far, down_far))
 
 
 def shared_back_split_kernel(
     sides, second, slope, gate_w, lift_w, down_w,
-    second_out, in_keep, in_give, out_keep, out_give, out_ref,
+    second_out, in_keep, in_give_even, in_give_odd, out_keep, out_give, out_ref,
 ):
     hidden, gate_slope, lift_slope = unit_back(
         second[...], slope[...], gate_w[...], lift_w[...], down_w[...]
@@ -390,7 +462,17 @@
     gate = mm_tn(second[...], gate_slope)
     lift = mm_tn(second[...], lift_slope)
     in_keep[0] = jnp.where(low, gate, lift)
-    in_give[0] = jnp.where(low, lift, gate)
+    given = jnp.where(low, lift, gate)
+    even = pl.program_id(0) % 2 == 0
+
+    @pl.when(even)
+    def _():
+        in_give_even[0] = given
+
+    @pl.when(jnp.logical_not(even))
+    def _():
+        in_give_odd[0] = given
+
     out_ref[...] = mm_tn(hidden, slope[...])
     quarter = out_keep.shape[1] // 2
     for shard in range(2):
@@ -434,11 +516,18 @@
     return [value[:, at : at + 128] for at in range(0, value.shape[1], 128)]
 
 
-def fold_kernel(in_keep, in_other, out_keep, out_other, keep, give):
+def fold_kernel(in_keep, in_even, in_odd, out_keep, out_other, keep, give):
     wide = in_keep.shape[2]
-    keep[:, :wide] = in_keep[0] + in_other[0]
+    half = wide // 2
+    keep[:, :half] = in_keep[0, :, :half] + in_even[0]
+    keep[:, half:wide] = in_keep[0, :, half:] + in_odd[0]
     keep[:, wide:] = out_keep[0] + out_other[0]
-    encode(give, tiles_of(in_keep[1] + in_other[1]) + tiles_of(out_keep[1] + out_other[1]))
+    encode(
+        give,
+        tiles_of(in_keep[1, :, :half] + in_even[1])
+        + tiles_of(in_keep[1, :, half:] + in_odd[1])
+        + tiles_of(out_keep[1] + out_other[1]),
+    )
 
 
 def add_code_kernel(keep, other, code):
@@ -450,15 +539,31 @@
         total[:, index * 128 : (index + 1) * 128] = jnp.sum(tile, 0)
 
 
-def expert_code_kernel(in_keep, in_other, out_keep, out_other, code):
-    encode(code, tiles_of(in_keep[...] + in_other[...]) + tiles_of(out_keep[...] + out_other[...]))
-
-
-def expert_sum_kernel(mine, other, in_total, out_total):
+def expert_split_kernel(sides, in_keep, in_other, out_keep, out_other, keep, code):
+    wide, half = in_keep.shape[2], in_keep.shape[1] // 2
+    here = pl.ds(pl.multiple_of(sides[1] * half, 8), half)
+    there = pl.ds(pl.multiple_of((1 - sides[1]) * half, 8), half)
+    keep[0, :, :wide] = in_keep[0, here, :] + in_other[0, here, :]
+    keep[0, :, wide:] = out_keep[0, here, :] + out_other[0, here, :]
+    encode(
+        code.at[0],
+        tiles_of(in_keep[0, there, :] + in_other[0, there, :])
+        + tiles_of(out_keep[0, there, :] + out_other[0, there, :]),
+    )
+
+
+def expert_far_kernel(keep, codes, own, far):
+    for index, tile in enumerate(decode(codes.at[0])):
+        here = slice(index * 128, (index + 1) * 128)
+        own[:, here] = keep[0, :, here] + tile
+    encode(far, [mine + theirs for mine, theirs in zip(tiles_of(keep[1]), decode(codes.at[1]))])
+
+
+def expert_total_kernel(own, code, in_total, out_total):
     split = in_total.shape[1] // 128
-    for index, (left, right) in enumerate(zip(decode(mine), decode(other))):
+    for index, tile in enumerate(decode(code)):
         ref, at = (in_total, index) if index < split else (out_total, index - split)
-        ref[:, at * 128 : (at + 1) * 128] = left + right
+        ref[:, at * 128 : (at + 1) * 128] = own[:, index * 128 : (index + 1) * 128] + tile
 
 
 def last_code_kernel(core, keep, other, code):
@@ -479,7 +584,7 @@
 
 
 def middle_kernel(
-    returned, known, slot_row, after, shared, logits, small, gains, target, ahead, weighting,
+    grouped, returned, known, slot_row, after, shared, logits, small, gains, target, ahead, weighting,
     mixer_out, shared_slope_out, slots_out, logits_slope_out, small_out, gain_out, sums_out,
 ):
     amount = after.shape[0]
@@ -489,8 +594,8 @@
     chosen = [
         (lane == integers[:, CHOICE + k : CHOICE + k + 1]).astype(F32) for k in range(2)
     ]
-    place = lax.broadcasted_iota(jnp.int32, (amount, SMALL), 0)
-    usable = (place + 1 + ahead[...] < integers[:, FINISH : FINISH + 1]).astype(F32)
+    point = lax.broadcasted_iota(jnp.int32, (amount, SMALL), 0)
+    usable = (point + 1 + ahead[...] < integers[:, FINISH : FINISH + 1]).astype(F32)
     logit = logits[...]
     routed = lane < EXPERTS
     top = jnp.max(jnp.where(routed, logit, -1e30), -1, keepdims=True)
@@ -502,12 +607,13 @@
     )
     picked = [jnp.zeros((amount, D), F32), jnp.zeros((amount, D), F32)]
     for expert in range(EXPERTS):
+        place = slot_place(grouped, expert)
         if len(returned.shape) == 2:
-            rows = returned[expert * CAP : (expert + 1) * CAP, :]
+            rows = returned[place * CAP : (place + 1) * CAP, :]
             scale = 1.0
         else:
-            rows = returned[expert, :CAP, :].astype(jnp.int32).astype(F32)
-            powers = returned[expert, CAP:, :].astype(jnp.int32).astype(F32)
+            rows = returned[place, :CAP, :].astype(jnp.int32).astype(F32)
+            powers = returned[place, CAP:, :].astype(jnp.int32).astype(F32)
             scale = jnp.exp2(powers[0:1, :CAP] - 15.0)
         high = rows.astype(BF16)
         rest = (rows - high.astype(F32)).astype(BF16)
@@ -554,21 +660,23 @@
     ).astype(BF16)
     slopes = [(gates[k] * mixer_slope).astype(BF16) for k in range(2)]
     for expert in range(EXPERTS):
-        slots_out[expert * CAP : (expert + 1) * CAP, :] = (
+        place = slot_place(grouped, expert)
+        slots_out[place * CAP : (place + 1) * CAP, :] = (
             mm(slot_rows_hot(slot_row[0:1, :], expert), slopes[0])
             + mm(slot_rows_hot(slot_row[1:2, :], expert), slopes[1])
         ).astype(BF16)
 
 
 def attend_back_kernel(
-    returned, known, second_slope, logits_slope, small, after, mixer_slope, gains, mixed, second,
+    grouped, returned, known, second_slope, logits_slope, small, after, mixer_slope, gains, mixed, second,
     output_w, small_before,
     attend_out, mixed_out, output_out, gain_out, small_out,
 ):
     slope = second_slope[...] + mm_nt(logits_slope[...], small[...])
     for expert in range(EXPERTS):
         hot = slot_cols_hot(known[:, 0:1], expert) + slot_cols_hot(known[:, 1:2], expert)
-        slope = slope + mm(hot, returned[expert * CAP : (expert + 1) * CAP, :])
+        place = slot_place(grouped, expert)
+        slope = slope + mm(hot, returned[place * CAP : (place + 1) * CAP, :])
     after_rows = after[...]
     part, gain_slope = rms_back(after_rows, inverse_rms(after_rows), gains[3:4], slope)
     gain_out[...] = gain_slope
@@ -684,20 +792,17 @@
     return pltpu.CompilerParams(vmem_limit_bytes=limit)
 
 
-def cost(flops, size):
-    return pl.CostEstimate(
-        flops=int(flops / 1000), bytes_accessed=int(size / 1000), transcendentals=0
-    )
+def cost(microseconds):
+    return pl.CostEstimate(flops=int(microseconds * 1.15e9), bytes_accessed=0, transcendentals=0)
 
 
 def columns(array, width, at):
     return (array, pl.BlockSpec((array.shape[0], width), lambda *unused: (0, at)))
 
 
-def simple_call(kernel, outs, args, flops, scratch=()):
+def simple_call(kernel, outs, args, microseconds, scratch=()):
     pairs = [a if isinstance(a, tuple) else (a, whole(a)) for a in args]
     args = [a for a, spec in pairs]
-    size = sum(a.size * a.dtype.itemsize for a in list(args) + list(outs))
     return pl.pallas_call(
         kernel,
         out_shape=outs,
@@ -706,7 +811,7 @@
         scratch_shapes=list(scratch),
         grid=(1,),
         compiler_params=params(),
-        cost_estimate=cost(flops, size),
+        cost_estimate=cost(microseconds),
     )(*args)
 
 
@@ -764,6 +869,32 @@
 
 def exchange(value):
     return lax.all_to_all(value, "expert", split_axis=0, concat_axis=0, tiled=True)
+
+
+def exchange_near(value):
+    return lax.all_to_all(
+        value,
+        "expert",
+        split_axis=0,
+        concat_axis=0,
+        tiled=True,
+        axis_index_groups=[[0, 1, 2, 3], [4, 5, 6, 7]],
+    )
+
+
+def pairs_of(value, sides):
+    far = flip(value, "expert", 4)
+    return pl.pallas_call(
+        pair_kernel,
+        out_shape=out((4, 2, *value.shape), BF16),
+        in_specs=[
+            pl.BlockSpec(memory_space=pltpu.SMEM),
+            *[pl.BlockSpec(memory_space=pltpu.VMEM)] * 2,
+        ],
+        out_specs=pl.BlockSpec(memory_space=pltpu.VMEM),
+        compiler_params=params(),
+        cost_estimate=cost(2),
+    )(sides, value, far)
 
 
 def spread(value):
@@ -809,6 +940,12 @@
 
 def tile_specs(arrays, steps):
     return [tile_spec(index, array.shape, steps) for index, array in enumerate(arrays)]
+
+
+def quarter_kernel(sides, gate_up, down, quarter):
+    wide = gate_up.shape[2]
+    quarter[:, :wide] = gate_up[0].astype(BF16)
+    quarter[:, wide:] = down[...].astype(BF16)
 
 
 def prepare_kernel(count, *refs):
@@ -881,7 +1018,6 @@
             return last_rows(3 * D, SMALL_AT)
         if not fast:
             return pieces[{4: 1, 5: 2, 7: 3, 8: 4}[index]][...]
-        low = sides[0] == 0
         me = sides[0] * 2 + sides[1]
         shared = pieces[2:6]
         wide = 2 * FFS // 4
@@ -897,10 +1033,21 @@
                 ],
                 0,
             )
+        routed = pieces[6:10] if index == 7 else pieces[10:14]
         if index == 7:
-            mine, other = pieces[6][...], pieces[7][...]
-            return jnp.stack([jnp.where(low, mine, other), jnp.where(low, other, mine)])
-        return jnp.where(step // 2 == sides[0], pieces[8][...], pieces[9][...])
+            rows = masters[7].shape[1]
+            here = pl.ds(pl.multiple_of((step % 2) * rows, 8), rows)
+            return jnp.stack(
+                [
+                    picked_piece(
+                        routed,
+                        jnp.bitwise_xor(side * 2 + step // 2, me),
+                        lambda ref: ref[here, :],
+                    )
+                    for side in range(2)
+                ]
+            )
+        return picked_piece(routed, jnp.bitwise_xor(step, me), lambda ref: ref[...])
 
     def update(index):
         gradient = gradient_of(index)
@@ -990,7 +1137,9 @@
         group_size == 1 and dp_count == 4 and local_rows % 16 == 0 and hidden_local == 2 * D
     )
     core = lax.axis_index("dp") & 1
-    sides = jnp.stack([core, lax.axis_index("dp") >> 1]).astype(jnp.int32)
+    sides = jnp.stack(
+        [core, lax.axis_index("dp") >> 1, lax.axis_index("expert") >> 2]
+    ).astype(jnp.int32)
     in_smem = pl.BlockSpec(memory_space=pltpu.SMEM)
     in_vmem = pl.BlockSpec(memory_space=pltpu.VMEM)
     ahead_row = jnp.pad(
@@ -998,13 +1147,13 @@
     )
     packed = pl.pallas_call(
         functools.partial(pack_kernel, small_end),
-        out_shape=out((expert_count, local_rows, 2 * D + SMALL), BF16),
+        out_shape=out((1 if fast else expert_count, local_rows, 2 * D + SMALL), BF16),
         in_specs=[*[in_smem] * 3, *[in_vmem] * 6],
         out_specs=in_vmem,
         compiler_params=params(),
-        cost_estimate=cost(1e6, 1e6),
+        cost_estimate=cost(2),
     )(sides, lengths, domains, ahead_row, attend_input, attend_output, router.T, horizon, vectors)
-    gathered = exchange(packed)
+    gathered = exchange_near(pairs_of(packed[0], sides)) if fast else exchange(packed)
 
     def state(group):
         return tuple(a.T if index == 3 else a for index, a in enumerate(group))
@@ -1043,8 +1192,27 @@
             whole(out((16, 128))),
         ],
         compiler_params=params(),
-        cost_estimate=cost(3e6, 7e6),
+        cost_estimate=cost(5),
     )(*masters)
+    weight_quarter = points
+    if fast:
+        weight_quarter = pl.pallas_call(
+            quarter_kernel,
+            out_shape=out((D // 2, hidden_local + D), BF16),
+            grid_spec=pltpu.PrefetchScalarGridSpec(
+                num_scalar_prefetch=1,
+                grid=(1,),
+                in_specs=[
+                    pl.BlockSpec(
+                        (1, D // 2, hidden_local), lambda i, sides: (sides[0], sides[1], 0)
+                    ),
+                    pl.BlockSpec((D // 2, D), lambda i, sides: (sides[0] * 2 + sides[1], 0)),
+                ],
+                out_specs=pl.BlockSpec((D // 2, hidden_local + D), lambda i, sides: (0, 0)),
+            ),
+            compiler_params=params(),
+            cost_estimate=cost(2.6),
+        )(sides, expert_input, expert_output)
     frequency = jnp.exp(-jnp.log(10000.0) * jnp.arange(HD // 2, dtype=F32) / (HD // 2))
     cosine, sine, known, rows_table = pl.pallas_call(
         tables_kernel,
@@ -1052,7 +1220,7 @@
         in_specs=[*[in_smem] * 2, *[in_vmem] * 3],
         out_specs=[in_vmem] * 4,
         compiler_params=params(),
-        cost_estimate=cost(1e6, 1e6),
+        cost_estimate=cost(3),
     )(
         lengths,
         domains,
@@ -1070,16 +1238,21 @@
     ).astype(BF16)
     for bit in dp_bits:
         shared_piece, unused = halves(shared_piece, 1, (lax.axis_index("dp") & bit) != 0)
-    gathered = ready(
-        gathered, known, gate_up_low, down_low, master_squares, shared_piece
-    ).reshape(D, -1)
+    if fast:
+        shared_piece = pairs_of(shared_piece, sides)
+    gathered = ready(gathered, known, shared_piece, weight_quarter).reshape(D, -1)
     gathered_other = flip(gathered, "dp", 1)
-    shared_pieces = spread(ready(shared_piece, gathered))
+    shared_piece = ready(shared_piece, gathered)
+    if fast:
+        shared_pieces = exchange_near(shared_piece)
+        weight_pieces = [flip(weight_quarter, "expert", 4)]
+    else:
+        shared_pieces = spread(shared_piece)
     (
         embedded, first, qkv, log_total, mixed, after, second, logits, slots, gains, pack,
         counts_half,
     ) = simple_call(
-        functools.partial(front_kernel, local_rows),
+        functools.partial(front_kernel, fast, local_rows),
         [
             out((amount, D)), out((amount, D), BF16), out((amount, 3 * D), BF16),
             out((amount, 128)), out((amount, D), BF16), out((amount, D)),
@@ -1087,7 +1260,7 @@
             out((8, D)), out((D, SMALL_AT + SMALL), BF16), out((1, SMALL)),
         ],
         [(sides, in_smem), gathered, gathered_other, cosine, sine, known, rows_table],
-        8e9,
+        15,
     )
 
     def to_devices(rows):
@@ -1102,50 +1275,78 @@
             rows = jnp.sum(rows, 1).astype(kind)
         return rows.reshape(-1, D)
 
-    arrived = to_devices(ready(slots, shared_pieces))
     first_bit = dp_bits[-1]
-    shared_pieces = ready(shared_pieces, slots)
-    shared_other = flip(shared_pieces, "dp", first_bit)
-    arrived = ready(arrived, shared_other)
     block = 512
-    total_rows = arrived.shape[0]
-    coded = group_size == 1
-    sources = block // CAP
-    expert_rows = pl.pallas_call(
-        expert_kernel,
-        out_shape=(
-            out((EXPERTS, CAP + CODE_ROWS, D), jnp.int16) if coded else out((total_rows, D))
-        ),
-        grid=(total_rows // block,),
-        in_specs=[
-            pl.BlockSpec((block, D), lambda i: (i, 0)), whole(gate_up_low), whole(down_low),
-        ],
-        out_specs=(
-            pl.BlockSpec((sources, CAP + CODE_ROWS, D), lambda i: (i, 0, 0))
-            if coded
-            else pl.BlockSpec((block, D), lambda i: (i, 0))
-        ),
-        compiler_params=params(),
-        cost_estimate=cost(total_rows * D * 3 * hidden_local * 2, 7e6),
-    )(arrived, gate_up_low, down_low)
-    returned = exchange(expert_rows) if coded else to_points(expert_rows)
-    shared_pieces = ready(shared_pieces, expert_rows)
-    side = (lax.axis_index("dp") & first_bit) != 0
-    shared_pack = jnp.concatenate(
-        [
-            jnp.where(side, shared_other, shared_pieces),
-            jnp.where(side, shared_pieces, shared_other),
-        ],
-        2,
-    )
-    shared_pack = join(shared_pack, 2, dp_bits[:-1])
-    shin_low = shared_pack[:, :, : 2 * FFS].reshape(D, -1)
-    shout_low = (
-        shared_pack[:, :, 2 * FFS :]
-        .reshape(expert_count, local_rows, folds, D)
-        .swapaxes(1, 2)
-        .reshape(FFS, D)
-    )
+    if fast:
+        arrived = exchange_near(
+            ready(slots, shared_pieces, weight_pieces[0]).reshape(4, 2, CAP, D)
+        )
+        weight_pieces.append(flip(ready(weight_pieces[0], slots), "dp", 2))
+        weight_pieces += [flip(piece, "dp", 1) for piece in weight_pieces]
+        gate_up_far, down_far = simple_call(
+            far_weights_kernel,
+            [out(expert_input.shape, BF16), out(expert_output.shape, BF16)],
+            [(sides, in_smem), ready(weight_pieces[0], gate_up_low), *weight_pieces[1:]],
+            3,
+        )
+        shared_pieces = ready(shared_pieces, weight_pieces[1])
+        shared_other = flip(shared_pieces, "dp", 2)
+        row_spec = pl.BlockSpec(
+            (4, 1, CAP, D), lambda i, sides: (0, jnp.bitwise_xor(i, sides[2]), 0, 0)
+        )
+        held = [gate_up_low, down_low, gate_up_far, down_far]
+        held_specs = [
+            pl.BlockSpec(a.shape, lambda *unused, a=a: (0,) * len(a.shape)) for a in held
+        ]
+        expert_rows = pl.pallas_call(
+            pair_expert_kernel,
+            out_shape=out((4, 2, CAP + CODE_ROWS, D), jnp.int16),
+            grid_spec=pltpu.PrefetchScalarGridSpec(
+                num_scalar_prefetch=1,
+                grid=(2,),
+                in_specs=[row_spec, *held_specs],
+                out_specs=pl.BlockSpec(
+                    (4, 1, CAP + CODE_ROWS, D),
+                    lambda i, sides: (0, jnp.bitwise_xor(i, sides[2]), 0, 0),
+                ),
+            ),
+            compiler_params=params(),
+            cost_estimate=cost(10),
+        )(sides, arrived, *held)
+        returned = exchange_near(ready(expert_rows, shared_other)).reshape(
+            EXPERTS, CAP + CODE_ROWS, D
+        )
+        shared_pieces = ready(shared_pieces, expert_rows)
+        shared_quarters = [shared_pieces, shared_other]
+        shared_quarters += [flip(piece, "dp", 1) for piece in shared_quarters]
+        shin_low, shout_low = simple_call(
+            functools.partial(shared_weights_kernel, local_rows),
+            [out((D, 2 * FFS), BF16), out((FFS, D), BF16)],
+            [(sides, in_smem), *[piece.reshape(D, -1) for piece in shared_quarters]],
+            4.3,
+        )
+    else:
+        arrived = to_devices(ready(slots, shared_pieces))
+        total_rows = arrived.shape[0]
+        row_spec = pl.BlockSpec((block, D), lambda i: (i, 0))
+        expert_rows = pl.pallas_call(
+            expert_kernel,
+            out_shape=out((total_rows, D)),
+            grid=(total_rows // block,),
+            in_specs=[row_spec, whole(gate_up_low), whole(down_low)],
+            out_specs=row_spec,
+            compiler_params=params(),
+            cost_estimate=cost(10),
+        )(arrived, gate_up_low, down_low)
+        returned = to_points(expert_rows)
+        shared_pack = join(ready(shared_pieces, expert_rows), 2, dp_bits)
+        shin_low = shared_pack[:, :, : 2 * FFS].reshape(D, -1)
+        shout_low = (
+            shared_pack[:, :, 2 * FFS :]
+            .reshape(expert_count, local_rows, folds, D)
+            .swapaxes(1, 2)
+            .reshape(FFS, D)
+        )
     chunk = 512
     chunks = FFS // chunk
     shared = pl.pallas_call(
@@ -1160,7 +1361,7 @@
         ],
         out_specs=pl.BlockSpec((amount, D), lambda i: (0, 0)),
         compiler_params=params(),
-        cost_estimate=cost(amount * D * 3 * FFS * 2, 5e6),
+        cost_estimate=cost(5.8),
     )(second, shin_low, shin_low, shout_low)
     counts = ready(counts_half, expert_rows)
     for bit in dp_bits[1:]:
@@ -1175,7 +1376,7 @@
     (
         mixer_slope, shared_slope, slope_slots, logits_slope, small_head, gain_three, local_sums,
     ) = simple_call(
-        middle_kernel,
+        functools.partial(middle_kernel, fast),
         [
             out((amount, D)), out((amount, D), BF16), out((EXPERTS * CAP, D), BF16),
             out((amount, SMALL), BF16), out((D, SMALL)), out((1, D)), out((1, SMALL)),
@@ -1184,9 +1385,9 @@
             returned, known, rows_table, after, shared, logits, small_low, gains, target,
             ahead_small, weighting,
         ],
-        7e9,
-    )
-    received = to_devices(slope_slots)
+        11.4,
+    )
+    received = exchange_near(slope_slots.reshape(4, 2, CAP, D)) if fast else to_devices(slope_slots)
     chunk = D
     chunks = FFS // chunk
     back_in = [
@@ -1198,27 +1399,28 @@
     ]
     second_spec = pl.BlockSpec((amount, D), lambda i, *unused: (0, 0))
     back_args = (second, shared_slope, shin_low, shin_low, shout_low)
-    back_cost = cost(amount * D * 8 * FFS * 2, 14e6)
     if fast:
         in_spec = pl.BlockSpec(
             (1, D, chunk), lambda i, sides: (jnp.bitwise_xor(i // 2, sides[1]), 0, i % 2)
         )
+        give_spec = pl.BlockSpec(
+            (1, D, chunk), lambda i, sides: (jnp.bitwise_xor(i // 2, sides[1]), 0, 0)
+        )
         out_spec = pl.BlockSpec((2, D // chunks, D), lambda i, sides: (0, i, 0))
-        shared_second_slope, in_keep, in_give, out_keep, out_give = pl.pallas_call(
+        shared_second_slope, in_keep, in_even, in_odd, out_keep, out_give = pl.pallas_call(
             shared_back_split_kernel,
             out_shape=[
-                out((amount, D)), out((2, D, FFS // 2)), out((2, D, FFS // 2)), out((2, D, D)),
-                out((2, D, D)),
+                out((amount, D)), out((2, D, FFS // 2)), *[out((2, D, D))] * 4,
             ],
             grid_spec=pltpu.PrefetchScalarGridSpec(
                 num_scalar_prefetch=1,
                 grid=(chunks,),
                 in_specs=back_in,
-                out_specs=[second_spec, in_spec, in_spec, out_spec, out_spec],
+                out_specs=[second_spec, in_spec, give_spec, give_spec, out_spec, out_spec],
                 scratch_shapes=[pltpu.VMEM((chunk, D), F32)],
             ),
             compiler_params=params(),
-            cost_estimate=back_cost,
+            cost_estimate=cost(14),
         )(sides, *back_args)
     else:
         shared_second_slope, grad_shin, grad_shout = pl.pallas_call(
@@ -1232,10 +1434,10 @@
                 pl.BlockSpec((chunk, D), lambda i: (i, 0)),
             ],
             compiler_params=params(),
-            cost_estimate=back_cost,
+            cost_estimate=cost(10),
         )(*back_args)
     if fast:
-        in_other, out_other = flip(in_give, "dp", 1), flip(out_give, "dp", 1)
+        in_even, in_odd, out_other = (flip(a, "dp", 1) for a in (in_even, in_odd, out_give))
         fold_in = pl.BlockSpec((2, D // 4, FFS // 2), lambda i: (0, i, 0))
         fold_out = pl.BlockSpec((2, D // 4, D), lambda i: (0, i, 0))
         wide = FFS // 2 + D
@@ -1245,29 +1447,39 @@
             fold_kernel,
             out_shape=[out((D, wide)), out((D, wide + 128), jnp.int16)],
             grid=(4,),
-            in_specs=[fold_in, fold_in, fold_out, fold_out],
+            in_specs=[fold_in, *[fold_out] * 4],
             out_specs=[fold_to, code_to],
             compiler_params=params(),
-            cost_estimate=cost(2e6, 10e6),
-        )(in_keep, in_other, out_keep, out_other)
+            cost_estimate=cost(5.3),
+        )(in_keep, in_even, in_odd, out_keep, out_other)
+        received = ready(received, shared_second_slope, shared_give)
         shared_other = flip(shared_give, "dp", 2)
-        received = ready(received, shared_second_slope, shared_give)
     else:
         received = ready(received, shared_second_slope)
-    row_spec = pl.BlockSpec((block, D), lambda i: (i, 0))
-    expert_cost = cost(total_rows * D * 8 * hidden_local * 2, 10e6)
-    weight_specs = [whole(gate_up_low), whole(down_low)]
     if fast:
-        half_shapes = [out((D, hidden_local))] * 2 + [out((hidden_local // 2, D))] * 2
+        half_shapes = [out((2, D, hidden_local))] * 2 + [out((2, D, D))] * 2
+        row_spec = pl.BlockSpec(
+            (2, 1, CAP, D), lambda i, j, sides: (j, jnp.bitwise_xor(i, sides[2]), 0, 0)
+        )
         grad_rows, expert_in, expert_in_give, expert_out, expert_out_give = pl.pallas_call(
             expert_back_split_kernel,
-            out_shape=[out((total_rows, D), BF16), *half_shapes],
-            grid=(total_rows // block,),
-            in_specs=[in_smem, row_spec, row_spec, *weight_specs],
-            out_specs=[row_spec, *[whole(a) for a in half_shapes]],
+            out_shape=[out((4, 2, CAP, D), BF16), *half_shapes],
+            grid_spec=pltpu.PrefetchScalarGridSpec(
+                num_scalar_prefetch=1,
+                grid=(2, 2),
+                in_specs=[row_spec, row_spec, *held_specs],
+                out_specs=[
+                    row_spec,
+                    *[
+                        pl.BlockSpec((1, *a.shape[1:]), lambda i, j, sides: (i, 0, 0))
+                        for a in half_shapes
+                    ],
+                ],
+            ),
             compiler_params=params(),
-            cost_estimate=expert_cost,
-        )(sides, arrived, received, gate_up_low, down_low)
+            cost_estimate=cost(19.5),
+        )(sides, arrived, received, *held)
+        routed_back = exchange_near(ready(grad_rows, shared_other)).reshape(-1, D)
     else:
         grad_rows, grad_expert_in, grad_expert_out = pl.pallas_call(
             expert_back_kernel,
@@ -1275,16 +1487,16 @@
                 out((total_rows, D), BF16), out((2, D, hidden_local)), out((hidden_local, D)),
             ],
             grid=(total_rows // block,),
-            in_specs=[row_spec, row_spec, *weight_specs],
+            in_specs=[row_spec, row_spec, whole(gate_up_low), whole(down_low)],
             out_specs=[
                 row_spec,
                 pl.BlockSpec((2, D, hidden_local), lambda i: (0, 0, 0)),
                 pl.BlockSpec((hidden_local, D), lambda i: (0, 0)),
             ],
             compiler_params=params(),
-            cost_estimate=expert_cost,
+            cost_estimate=cost(10),
         )(arrived, received, gate_up_low, down_low)
-    routed_back = to_points(grad_rows)
+        routed_back = to_points(grad_rows)
     if fast:
         shared_code = pl.pallas_call(
             add_code_kernel,
@@ -1293,26 +1505,29 @@
             in_specs=[fold_to, code_to],
             out_specs=code_to,
             compiler_params=params(),
-            cost_estimate=cost(2e6, 4e6),
+            cost_estimate=cost(4.4),
         )(shared_keep, shared_other)
         expert_in_other = flip(expert_in_give, "dp", 1)
         expert_out_other = flip(expert_out_give, "dp", 1)
-        sum_in = pl.BlockSpec((D // 4, hidden_local), lambda i: (i, 0))
-        sum_out = pl.BlockSpec((D // 4, D), lambda i: (i, 0))
-        expert_code = pl.pallas_call(
-            expert_code_kernel,
-            out_shape=out((D, wide + 128), jnp.int16),
-            grid=(4,),
-            in_specs=[sum_in, sum_in, sum_out, sum_out],
-            out_specs=code_to,
+        half_in = pl.BlockSpec((1, D, hidden_local), lambda i: (i, 0, 0))
+        half_out = pl.BlockSpec((1, D, D), lambda i: (i, 0, 0))
+        expert_keep, expert_code = pl.pallas_call(
+            expert_split_kernel,
+            out_shape=[out((2, D // 2, wide)), out((2, D // 2, wide + 128), jnp.int16)],
+            grid=(2,),
+            in_specs=[in_smem, half_in, half_in, half_out, half_out],
+            out_specs=[
+                pl.BlockSpec((1, D // 2, wide), lambda i: (i, 0, 0)),
+                pl.BlockSpec((1, D // 2, wide + 128), lambda i: (i, 0, 0)),
+            ],
             compiler_params=params(),
-            cost_estimate=cost(2e6, 8e6),
-        )(expert_in, expert_in_other, expert_out, expert_out_other)
+            cost_estimate=cost(4.6),
+        )(sides, expert_in, expert_in_other, expert_out, expert_out_other)
         sums = local_sums + flip(local_sums, "dp", 2)
         routed_plain = routed_back
         routed_back = ready(routed_back, shared_code, expert_code, sums)
     attend_slope, mixed_slope, grad_output, gain_two, small_routed = simple_call(
-        attend_back_kernel,
+        functools.partial(attend_back_kernel, fast),
         [
             out((amount, D)), out((amount, D), BF16), out((D, D)), out((1, D)), out((D, SMALL)),
         ],
@@ -1320,8 +1535,17 @@
             routed_back, known, shared_second_slope, logits_slope, small_low, after,
             mixer_slope, gains, mixed, second, columns(pack, D, 3), small_head,
         ],
-        2e9,
-    )
+        6,
+    )
+    if fast:
+        expert_code_other = flip(expert_code, "dp", 2)
+        expert_own, expert_far = simple_call(
+            expert_far_kernel,
+            [out((D // 2, wide)), out((D // 2, wide + 128), jnp.int16)],
+            [expert_keep, expert_code_other],
+            3.5,
+        )
+        mixed_slope = ready(mixed_slope, expert_far)
     pack_columns = SMALL_AT + SMALL
     half_columns = SMALL_AT // 2 + SMALL
     last_keep, last_give = simple_call(
@@ -1335,7 +1559,7 @@
             embedded, gains, columns(pack, 3 * D, 0), attend_slope, small_routed, gain_two,
             gain_three, grad_output,
         ],
-        16e9,
+        18.4,
         [
             pltpu.VMEM((D, 2 * half_columns), F32),
             pltpu.VMEM((amount, D), F32),
@@ -1348,46 +1572,47 @@
     if fast:
         shared_code = ready(shared_code, routed_plain).reshape(expert_count, local_rows, -1)
         (shared_sum,) = simple_call(
-            shard_sum_kernel, [out((local_rows, wide))], [exchange(shared_code)], 4e6
-        )
-        expert_code_other = flip(ready(expert_code, mixed_slope), "dp", 2)
-        last_give = ready(last_give, expert_code_other)
+            shard_sum_kernel, [out((local_rows, wide))], [exchange(shared_code)], 2.5
+        )
+        expert_far_other = flip(expert_far, "expert", 4)
+        last_give = ready(last_give, expert_far_other)
         (last_code,) = simple_call(
             last_code_kernel,
             [out((D, half_columns + 128), jnp.int16)],
             [(sides, in_smem), last_keep, flip(last_give, "dp", 1)],
-            4e6,
+            3.3,
         )
         last_code = ready(last_code, shared_sum).reshape(expert_count, local_rows, -1)
         (last_part,) = simple_call(
             last_sum_kernel,
             [out((local_rows, half_columns))],
             [(sides, in_smem), exchange(last_code)],
-            4e6,
+            2.2,
         )
         last_part = last_part + flip(last_part, "dp", 2)
-        expert_in, expert_out = pl.pallas_call(
-            expert_sum_kernel,
-            out_shape=[out((D, hidden_local)), out((D, D))],
-            grid=(4,),
-            in_specs=[code_to, code_to],
-            out_specs=[sum_in, sum_out],
-            compiler_params=params(),
-            cost_estimate=cost(2e6, 8e6),
-        )(ready(expert_code, mixed_slope), expert_code_other)
+        expert_in, expert_out = simple_call(
+            expert_total_kernel,
+            [out((D // 2, hidden_local)), out((D // 2, D))],
+            [ready(expert_own, last_code), expert_far_other],
+            2.5,
+        )
+        expert_in_cross = flip(expert_in, "dp", 2)
+        expert_out_cross = flip(expert_out, "dp", 2)
         shared_cross = flip(shared_sum, "dp", 2)
-        square_pieces = [expert_in, expert_out, shared_sum, shared_cross, last_part]
-        weights = (1.0,) * 5
+        square_pieces = [
+            expert_in, expert_in_cross, expert_out, expert_out_cross, shared_sum, shared_cross,
+            last_part,
+        ]
+        weights = (1.0,) * 7
         square_bits = [1]
         pieces = [
             last_part, flip(last_part, "dp", 1), shared_sum, shared_cross,
-            flip(shared_sum, "dp", 1), flip(shared_cross, "dp", 1), expert_in,
-            flip(expert_in, "dp", 1), expert_out, flip(expert_out, "dp", 1),
+            flip(shared_sum, "dp", 1), flip(shared_cross, "dp", 1),
+            expert_in, expert_in_cross, flip(expert_in, "dp", 1), flip(expert_in_cross, "dp", 1),
+            expert_out, expert_out_cross, flip(expert_out, "dp", 1),
+            flip(expert_out_cross, "dp", 1),
         ]
-        tile_in = pl.BlockSpec((D // steps, hidden_local), lambda i: (i, 0))
-        half_steps = steps // 2
-        tile_out = pl.BlockSpec((hidden_local // steps, D), lambda i: (i % half_steps, 0))
-        piece_specs = [*[whole(a) for a in pieces[:6]], tile_in, tile_in, tile_out, tile_out]
+        piece_specs = [whole(a) for a in pieces]
     else:
         sums = local_sums
         shin_part = scatter_sum(grad_shin, 0, [1])[0].reshape(expert_count, local_rows, FFS)
@@ -1414,7 +1639,7 @@
             *[tile_spec(i, a.shape, steps) for i, a in zip((4, 5, 7, 8), pieces[1:])],
         ]
     (both_sums,) = simple_call(
-        functools.partial(squares_kernel, weights), [out((2, 128))], [sums, *square_pieces], 3e6
+        functools.partial(squares_kernel, weights), [out((2, 128))], [sums, *square_pieces], 2.4
     )
     for bit in square_bits:
         both_sums = both_sums + flip(both_sums, "dp", bit)
@@ -1432,7 +1657,7 @@
         ],
         out_specs=[*state_specs, *state_specs, *state_specs, whole(out((16, 128)))],
         compiler_params=params(),
-        cost_estimate=cost(3e7, 34e6),
+        cost_estimate=cost(17),
     )(sides, both_sums, *masters, *first_moments, *second_moments, *pieces)
     directions = updates[:count]
     all_totals = sum_small(
@@ -1446,7 +1671,7 @@
         in_specs=[whole(totals), whole(master_totals), *state_specs, *state_specs],
         out_specs=state_specs,
         compiler_params=params(),
-        cost_estimate=cost(3e6, 15e6),
+        cost_estimate=cost(7),
     )(totals, master_totals, *masters, *directions)
     results = []
     for index in range(count):

time: 408 us -> 376 us (0.922)
  waiting for transfers between devices: 155 us -> 85.3 us
  starting transfers between devices: 49.8 us -> 79.9 us
  Pallas kernels: 159 us -> 178 us
  other arithmetic: 13.8 us -> 7.28 us
    all_to_all x8 -> x2, waiting for transfers between devices: 80.5 us -> 14.8 us  [exchange(): lax.all_to_all(value, 'expert', split_axis=0, concat_axis=0, tiled=True)]
    ppermute x26 -> x39, starting transfers between devices: 14 us -> 44.2 us  [flip(): return lax.ppermute(value, axis_name, [(i, i ^ bit) for i in range(count)])]
    all_to_all x8 -> x2, starting transfers between devices: 35.9 us -> 11.6 us  [exchange(): lax.all_to_all(value, 'expert', split_axis=0, concat_axis=0, tiled=True)]
    all_to_all x0 -> x6, starting transfers between devices: none -> 24.1 us  [exchange_near(): lax.all_to_all(value, 'expert', split_axis=0, concat_axis=0, tiled=True,...]
    ppermute x26 -> x39, waiting for transfers between devices: 74.3 us -> 60.7 us  [flip(): return lax.ppermute(value, axis_name, [(i, i ^ bit) for i in range(count)])]
    pallas_call x8 -> x12, Pallas kernels: 60.9 us -> 74.2 us  [simple_call(): pl.pallas_call(kernel, out_shape=outs, in_specs=[spec for a, spec in pair...]
    all_to_all x0 -> x6, waiting for transfers between devices: none -> 9.79 us  [exchange_near(): lax.all_to_all(value, 'expert', split_axis=0, concat_axis=0, tiled=True,...]
    pallas_call x4 -> x6, Pallas kernels: 36.2 us -> 40.1 us  [the longest x1 19.5 us: shards(): pl.pallas_call(expert_back_split_kernel, out_shape=[out((4, 2, CAP, D), B...]
  transfers between devices with their start and end apart: 34 -> 47, of which waited for: 21 -> 26; matrix products, arithmetic and copies ran while one was open for 4% -> 2% of each run, Pallas kernels for 21% -> 36%
where the time goes in v4:
time: 376 us; the launch traced here: 372 us
  Pallas kernels  178 us (47%)
  waiting for transfers between devices  85.3 us (23%)
  starting transfers between devices  79.9 us (21%)
  local copies, waits for them, and re-layouts  18.9 us (5%)
  other arithmetic  7.28 us (2%)
    pallas_call x12, Pallas kernels, simple_call(): pl.pallas_call(kernel, out_shape=outs, in_specs=[spec for a, spec in pair...  74.2 us
    ppermute x39, waiting for transfers between devices, flip(): return lax.ppermute(value, axis_name, [(i, i ^ bit) for i in range(count)])  60.7 us
    ppermute x39, starting transfers between devices, flip(): return lax.ppermute(value, axis_name, [(i, i ^ bit) for i in range(count)])  44.2 us
    all_to_all x6, starting transfers between devices, exchange_near(): lax.all_to_all(value, 'expert', split_axis=0, concat_axis=0, tiled=True,...  24.1 us
    pallas_call x1, Pallas kernels, shards(): pl.pallas_call(expert_back_split_kernel, out_shape=[out((4, 2, CAP, D), B...  19.5 us
    pallas_call x1, Pallas kernels, shards(): pl.pallas_call(functools.partial(moments_kernel, fast, count, small_end),...  16.9 us
    all_to_all x2, waiting for transfers between devices, exchange(): lax.all_to_all(value, 'expert', split_axis=0, concat_axis=0, tiled=True)  14.8 us
    unnamed x97, local copies, waits for them, and re-layouts  14.6 us
  transfers between devices with their start and end apart: 47, of which 26 were waited for; matrix products, arithmetic and copies ran while one was open for 2% of the time, Pallas kernels for 36%

profile of v4, /device:TPU:0, one launch (start us, length us, event | category | flops | bytes accessed | tf_op | source)
XLA Modules:
  0.0 372.2 jit_solution(8674276389412324134)
XLA Ops:
  3.2 4.0 %collective-permute-start = (bf16[48,896]{1,0:T(8,128)(2,1)}, bf16[48,896]{1,0:T(8,128)(2,1)S(1)}, u32[]{:S(2)}, u32[]{:S(2)}) collective-permute-start(bf16[48,896]{1,0:T(8,128)(2,1)} %bitcast.181), channel_id=1, source_target_pairs={{0,4},{1,5},{2,6},{3,7},{4,0},{5,1},{6,2},{7,3},{8,12},{9,13},{10,... | collective-permute-start | bytes 258056 | tf_op jit(solution)/shard_map/ppermute | solution.py:824
  7.4 4.4 %collective-permute-done.far = bf16[48,896]{1,0:T(8,128)(2,1)S(1)} collective-permute-done((bf16[48,896]{1,0:T(8,128)(2,1)}, bf16[48,896]{1,0:T(8,128)(2,1)S(1)}, u32[]{:S(2)}, u32[]{:S(2)}) %collective-permute-start) | collective-permute-done | bytes 86048 | tf_op jit(solution)/shard_map/ppermute | solution.py:824
  14.3 3.5 all-to-all-start
  18.0 2.9 collective-permute-start.1
  21.5 3.0 shard_map.573
  24.5 2.6 shard_map.575
  29.9 3.4 collective-permute-start.3
  33.4 4.6 %all-to-all-start.1 = ((bf16[4,2,48,1152]{3,2,1,0:T(8,128)(2,1)}), bf16[4,2,48,1152]{3,2,1,0:T(8,128)(2,1)S(1)}, u32[]{:S(2)}, u32[]{:S(2)}) async-start(bf16[4,2,48,1152]{3,2,1,0:T(8,128)(2,1)} %shard_map.574), calls=%async_computation.1 | async-start | bytes 1769472 | tf_op jit(solution)/shard_map/all_to_all | solution.py:875
  38.8 14.8 %shard_map.576 = (f32[512,384]{1,0:T(8,128)}, bf16[512,384]{1,0:T(8,128)(2,1)}, bf16[512,1152]{1,0:T(8,128)(2,1)}, f32[512,128]{1,0:T(8,128)}, bf16[512,384]{1,0...) custom-call(s32[3]{0:T(128)} %pad_add_fusion.core.sides, ...), custom_call_target="tpu_custom_call" | custom-call | flops 17250000896 | tf_op jit(solution)/shard_map/pallas_call | solution.py:806
  55.6 4.1 %all-to-all-start.2 = ((bf16[4,2,256,384]{3,2,1,0:T(8,128)(2,1)}), bf16[4,2,256,384]{3,2,1,0:T(8,128)(2,1)S(1)}, u32[]{:S(2)}, u32[]{:S(2)}) async-start(bf16[4,2,256,384]{3,2,1,0:T(8,128)(2,1)} %bitcast.100), calls=%async_computation.2 | async-start | bytes 3145728 | tf_op jit(solution)/shard_map/all_to_all | solution.py:875
  61.3 9.9 %collective-permute-done.4.refs_1_ = bf16[192,1152]{1,0:T(8,128)(2,1)S(1)} collective-permute-done((bf16[192,1152]{1,0:T(8,128)(2,1)S(1)}, bf16[192,1152]{1,0:T(8,128)(2,1)S(1)}, u32[]{:S(2)}, u32[]{:S(2)}) %collective-permute-start.4) | collective-permute-done | bytes 442400 | tf_op jit(solution)/shard_map/ppermute | solution.py:824
  71.3 5.0 %shard_map.577 = (bf16[2,384,768]{2,1,0:T(8,128)(2,1)}, bf16[768,384]{1,0:T(8,128)(2,1)}, f32[16,128]{1,0:T(8,128)}) custom-call(f32[5,48]{1,0:T(8,128)} %refs_0_.5, f32[48,1152]{1,0:T(8,128)} %refs_1_.5, f32[48,384]{1,0:T(8,128)} %refs_2_.5, f32[9,48]{1,0:T(8,128)} %bitcast.186, f32[48,3072]{1,0:T(8,128)} %refs_4_.5, f32[192,384]{1,0:T(8,128)} %refs_5_.5, ...), custom_call_target="tpu_custom_call" | custom-call | flops 5750000128 | tf_op jit(solution)/shard_map/pallas_call | solution.py:1182
  79.3 2.9 shard_map.578
  83.4 9.6 %shard_map.579 = s16[4,2,272,384]{3,2,1,0:T(8,128)(2,1)} custom-call(s32[3]{0:T(128)} %pad_add_fusion.core.sides, bf16[4,2,256,384]{3,2,1,0:T(8,128)(2,1)} %copy-done.1, bf16[2,384,768]{2,1,0:T(8,128)(2,1)} %get-tuple-element.148.gate_up, bf16[768,384]{1,0:T(8,128)(2,1)} %get-tuple-element.149.down, bf16[2,384,768]{2,1,0:T(8,128)(2,1)} %get-tuple-element.152.gate_up_far, ...), custom_call_target="tpu_custom_call" | custom-call | flops 11500000256 | tf_op jit(solution)/shard_map/pallas_call | solution.py:1301
  93.0 5.3 %collective-permute-done.7 = bf16[4,2,48,1152]{3,2,1,0:T(8,128)(2,1)} collective-permute-done((bf16[4,2,48,1152]{3,2,1,0:T(8,128)(2,1)S(1)}, bf16[4,2,48,1152]{3,2,1,0:T(8,128)(2,1)}, u32[]{:S(2)}, u32[]{:S(2)}) %collective-permute-start.7) | collective-permute-done | bytes 884768 | tf_op jit(solution)/shard_map/ppermute | solution.py:824
  98.3 3.9 %all-to-all-start.3 = ((s16[4,2,272,384]{3,2,1,0:T(8,128)(2,1)}), s16[4,2,272,384]{3,2,1,0:T(8,128)(2,1)S(1)}, u32[]{:S(2)}, u32[]{:S(2)}) async-start(s16[4,2,272,384]{3,2,1,0:T(8,128)(2,1)} %shard_map.579), calls=%async_computation.3 | async-start | bytes 3342336 | tf_op jit(solution)/shard_map/all_to_all | solution.py:875
  107.2 4.3 %shard_map.580 = (bf16[384,3072]{1,0:T(8,128)(2,1)}, bf16[1536,384]{1,0:T(8,128)(2,1)}) custom-call(s32[3]{0:T(128)} %pad_add_fusion.core.sides, bf16[384,1152]{1,0:T(8,128)(2,1)} %bitcast.104, bf16[384,1152]{1,0:T(8,128)(2,1)} %bitcast.13.refs_1_, bf16[384,1152]{1,0:T(8,128)(2,1)} %bitcast.14.refs_2_, bf16[384,1152]{1,0:T(8,128)(2,1)} %bitcast.15.refs_3_), custom_call_target="tpu_custom_call" | custom-call | flops 4944999936 | tf_op jit(solution)/shard_map/pallas_call | solution.py:806
  111.6 5.7 %shard_map.581.shared = f32[512,384]{1,0:T(8,128)} custom-call(bf16[512,384]{1,0:T(8,128)(2,1)} %get-tuple-element.157.second, bf16[384,3072]{1,0:T(8,128)(2,1)} %get-tuple-element.159.gate_w.lift_w, bf16[384,3072]{1,0:T(8,128)(2,1)} %get-tuple-element.159.gate_w.lift_w, bf16[1536,384]{1,0:T(8,128)(2,1)} %get-tuple-element.160.down_w), custom_call_target="tpu_custom_call" | custom-call | flops 6670000128 | tf_op jit(solution)/shard_map/pallas_call | solution.py:1352
  117.3 4.9 %all-to-all-done.3 = s16[4,2,272,384]{3,2,1,0:T(8,128)(2,1)S(1)} async-done(((s16[4,2,272,384]{3,2,1,0:T(8,128)(2,1)}), s16[4,2,272,384]{3,2,1,0:T(8,128)(2,1)S(1)}, u32[]{:S(2)}, u32[]{:S(2)}) %all-to-all-start.3) | async-done | bytes 1671200 | tf_op jit(solution)/shard_map/all_to_all | solution.py:875
  123.4 11.4 %shard_map.582 = (f32[512,384]{1,0:T(8,128)}, bf16[512,384]{1,0:T(8,128)(2,1)}, bf16[2048,384]{1,0:T(8,128)(2,1)}, bf16[512,128]{1,0:T(8,128)(2,1)}, f32[384,128...) custom-call(s16[8,272,384]{2,1,0:T(8,128)(2,1)} %bitcast.98, f32[512,128]{1,0:T(8,128)} %get-tuple-element.140.known, ...), custom_call_target="tpu_custom_call" | custom-call | flops 13109999616 | tf_op jit(solution)/shard_map/pallas_call | solution.py:806
  134.8 3.7 %all-to-all-start.4 = ((bf16[4,2,256,384]{3,2,1,0:T(8,128)(2,1)}), bf16[4,2,256,384]{3,2,1,0:T(8,128)(2,1)S(1)}, u32[]{:S(2)}, u32[]{:S(2)}) async-start(bf16[4,2,256,384]{3,2,1,0:T(8,128)(2,1)} %bitcast.101), calls=%async_computation.4 | async-start | bytes 3145728 | tf_op jit(solution)/shard_map/all_to_all | solution.py:875
  138.5 14.4 %shard_map.583 = (f32[512,384]{1,0:T(8,128)}, f32[2,384,768]{2,1,0:T(8,128)}, f32[2,384,384]{2,1,0:T(8,128)}, f32[2,384,384]{2,1,0:T(8,128)}, f32[2,384,384]{2,1,0:T(8,128)}, /*index=5*/f32[2,384,384]{2,1,0:T(8,128)}) custom-call(s32[3]{0:T(128)} %pad_add_fusion.core.sides, bf16[512,384]{1,0:T(8,128)(2,1)} %get-tuple-element.157.second, ...), custom_call_target="tpu_custom_call" | custom-call | flops 16099999744 | tf_op jit(solution)/shard_map/pallas_call | solution.py:1410
  153.5 2.5 collective-permute-done.12.in_even
  160.4 5.3 %shard_map.584 = (f32[384,1152]{1,0:T(8,128)}, s16[384,1280]{1,0:T(8,128)(2,1)}) custom-call(f32[2,384,768]{2,1,0:T(8,128)} %get-tuple-element.170.in_keep, f32[2,384,384]{2,1,0:T(8,128)} %copy-done.21, f32[2,384,384]{2,1,0:T(8,128)} %copy-done.23, f32[2,384,384]{2,1,0:T(8,128)} %get-tuple-element.173.out_keep, f32[2,384,384]{2,1,0:T(8,128)} %copy-done.24), custom_call_target="tpu_custom_call" | custom-call | flops 6095000064 | tf_op jit(solution)/shard_map/pallas_call | solution.py:1446
  168.4 19.5 %shard_map.585 = (bf16[4,2,256,384]{3,2,1,0:T(8,128)(2,1)}, f32[2,384,768]{2,1,0:T(8,128)}, f32[2,384,768]{2,1,0:T(8,128)}, f32[2,384,384]{2,1,0:T(8,128)}, f32[2,384,384]{2,1,0:T(8,128)}) custom-call(s32[3]{0:T(128)} %pad_add_fusion.core.sides, bf16[4,2,256,384]{3,2,1,0:T(8,128)(2,1)} %copy-done.1, bf16[4,2,256,384]{3,2,1,0:T(8,128)(2,1)} %copy-done.2, ...), custom_call_target="tpu_custom_call" | custom-call | flops 22424999936 | tf_op jit(solution)/shard_map/pallas_call | solution.py:1464
  190.7 4.3 %all-to-all-start.5 = ((bf16[4,2,256,384]{3,2,1,0:T(8,128)(2,1)}), bf16[4,2,256,384]{3,2,1,0:T(8,128)(2,1)S(1)}, u32[]{:S(2)}, u32[]{:S(2)}) async-start(bf16[4,2,256,384]{3,2,1,0:T(8,128)(2,1)} %get-tuple-element.185), calls=%async_computation.5 | async-start | bytes 3145728 | tf_op jit(solution)/shard_map/all_to_all | solution.py:875
  196.5 2.1 collective-permute-done.11
  200.1 4.6 %shard_map.586 = (f32[2,192,1152]{2,1,0:T(8,128)}, s16[2,192,1280]{2,1,0:T(8,128)(2,1)}) custom-call(s32[3]{0:T(128)} %pad_add_fusion.core.sides, f32[2,384,768]{2,1,0:T(8,128)} %get-tuple-element.177.in_keep, f32[2,384,768]{2,1,0:T(8,128)} %collective-permute-done.15.in_other, f32[2,384,384]{2,1,0:T(8,128)} %get-tuple-element.179.out_keep, ...), custom_call_target="tpu_custom_call" | custom-call | flops 5289999872 | tf_op jit(solution)/shard_map/pallas_call | solution.py:1514
  206.2 4.4 %shard_map.588 = s16[384,1280]{1,0:T(8,128)(2,1)} custom-call(f32[384,1152]{1,0:T(8,128)} %get-tuple-element.186.keep, s16[384,1280]{1,0:T(8,128)(2,1)} %copy-done.25), custom_call_target="tpu_custom_call" | custom-call | flops 5059999744 | tf_op jit(solution)/shard_map/pallas_call | solution.py:1501
  210.6 3.2 all-to-all-done.5
  213.7 7.8 %all-to-all-start.6 = ((s16[8,48,1280]{2,1,0:T(8,128)(2,1)}), s16[8,48,1280]{2,1,0:T(8,128)(2,1)S(1)}, u32[]{:S(2)}, u32[]{:S(2)}) async-start(s16[8,48,1280]{2,1,0:T(8,128)(2,1)} %bitcast.103), calls=%async_computation.6 | async-start | bytes 1966080 | tf_op jit(solution)/shard_map/all_to_all | solution.py:871
  221.5 5.9 %shard_map.589 = (f32[512,384]{1,0:T(8,128)}, bf16[512,384]{1,0:T(8,128)(2,1)}, f32[384,384]{1,0:T(8,128)}, f32[1,384]{1,0:T(1,128)}, f32[384,128]{1,0:T(8,128)}) custom-call(bf16[2048,384]{1,0:T(8,128)(2,1)} %bitcast.99, f32[512,128]{1,0:T(8,128)} %get-tuple-element.140.known, f32[512,384]{1,0:T(8,128)} %get-tuple-element.169.second_slope, ...), custom_call_target="tpu_custom_call" | custom-call | flops 6899999744 | tf_op jit(solution)/shard_map/pallas_call | solution.py:806
  228.0 3.4 shard_map.587
  231.4 5.4 %collective-permute-start.19 = (s16[192,1280]{1,0:T(8,128)(2,1)}, s16[192,1280]{1,0:T(8,128)(2,1)S(1)}, u32[]{:S(2)}, u32[]{:S(2)}) collective-permute-start(s16[192,1280]{1,0:T(8,128)(2,1)} %get-tuple-element.193), channel_id=1, source_target_pairs={{0,4},{1,5},{2,6},{3,7},{4,0},{5,1},{6,2},{7,3},{8,12},{9,13},{10,... | collective-permute-start | bytes 1474568 | tf_op jit(solution)/shard_map/ppermute | solution.py:824
  236.8 18.6 %shard_map.590 = (f32[384,896]{1,0:T(8,128)}, f32[384,896]{1,0:T(8,128)}) custom-call(s32[3]{0:T(128)} %pad_add_fusion.core.sides, bf16[512,384]{1,0:T(8,128)(2,1)} %get-tuple-element.194.mixed_slope, bf16[512,1152]{1,0:T(8,128)(2,1)} %get-tuple-element.195.qkv, f32[512,128]{1,0:T(8,128)} %get-tuple-element.196.log_total, ...), custom_call_target="tpu_custom_call" | custom-call | flops 21159999488 | tf_op jit(solution)/shard_map/pallas_call | solution.py:806
  255.4 11.6 %collective-permute-done.19.code = s16[192,1280]{1,0:T(8,128)(2,1)S(1)} collective-permute-done((s16[192,1280]{1,0:T(8,128)(2,1)}, s16[192,1280]{1,0:T(8,128)(2,1)S(1)}, u32[]{:S(2)}, u32[]{:S(2)}) %collective-permute-start.19) | collective-permute-done | bytes 491552 | tf_op jit(solution)/shard_map/ppermute | solution.py:824
  268.0 2.4 shard_map.592.refs_4_.refs_29_
  271.5 3.3 shard_map.591
  274.8 3.9 %all-to-all-start.7 = ((s16[8,48,1024]{2,1,0:T(8,128)(2,1)}), s16[8,48,1024]{2,1,0:T(8,128)(2,1)S(1)}, u32[]{:S(2)}, u32[]{:S(2)}) async-start(s16[8,48,1024]{2,1,0:T(8,128)(2,1)} %bitcast.105), calls=%async_computation.7 | async-start | bytes 1572864 | tf_op jit(solution)/shard_map/all_to_all | solution.py:871
  278.7 2.5 shard_map.593
  284.7 14.8 %all-to-all-done.7.codes = s16[8,48,1024]{2,1,0:T(8,128)(2,1)S(1)} async-done(((s16[8,48,1024]{2,1,0:T(8,128)(2,1)}), s16[8,48,1024]{2,1,0:T(8,128)(2,1)S(1)}, u32[]{:S(2)}, u32[]{:S(2)}) %all-to-all-start.7) | async-done | bytes 786464 | tf_op jit(solution)/shard_map/all_to_all | solution.py:871
  300.4 2.3 shard_map.594
  304.7 6.9 %collective-permute-done.24 = f32[48,896]{1,0:T(8,128)S(1)} collective-permute-done((f32[48,896]{1,0:T(8,128)}, f32[48,896]{1,0:T(8,128)S(1)}, u32[]{:S(2)}, u32[]{:S(2)}) %collective-permute-start.24) | collective-permute-done | bytes 172064 | tf_op jit(solution)/shard_map/ppermute | solution.py:824
  314.1 2.4 shard_map.595
  325.8 2.7 collective-permute-start.28
  332.5 16.9 %shard_map.596 = (f32[5,48]{1,0:T(8,128)}, f32[48,1152]{1,0:T(8,128)}, f32[48,384]{1,0:T(8,128)}, f32[9,48]{1,0:T(8,128)}, f32[48,3072]{1,0:T(8,128)}, /*index=5...) custom-call(s32[3]{0:T(128)} %pad_add_fusion.core.sides, ...), custom_call_target="tpu_custom_call" | custom-call | flops 19549999104 | tf_op jit(solution)/shard_map/pallas_call | solution.py:1651
  358.2 2.6 collective-permute-start.38
  364.1 6.7 %shard_map.597 = (f32[5,48]{1,0:T(8,128)}, f32[48,1152]{1,0:T(8,128)}, f32[48,384]{1,0:T(8,128)}, f32[9,48]{1,0:T(8,128)}, f32[48,3072]{1,0:T(8,128)}, /*index=5...) custom-call(f32[9,128]{1,0:T(8,128)} %get-tuple-element.285.totals, ...), custom_call_target="tpu_custom_call" | custom-call | flops 8049999872 | tf_op jit(solution)/shard_map/pallas_call | solution.py:1667
  (207 shorter events, 74.8 us)
Async XLA Ops:
  3.2 8.6 %collective-permute-start = (bf16[48,896]{1,0:T(8,128)(2,1)}, bf16[48,896]{1,0:T(8,128)(2,1)S(1)}, u32[]{:S(2)}, u32[]{:S(2)}) collective-permute-start(bf16[48,896]{1,0:T(8,128)(2,1)} %bitcast.181), channel_id=1, source_target_pairs={{0,4},{1,5},{2,6},{3,7},{4,0},{5,1},{6,2},{7,3},{8,12},{9,13},{10,... | collective-permute-start | bytes 258056 | tf_op jit(solution)/shard_map/ppermute | solution.py:824
  14.3 15.6 %all-to-all-start = ((bf16[4,2,48,896]{3,2,1,0:T(8,128)(2,1)}), bf16[4,2,48,896]{3,2,1,0:T(8,128)(2,1)S(1)}, u32[]{:S(2)}, u32[]{:S(2)}) async-start(bf16[4,2,48,896]{3,2,1,0:T(8,128)(2,1)} %shard_map.572), calls=%async_computation | async-start | bytes 1376256 | tf_op jit(solution)/shard_map/all_to_all | solution.py:875
  18.0 9.4 %collective-permute-start.1 = (bf16[48,1152]{1,0:T(8,128)(2,1)S(1)}, bf16[48,1152]{1,0:T(8,128)(2,1)S(1)}, u32[]{:S(2)}, u32[]{:S(2)}) collective-permute-start(bf16[48,1152]{1,0:T(8,128)(2,1)S(1)} %fusion.own), channel_id=1, source_target_pairs={{0,4},{1,5},{2,6},{3,7},{4,0},{5,1},{6,2},{7,3},{8,12},{9,13},{10,... | collective-permute-start | bytes 331784 | tf_op jit(solution)/shard_map/ppermute | solution.py:824
  29.9 8.1 %collective-permute-start.2 = (bf16[384,896]{1,0:T(8,128)(2,1)S(1)}, bf16[384,896]{1,0:T(8,128)(2,1)S(1)}, u32[]{:S(2)}, u32[]{:S(2)}) collective-permute-start(bf16[384,896]{1,0:T(8,128)(2,1)S(1)} %bitcast.106), channel_id=1, source_target_pairs={{0,8},{8,0},{16,24},{24,16},{1,9},{9,1},{17,25},{25,17},{2,10},{10... | collective-permute-start | bytes 2064392 | tf_op jit(solution)/shard_map/ppermute | solution.py:824
  29.9 24.0 %collective-permute-start.3 = (bf16[192,1152]{1,0:T(8,128)(2,1)}, bf16[192,1152]{1,0:T(8,128)(2,1)S(1)}, u32[]{:S(2)}, u32[]{:S(2)}) collective-permute-start(bf16[192,1152]{1,0:T(8,128)(2,1)} %shard_map.575), channel_id=1, source_target_pairs={{0,4},{1,5},{2,6},{3,7},{4,0},{5,1},{6,2},{7,3},{8,12},{9,13},{10,... | collective-permute-start | bytes 1327112 | tf_op jit(solution)/shard_map/ppermute | solution.py:824
  33.4 22.3 %all-to-all-start.1 = ((bf16[4,2,48,1152]{3,2,1,0:T(8,128)(2,1)}), bf16[4,2,48,1152]{3,2,1,0:T(8,128)(2,1)S(1)}, u32[]{:S(2)}, u32[]{:S(2)}) async-start(bf16[4,2,48,1152]{3,2,1,0:T(8,128)(2,1)} %shard_map.574), calls=%async_computation.1 | async-start | bytes 1769472 | tf_op jit(solution)/shard_map/all_to_all | solution.py:875
  55.6 46.6 %copy-start.5 = (bf16[4,2,48,1152]{3,2,1,0:T(8,128)(2,1)}, bf16[4,2,48,1152]{3,2,1,0:T(8,128)(2,1)S(1)}, u32[]{:S(2)}) copy-start(bf16[4,2,48,1152]{3,2,1,0:T(8,128)(2,1)S(1)} %all-to-all-done.1) | copy-start | bytes 2654212
  55.6 26.7 %all-to-all-start.2 = ((bf16[4,2,256,384]{3,2,1,0:T(8,128)(2,1)}), bf16[4,2,256,384]{3,2,1,0:T(8,128)(2,1)S(1)}, u32[]{:S(2)}, u32[]{:S(2)}) async-start(bf16[4,2,256,384]{3,2,1,0:T(8,128)(2,1)} %bitcast.100), calls=%async_computation.2 | async-start | bytes 3145728 | tf_op jit(solution)/shard_map/all_to_all | solution.py:875
  59.8 11.5 %collective-permute-start.4 = (bf16[192,1152]{1,0:T(8,128)(2,1)S(1)}, bf16[192,1152]{1,0:T(8,128)(2,1)S(1)}, u32[]{:S(2)}, u32[]{:S(2)}) collective-permute-start(bf16[192,1152]{1,0:T(8,128)(2,1)S(1)} %collective-permute-done.3.refs_0_), channel_id=1, source_target_pairs={{0,16},{8,24},{16,0},{24,8},{1,17},{9,25},{17,1},{25,9},{2,18},{10... | collective-permute-start | bytes 1327112 | tf_op jit(solution)/shard_map/ppermute | solution.py:824
  61.3 16.5 %collective-permute-start.5 = (bf16[192,1152]{1,0:T(8,128)(2,1)S(1)}, bf16[192,1152]{1,0:T(8,128)(2,1)S(1)}, u32[]{:S(2)}, u32[]{:S(2)}) collective-permute-start(bf16[192,1152]{1,0:T(8,128)(2,1)S(1)} %collective-permute-done.3.refs_0_), channel_id=1, source_target_pairs={{0,8},{8,0},{16,24},{24,16},{1,9},{9,1},{17,25},{25,17},{2,10},{10... | collective-permute-start | bytes 1327112 | tf_op jit(solution)/shard_map/ppermute | solution.py:824
  71.3 6.5 %collective-permute-start.6 = (bf16[192,1152]{1,0:T(8,128)(2,1)S(1)}, bf16[192,1152]{1,0:T(8,128)(2,1)S(1)}, u32[]{:S(2)}, u32[]{:S(2)}) collective-permute-start(bf16[192,1152]{1,0:T(8,128)(2,1)S(1)} %collective-permute-done.4.refs_1_), channel_id=1, source_target_pairs={{0,8},{8,0},{16,24},{24,16},{1,9},{9,1},{17,25},{25,17},{2,10},{10... | collective-permute-start | bytes 1327112 | tf_op jit(solution)/shard_map/ppermute | solution.py:824
  76.2 22.1 %collective-permute-start.7 = (bf16[4,2,48,1152]{3,2,1,0:T(8,128)(2,1)S(1)}, bf16[4,2,48,1152]{3,2,1,0:T(8,128)(2,1)}, u32[]{:S(2)}, u32[]{:S(2)}) collective-permute-start(bf16[4,2,48,1152]{3,2,1,0:T(8,128)(2,1)S(1)} %all-to-all-done.1), channel_id=1, source_target_pairs={{0,16},{8,24},{16,0},{24,8},{1,17},{9,25},{17,1},{25,9},{2,18},{10... | collective-permute-start | bytes 2654216 | tf_op jit(solution)/shard_map/ppermute | solution.py:824
  98.3 23.9 %all-to-all-start.3 = ((s16[4,2,272,384]{3,2,1,0:T(8,128)(2,1)}), s16[4,2,272,384]{3,2,1,0:T(8,128)(2,1)S(1)}, u32[]{:S(2)}, u32[]{:S(2)}) async-start(s16[4,2,272,384]{3,2,1,0:T(8,128)(2,1)} %shard_map.579), calls=%async_computation.3 | async-start | bytes 3342336 | tf_op jit(solution)/shard_map/all_to_all | solution.py:875
  102.2 5.0 %collective-permute-start.9 = (bf16[4,2,48,1152]{3,2,1,0:T(8,128)(2,1)}, bf16[4,2,48,1152]{3,2,1,0:T(8,128)(2,1)}, u32[]{:S(2)}, u32[]{:S(2)}) collective-permute-start(bf16[4,2,48,1152]{3,2,1,0:T(8,128)(2,1)} %collective-permute-done.7), channel_id=1, source_target_pairs={{0,8},{8,0},{16,24},{24,16},{1,9},{9,1},{17,25},{25,17},{2,10},{10... | collective-permute-start | bytes 2654216 | tf_op jit(solution)/shard_map/ppermute | solution.py:824
  102.2 5.0 %collective-permute-start.8 = (bf16[4,2,48,1152]{3,2,1,0:T(8,128)(2,1)S(1)}, bf16[4,2,48,1152]{3,2,1,0:T(8,128)(2,1)}, u32[]{:S(2)}, u32[]{:S(2)}) collective-permute-start(bf16[4,2,48,1152]{3,2,1,0:T(8,128)(2,1)S(1)} %all-to-all-done.1), channel_id=1, source_target_pairs={{0,8},{8,0},{16,24},{24,16},{1,9},{9,1},{17,25},{25,17},{2,10},{10... | collective-permute-start | bytes 2654216 | tf_op jit(solution)/shard_map/ppermute | solution.py:824
  103.1 3.6 collective-permute-start.10
  134.8 32.4 %all-to-all-start.4 = ((bf16[4,2,256,384]{3,2,1,0:T(8,128)(2,1)}), bf16[4,2,256,384]{3,2,1,0:T(8,128)(2,1)S(1)}, u32[]{:S(2)}, u32[]{:S(2)}) async-start(bf16[4,2,256,384]{3,2,1,0:T(8,128)(2,1)} %bitcast.101), calls=%async_computation.4 | async-start | bytes 3145728 | tf_op jit(solution)/shard_map/all_to_all | solution.py:875
  152.9 3.1 collective-permute-start.12
  152.9 4.7 %collective-permute-start.13 = (f32[2,384,384]{2,1,0:T(8,128)}, f32[2,384,384]{2,1,0:T(8,128)S(1)}, u32[]{:S(2)}, u32[]{:S(2)}) collective-permute-start(f32[2,384,384]{2,1,0:T(8,128)} %get-tuple-element.172), channel_id=1, source_target_pairs={{0,8},{8,0},{16,24},{24,16},{1,9},{9,1},{17,25},{25,17},{2,10},{10... | collective-permute-start | bytes 3538952 | tf_op jit(solution)/shard_map/ppermute | solution.py:824
  153.4 5.9 %collective-permute-start.14 = (f32[2,384,384]{2,1,0:T(8,128)}, f32[2,384,384]{2,1,0:T(8,128)S(1)}, u32[]{:S(2)}, u32[]{:S(2)}) collective-permute-start(f32[2,384,384]{2,1,0:T(8,128)} %get-tuple-element.174), channel_id=1, source_target_pairs={{0,8},{8,0},{16,24},{24,16},{1,9},{9,1},{17,25},{25,17},{2,10},{10... | collective-permute-start | bytes 3538952 | tf_op jit(solution)/shard_map/ppermute | solution.py:824
  165.7 24.0 %collective-permute-start.18 = (s16[384,1280]{1,0:T(8,128)(2,1)}, s16[384,1280]{1,0:T(8,128)(2,1)S(1)}, u32[]{:S(2)}, u32[]{:S(2)}) collective-permute-start(s16[384,1280]{1,0:T(8,128)(2,1)} %get-tuple-element.175), channel_id=1, source_target_pairs={{0,16},{8,24},{16,0},{24,8},{1,17},{9,25},{17,1},{25,9},{2,18},{10... | collective-permute-start | bytes 2949128 | tf_op jit(solution)/shard_map/ppermute | solution.py:824
  187.9 11.2 %collective-permute-start.15 = (f32[2,384,768]{2,1,0:T(8,128)}, f32[2,384,768]{2,1,0:T(8,128)}, u32[]{:S(2)}, u32[]{:S(2)}) collective-permute-start(f32[2,384,768]{2,1,0:T(8,128)} %get-tuple-element.178), channel_id=1, source_target_pairs={{0,8},{8,0},{16,24},{24,16},{1,9},{9,1},{17,25},{25,17},{2,10},{10... | collective-permute-start | bytes 7077896 | tf_op jit(solution)/shard_map/ppermute | solution.py:824
  190.7 23.0 %all-to-all-start.5 = ((bf16[4,2,256,384]{3,2,1,0:T(8,128)(2,1)}), bf16[4,2,256,384]{3,2,1,0:T(8,128)(2,1)S(1)}, u32[]{:S(2)}, u32[]{:S(2)}) async-start(bf16[4,2,256,384]{3,2,1,0:T(8,128)(2,1)} %get-tuple-element.185), calls=%async_computation.5 | async-start | bytes 3145728 | tf_op jit(solution)/shard_map/all_to_all | solution.py:875
  195.0 4.1 %collective-permute-start.16 = (f32[2,384,384]{2,1,0:T(8,128)S(1)}, f32[2,384,384]{2,1,0:T(8,128)S(1)}, u32[]{:S(2)}, u32[]{:S(2)}) collective-permute-start(f32[2,384,384]{2,1,0:T(8,128)S(1)} %copy-done.20), channel_id=1, source_target_pairs={{0,8},{8,0},{16,24},{24,16},{1,9},{9,1},{17,25},{25,17},{2,10},{10... | collective-permute-start | bytes 3538952 | tf_op jit(solution)/shard_map/ppermute | solution.py:824
  195.0 3.6 collective-permute-start.11
  204.7 23.3 %collective-permute-start.17 = (s16[2,192,1280]{2,1,0:T(8,128)(2,1)}, s16[2,192,1280]{2,1,0:T(8,128)(2,1)}, u32[]{:S(2)}, u32[]{:S(2)}) collective-permute-start(s16[2,192,1280]{2,1,0:T(8,128)(2,1)} %get-tuple-element.182), channel_id=1, source_target_pairs={{0,16},{8,24},{16,0},{24,8},{1,17},{9,25},{17,1},{25,9},{2,18},{10... | collective-permute-start | bytes 2949128 | tf_op jit(solution)/shard_map/ppermute | solution.py:824
  213.7 53.3 %all-to-all-start.6 = ((s16[8,48,1280]{2,1,0:T(8,128)(2,1)}), s16[8,48,1280]{2,1,0:T(8,128)(2,1)S(1)}, u32[]{:S(2)}, u32[]{:S(2)}) async-start(s16[8,48,1280]{2,1,0:T(8,128)(2,1)} %bitcast.103), calls=%async_computation.6 | async-start | bytes 1966080 | tf_op jit(solution)/shard_map/all_to_all | solution.py:871
  231.4 35.6 %collective-permute-start.19 = (s16[192,1280]{1,0:T(8,128)(2,1)}, s16[192,1280]{1,0:T(8,128)(2,1)S(1)}, u32[]{:S(2)}, u32[]{:S(2)}) collective-permute-start(s16[192,1280]{1,0:T(8,128)(2,1)} %get-tuple-element.193), channel_id=1, source_target_pairs={{0,4},{1,5},{2,6},{3,7},{4,0},{5,1},{6,2},{7,3},{8,12},{9,13},{10,... | collective-permute-start | bytes 1474568 | tf_op jit(solution)/shard_map/ppermute | solution.py:824
  267.0 3.5 collective-permute-start.20
  274.8 24.7 %all-to-all-start.7 = ((s16[8,48,1024]{2,1,0:T(8,128)(2,1)}), s16[8,48,1024]{2,1,0:T(8,128)(2,1)S(1)}, u32[]{:S(2)}, u32[]{:S(2)}) async-start(s16[8,48,1024]{2,1,0:T(8,128)(2,1)} %bitcast.105), calls=%async_computation.7 | async-start | bytes 1572864 | tf_op jit(solution)/shard_map/all_to_all | solution.py:871
  281.2 23.0 %collective-permute-start.21 = (f32[192,768]{1,0:T(8,128)}, f32[192,768]{1,0:T(8,128)S(1)}, u32[]{:S(2)}, u32[]{:S(2)}) collective-permute-start(f32[192,768]{1,0:T(8,128)} %get-tuple-element.210.refs_0_.refs_33_), channel_id=1, source_target_pairs={{0,16},{8,24},{16,0},{24,8},{1,17},{9,25},{17,1},{25,9},{2,18},{10... | collective-permute-start | bytes 1769480 | tf_op jit(solution)/shard_map/ppermute | solution.py:824
  282.7 22.0 %collective-permute-start.23 = (f32[48,1152]{1,0:T(8,128)S(1)}, f32[48,1152]{1,0:T(8,128)S(1)}, u32[]{:S(2)}, u32[]{:S(2)}) collective-permute-start(f32[48,1152]{1,0:T(8,128)S(1)} %copy-done.40), channel_id=1, source_target_pairs={{0,16},{8,24},{16,0},{24,8},{1,17},{9,25},{17,1},{25,9},{2,18},{10... | collective-permute-start | bytes 663560 | tf_op jit(solution)/shard_map/ppermute | solution.py:824
  283.2 30.1 %collective-permute-start.22 = (f32[192,384]{1,0:T(8,128)}, f32[192,384]{1,0:T(8,128)S(1)}, u32[]{:S(2)}, u32[]{:S(2)}) collective-permute-start(f32[192,384]{1,0:T(8,128)} %get-tuple-element.211.refs_2_.refs_37_), channel_id=1, source_target_pairs={{0,16},{8,24},{16,0},{24,8},{1,17},{9,25},{17,1},{25,9},{2,18},{10... | collective-permute-start | bytes 884744 | tf_op jit(solution)/shard_map/ppermute | solution.py:824
  302.6 9.0 %collective-permute-start.24 = (f32[48,896]{1,0:T(8,128)}, f32[48,896]{1,0:T(8,128)S(1)}, u32[]{:S(2)}, u32[]{:S(2)}) collective-permute-start(f32[48,896]{1,0:T(8,128)} %shard_map.594), channel_id=1, source_target_pairs={{0,16},{8,24},{16,0},{24,8},{1,17},{9,25},{17,1},{25,9},{2,18},{10... | collective-permute-start | bytes 516104 | tf_op jit(solution)/shard_map/ppermute | solution.py:824
  304.1 26.8 %collective-permute-start.32 = (f32[192,768]{1,0:T(8,128)S(1)}, f32[192,768]{1,0:T(8,128)S(1)}, u32[]{:S(2)}, u32[]{:S(2)}) collective-permute-start(f32[192,768]{1,0:T(8,128)S(1)} %copy-done.27), channel_id=1, source_target_pairs={{0,8},{8,0},{16,24},{24,16},{1,9},{9,1},{17,25},{25,17},{2,10},{10... | collective-permute-start | bytes 1769480 | tf_op jit(solution)/shard_map/ppermute | solution.py:824
  304.2 26.8 %collective-permute-start.33 = (f32[192,768]{1,0:T(8,128)S(1)}, f32[192,768]{1,0:T(8,128)S(1)}, u32[]{:S(2)}, u32[]{:S(2)}) collective-permute-start(f32[192,768]{1,0:T(8,128)S(1)} %collective-permute-done.21.refs_1_.refs_34_), channel_id=1, source_target_pairs={{0,8},{8,0},{16,24},{24,16},{1,9},{9,1},{17,25},{25,17},{2,10},{10... | collective-permute-start | bytes 1769480 | tf_op jit(solution)/shard_map/ppermute | solution.py:824
  304.7 19.3 %collective-permute-start.30 = (f32[48,1152]{1,0:T(8,128)S(1)}, f32[48,1152]{1,0:T(8,128)S(1)}, u32[]{:S(2)}, u32[]{:S(2)}) collective-permute-start(f32[48,1152]{1,0:T(8,128)S(1)} %copy-done.40), channel_id=1, source_target_pairs={{0,8},{8,0},{16,24},{24,16},{1,9},{9,1},{17,25},{25,17},{2,10},{10... | collective-permute-start | bytes 663560 | tf_op jit(solution)/shard_map/ppermute | solution.py:824
  311.7 14.1 %collective-permute-start.31 = (f32[48,1152]{1,0:T(8,128)S(1)}, f32[48,1152]{1,0:T(8,128)S(1)}, u32[]{:S(2)}, u32[]{:S(2)}) collective-permute-start(f32[48,1152]{1,0:T(8,128)S(1)} %collective-permute-done.23.refs_5_.refs_30_), channel_id=1, source_target_pairs={{0,8},{8,0},{16,24},{24,16},{1,9},{9,1},{17,25},{25,17},{2,10},{10... | collective-permute-start | bytes 663560 | tf_op jit(solution)/shard_map/ppermute | solution.py:824
  316.4 1.5 collective-permute-start.25
  318.7 3.6 collective-permute-start.26
  322.2 3.6 collective-permute-start.27
  323.9 7.0 %collective-permute-start.34 = (f32[192,384]{1,0:T(8,128)S(1)}, f32[192,384]{1,0:T(8,128)S(1)}, u32[]{:S(2)}, u32[]{:S(2)}) collective-permute-start(f32[192,384]{1,0:T(8,128)S(1)} %copy-done.36), channel_id=1, source_target_pairs={{0,8},{8,0},{16,24},{24,16},{1,9},{9,1},{17,25},{25,17},{2,10},{10... | collective-permute-start | bytes 884744 | tf_op jit(solution)/shard_map/ppermute | solution.py:824
  325.8 5.1 %collective-permute-start.35 = (f32[192,384]{1,0:T(8,128)}, f32[192,384]{1,0:T(8,128)S(1)}, u32[]{:S(2)}, u32[]{:S(2)}) collective-permute-start(f32[192,384]{1,0:T(8,128)} %copy-done.37), channel_id=1, source_target_pairs={{0,8},{8,0},{16,24},{24,16},{1,9},{9,1},{17,25},{25,17},{2,10},{10... | collective-permute-start | bytes 884744 | tf_op jit(solution)/shard_map/ppermute | solution.py:824
  325.8 4.5 %collective-permute-start.28 = (f32[2,128]{1,0:T(2,128)S(1)}, f32[2,128]{1,0:T(2,128)S(1)}, u32[]{:S(2)}, u32[]{:S(2)}) collective-permute-start(f32[2,128]{1,0:T(2,128)S(1)} %add.57), channel_id=1, source_target_pairs={{0,4},{1,5},{2,6},{3,7},{4,0},{5,1},{6,2},{7,3},{8,12},{9,13},{10,... | collective-permute-start | bytes 3080 | tf_op jit(solution)/shard_map/ppermute | solution.py:824
  330.4 1.4 collective-permute-start.29
  350.1 3.7 collective-permute-start.36
  354.5 3.7 collective-permute-start.37
  358.2 4.6 %collective-permute-start.38 = (f32[18,128]{1,0:T(8,128)S(1)}, f32[18,128]{1,0:T(8,128)S(1)}, u32[]{:S(2)}, u32[]{:S(2)}) collective-permute-start(f32[18,128]{1,0:T(8,128)S(1)} %add.60), channel_id=1, source_target_pairs={{0,4},{1,5},{2,6},{3,7},{4,0},{5,1},{6,2},{7,3},{8,12},{9,13},{10,... | collective-permute-start | bytes 27656 | tf_op jit(solution)/shard_map/ppermute | solution.py:824
  (47 other events, 264.7 us)

commit v5 on v4

--- a/solution.py
+++ b/solution.py
@@ -463,19 +463,13 @@
     lift = mm_tn(second[...], lift_slope)
     in_keep[0] = jnp.where(low, gate, lift)
     given = jnp.where(low, lift, gate)
-    even = pl.program_id(0) % 2 == 0
-
-    @pl.when(even)
-    def _():
-        in_give_even[0] = given
-
-    @pl.when(jnp.logical_not(even))
-    def _():
-        in_give_odd[0] = given
-
+    half = given.shape[1] // 2
+    in_give_even[0] = given[:, :half]
+    in_give_odd[0] = given[:, half:]
     out_ref[...] = mm_tn(hidden, slope[...])
-    quarter = out_keep.shape[1] // 2
-    for shard in range(2):
+    quarter = D // EXPERTS
+    shards = out_keep.shape[1] // quarter
+    for shard in range(shards):
         for side in range(2):
             for ref, half in ((out_keep, core), (out_give, 1 - core)):
                 piece = half * 2 + jnp.bitwise_xor(cross, side)
@@ -559,11 +553,10 @@
     encode(far, [mine + theirs for mine, theirs in zip(tiles_of(keep[1]), decode(codes.at[1]))])
 
 
-def expert_total_kernel(own, code, in_total, out_total):
-    split = in_total.shape[1] // 128
-    for index, tile in enumerate(decode(code)):
-        ref, at = (in_total, index) if index < split else (out_total, index - split)
-        ref[:, at * 128 : (at + 1) * 128] = own[:, index * 128 : (index + 1) * 128] + tile
+def expert_total_kernel(own, code, total):
+    encode(
+        total, [mine + theirs for mine, theirs in zip(tiles_of(own[...]), decode(code))]
+    )
 
 
 def last_code_kernel(core, keep, other, code):
@@ -836,6 +829,25 @@
     return value
 
 
+def expert_parts(value):
+    if lax.axis_size("expert") != 8:
+        return [sum_small(value, ("expert",))]
+    value = value + flip(value, "expert", 1)
+    return [value] + [flip(value, "expert", bit) for bit in (2, 4, 6)]
+
+
+def ordered_sum(parts, me):
+    values = [part[...] for part in parts]
+    total = None
+    for index in range(len(values)):
+        at = jnp.bitwise_xor(index, me)
+        part = values[0]
+        for other in range(1, len(values)):
+            part = jnp.where(at == other, values[other], part)
+        total = part if total is None else total + part
+    return total
+
+
 def halves(value, axis, take_high):
     size = value.shape[axis] // 2
     side = take_high.astype(jnp.int32)
@@ -909,9 +921,9 @@
 def squares_kernel(weights, sums, *refs):
     total = jnp.zeros((1, 1), F32)
     for weight, ref in zip(weights, refs[:-1]):
-        piece = ref[...]
-        part = jnp.sum(jnp.sum(piece * piece, -1, keepdims=True), 0, keepdims=True)
-        total = total + part * weight
+        for piece in decode(ref) if ref.dtype == jnp.int16 else [ref[...]]:
+            part = jnp.sum(jnp.sum(piece * piece, -1, keepdims=True), 0, keepdims=True)
+            total = total + part * weight
     refs[-1][0:1, :] = jnp.broadcast_to(total, (1, 128))
     refs[-1][1:2, :] = sums[...]
 
@@ -980,12 +992,15 @@
     return value
 
 
-def moments_kernel(fast, count, small_end, sides, square_ref, *refs):
+def moments_kernel(fast, count, part_count, small_end, sides, *refs):
+    square_parts, refs = refs[:part_count], refs[part_count:]
     masters, means, squares = (refs[k * count : (k + 1) * count] for k in range(3))
-    results = refs[-3 * count - 1 :]
-    pieces = refs[3 * count : -3 * count - 1]
-    totals = results[-1]
-    factor = jnp.minimum(1.0, CLIP / jnp.sqrt(square_ref[0:1, 0:1]))
+    results = refs[-3 * count - 2 :]
+    pieces = refs[3 * count : -3 * count - 2]
+    totals, sums = results[-2:]
+    both_sums = ordered_sum(square_parts, sides[3])
+    sums[...] = both_sums
+    factor = jnp.minimum(1.0, CLIP / jnp.sqrt(both_sums[0:1, 0:1]))
     step = pl.program_id(0)
 
     @pl.when(step == 0)
@@ -1033,21 +1048,34 @@
                 ],
                 0,
             )
-        routed = pieces[6:10] if index == 7 else pieces[10:14]
+        routed = pieces[6:10]
+        split = masters[7].shape[2] // 128
+        count_tiles = routed[0].shape[1] // 128 - 1
+
+        def decoded(at, here, first, last):
+            powers = picked_piece(routed, at, lambda ref: ref[here, count_tiles * 128 :])
+            scale = jnp.exp2(powers.astype(jnp.int32).astype(F32) - 15.0)
+            codes = picked_piece(routed, at, lambda ref: ref[here, first * 128 : last * 128])
+            codes = codes.astype(jnp.int32).astype(F32)
+            return jnp.concatenate(
+                [
+                    codes[:, (tile - first) * 128 : (tile - first + 1) * 128]
+                    * scale[:, tile : tile + 1]
+                    for tile in range(first, last)
+                ],
+                1,
+            )
+
         if index == 7:
             rows = masters[7].shape[1]
-            here = pl.ds(pl.multiple_of((step % 2) * rows, 8), rows)
+            here = pl.ds(pl.multiple_of((step % 2) * rows, 16), rows)
             return jnp.stack(
                 [
-                    picked_piece(
-                        routed,
-                        jnp.bitwise_xor(side * 2 + step // 2, me),
-                        lambda ref: ref[here, :],
-                    )
+                    decoded(jnp.bitwise_xor(side * 2 + step // 2, me), here, 0, split)
                     for side in range(2)
                 ]
             )
-        return picked_piece(routed, jnp.bitwise_xor(step, me), lambda ref: ref[...])
+        return decoded(jnp.bitwise_xor(step, me), slice(None), split, count_tiles)
 
     def update(index):
         gradient = gradient_of(index)
@@ -1069,9 +1097,13 @@
             pl.when(step == min(index, 3))(functools.partial(update, index))
 
 
-def step_kernel(count, totals, master_totals, *refs):
+def step_kernel(count, part_count, sides, *refs):
+    parts, refs = refs[:part_count], refs[part_count:]
     masters, directions = refs[:count], refs[count : 2 * count]
     results = refs[2 * count :]
+    all_totals = ordered_sum(parts, sides[3])
+    results[-1][...] = all_totals
+    totals, master_totals = all_totals[:count], all_totals[count:]
     step = pl.program_id(0)
 
     def update(index):
@@ -1138,7 +1170,10 @@
     )
     core = lax.axis_index("dp") & 1
     sides = jnp.stack(
-        [core, lax.axis_index("dp") >> 1, lax.axis_index("expert") >> 2]
+        [
+            core, lax.axis_index("dp") >> 1, lax.axis_index("expert") >> 2,
+            lax.axis_index("expert") >> 1 if fast else core * 0,
+        ]
     ).astype(jnp.int32)
     in_smem = pl.BlockSpec(memory_space=pltpu.SMEM)
     in_vmem = pl.BlockSpec(memory_space=pltpu.VMEM)
@@ -1313,7 +1348,7 @@
             compiler_params=params(),
             cost_estimate=cost(10),
         )(sides, arrived, *held)
-        returned = exchange_near(ready(expert_rows, shared_other)).reshape(
+        returned = exchange_near(expert_rows).reshape(
             EXPERTS, CAP + CODE_ROWS, D
         )
         shared_pieces = ready(shared_pieces, expert_rows)
@@ -1388,7 +1423,7 @@
         11.4,
     )
     received = exchange_near(slope_slots.reshape(4, 2, CAP, D)) if fast else to_devices(slope_slots)
-    chunk = D
+    chunk = 2 * D
     chunks = FFS // chunk
     back_in = [
         pl.BlockSpec((amount, D), lambda i, *unused: (0, 0)),
@@ -1401,10 +1436,10 @@
     back_args = (second, shared_slope, shin_low, shin_low, shout_low)
     if fast:
         in_spec = pl.BlockSpec(
-            (1, D, chunk), lambda i, sides: (jnp.bitwise_xor(i // 2, sides[1]), 0, i % 2)
+            (1, D, chunk), lambda i, sides: (jnp.bitwise_xor(i, sides[1]), 0, 0)
         )
         give_spec = pl.BlockSpec(
-            (1, D, chunk), lambda i, sides: (jnp.bitwise_xor(i // 2, sides[1]), 0, 0)
+            (1, D, D), lambda i, sides: (jnp.bitwise_xor(i, sides[1]), 0, 0)
         )
         out_spec = pl.BlockSpec((2, D // chunks, D), lambda i, sides: (0, i, 0))
         shared_second_slope, in_keep, in_even, in_odd, out_keep, out_give = pl.pallas_call(
@@ -1570,19 +1605,20 @@
     )
 
     if fast:
-        shared_code = ready(shared_code, routed_plain).reshape(expert_count, local_rows, -1)
-        (shared_sum,) = simple_call(
-            shard_sum_kernel, [out((local_rows, wide))], [exchange(shared_code)], 2.5
-        )
+        shared_code = ready(shared_code, routed_plain, expert_code).reshape(expert_count, local_rows, -1)
+        shared_code = exchange(shared_code)
         expert_far_other = flip(expert_far, "expert", 4)
-        last_give = ready(last_give, expert_far_other)
+        last_give = ready(last_give, expert_far_other, shared_code)
         (last_code,) = simple_call(
             last_code_kernel,
             [out((D, half_columns + 128), jnp.int16)],
             [(sides, in_smem), last_keep, flip(last_give, "dp", 1)],
             3.3,
         )
-        last_code = ready(last_code, shared_sum).reshape(expert_count, local_rows, -1)
+        (shared_sum,) = simple_call(
+            shard_sum_kernel, [out((local_rows, wide))], [ready(shared_code, last_code)], 2.5
+        )
+        last_code = ready(last_code, shared_code).reshape(expert_count, local_rows, -1)
         (last_part,) = simple_call(
             last_sum_kernel,
             [out((local_rows, half_columns))],
@@ -1590,27 +1626,23 @@
             2.2,
         )
         last_part = last_part + flip(last_part, "dp", 2)
-        expert_in, expert_out = simple_call(
+        (expert_total,) = simple_call(
             expert_total_kernel,
-            [out((D // 2, hidden_local)), out((D // 2, D))],
+            [out((D // 2, wide + 128), jnp.int16)],
             [ready(expert_own, last_code), expert_far_other],
             2.5,
         )
-        expert_in_cross = flip(expert_in, "dp", 2)
-        expert_out_cross = flip(expert_out, "dp", 2)
+        expert_cross = flip(expert_total, "dp", 2)
         shared_cross = flip(shared_sum, "dp", 2)
         square_pieces = [
-            expert_in, expert_in_cross, expert_out, expert_out_cross, shared_sum, shared_cross,
-            last_part,
+            shared_sum, shared_cross, last_part, expert_total, expert_cross,
         ]
-        weights = (1.0,) * 7
+        weights = (1.0,) * 5
         square_bits = [1]
         pieces = [
             last_part, flip(last_part, "dp", 1), shared_sum, shared_cross,
             flip(shared_sum, "dp", 1), flip(shared_cross, "dp", 1),
-            expert_in, expert_in_cross, flip(expert_in, "dp", 1), flip(expert_in_cross, "dp", 1),
-            expert_out, expert_out_cross, flip(expert_out, "dp", 1),
-            flip(expert_out_cross, "dp", 1),
+            expert_total, expert_cross, flip(expert_total, "dp", 1), flip(expert_cross, "dp", 1),
         ]
         piece_specs = [whole(a) for a in pieces]
     else:
@@ -1643,36 +1675,40 @@
     )
     for bit in square_bits:
         both_sums = both_sums + flip(both_sums, "dp", bit)
-    both_sums = sum_small(both_sums, ("expert",))
-    domain_sums = both_sums[1, :DOMAINS]
-    grad_norm = jnp.sqrt(both_sums[0, 0:1])
+    square_parts = expert_parts(both_sums)
+    part_count = len(square_parts)
     shapes = [out(a.shape) for a in masters]
     state_specs = tile_specs(masters, steps)
     updates = pl.pallas_call(
-        functools.partial(moments_kernel, fast, count, small_end),
-        out_shape=[*shapes, *shapes, *shapes, out((16, 128))],
+        functools.partial(moments_kernel, fast, count, part_count, small_end),
+        out_shape=[*shapes, *shapes, *shapes, out((16, 128)), out((2, 128))],
         grid=(steps,),
         in_specs=[
-            in_smem, whole(both_sums), *state_specs, *state_specs, *state_specs, *piece_specs,
+            in_smem, *[whole(a) for a in square_parts], *state_specs, *state_specs, *state_specs,
+            *piece_specs,
         ],
-        out_specs=[*state_specs, *state_specs, *state_specs, whole(out((16, 128)))],
+        out_specs=[
+            *state_specs, *state_specs, *state_specs, whole(out((16, 128))), whole(out((2, 128))),
+        ],
         compiler_params=params(),
         cost_estimate=cost(17),
-    )(sides, both_sums, *masters, *first_moments, *second_moments, *pieces)
+    )(sides, *square_parts, *masters, *first_moments, *second_moments, *pieces)
+    both_sums = updates[-1]
+    domain_sums = both_sums[1, :DOMAINS]
+    grad_norm = jnp.sqrt(both_sums[0, 0:1])
     directions = updates[:count]
-    all_totals = sum_small(
-        jnp.concatenate([updates[-1][:count], master_squares[:count]], 0), ("expert",)
-    )
-    totals, master_totals = all_totals[:count], all_totals[count:]
-    next_masters = pl.pallas_call(
-        functools.partial(step_kernel, count),
-        out_shape=shapes,
+    total_parts = expert_parts(
+        jnp.concatenate([updates[-2][:count], master_squares[:count]], 0)
+    )
+    *next_masters, all_totals = pl.pallas_call(
+        functools.partial(step_kernel, count, part_count),
+        out_shape=[*shapes, out((2 * count, 128))],
         grid=(steps,),
-        in_specs=[whole(totals), whole(master_totals), *state_specs, *state_specs],
-        out_specs=state_specs,
+        in_specs=[in_smem, *[whole(a) for a in total_parts], *state_specs, *state_specs],
+        out_specs=[*state_specs, whole(out((2 * count, 128)))],
         compiler_params=params(),
         cost_estimate=cost(7),
-    )(totals, master_totals, *masters, *directions)
+    )(sides, *total_parts, *masters, *directions)
     results = []
     for index in range(count):
         for group in (next_masters, updates[count : 2 * count], updates[2 * count : 3 * count]):

time: 376 us -> 359 us (0.955)
  waiting for transfers between devices: 85.3 us -> 77.1 us
  starting transfers between devices: 79.9 us -> 74.3 us
  Pallas kernels: 178 us -> 174 us
    ppermute x39 -> x38, waiting for transfers between devices: 60.7 us -> 53.9 us  [flip(): return lax.ppermute(value, axis_name, [(i, i ^ bit) for i in range(count)])]
    ppermute x39 -> x38, starting transfers between devices: 44.2 us -> 38.7 us  [flip(): return lax.ppermute(value, axis_name, [(i, i ^ bit) for i in range(count)])]
    unnamed x97 -> x105, local copies, waits for them, and re-layouts: 14.6 us -> 14.4 us
  transfers between devices with their start and end apart: 47 -> 46, of which waited for: 26 -> 24; matrix products, arithmetic and copies ran while one was open for 2% -> 3% of each run, Pallas kernels for 36% -> 38%
where the time goes in v5:
time: 359 us; the launch traced here: 355 us
  Pallas kernels  174 us (48%)
  waiting for transfers between devices  77.1 us (21%)
  starting transfers between devices  74.3 us (21%)
  local copies, waits for them, and re-layouts  20 us (6%)
  other arithmetic  6.8 us (2%)
    pallas_call x12, Pallas kernels, simple_call(): pl.pallas_call(kernel, out_shape=outs, in_specs=[spec for a, spec in pair...  75.1 us
    ppermute x38, waiting for transfers between devices, flip(): return lax.ppermute(value, axis_name, [(i, i ^ bit) for i in range(count)])  53.9 us
    ppermute x38, starting transfers between devices, flip(): return lax.ppermute(value, axis_name, [(i, i ^ bit) for i in range(count)])  38.7 us
    all_to_all x6, starting transfers between devices, exchange_near(): lax.all_to_all(value, 'expert', split_axis=0, concat_axis=0, tiled=True,...  24 us
    pallas_call x1, Pallas kernels, shards(): pl.pallas_call(expert_back_split_kernel, out_shape=[out((4, 2, CAP, D), B...  19.5 us
    pallas_call x1, Pallas kernels, shards(): pl.pallas_call(functools.partial(moments_kernel, fast, count, part_count,...  14.4 us
    unnamed x105, local copies, waits for them, and re-layouts  14.4 us
    all_to_all x2, waiting for transfers between devices, exchange(): lax.all_to_all(value, 'expert', split_axis=0, concat_axis=0, tiled=True)  13.3 us
  transfers between devices with their start and end apart: 46, of which 24 were waited for; matrix products, arithmetic and copies ran while one was open for 3% of the time, Pallas kernels for 38%

profile of v5, /device:TPU:0, one launch (start us, length us, event | category | flops | bytes accessed | tf_op | source)
XLA Modules:
  0.0 355.1 jit_solution(12315615597742602489)
XLA Ops:
  3.3 4.0 %collective-permute-start = (bf16[48,896]{1,0:T(8,128)(2,1)}, bf16[48,896]{1,0:T(8,128)(2,1)S(1)}, u32[]{:S(2)}, u32[]{:S(2)}) collective-permute-start(bf16[48,896]{1,0:T(8,128)(2,1)} %bitcast.182), channel_id=1, source_target_pairs={{0,4},{1,5},{2,6},{3,7},{4,0},{5,1},{6,2},{7,3},{8,12},{9,13},{10,... | collective-permute-start | bytes 258056 | tf_op jit(solution)/shard_map/ppermute | solution.py:817
  7.5 4.4 %collective-permute-done.far = bf16[48,896]{1,0:T(8,128)(2,1)S(1)} collective-permute-done((bf16[48,896]{1,0:T(8,128)(2,1)}, bf16[48,896]{1,0:T(8,128)(2,1)S(1)}, u32[]{:S(2)}, u32[]{:S(2)}) %collective-permute-start) | collective-permute-done | bytes 86048 | tf_op jit(solution)/shard_map/ppermute | solution.py:817
  14.4 3.5 all-to-all-start
  18.0 2.9 collective-permute-start.1
  21.5 3.0 shard_map.573
  24.5 2.6 shard_map.575
  30.0 3.4 collective-permute-start.3
  33.5 4.5 %all-to-all-start.1 = ((bf16[4,2,48,1152]{3,2,1,0:T(8,128)(2,1)}), bf16[4,2,48,1152]{3,2,1,0:T(8,128)(2,1)S(1)}, u32[]{:S(2)}, u32[]{:S(2)}) async-start(bf16[4,2,48,1152]{3,2,1,0:T(8,128)(2,1)} %shard_map.574), calls=%async_computation.1 | async-start | bytes 1769472 | tf_op jit(solution)/shard_map/all_to_all | solution.py:887
  38.8 14.8 %shard_map.576 = (f32[512,384]{1,0:T(8,128)}, bf16[512,384]{1,0:T(8,128)(2,1)}, bf16[512,1152]{1,0:T(8,128)(2,1)}, f32[512,128]{1,0:T(8,128)}, bf16[512,384]{1,0...) custom-call(s32[4]{0:T(128)} %pad_add_fusion.core.sides, ...), custom_call_target="tpu_custom_call" | custom-call | flops 17250000896 | tf_op jit(solution)/shard_map/pallas_call | solution.py:799
  55.6 4.0 %all-to-all-start.2 = ((bf16[4,2,256,384]{3,2,1,0:T(8,128)(2,1)}), bf16[4,2,256,384]{3,2,1,0:T(8,128)(2,1)S(1)}, u32[]{:S(2)}, u32[]{:S(2)}) async-start(bf16[4,2,256,384]{3,2,1,0:T(8,128)(2,1)} %bitcast.101), calls=%async_computation.2 | async-start | bytes 3145728 | tf_op jit(solution)/shard_map/all_to_all | solution.py:887
  61.1 9.9 %collective-permute-done.4.refs_1_ = bf16[192,1152]{1,0:T(8,128)(2,1)S(1)} collective-permute-done((bf16[192,1152]{1,0:T(8,128)(2,1)S(1)}, bf16[192,1152]{1,0:T(8,128)(2,1)S(1)}, u32[]{:S(2)}, u32[]{:S(2)}) %collective-permute-start.4) | collective-permute-done | bytes 442400 | tf_op jit(solution)/shard_map/ppermute | solution.py:817
  71.0 5.0 %shard_map.577 = (bf16[2,384,768]{2,1,0:T(8,128)(2,1)}, bf16[768,384]{1,0:T(8,128)(2,1)}, f32[16,128]{1,0:T(8,128)}) custom-call(f32[5,48]{1,0:T(8,128)} %refs_4_.5, f32[48,1152]{1,0:T(8,128)} %refs_5_.5, f32[48,384]{1,0:T(8,128)} %refs_6_.5, f32[9,48]{1,0:T(8,128)} %bitcast.187, f32[48,3072]{1,0:T(8,128)} %refs_8_.5, f32[192,384]{1,0:T(8,128)} %refs_9_.3, ...), custom_call_target="tpu_custom_call" | custom-call | flops 5750000128 | tf_op jit(solution)/shard_map/pallas_call | solution.py:1217
  79.1 2.9 shard_map.578
  83.2 9.6 %shard_map.579 = s16[4,2,272,384]{3,2,1,0:T(8,128)(2,1)} custom-call(s32[4]{0:T(128)} %pad_add_fusion.core.sides, bf16[4,2,256,384]{3,2,1,0:T(8,128)(2,1)} %copy-done.1, bf16[2,384,768]{2,1,0:T(8,128)(2,1)} %get-tuple-element.148.gate_up, bf16[768,384]{1,0:T(8,128)(2,1)} %get-tuple-element.149.down, bf16[2,384,768]{2,1,0:T(8,128)(2,1)} %get-tuple-element.152.gate_up_far, ...), custom_call_target="tpu_custom_call" | custom-call | flops 11500000256 | tf_op jit(solution)/shard_map/pallas_call | solution.py:1336
  92.8 4.0 %all-to-all-start.3 = ((s16[4,2,272,384]{3,2,1,0:T(8,128)(2,1)}), s16[4,2,272,384]{3,2,1,0:T(8,128)(2,1)S(1)}, u32[]{:S(2)}, u32[]{:S(2)}) async-start(s16[4,2,272,384]{3,2,1,0:T(8,128)(2,1)} %shard_map.579), calls=%async_computation.3 | async-start | bytes 3342336 | tf_op jit(solution)/shard_map/all_to_all | solution.py:887
  103.2 4.3 %shard_map.580 = (bf16[384,3072]{1,0:T(8,128)(2,1)}, bf16[1536,384]{1,0:T(8,128)(2,1)}) custom-call(s32[4]{0:T(128)} %pad_add_fusion.core.sides, bf16[384,1152]{1,0:T(8,128)(2,1)} %bitcast.105, bf16[384,1152]{1,0:T(8,128)(2,1)} %bitcast.14.refs_1_, bf16[384,1152]{1,0:T(8,128)(2,1)} %bitcast.15.refs_2_, bf16[384,1152]{1,0:T(8,128)(2,1)} %bitcast.16.refs_3_), custom_call_target="tpu_custom_call" | custom-call | flops 4944999936 | tf_op jit(solution)/shard_map/pallas_call | solution.py:799
  107.5 5.7 %shard_map.581.shared = f32[512,384]{1,0:T(8,128)} custom-call(bf16[512,384]{1,0:T(8,128)(2,1)} %get-tuple-element.155.second, bf16[384,3072]{1,0:T(8,128)(2,1)} %get-tuple-element.158.gate_w.lift_w, bf16[384,3072]{1,0:T(8,128)(2,1)} %get-tuple-element.158.gate_w.lift_w, bf16[1536,384]{1,0:T(8,128)(2,1)} %get-tuple-element.159.down_w), custom_call_target="tpu_custom_call" | custom-call | flops 6670000128 | tf_op jit(solution)/shard_map/pallas_call | solution.py:1387
  113.2 4.2 %all-to-all-done.3 = s16[4,2,272,384]{3,2,1,0:T(8,128)(2,1)S(1)} async-done(((s16[4,2,272,384]{3,2,1,0:T(8,128)(2,1)}), s16[4,2,272,384]{3,2,1,0:T(8,128)(2,1)S(1)}, u32[]{:S(2)}, u32[]{:S(2)}) %all-to-all-start.3) | async-done | bytes 1671200 | tf_op jit(solution)/shard_map/all_to_all | solution.py:887
  118.6 11.4 %shard_map.582 = (f32[512,384]{1,0:T(8,128)}, bf16[512,384]{1,0:T(8,128)(2,1)}, bf16[2048,384]{1,0:T(8,128)(2,1)}, bf16[512,128]{1,0:T(8,128)(2,1)}, f32[384,128...) custom-call(s16[8,272,384]{2,1,0:T(8,128)(2,1)} %bitcast.99, f32[512,128]{1,0:T(8,128)} %get-tuple-element.140.known, ...), custom_call_target="tpu_custom_call" | custom-call | flops 13109999616 | tf_op jit(solution)/shard_map/pallas_call | solution.py:799
  129.9 3.7 %all-to-all-start.4 = ((bf16[4,2,256,384]{3,2,1,0:T(8,128)(2,1)}), bf16[4,2,256,384]{3,2,1,0:T(8,128)(2,1)S(1)}, u32[]{:S(2)}, u32[]{:S(2)}) async-start(bf16[4,2,256,384]{3,2,1,0:T(8,128)(2,1)} %bitcast.102), calls=%async_computation.4 | async-start | bytes 3145728 | tf_op jit(solution)/shard_map/all_to_all | solution.py:887
  133.7 12.1 %shard_map.583 = (f32[512,384]{1,0:T(8,128)}, f32[2,384,768]{2,1,0:T(8,128)}, f32[2,384,384]{2,1,0:T(8,128)}, f32[2,384,384]{2,1,0:T(8,128)}, f32[2,384,384]{2,1,0:T(8,128)}, /*index=5*/f32[2,384,384]{2,1,0:T(8,128)}) custom-call(s32[4]{0:T(128)} %pad_add_fusion.core.sides, bf16[512,384]{1,0:T(8,128)(2,1)} %get-tuple-element.155.second, ...), custom_call_target="tpu_custom_call" | custom-call | flops 16099999744 | tf_op jit(solution)/shard_map/pallas_call | solution.py:1445
  146.3 2.5 collective-permute-done.12.in_even
  153.2 5.3 %shard_map.584 = (f32[384,1152]{1,0:T(8,128)}, s16[384,1280]{1,0:T(8,128)(2,1)}) custom-call(f32[2,384,768]{2,1,0:T(8,128)} %get-tuple-element.167.in_keep, f32[2,384,384]{2,1,0:T(8,128)} %copy-done.22, f32[2,384,384]{2,1,0:T(8,128)} %copy-done.24, f32[2,384,384]{2,1,0:T(8,128)} %get-tuple-element.170.out_keep, f32[2,384,384]{2,1,0:T(8,128)} %copy-done.25), custom_call_target="tpu_custom_call" | custom-call | flops 6095000064 | tf_op jit(solution)/shard_map/pallas_call | solution.py:1481
  160.3 19.5 %shard_map.586 = (bf16[4,2,256,384]{3,2,1,0:T(8,128)(2,1)}, f32[2,384,768]{2,1,0:T(8,128)}, f32[2,384,768]{2,1,0:T(8,128)}, f32[2,384,384]{2,1,0:T(8,128)}, f32[2,384,384]{2,1,0:T(8,128)}) custom-call(s32[4]{0:T(128)} %pad_add_fusion.core.sides, bf16[4,2,256,384]{3,2,1,0:T(8,128)(2,1)} %copy-done.1, bf16[4,2,256,384]{3,2,1,0:T(8,128)(2,1)} %copy-done.2, ...), custom_call_target="tpu_custom_call" | custom-call | flops 22424999936 | tf_op jit(solution)/shard_map/pallas_call | solution.py:1499
  179.9 2.7 collective-permute-done.15.other
  183.5 4.3 %all-to-all-start.5 = ((bf16[4,2,256,384]{3,2,1,0:T(8,128)(2,1)}), bf16[4,2,256,384]{3,2,1,0:T(8,128)(2,1)S(1)}, u32[]{:S(2)}, u32[]{:S(2)}) async-start(bf16[4,2,256,384]{3,2,1,0:T(8,128)(2,1)} %get-tuple-element.178), calls=%async_computation.5 | async-start | bytes 3145728 | tf_op jit(solution)/shard_map/all_to_all | solution.py:887
  188.5 3.0 collective-permute-done.11
  193.0 4.6 %shard_map.587 = (f32[2,192,1152]{2,1,0:T(8,128)}, s16[2,192,1280]{2,1,0:T(8,128)(2,1)}) custom-call(s32[4]{0:T(128)} %pad_add_fusion.core.sides, f32[2,384,768]{2,1,0:T(8,128)} %get-tuple-element.179.in_keep, f32[2,384,768]{2,1,0:T(8,128)} %collective-permute-done.16.in_other, f32[2,384,384]{2,1,0:T(8,128)} %get-tuple-element.181.out_keep, ...), custom_call_target="tpu_custom_call" | custom-call | flops 5289999872 | tf_op jit(solution)/shard_map/pallas_call | solution.py:1549
  198.1 4.4 %shard_map.585 = s16[384,1280]{1,0:T(8,128)(2,1)} custom-call(f32[384,1152]{1,0:T(8,128)} %get-tuple-element.172.keep, s16[384,1280]{1,0:T(8,128)(2,1)} %copy-done.26), custom_call_target="tpu_custom_call" | custom-call | flops 5059999744 | tf_op jit(solution)/shard_map/pallas_call | solution.py:1536
  202.5 4.1 %all-to-all-done.5 = bf16[4,2,256,384]{3,2,1,0:T(8,128)(2,1)S(1)} async-done(((bf16[4,2,256,384]{3,2,1,0:T(8,128)(2,1)}), bf16[4,2,256,384]{3,2,1,0:T(8,128)(2,1)S(1)}, u32[]{:S(2)}, u32[]{:S(2)}) %all-to-all-start.5) | async-done | bytes 1572896 | tf_op jit(solution)/shard_map/all_to_all | solution.py:887
  206.6 8.0 %all-to-all-start.6 = ((s16[8,48,1280]{2,1,0:T(8,128)(2,1)}), s16[8,48,1280]{2,1,0:T(8,128)(2,1)S(1)}, u32[]{:S(2)}, u32[]{:S(2)}) async-start(s16[8,48,1280]{2,1,0:T(8,128)(2,1)} %bitcast.104), calls=%async_computation.6 | async-start | bytes 1966080 | tf_op jit(solution)/shard_map/all_to_all | solution.py:883
  214.6 5.9 %shard_map.588 = (f32[512,384]{1,0:T(8,128)}, bf16[512,384]{1,0:T(8,128)(2,1)}, f32[384,384]{1,0:T(8,128)}, f32[1,384]{1,0:T(1,128)}, f32[384,128]{1,0:T(8,128)}) custom-call(bf16[2048,384]{1,0:T(8,128)(2,1)} %bitcast.100, f32[512,128]{1,0:T(8,128)} %get-tuple-element.140.known, f32[512,384]{1,0:T(8,128)} %get-tuple-element.175.second_slope, ...), custom_call_target="tpu_custom_call" | custom-call | flops 6899999744 | tf_op jit(solution)/shard_map/pallas_call | solution.py:799
  221.7 3.4 shard_map.589
  225.1 5.4 %collective-permute-start.19 = (s16[192,1280]{1,0:T(8,128)(2,1)}, s16[192,1280]{1,0:T(8,128)(2,1)S(1)}, u32[]{:S(2)}, u32[]{:S(2)}) collective-permute-start(s16[192,1280]{1,0:T(8,128)(2,1)} %get-tuple-element.192), channel_id=1, source_target_pairs={{0,4},{1,5},{2,6},{3,7},{4,0},{5,1},{6,2},{7,3},{8,12},{9,13},{10,... | collective-permute-start | bytes 1474568 | tf_op jit(solution)/shard_map/ppermute | solution.py:817
  230.5 18.3 %shard_map.590 = (f32[384,896]{1,0:T(8,128)}, f32[384,896]{1,0:T(8,128)}) custom-call(s32[4]{0:T(128)} %pad_add_fusion.core.sides, bf16[512,384]{1,0:T(8,128)(2,1)} %get-tuple-element.193.mixed_slope, bf16[512,1152]{1,0:T(8,128)(2,1)} %get-tuple-element.194.qkv, f32[512,128]{1,0:T(8,128)} %get-tuple-element.195.log_total, ...), custom_call_target="tpu_custom_call" | custom-call | flops 21159999488 | tf_op jit(solution)/shard_map/pallas_call | solution.py:799
  248.9 10.9 %collective-permute-done.19.code = s16[192,1280]{1,0:T(8,128)(2,1)S(1)} collective-permute-done((s16[192,1280]{1,0:T(8,128)(2,1)}, s16[192,1280]{1,0:T(8,128)(2,1)S(1)}, u32[]{:S(2)}, u32[]{:S(2)}) %collective-permute-start.19) | collective-permute-done | bytes 491552 | tf_op jit(solution)/shard_map/ppermute | solution.py:817
  259.8 3.3 collective-permute-done.20.other
  264.2 3.3 shard_map.591
  267.6 3.6 %all-to-all-start.7 = ((s16[8,48,1024]{2,1,0:T(8,128)(2,1)}), s16[8,48,1024]{2,1,0:T(8,128)(2,1)S(1)}, u32[]{:S(2)}, u32[]{:S(2)}) async-start(s16[8,48,1024]{2,1,0:T(8,128)(2,1)} %bitcast.106), calls=%async_computation.7 | async-start | bytes 1572864 | tf_op jit(solution)/shard_map/all_to_all | solution.py:883
  271.2 2.8 shard_map.594.refs_3_.refs_37_
  274.5 2.4 shard_map.592.refs_0_.refs_33_
  278.4 13.3 %all-to-all-done.7.codes = s16[8,48,1024]{2,1,0:T(8,128)(2,1)S(1)} async-done(((s16[8,48,1024]{2,1,0:T(8,128)(2,1)}), s16[8,48,1024]{2,1,0:T(8,128)(2,1)S(1)}, u32[]{:S(2)}, u32[]{:S(2)}) %all-to-all-start.7) | async-done | bytes 786464 | tf_op jit(solution)/shard_map/all_to_all | solution.py:883
  292.6 2.3 shard_map.593
  296.5 4.1 %collective-permute-done.22 = f32[48,896]{1,0:T(8,128)S(1)} collective-permute-done((f32[48,896]{1,0:T(8,128)}, f32[48,896]{1,0:T(8,128)S(1)}, u32[]{:S(2)}, u32[]{:S(2)}) %collective-permute-start.22) | collective-permute-done | bytes 172064 | tf_op jit(solution)/shard_map/ppermute | solution.py:817
  302.2 3.2 shard_map.595
  311.0 2.4 collective-permute-start.28
  318.6 14.4 %shard_map.596 = (f32[5,48]{1,0:T(8,128)}, f32[48,1152]{1,0:T(8,128)}, f32[48,384]{1,0:T(8,128)}, f32[9,48]{1,0:T(8,128)}, f32[48,3072]{1,0:T(8,128)}, /*index=5...) custom-call(s32[4]{0:T(128)} %pad_add_fusion.core.sides, ...), custom_call_target="tpu_custom_call" | custom-call | flops 19549999104 | tf_op jit(solution)/shard_map/pallas_call | solution.py:1682
  345.6 6.7 %shard_map.597 = (f32[5,48]{1,0:T(8,128)}, f32[48,1152]{1,0:T(8,128)}, f32[48,384]{1,0:T(8,128)}, f32[9,48]{1,0:T(8,128)}, f32[48,3072]{1,0:T(8,128)}, /*index=5...) custom-call(s32[4]{0:T(128)} %pad_add_fusion.core.sides, ...), custom_call_target="tpu_custom_call" | custom-call | flops 8049999872 | tf_op jit(solution)/shard_map/pallas_call | solution.py:1703
  (208 shorter events, 67.7 us)
Async XLA Ops:
  3.3 8.6 %collective-permute-start = (bf16[48,896]{1,0:T(8,128)(2,1)}, bf16[48,896]{1,0:T(8,128)(2,1)S(1)}, u32[]{:S(2)}, u32[]{:S(2)}) collective-permute-start(bf16[48,896]{1,0:T(8,128)(2,1)} %bitcast.182), channel_id=1, source_target_pairs={{0,4},{1,5},{2,6},{3,7},{4,0},{5,1},{6,2},{7,3},{8,12},{9,13},{10,... | collective-permute-start | bytes 258056 | tf_op jit(solution)/shard_map/ppermute | solution.py:817
  14.4 15.6 %all-to-all-start = ((bf16[4,2,48,896]{3,2,1,0:T(8,128)(2,1)}), bf16[4,2,48,896]{3,2,1,0:T(8,128)(2,1)S(1)}, u32[]{:S(2)}, u32[]{:S(2)}) async-start(bf16[4,2,48,896]{3,2,1,0:T(8,128)(2,1)} %shard_map.572), calls=%async_computation | async-start | bytes 1376256 | tf_op jit(solution)/shard_map/all_to_all | solution.py:887
  18.0 9.4 %collective-permute-start.1 = (bf16[48,1152]{1,0:T(8,128)(2,1)S(1)}, bf16[48,1152]{1,0:T(8,128)(2,1)S(1)}, u32[]{:S(2)}, u32[]{:S(2)}) collective-permute-start(bf16[48,1152]{1,0:T(8,128)(2,1)S(1)} %fusion.own), channel_id=1, source_target_pairs={{0,4},{1,5},{2,6},{3,7},{4,0},{5,1},{6,2},{7,3},{8,12},{9,13},{10,... | collective-permute-start | bytes 331784 | tf_op jit(solution)/shard_map/ppermute | solution.py:817
  30.0 7.9 %collective-permute-start.2 = (bf16[384,896]{1,0:T(8,128)(2,1)S(1)}, bf16[384,896]{1,0:T(8,128)(2,1)S(1)}, u32[]{:S(2)}, u32[]{:S(2)}) collective-permute-start(bf16[384,896]{1,0:T(8,128)(2,1)S(1)} %bitcast.107), channel_id=1, source_target_pairs={{0,8},{8,0},{16,24},{24,16},{1,9},{9,1},{17,25},{25,17},{2,10},{10... | collective-permute-start | bytes 2064392 | tf_op jit(solution)/shard_map/ppermute | solution.py:817
  30.0 24.0 %collective-permute-start.3 = (bf16[192,1152]{1,0:T(8,128)(2,1)}, bf16[192,1152]{1,0:T(8,128)(2,1)S(1)}, u32[]{:S(2)}, u32[]{:S(2)}) collective-permute-start(bf16[192,1152]{1,0:T(8,128)(2,1)} %shard_map.575), channel_id=1, source_target_pairs={{0,4},{1,5},{2,6},{3,7},{4,0},{5,1},{6,2},{7,3},{8,12},{9,13},{10,... | collective-permute-start | bytes 1327112 | tf_op jit(solution)/shard_map/ppermute | solution.py:817
  33.5 22.1 %all-to-all-start.1 = ((bf16[4,2,48,1152]{3,2,1,0:T(8,128)(2,1)}), bf16[4,2,48,1152]{3,2,1,0:T(8,128)(2,1)S(1)}, u32[]{:S(2)}, u32[]{:S(2)}) async-start(bf16[4,2,48,1152]{3,2,1,0:T(8,128)(2,1)} %shard_map.574), calls=%async_computation.1 | async-start | bytes 1769472 | tf_op jit(solution)/shard_map/all_to_all | solution.py:887
  55.6 42.5 %copy-start.5 = (bf16[4,2,48,1152]{3,2,1,0:T(8,128)(2,1)}, bf16[4,2,48,1152]{3,2,1,0:T(8,128)(2,1)S(1)}, u32[]{:S(2)}) copy-start(bf16[4,2,48,1152]{3,2,1,0:T(8,128)(2,1)S(1)} %all-to-all-done.1) | copy-start | bytes 2654212
  55.6 26.5 %all-to-all-start.2 = ((bf16[4,2,256,384]{3,2,1,0:T(8,128)(2,1)}), bf16[4,2,256,384]{3,2,1,0:T(8,128)(2,1)S(1)}, u32[]{:S(2)}, u32[]{:S(2)}) async-start(bf16[4,2,256,384]{3,2,1,0:T(8,128)(2,1)} %bitcast.101), calls=%async_computation.2 | async-start | bytes 3145728 | tf_op jit(solution)/shard_map/all_to_all | solution.py:887
  59.6 11.5 %collective-permute-start.4 = (bf16[192,1152]{1,0:T(8,128)(2,1)S(1)}, bf16[192,1152]{1,0:T(8,128)(2,1)S(1)}, u32[]{:S(2)}, u32[]{:S(2)}) collective-permute-start(bf16[192,1152]{1,0:T(8,128)(2,1)S(1)} %collective-permute-done.3.refs_0_), channel_id=1, source_target_pairs={{0,16},{8,24},{16,0},{24,8},{1,17},{9,25},{17,1},{25,9},{2,18},{10... | collective-permute-start | bytes 1327112 | tf_op jit(solution)/shard_map/ppermute | solution.py:817
  61.1 16.5 %collective-permute-start.5 = (bf16[192,1152]{1,0:T(8,128)(2,1)S(1)}, bf16[192,1152]{1,0:T(8,128)(2,1)S(1)}, u32[]{:S(2)}, u32[]{:S(2)}) collective-permute-start(bf16[192,1152]{1,0:T(8,128)(2,1)S(1)} %collective-permute-done.3.refs_0_), channel_id=1, source_target_pairs={{0,8},{8,0},{16,24},{24,16},{1,9},{9,1},{17,25},{25,17},{2,10},{10... | collective-permute-start | bytes 1327112 | tf_op jit(solution)/shard_map/ppermute | solution.py:817
  71.0 6.5 %collective-permute-start.6 = (bf16[192,1152]{1,0:T(8,128)(2,1)S(1)}, bf16[192,1152]{1,0:T(8,128)(2,1)S(1)}, u32[]{:S(2)}, u32[]{:S(2)}) collective-permute-start(bf16[192,1152]{1,0:T(8,128)(2,1)S(1)} %collective-permute-done.4.refs_1_), channel_id=1, source_target_pairs={{0,8},{8,0},{16,24},{24,16},{1,9},{9,1},{17,25},{25,17},{2,10},{10... | collective-permute-start | bytes 1327112 | tf_op jit(solution)/shard_map/ppermute | solution.py:817
  76.0 22.1 %collective-permute-start.7 = (bf16[4,2,48,1152]{3,2,1,0:T(8,128)(2,1)S(1)}, bf16[4,2,48,1152]{3,2,1,0:T(8,128)(2,1)}, u32[]{:S(2)}, u32[]{:S(2)}) collective-permute-start(bf16[4,2,48,1152]{3,2,1,0:T(8,128)(2,1)S(1)} %all-to-all-done.1), channel_id=1, source_target_pairs={{0,16},{8,24},{16,0},{24,8},{1,17},{9,25},{17,1},{25,9},{2,18},{10... | collective-permute-start | bytes 2654216 | tf_op jit(solution)/shard_map/ppermute | solution.py:817
  92.8 24.6 %all-to-all-start.3 = ((s16[4,2,272,384]{3,2,1,0:T(8,128)(2,1)}), s16[4,2,272,384]{3,2,1,0:T(8,128)(2,1)S(1)}, u32[]{:S(2)}, u32[]{:S(2)}) async-start(s16[4,2,272,384]{3,2,1,0:T(8,128)(2,1)} %shard_map.579), calls=%async_computation.3 | async-start | bytes 3342336 | tf_op jit(solution)/shard_map/all_to_all | solution.py:887
  98.1 5.1 %collective-permute-start.9 = (bf16[4,2,48,1152]{3,2,1,0:T(8,128)(2,1)}, bf16[4,2,48,1152]{3,2,1,0:T(8,128)(2,1)}, u32[]{:S(2)}, u32[]{:S(2)}) collective-permute-start(bf16[4,2,48,1152]{3,2,1,0:T(8,128)(2,1)} %collective-permute-done.7), channel_id=1, source_target_pairs={{0,8},{8,0},{16,24},{24,16},{1,9},{9,1},{17,25},{25,17},{2,10},{10... | collective-permute-start | bytes 2654216 | tf_op jit(solution)/shard_map/ppermute | solution.py:817
  98.1 5.1 %collective-permute-start.8 = (bf16[4,2,48,1152]{3,2,1,0:T(8,128)(2,1)S(1)}, bf16[4,2,48,1152]{3,2,1,0:T(8,128)(2,1)}, u32[]{:S(2)}, u32[]{:S(2)}) collective-permute-start(bf16[4,2,48,1152]{3,2,1,0:T(8,128)(2,1)S(1)} %all-to-all-done.1), channel_id=1, source_target_pairs={{0,8},{8,0},{16,24},{24,16},{1,9},{9,1},{17,25},{25,17},{2,10},{10... | collective-permute-start | bytes 2654216 | tf_op jit(solution)/shard_map/ppermute | solution.py:817
  99.0 3.6 %collective-permute-start.10 = (f32[1,128]{1,0:T(1,128)S(1)}, f32[1,128]{1,0:T(1,128)S(1)}, u32[]{:S(2)}, u32[]{:S(2)}) collective-permute-start(f32[1,128]{1,0:T(1,128)S(1)} %copy-done.18), channel_id=1, source_target_pairs={{0,16},{8,24},{16,0},{24,8},{1,17},{9,25},{17,1},{25,9},{2,18},{10... | collective-permute-start | bytes 1544 | tf_op jit(solution)/shard_map/ppermute | solution.py:817
  129.9 29.2 %all-to-all-start.4 = ((bf16[4,2,256,384]{3,2,1,0:T(8,128)(2,1)}), bf16[4,2,256,384]{3,2,1,0:T(8,128)(2,1)S(1)}, u32[]{:S(2)}, u32[]{:S(2)}) async-start(bf16[4,2,256,384]{3,2,1,0:T(8,128)(2,1)} %bitcast.102), calls=%async_computation.4 | async-start | bytes 3145728 | tf_op jit(solution)/shard_map/all_to_all | solution.py:887
  145.8 3.1 collective-permute-start.12
  145.8 4.7 %collective-permute-start.13 = (f32[2,384,384]{2,1,0:T(8,128)}, f32[2,384,384]{2,1,0:T(8,128)S(1)}, u32[]{:S(2)}, u32[]{:S(2)}) collective-permute-start(f32[2,384,384]{2,1,0:T(8,128)} %get-tuple-element.169), channel_id=1, source_target_pairs={{0,8},{8,0},{16,24},{24,16},{1,9},{9,1},{17,25},{25,17},{2,10},{10... | collective-permute-start | bytes 3538952 | tf_op jit(solution)/shard_map/ppermute | solution.py:817
  146.3 5.9 %collective-permute-start.14 = (f32[2,384,384]{2,1,0:T(8,128)}, f32[2,384,384]{2,1,0:T(8,128)S(1)}, u32[]{:S(2)}, u32[]{:S(2)}) collective-permute-start(f32[2,384,384]{2,1,0:T(8,128)} %get-tuple-element.171), channel_id=1, source_target_pairs={{0,8},{8,0},{16,24},{24,16},{1,9},{9,1},{17,25},{25,17},{2,10},{10... | collective-permute-start | bytes 3538952 | tf_op jit(solution)/shard_map/ppermute | solution.py:817
  158.6 24.0 %collective-permute-start.15 = (s16[384,1280]{1,0:T(8,128)(2,1)}, s16[384,1280]{1,0:T(8,128)(2,1)S(1)}, u32[]{:S(2)}, u32[]{:S(2)}) collective-permute-start(s16[384,1280]{1,0:T(8,128)(2,1)} %get-tuple-element.173), channel_id=1, source_target_pairs={{0,16},{8,24},{16,0},{24,8},{1,17},{9,25},{17,1},{25,9},{2,18},{10... | collective-permute-start | bytes 2949128 | tf_op jit(solution)/shard_map/ppermute | solution.py:817
  179.9 12.1 %collective-permute-start.16 = (f32[2,384,768]{2,1,0:T(8,128)}, f32[2,384,768]{2,1,0:T(8,128)}, u32[]{:S(2)}, u32[]{:S(2)}) collective-permute-start(f32[2,384,768]{2,1,0:T(8,128)} %get-tuple-element.180), channel_id=1, source_target_pairs={{0,8},{8,0},{16,24},{24,16},{1,9},{9,1},{17,25},{25,17},{2,10},{10... | collective-permute-start | bytes 7077896 | tf_op jit(solution)/shard_map/ppermute | solution.py:817
  183.5 23.0 %all-to-all-start.5 = ((bf16[4,2,256,384]{3,2,1,0:T(8,128)(2,1)}), bf16[4,2,256,384]{3,2,1,0:T(8,128)(2,1)S(1)}, u32[]{:S(2)}, u32[]{:S(2)}) async-start(bf16[4,2,256,384]{3,2,1,0:T(8,128)(2,1)} %get-tuple-element.178), calls=%async_computation.5 | async-start | bytes 3145728 | tf_op jit(solution)/shard_map/all_to_all | solution.py:887
  187.8 4.1 %collective-permute-start.17 = (f32[2,384,384]{2,1,0:T(8,128)S(1)}, f32[2,384,384]{2,1,0:T(8,128)S(1)}, u32[]{:S(2)}, u32[]{:S(2)}) collective-permute-start(f32[2,384,384]{2,1,0:T(8,128)S(1)} %copy-done.21), channel_id=1, source_target_pairs={{0,8},{8,0},{16,24},{24,16},{1,9},{9,1},{17,25},{25,17},{2,10},{10... | collective-permute-start | bytes 3538952 | tf_op jit(solution)/shard_map/ppermute | solution.py:817
  187.9 3.6 %collective-permute-start.11 = (f32[1,128]{1,0:T(1,128)S(1)}, f32[1,128]{1,0:T(1,128)S(1)}, u32[]{:S(2)}, u32[]{:S(2)}) collective-permute-start(f32[1,128]{1,0:T(1,128)S(1)} %copy-done.51), channel_id=1, source_target_pairs={{0,16},{8,24},{16,0},{24,8},{1,17},{9,25},{17,1},{25,9},{2,18},{10... | collective-permute-start | bytes 1544 | tf_op jit(solution)/shard_map/ppermute | solution.py:817
  197.6 23.2 %collective-permute-start.18 = (s16[2,192,1280]{2,1,0:T(8,128)(2,1)}, s16[2,192,1280]{2,1,0:T(8,128)(2,1)S(1)}, u32[]{:S(2)}, u32[]{:S(2)}) collective-permute-start(s16[2,192,1280]{2,1,0:T(8,128)(2,1)} %get-tuple-element.183), channel_id=1, source_target_pairs={{0,16},{8,24},{16,0},{24,8},{1,17},{9,25},{17,1},{25,9},{2,18},{10... | collective-permute-start | bytes 2949128 | tf_op jit(solution)/shard_map/ppermute | solution.py:817
  206.6 53.2 %all-to-all-start.6 = ((s16[8,48,1280]{2,1,0:T(8,128)(2,1)}), s16[8,48,1280]{2,1,0:T(8,128)(2,1)S(1)}, u32[]{:S(2)}, u32[]{:S(2)}) async-start(s16[8,48,1280]{2,1,0:T(8,128)(2,1)} %bitcast.104), calls=%async_computation.6 | async-start | bytes 1966080 | tf_op jit(solution)/shard_map/all_to_all | solution.py:883
  225.1 34.6 %collective-permute-start.19 = (s16[192,1280]{1,0:T(8,128)(2,1)}, s16[192,1280]{1,0:T(8,128)(2,1)S(1)}, u32[]{:S(2)}, u32[]{:S(2)}) collective-permute-start(s16[192,1280]{1,0:T(8,128)(2,1)} %get-tuple-element.192), channel_id=1, source_target_pairs={{0,4},{1,5},{2,6},{3,7},{4,0},{5,1},{6,2},{7,3},{8,12},{9,13},{10,... | collective-permute-start | bytes 1474568 | tf_op jit(solution)/shard_map/ppermute | solution.py:817
  259.7 3.4 collective-permute-start.20
  267.6 24.2 %all-to-all-start.7 = ((s16[8,48,1024]{2,1,0:T(8,128)(2,1)}), s16[8,48,1024]{2,1,0:T(8,128)(2,1)S(1)}, u32[]{:S(2)}, u32[]{:S(2)}) async-start(s16[8,48,1024]{2,1,0:T(8,128)(2,1)} %bitcast.106), calls=%async_computation.7 | async-start | bytes 1572864 | tf_op jit(solution)/shard_map/all_to_all | solution.py:883
  274.0 21.5 %collective-permute-start.23 = (s16[192,1280]{1,0:T(8,128)(2,1)}, s16[192,1280]{1,0:T(8,128)(2,1)S(1)}, u32[]{:S(2)}, u32[]{:S(2)}) collective-permute-start(s16[192,1280]{1,0:T(8,128)(2,1)} %shard_map.594.refs_3_.refs_37_), channel_id=1, source_target_pairs={{0,16},{8,24},{16,0},{24,8},{1,17},{9,25},{17,1},{25,9},{2,18},{10... | collective-permute-start | bytes 1474568 | tf_op jit(solution)/shard_map/ppermute | solution.py:817
  277.0 19.1 %collective-permute-start.21 = (f32[48,1152]{1,0:T(8,128)}, f32[48,1152]{1,0:T(8,128)S(1)}, u32[]{:S(2)}, u32[]{:S(2)}) collective-permute-start(f32[48,1152]{1,0:T(8,128)} %shard_map.592.refs_0_.refs_33_), channel_id=1, source_target_pairs={{0,16},{8,24},{16,0},{24,8},{1,17},{9,25},{17,1},{25,9},{2,18},{10... | collective-permute-start | bytes 663560 | tf_op jit(solution)/shard_map/ppermute | solution.py:817
  294.9 5.6 %collective-permute-start.22 = (f32[48,896]{1,0:T(8,128)}, f32[48,896]{1,0:T(8,128)S(1)}, u32[]{:S(2)}, u32[]{:S(2)}) collective-permute-start(f32[48,896]{1,0:T(8,128)} %shard_map.593), channel_id=1, source_target_pairs={{0,16},{8,24},{16,0},{24,8},{1,17},{9,25},{17,1},{25,9},{2,18},{10... | collective-permute-start | bytes 516104 | tf_op jit(solution)/shard_map/ppermute | solution.py:817
  295.4 18.0 %collective-permute-start.32 = (s16[192,1280]{1,0:T(8,128)(2,1)S(1)}, s16[192,1280]{1,0:T(8,128)(2,1)S(1)}, u32[]{:S(2)}, u32[]{:S(2)}) collective-permute-start(s16[192,1280]{1,0:T(8,128)(2,1)S(1)} %copy-done.29), channel_id=1, source_target_pairs={{0,8},{8,0},{16,24},{24,16},{1,9},{9,1},{17,25},{25,17},{2,10},{10... | collective-permute-start | bytes 1474568 | tf_op jit(solution)/shard_map/ppermute | solution.py:817
  295.5 20.0 %collective-permute-start.33 = (s16[192,1280]{1,0:T(8,128)(2,1)S(1)}, s16[192,1280]{1,0:T(8,128)(2,1)S(1)}, u32[]{:S(2)}, u32[]{:S(2)}) collective-permute-start(s16[192,1280]{1,0:T(8,128)(2,1)S(1)} %collective-permute-done.23.refs_4_.refs_38_), channel_id=1, source_target_pairs={{0,8},{8,0},{16,24},{24,16},{1,9},{9,1},{17,25},{25,17},{2,10},{10... | collective-permute-start | bytes 1474568 | tf_op jit(solution)/shard_map/ppermute | solution.py:817
  296.0 15.1 %collective-permute-start.30 = (f32[48,1152]{1,0:T(8,128)S(1)}, f32[48,1152]{1,0:T(8,128)S(1)}, u32[]{:S(2)}, u32[]{:S(2)}) collective-permute-start(f32[48,1152]{1,0:T(8,128)S(1)} %copy-done.38), channel_id=1, source_target_pairs={{0,8},{8,0},{16,24},{24,16},{1,9},{9,1},{17,25},{25,17},{2,10},{10... | collective-permute-start | bytes 663560 | tf_op jit(solution)/shard_map/ppermute | solution.py:817
  296.0 17.3 %collective-permute-start.31 = (f32[48,1152]{1,0:T(8,128)S(1)}, f32[48,1152]{1,0:T(8,128)S(1)}, u32[]{:S(2)}, u32[]{:S(2)}) collective-permute-start(f32[48,1152]{1,0:T(8,128)S(1)} %collective-permute-done.21.refs_1_.refs_34_), channel_id=1, source_target_pairs={{0,8},{8,0},{16,24},{24,16},{1,9},{9,1},{17,25},{25,17},{2,10},{10... | collective-permute-start | bytes 663560 | tf_op jit(solution)/shard_map/ppermute | solution.py:817
  305.4 1.4 collective-permute-start.24
  307.4 3.6 %collective-permute-start.25 = (f32[2,128]{1,0:T(2,128)S(1)}, f32[2,128]{1,0:T(2,128)S(1)}, u32[]{:S(2)}, u32[]{:S(2)}) collective-permute-start(f32[2,128]{1,0:T(2,128)S(1)} %add.43), channel_id=1, source_target_pairs={{0,1},{1,0},{2,3},{3,2},{4,5},{5,4},{6,7},{7,6},{8,9},{9,8},{10,11... | collective-permute-start | bytes 3080 | tf_op jit(solution)/shard_map/ppermute | solution.py:817
  311.0 6.9 %collective-permute-start.29 = (f32[48,896]{1,0:T(8,128)S(1)}, f32[48,896]{1,0:T(8,128)S(1)}, u32[]{:S(2)}, u32[]{:S(2)}) collective-permute-start(f32[48,896]{1,0:T(8,128)S(1)} %copy-done.10), channel_id=1, source_target_pairs={{0,8},{8,0},{16,24},{24,16},{1,9},{9,1},{17,25},{25,17},{2,10},{10... | collective-permute-start | bytes 516104 | tf_op jit(solution)/shard_map/ppermute | solution.py:817
  311.0 5.4 %collective-permute-start.28 = (f32[2,128]{1,0:T(2,128)S(1)}, f32[2,128]{1,0:T(2,128)S(1)}, u32[]{:S(2)}, u32[]{:S(2)}) collective-permute-start(f32[2,128]{1,0:T(2,128)S(1)} %add.44.refs_0_), channel_id=1, source_target_pairs={{0,6},{1,7},{2,4},{3,5},{4,2},{5,3},{6,0},{7,1},{8,14},{9,15},{10,... | collective-permute-start | bytes 3080 | tf_op jit(solution)/shard_map/ppermute | solution.py:817
  313.4 4.5 %collective-permute-start.27 = (f32[2,128]{1,0:T(2,128)S(1)}, f32[2,128]{1,0:T(2,128)S(1)}, u32[]{:S(2)}, u32[]{:S(2)}) collective-permute-start(f32[2,128]{1,0:T(2,128)S(1)} %add.44.refs_0_), channel_id=1, source_target_pairs={{0,4},{1,5},{2,6},{3,7},{4,0},{5,1},{6,2},{7,3},{8,12},{9,13},{10,... | collective-permute-start | bytes 3080 | tf_op jit(solution)/shard_map/ppermute | solution.py:817
  313.4 4.4 %collective-permute-start.26 = (f32[2,128]{1,0:T(2,128)S(1)}, f32[2,128]{1,0:T(2,128)S(1)}, u32[]{:S(2)}, u32[]{:S(2)}) collective-permute-start(f32[2,128]{1,0:T(2,128)S(1)} %add.44.refs_0_), channel_id=1, source_target_pairs={{0,2},{1,3},{2,0},{3,1},{4,6},{5,7},{6,4},{7,5},{8,10},{9,11},{10,... | collective-permute-start | bytes 3080 | tf_op jit(solution)/shard_map/ppermute | solution.py:817
  318.6 24.0 %copy-start.15 = (f32[1,128]{1,0:T(1,128)S(1)}, f32[1,128]{1,0:T(1,128)}, u32[]{:S(2)}) copy-start(f32[1,128]{1,0:T(1,128)} %get-tuple-element.281) | copy-start | bytes 1540
  333.7 3.7 %collective-permute-start.34 = (f32[18,128]{1,0:T(8,128)S(1)}, f32[18,128]{1,0:T(8,128)S(1)}, u32[]{:S(2)}, u32[]{:S(2)}) collective-permute-start(f32[18,128]{1,0:T(8,128)S(1)} %pad_maximum_fusion), channel_id=1, source_target_pairs={{0,1},{1,0},{2,3},{3,2},{4,5},{5,4},{6,7},{7,6},{8,9},{9,8},{10,11... | collective-permute-start | bytes 27656 | tf_op jit(solution)/shard_map/ppermute | solution.py:817
  338.1 6.8 %collective-permute-start.37 = (f32[18,128]{1,0:T(8,128)S(1)}, f32[18,128]{1,0:T(8,128)S(1)}, u32[]{:S(2)}, u32[]{:S(2)}) collective-permute-start(f32[18,128]{1,0:T(8,128)S(1)} %fusion.2.refs_0_), channel_id=1, source_target_pairs={{0,6},{1,7},{2,4},{3,5},{4,2},{5,3},{6,0},{7,1},{8,14},{9,15},{10,... | collective-permute-start | bytes 27656 | tf_op jit(solution)/shard_map/ppermute | solution.py:817
  339.7 5.3 %collective-permute-start.36 = (f32[18,128]{1,0:T(8,128)S(1)}, f32[18,128]{1,0:T(8,128)S(1)}, u32[]{:S(2)}, u32[]{:S(2)}) collective-permute-start(f32[18,128]{1,0:T(8,128)S(1)} %fusion.2.refs_0_), channel_id=1, source_target_pairs={{0,4},{1,5},{2,6},{3,7},{4,0},{5,1},{6,2},{7,3},{8,12},{9,13},{10,... | collective-permute-start | bytes 27656 | tf_op jit(solution)/shard_map/ppermute | solution.py:817
  340.7 4.3 %collective-permute-start.35 = (f32[18,128]{1,0:T(8,128)S(1)}, f32[18,128]{1,0:T(8,128)S(1)}, u32[]{:S(2)}, u32[]{:S(2)}) collective-permute-start(f32[18,128]{1,0:T(8,128)S(1)} %fusion.2.refs_0_), channel_id=1, source_target_pairs={{0,2},{1,3},{2,0},{3,1},{4,6},{5,7},{6,4},{7,5},{8,10},{9,11},{10,... | collective-permute-start | bytes 27656 | tf_op jit(solution)/shard_map/ppermute | solution.py:817
  (50 other events, 217.4 us)

commit v6 on v5

--- a/solution.py
+++ b/solution.py
@@ -524,13 +524,30 @@
     )
 
 
-def add_code_kernel(keep, other, code):
-    encode(code, [mine + theirs for mine, theirs in zip(tiles_of(keep[...]), decode(other))])
-
-
-def shard_sum_kernel(codes, total):
-    for index, tile in enumerate(decode(codes)):
-        total[:, index * 128 : (index + 1) * 128] = jnp.sum(tile, 0)
+def add_code_kernel(rows, keep, other, code):
+    for index in range(keep.shape[0] // rows):
+        here = slice(index * rows, (index + 1) * rows)
+        place = slot_place(True, index)
+        encode(
+            code.at[place * rows : (place + 1) * rows],
+            [
+                mine + theirs
+                for mine, theirs in zip(tiles_of(keep[here, :]), decode(other.at[here]))
+            ],
+        )
+
+
+def near_sum_kernel(sides, codes, own, far):
+    mine = [jnp.sum(tile, 0) for tile in decode(codes.at[:, sides[2]])]
+    for index, tile in enumerate(mine):
+        own[:, index * 128 : (index + 1) * 128] = tile
+    encode(far, [jnp.sum(tile, 0) for tile in decode(codes.at[:, 1 - sides[2]])])
+
+
+def add_kernel(own, code, total):
+    for index, tile in enumerate(decode(code)):
+        here = slice(index * 128, (index + 1) * 128)
+        total[:, here] = own[:, here] + tile
 
 
 def expert_split_kernel(sides, in_keep, in_other, out_keep, out_other, keep, code):
@@ -559,21 +576,50 @@
     )
 
 
-def last_code_kernel(core, keep, other, code):
-    tiles = tiles_of(keep[...] + other[...])
+def encode_last(ref, tiles, high):
     rough, power = coded_tile(tiles[5])
-    tiles[6] = jnp.where(core[0] == 1, tiles[5] - rough * jnp.exp2(power - 15.0), tiles[6])
-    encode(code, tiles)
-
-
-def last_sum_kernel(core, codes, total):
-    tiles = decode(codes)
-    high = core[0] == 1
-    fine = tiles[6]
-    tiles[5] = jnp.where(high, tiles[5] + fine, tiles[5])
-    tiles[6] = jnp.where(high, 0.0, fine)
-    for index, tile in enumerate(tiles):
-        total[:, index * 128 : (index + 1) * 128] = jnp.sum(tile, 0)
+    rest = tiles[5] - rough * jnp.exp2(power - 15.0)
+    encode(ref, [*tiles[:6], jnp.where(high, rest, tiles[6])])
+
+
+def whole_tiles(tiles, high):
+    return [
+        *tiles[:5],
+        jnp.where(high, tiles[5] + tiles[6], tiles[5]),
+        jnp.where(high, 0.0, tiles[6]),
+    ]
+
+
+def last_code_kernel(rows, sides, keep, other, *codes):
+    for target, code in enumerate(codes):
+        for half in range(2):
+            shard = jnp.bitwise_xor(sides[4], target) + 4 * half
+            here = pl.ds(pl.multiple_of(shard * rows, 8), rows)
+            tiles = tiles_of(keep[here, :] + other[here, :])
+            encode_last(code.at[half * rows : (half + 1) * rows], tiles, sides[0] == 1)
+
+
+def last_near_kernel(rows, sides, *refs):
+    codes, (own, far) = refs[:-2], refs[-2:]
+    high = sides[0] == 1
+
+    def gathered(half):
+        here = pl.ds(pl.multiple_of(half * rows, 16), rows)
+        sums = None
+        for code in codes:
+            tiles = decode(code.at[here])
+            sums = tiles if sums is None else [a + b for a, b in zip(sums, tiles)]
+        return whole_tiles(sums, high)
+
+    for index, tile in enumerate(gathered(sides[2])):
+        own[:, index * 128 : (index + 1) * 128] = tile
+    encode_last(far, gathered(1 - sides[2]), high)
+
+
+def last_sum_kernel(sides, own, code, total):
+    for index, tile in enumerate(whole_tiles(decode(code), sides[0] == 1)):
+        here = slice(index * 128, (index + 1) * 128)
+        total[:, here] = own[:, here] + tile
 
 
 def middle_kernel(
@@ -610,10 +656,12 @@
             scale = jnp.exp2(powers[0:1, :CAP] - 15.0)
         high = rows.astype(BF16)
         rest = (rows - high.astype(F32)).astype(BF16)
+        halves_of_rows = jnp.concatenate([high, rest], 1)
         for k in range(2):
             slot = expert * CAP + lax.broadcasted_iota(jnp.int32, (amount, CAP), 1)
             hot = jnp.where(integers[:, SLOT + k : SLOT + k + 1] == slot, scale, 0.0).astype(BF16)
-            picked[k] = picked[k] + (mm(hot, high) + mm(hot, rest))
+            both = mm(hot, halves_of_rows)
+            picked[k] = picked[k] + (both[:, :D] + both[:, D:])
     mixer = (
         after[...] + shared_gate * shared[...] + (gates[0] * picked[0] + gates[1] * picked[1])
     )
@@ -918,14 +966,16 @@
     return jnp.sum(exchange(value), 0)
 
 
-def squares_kernel(weights, sums, *refs):
+def squares_kernel(weights, sums, last, last_other, *refs):
+    total_last, both = refs[-2:]
+    total_last[...] = last[...] + last_other[...]
     total = jnp.zeros((1, 1), F32)
-    for weight, ref in zip(weights, refs[:-1]):
+    for weight, ref in zip(weights, (total_last, *refs[:-2])):
         for piece in decode(ref) if ref.dtype == jnp.int16 else [ref[...]]:
             part = jnp.sum(jnp.sum(piece * piece, -1, keepdims=True), 0, keepdims=True)
             total = total + part * weight
-    refs[-1][0:1, :] = jnp.broadcast_to(total, (1, 128))
-    refs[-1][1:2, :] = sums[...]
+    both[0:1, :] = jnp.broadcast_to(total, (1, 128))
+    both[1:2, :] = sums[...]
 
 
 def sum_all(value):
@@ -992,7 +1042,7 @@
     return value
 
 
-def moments_kernel(fast, count, part_count, small_end, sides, *refs):
+def moments_kernel(fast, count, part_count, small_end, sides, master_squares, *refs):
     square_parts, refs = refs[:part_count], refs[part_count:]
     masters, means, squares = (refs[k * count : (k + 1) * count] for k in range(3))
     results = refs[-3 * count - 2 :]
@@ -1005,7 +1055,8 @@
 
     @pl.when(step == 0)
     def _():
-        totals[...] = jnp.zeros_like(totals)
+        totals[:16] = jnp.zeros_like(master_squares)
+        totals[16:] = master_squares[...]
 
     def last_rows(start, stop):
         if not fast:
@@ -1102,8 +1153,11 @@
     masters, directions = refs[:count], refs[count : 2 * count]
     results = refs[2 * count :]
     all_totals = ordered_sum(parts, sides[3])
-    results[-1][...] = all_totals
-    totals, master_totals = all_totals[:count], all_totals[count:]
+    totals, master_totals = all_totals[:count], all_totals[16 : 16 + count]
+    diagonal = lax.broadcasted_iota(jnp.int32, (count, 128), 0) == lanes_of((count, 128))
+    for row, sums in enumerate((master_totals, totals)):
+        flat = jnp.sum(jnp.where(diagonal, jnp.sqrt(sums[:, 0:1]), 0.0), 0, keepdims=True)
+        results[-1][row : row + 1, :] = flat[:, :count]
     step = pl.program_id(0)
 
     def update(index):
@@ -1172,7 +1226,7 @@
     sides = jnp.stack(
         [
             core, lax.axis_index("dp") >> 1, lax.axis_index("expert") >> 2,
-            lax.axis_index("expert") >> 1 if fast else core * 0,
+            lax.axis_index("expert") >> 1 if fast else core * 0, lax.axis_index("expert") & 3,
         ]
     ).astype(jnp.int32)
     in_smem = pl.BlockSpec(memory_space=pltpu.SMEM)
@@ -1533,15 +1587,12 @@
         )(arrived, received, gate_up_low, down_low)
         routed_back = to_points(grad_rows)
     if fast:
-        shared_code = pl.pallas_call(
-            add_code_kernel,
-            out_shape=out((D, wide + 128), jnp.int16),
-            grid=(4,),
-            in_specs=[fold_to, code_to],
-            out_specs=code_to,
-            compiler_params=params(),
-            cost_estimate=cost(4.4),
-        )(shared_keep, shared_other)
+        (shared_code,) = simple_call(
+            functools.partial(add_code_kernel, local_rows),
+            [out((D, wide + 128), jnp.int16)],
+            [shared_keep, shared_other],
+            4.4,
+        )
         expert_in_other = flip(expert_in_give, "dp", 1)
         expert_out_other = flip(expert_out_give, "dp", 1)
         half_in = pl.BlockSpec((1, D, hidden_local), lambda i: (i, 0, 0))
@@ -1605,27 +1656,48 @@
     )
 
     if fast:
-        shared_code = ready(shared_code, routed_plain, expert_code).reshape(expert_count, local_rows, -1)
-        shared_code = exchange(shared_code)
+        shared_code = ready(shared_code, routed_plain, expert_code)
+        shared_code = exchange_near(shared_code.reshape(4, 2, local_rows, wide + 128))
         expert_far_other = flip(expert_far, "expert", 4)
         last_give = ready(last_give, expert_far_other, shared_code)
-        (last_code,) = simple_call(
-            last_code_kernel,
-            [out((D, half_columns + 128), jnp.int16)],
+        shared_own, shared_far = simple_call(
+            near_sum_kernel,
+            [out((local_rows, wide)), out((local_rows, wide + 128), jnp.int16)],
+            [(sides, in_smem), ready(shared_code, last_keep)],
+            2.5,
+        )
+        last_keep = ready(last_keep, shared_far)
+        last_codes = simple_call(
+            functools.partial(last_code_kernel, local_rows),
+            [out((2 * local_rows, half_columns + 128), jnp.int16)] * 4,
             [(sides, in_smem), last_keep, flip(last_give, "dp", 1)],
             3.3,
         )
         (shared_sum,) = simple_call(
-            shard_sum_kernel, [out((local_rows, wide))], [ready(shared_code, last_code)], 2.5
-        )
-        last_code = ready(last_code, shared_code).reshape(expert_count, local_rows, -1)
+            add_kernel, [out((local_rows, wide))], [shared_own, flip(shared_far, "expert", 4)], 1.5
+        )
+        last_code = last_codes[0]
+        last_codes = [last_code] + [
+            flip(ready(code, shared_code), "expert", bit)
+            for bit, code in enumerate(last_codes)
+            if bit
+        ]
+        last_own, last_far = simple_call(
+            functools.partial(last_near_kernel, local_rows),
+            [
+                out((local_rows, half_columns)),
+                out((local_rows, half_columns + 128), jnp.int16),
+            ],
+            [(sides, in_smem), *last_codes],
+            2.5,
+        )
         (last_part,) = simple_call(
             last_sum_kernel,
             [out((local_rows, half_columns))],
-            [(sides, in_smem), exchange(last_code)],
-            2.2,
-        )
-        last_part = last_part + flip(last_part, "dp", 2)
+            [(sides, in_smem), last_own, flip(last_far, "expert", 4)],
+            1.5,
+        )
+        last_other = flip(last_part, "dp", 2)
         (expert_total,) = simple_call(
             expert_total_kernel,
             [out((D // 2, wide + 128), jnp.int16)],
@@ -1635,13 +1707,12 @@
         expert_cross = flip(expert_total, "dp", 2)
         shared_cross = flip(shared_sum, "dp", 2)
         square_pieces = [
-            shared_sum, shared_cross, last_part, expert_total, expert_cross,
+            shared_sum, shared_cross, expert_total, expert_cross,
         ]
         weights = (1.0,) * 5
         square_bits = [1]
         pieces = [
-            last_part, flip(last_part, "dp", 1), shared_sum, shared_cross,
-            flip(shared_sum, "dp", 1), flip(shared_cross, "dp", 1),
+            shared_sum, shared_cross, flip(shared_sum, "dp", 1), flip(shared_cross, "dp", 1),
             expert_total, expert_cross, flip(expert_total, "dp", 1), flip(expert_cross, "dp", 1),
         ]
         piece_specs = [whole(a) for a in pieces]
@@ -1655,24 +1726,28 @@
         expert_out_part = scatter_sum(grad_expert_out, 0, dp_bits)
         last_part = expert_scatter(last_keep.reshape(expert_count, local_rows, -1))
         for bit in dp_bits:
-            last_part = last_part + flip(last_part, "dp", bit)
-        square_pieces = [expert_in_part, expert_out_part, shin_part, shout_part, last_part]
-        weights = (1.0, 1.0, 1.0, 1.0, 1.0 / dp_count)
+            last_other = flip(last_part, "dp", bit)
+            if bit != dp_bits[-1]:
+                last_part = last_part + last_other
+        square_pieces = [expert_in_part, expert_out_part, shin_part, shout_part]
+        weights = (1.0 / dp_count, 1.0, 1.0, 1.0, 1.0)
         square_bits = dp_bits
         pieces = [
-            last_part,
             join(join(shin_part, 1, dp_bits[1:])[None], 0, [1]),
             join(shout_part, 0, dp_bits),
             join(expert_in_part, 0, dp_bits).reshape(expert_input.shape),
             join(expert_out_part, 0, dp_bits),
         ]
-        piece_specs = [
-            whole(last_part),
-            *[tile_spec(i, a.shape, steps) for i, a in zip((4, 5, 7, 8), pieces[1:])],
-        ]
-    (both_sums,) = simple_call(
-        functools.partial(squares_kernel, weights), [out((2, 128))], [sums, *square_pieces], 2.4
-    )
+        piece_specs = [tile_spec(i, a.shape, steps) for i, a in zip((4, 5, 7, 8), pieces)]
+    last_part, both_sums = simple_call(
+        functools.partial(squares_kernel, weights),
+        [out(last_part.shape), out((2, 128))],
+        [sums, last_part, last_other, *square_pieces],
+        3.5,
+    )
+    last_pieces = [last_part] + ([flip(last_part, "dp", 1)] if fast else [])
+    pieces = last_pieces + pieces
+    piece_specs = [whole(a) for a in last_pieces] + piece_specs
     for bit in square_bits:
         both_sums = both_sums + flip(both_sums, "dp", bit)
     square_parts = expert_parts(both_sums)
@@ -1681,31 +1756,29 @@
     state_specs = tile_specs(masters, steps)
     updates = pl.pallas_call(
         functools.partial(moments_kernel, fast, count, part_count, small_end),
-        out_shape=[*shapes, *shapes, *shapes, out((16, 128)), out((2, 128))],
+        out_shape=[*shapes, *shapes, *shapes, out((32, 128)), out((2, 128))],
         grid=(steps,),
         in_specs=[
-            in_smem, *[whole(a) for a in square_parts], *state_specs, *state_specs, *state_specs,
+            in_smem, whole(master_squares), *[whole(a) for a in square_parts], *state_specs, *state_specs, *state_specs,
             *piece_specs,
         ],
         out_specs=[
-            *state_specs, *state_specs, *state_specs, whole(out((16, 128))), whole(out((2, 128))),
+            *state_specs, *state_specs, *state_specs, whole(out((32, 128))), whole(out((2, 128))),
         ],
         compiler_params=params(),
         cost_estimate=cost(17),
-    )(sides, *square_parts, *masters, *first_moments, *second_moments, *pieces)
+    )(sides, master_squares, *square_parts, *masters, *first_moments, *second_moments, *pieces)
     both_sums = updates[-1]
     domain_sums = both_sums[1, :DOMAINS]
     grad_norm = jnp.sqrt(both_sums[0, 0:1])
     directions = updates[:count]
-    total_parts = expert_parts(
-        jnp.concatenate([updates[-2][:count], master_squares[:count]], 0)
-    )
-    *next_masters, all_totals = pl.pallas_call(
+    total_parts = expert_parts(updates[-2])
+    *next_masters, trust = pl.pallas_call(
         functools.partial(step_kernel, count, part_count),
-        out_shape=[*shapes, out((2 * count, 128))],
+        out_shape=[*shapes, out((2, count))],
         grid=(steps,),
         in_specs=[in_smem, *[whole(a) for a in total_parts], *state_specs, *state_specs],
-        out_specs=[*state_specs, whole(out((2 * count, 128)))],
+        out_specs=[*state_specs, whole(out((2, count)))],
         compiler_params=params(),
         cost_estimate=cost(7),
     )(sides, *total_parts, *masters, *directions)
@@ -1713,10 +1786,9 @@
     for index in range(count):
         for group in (next_masters, updates[count : 2 * count], updates[2 * count : 3 * count]):
             results.append(group[index].T if index == 3 else group[index])
-    norms = jnp.sqrt(all_totals[:, 0])
     results.append(jnp.stack([domain_sums, counts[0, :DOMAINS]]))
     results.append(grad_norm)
-    results.append(jnp.stack([norms[count:], norms[:count]], 1))
+    results.append(trust.T)
     return tuple(results)
 
 

time: 359 us -> 348 us (0.969)
  waiting for transfers between devices: 77.1 us -> 65.8 us
    all_to_all x2 -> x0, waiting for transfers between devices: 13.3 us -> none  [exchange(): lax.all_to_all(value, 'expert', split_axis=0, concat_axis=0, tiled=True)]
    all_to_all x2 -> x0, starting transfers between devices: 11.6 us -> none  [exchange(): lax.all_to_all(value, 'expert', split_axis=0, concat_axis=0, tiled=True)]
    pallas_call x12 -> x15, Pallas kernels: 75.1 us -> 82.8 us  [simple_call(): pl.pallas_call(kernel, out_shape=outs, in_specs=[spec for a, spec in pair...]
    ppermute x38 -> x43, starting transfers between devices: 38.7 us -> 44.3 us  [flip(): return lax.ppermute(value, axis_name, [(i, i ^ bit) for i in range(count)])]
    pallas_call x1 -> x0, Pallas kernels: 4.37 us -> none  [shards(): pl.pallas_call(add_code_kernel, out_shape=out((D, wide + 128), jnp.int16)...]
    all_to_all x6 -> x7, starting transfers between devices: 24 us -> 27.9 us  [exchange_near(): lax.all_to_all(value, 'expert', split_axis=0, concat_axis=0, tiled=True,...]
    unnamed x105 -> x111, local copies, waits for them, and re-layouts: 14.4 us -> 16.3 us
    ppermute x38 -> x43, waiting for transfers between devices: 53.9 us -> 55.8 us  [flip(): return lax.ppermute(value, axis_name, [(i, i ^ bit) for i in range(count)])]
  transfers between devices with their start and end apart: 46 -> 50, of which waited for: 24 -> 26; matrix products, arithmetic and copies ran while one was open for 3% -> 2% of each run, Pallas kernels for 38% -> 41%
where the time goes in v6:
time: 348 us; the launch traced here: 343 us
  Pallas kernels  177 us (51%)
  starting transfers between devices  72.2 us (21%)
  waiting for transfers between devices  65.8 us (19%)
  local copies, waits for them, and re-layouts  21.7 us (6%)
    pallas_call x15, Pallas kernels, simple_call(): pl.pallas_call(kernel, out_shape=outs, in_specs=[spec for a, spec in pair...  82.8 us
    ppermute x43, waiting for transfers between devices, flip(): return lax.ppermute(value, axis_name, [(i, i ^ bit) for i in range(count)])  55.8 us
    ppermute x43, starting transfers between devices, flip(): return lax.ppermute(value, axis_name, [(i, i ^ bit) for i in range(count)])  44.3 us
    all_to_all x7, starting transfers between devices, exchange_near(): lax.all_to_all(value, 'expert', split_axis=0, concat_axis=0, tiled=True,...  27.9 us
    pallas_call x1, Pallas kernels, shards(): pl.pallas_call(expert_back_split_kernel, out_shape=[out((4, 2, CAP, D), B...  19.5 us
    unnamed x111, local copies, waits for them, and re-layouts  16.3 us
    pallas_call x1, Pallas kernels, shards(): pl.pallas_call(functools.partial(moments_kernel, fast, count, part_count,...  14.5 us
    pallas_call x1, Pallas kernels, shards(): pl.pallas_call(shared_back_split_kernel, out_shape=[out((amount, D)), out...  12 us
  transfers between devices with their start and end apart: 50, of which 26 were waited for; matrix products, arithmetic and copies ran while one was open for 2% of the time, Pallas kernels for 41%

profile of v6, /device:TPU:0, one launch (start us, length us, event | category | flops | bytes accessed | tf_op | source)
XLA Modules:
  0.0 343.4 jit_solution(15736861702025143085)
XLA Ops:
  3.2 4.0 %collective-permute-start = (bf16[48,896]{1,0:T(8,128)(2,1)}, bf16[48,896]{1,0:T(8,128)(2,1)S(1)}, u32[]{:S(2)}, u32[]{:S(2)}) collective-permute-start(bf16[48,896]{1,0:T(8,128)(2,1)} %bitcast.176), channel_id=1, source_target_pairs={{0,4},{1,5},{2,6},{3,7},{4,0},{5,1},{6,2},{7,3},{8,12},{9,13},{10,... | collective-permute-start | bytes 258056 | tf_op jit(solution)/shard_map/ppermute | solution.py:865
  7.4 4.4 %collective-permute-done.far = bf16[48,896]{1,0:T(8,128)(2,1)S(1)} collective-permute-done((bf16[48,896]{1,0:T(8,128)(2,1)}, bf16[48,896]{1,0:T(8,128)(2,1)S(1)}, u32[]{:S(2)}, u32[]{:S(2)}) %collective-permute-start) | collective-permute-done | bytes 86048 | tf_op jit(solution)/shard_map/ppermute | solution.py:865
  14.3 3.5 %all-to-all-start = ((bf16[4,2,48,896]{3,2,1,0:T(8,128)(2,1)}), bf16[4,2,48,896]{3,2,1,0:T(8,128)(2,1)S(1)}, u32[]{:S(2)}, u32[]{:S(2)}) async-start(bf16[4,2,48,896]{3,2,1,0:T(8,128)(2,1)} %shard_map.573), calls=%async_computation | async-start | bytes 1376256 | tf_op jit(solution)/shard_map/all_to_all | solution.py:935
  18.0 2.9 collective-permute-start.1
  21.5 3.0 shard_map.574
  24.5 2.6 shard_map.576
  30.0 3.4 %collective-permute-start.3 = (bf16[192,1152]{1,0:T(8,128)(2,1)}, bf16[192,1152]{1,0:T(8,128)(2,1)S(1)}, u32[]{:S(2)}, u32[]{:S(2)}) collective-permute-start(bf16[192,1152]{1,0:T(8,128)(2,1)} %shard_map.576), channel_id=1, source_target_pairs={{0,4},{1,5},{2,6},{3,7},{4,0},{5,1},{6,2},{7,3},{8,12},{9,13},{10,... | collective-permute-start | bytes 1327112 | tf_op jit(solution)/shard_map/ppermute | solution.py:865
  33.4 4.5 %all-to-all-start.1 = ((bf16[4,2,48,1152]{3,2,1,0:T(8,128)(2,1)}), bf16[4,2,48,1152]{3,2,1,0:T(8,128)(2,1)S(1)}, u32[]{:S(2)}, u32[]{:S(2)}) async-start(bf16[4,2,48,1152]{3,2,1,0:T(8,128)(2,1)} %shard_map.575), calls=%async_computation.1 | async-start | bytes 1769472 | tf_op jit(solution)/shard_map/all_to_all | solution.py:935
  38.7 14.8 %shard_map.577 = (f32[512,384]{1,0:T(8,128)}, bf16[512,384]{1,0:T(8,128)(2,1)}, bf16[512,1152]{1,0:T(8,128)(2,1)}, f32[512,128]{1,0:T(8,128)}, bf16[512,384]{1,0...) custom-call(s32[5]{0:T(128)} %stack.221.core.sides, ...), custom_call_target="tpu_custom_call" | custom-call | flops 17250000896 | tf_op jit(solution)/shard_map/pallas_call | solution.py:847
  55.5 4.0 %all-to-all-start.2 = ((bf16[4,2,256,384]{3,2,1,0:T(8,128)(2,1)}), bf16[4,2,256,384]{3,2,1,0:T(8,128)(2,1)S(1)}, u32[]{:S(2)}, u32[]{:S(2)}) async-start(bf16[4,2,256,384]{3,2,1,0:T(8,128)(2,1)} %bitcast.100), calls=%async_computation.2 | async-start | bytes 3145728 | tf_op jit(solution)/shard_map/all_to_all | solution.py:935
  61.1 9.9 %collective-permute-done.4.refs_1_ = bf16[192,1152]{1,0:T(8,128)(2,1)S(1)} collective-permute-done((bf16[192,1152]{1,0:T(8,128)(2,1)S(1)}, bf16[192,1152]{1,0:T(8,128)(2,1)S(1)}, u32[]{:S(2)}, u32[]{:S(2)}) %collective-permute-start.4) | collective-permute-done | bytes 442400 | tf_op jit(solution)/shard_map/ppermute | solution.py:865
  71.0 5.0 %shard_map.571 = (bf16[2,384,768]{2,1,0:T(8,128)(2,1)}, bf16[768,384]{1,0:T(8,128)(2,1)}, f32[16,128]{1,0:T(8,128)}) custom-call(f32[5,48]{1,0:T(8,128)} %refs_4_.5, f32[48,1152]{1,0:T(8,128)} %refs_5_.5, f32[48,384]{1,0:T(8,128)} %refs_6_.5, f32[9,48]{1,0:T(8,128)} %bitcast.181, f32[48,3072]{1,0:T(8,128)} %refs_8_.5, f32[192,384]{1,0:T(8,128)} %refs_9_.3, ...), custom_call_target="tpu_custom_call" | custom-call | flops 5750000128 | tf_op jit(solution)/shard_map/pallas_call | solution.py:1271
  79.0 2.9 shard_map.578
  83.1 9.6 %shard_map.579 = s16[4,2,272,384]{3,2,1,0:T(8,128)(2,1)} custom-call(s32[5]{0:T(128)} %stack.221.core.sides, bf16[4,2,256,384]{3,2,1,0:T(8,128)(2,1)} %copy-done.1, bf16[2,384,768]{2,1,0:T(8,128)(2,1)} %get-tuple-element.162.gate_up, bf16[768,384]{1,0:T(8,128)(2,1)} %get-tuple-element.163.down, bf16[2,384,768]{2,1,0:T(8,128)(2,1)} %get-tuple-element.166.gate_up_far, ...), custom_call_target="tpu_custom_call" | custom-call | flops 11500000256 | tf_op jit(solution)/shard_map/pallas_call | solution.py:1390
  92.8 4.0 %all-to-all-start.3 = ((s16[4,2,272,384]{3,2,1,0:T(8,128)(2,1)}), s16[4,2,272,384]{3,2,1,0:T(8,128)(2,1)S(1)}, u32[]{:S(2)}, u32[]{:S(2)}) async-start(s16[4,2,272,384]{3,2,1,0:T(8,128)(2,1)} %shard_map.579), calls=%async_computation.3 | async-start | bytes 3342336 | tf_op jit(solution)/shard_map/all_to_all | solution.py:935
  103.1 4.3 %shard_map.580 = (bf16[384,3072]{1,0:T(8,128)(2,1)}, bf16[1536,384]{1,0:T(8,128)(2,1)}) custom-call(s32[5]{0:T(128)} %stack.221.core.sides, bf16[384,1152]{1,0:T(8,128)(2,1)} %bitcast.104, bf16[384,1152]{1,0:T(8,128)(2,1)} %bitcast.15.refs_1_, bf16[384,1152]{1,0:T(8,128)(2,1)} %bitcast.16.refs_2_, bf16[384,1152]{1,0:T(8,128)(2,1)} %bitcast.17.refs_3_), custom_call_target="tpu_custom_call" | custom-call | flops 4944999936 | tf_op jit(solution)/shard_map/pallas_call | solution.py:847
  107.5 5.7 %shard_map.581.shared = f32[512,384]{1,0:T(8,128)} custom-call(bf16[512,384]{1,0:T(8,128)(2,1)} %get-tuple-element.169.second, bf16[384,3072]{1,0:T(8,128)(2,1)} %get-tuple-element.172.gate_w.lift_w, bf16[384,3072]{1,0:T(8,128)(2,1)} %get-tuple-element.172.gate_w.lift_w, bf16[1536,384]{1,0:T(8,128)(2,1)} %get-tuple-element.173.down_w), custom_call_target="tpu_custom_call" | custom-call | flops 6670000128 | tf_op jit(solution)/shard_map/pallas_call | solution.py:1441
  113.2 4.2 %all-to-all-done.3 = s16[4,2,272,384]{3,2,1,0:T(8,128)(2,1)S(1)} async-done(((s16[4,2,272,384]{3,2,1,0:T(8,128)(2,1)}), s16[4,2,272,384]{3,2,1,0:T(8,128)(2,1)S(1)}, u32[]{:S(2)}, u32[]{:S(2)}) %all-to-all-start.3) | async-done | bytes 1671200 | tf_op jit(solution)/shard_map/all_to_all | solution.py:935
  118.5 10.5 %shard_map.582 = (f32[512,384]{1,0:T(8,128)}, bf16[512,384]{1,0:T(8,128)(2,1)}, bf16[2048,384]{1,0:T(8,128)(2,1)}, bf16[512,128]{1,0:T(8,128)(2,1)}, f32[384,128...) custom-call(s16[8,272,384]{2,1,0:T(8,128)(2,1)} %bitcast.98, f32[512,128]{1,0:T(8,128)} %get-tuple-element.154.known, ...), custom_call_target="tpu_custom_call" | custom-call | flops 13109999616 | tf_op jit(solution)/shard_map/pallas_call | solution.py:847
  129.1 3.7 %all-to-all-start.4 = ((bf16[4,2,256,384]{3,2,1,0:T(8,128)(2,1)}), bf16[4,2,256,384]{3,2,1,0:T(8,128)(2,1)S(1)}, u32[]{:S(2)}, u32[]{:S(2)}) async-start(bf16[4,2,256,384]{3,2,1,0:T(8,128)(2,1)} %bitcast.101), calls=%async_computation.4 | async-start | bytes 3145728 | tf_op jit(solution)/shard_map/all_to_all | solution.py:935
  132.8 12.0 %shard_map.583 = (f32[512,384]{1,0:T(8,128)}, f32[2,384,768]{2,1,0:T(8,128)}, f32[2,384,384]{2,1,0:T(8,128)}, f32[2,384,384]{2,1,0:T(8,128)}, f32[2,384,384]{2,1,0:T(8,128)}, /*index=5*/f32[2,384,384]{2,1,0:T(8,128)}) custom-call(s32[5]{0:T(128)} %stack.221.core.sides, bf16[512,384]{1,0:T(8,128)(2,1)} %get-tuple-element.169.second, ...), custom_call_target="tpu_custom_call" | custom-call | flops 16099999744 | tf_op jit(solution)/shard_map/pallas_call | solution.py:1499
  145.4 2.5 collective-permute-done.12.in_even
  152.3 5.3 %shard_map.584 = (f32[384,1152]{1,0:T(8,128)}, s16[384,1280]{1,0:T(8,128)(2,1)}) custom-call(f32[2,384,768]{2,1,0:T(8,128)} %get-tuple-element.183.in_keep, f32[2,384,384]{2,1,0:T(8,128)} %copy-done.19, f32[2,384,384]{2,1,0:T(8,128)} %copy-done.21, f32[2,384,384]{2,1,0:T(8,128)} %get-tuple-element.186.out_keep, f32[2,384,384]{2,1,0:T(8,128)} %copy-done.22), custom_call_target="tpu_custom_call" | custom-call | flops 6095000064 | tf_op jit(solution)/shard_map/pallas_call | solution.py:1535
  159.3 19.5 %shard_map.585 = (bf16[4,2,256,384]{3,2,1,0:T(8,128)(2,1)}, f32[2,384,768]{2,1,0:T(8,128)}, f32[2,384,768]{2,1,0:T(8,128)}, f32[2,384,384]{2,1,0:T(8,128)}, f32[2,384,384]{2,1,0:T(8,128)}) custom-call(s32[5]{0:T(128)} %stack.221.core.sides, bf16[4,2,256,384]{3,2,1,0:T(8,128)(2,1)} %copy-done.1, bf16[4,2,256,384]{3,2,1,0:T(8,128)(2,1)} %copy-done.2, ...), custom_call_target="tpu_custom_call" | custom-call | flops 22424999936 | tf_op jit(solution)/shard_map/pallas_call | solution.py:1553
  178.9 2.8 collective-permute-done.15.other
  182.6 4.3 %all-to-all-start.5 = ((bf16[4,2,256,384]{3,2,1,0:T(8,128)(2,1)}), bf16[4,2,256,384]{3,2,1,0:T(8,128)(2,1)S(1)}, u32[]{:S(2)}, u32[]{:S(2)}) async-start(bf16[4,2,256,384]{3,2,1,0:T(8,128)(2,1)} %get-tuple-element.191), calls=%async_computation.5 | async-start | bytes 3145728 | tf_op jit(solution)/shard_map/all_to_all | solution.py:935
  187.5 3.0 collective-permute-done.11
  192.0 4.6 %shard_map.587 = (f32[2,192,1152]{2,1,0:T(8,128)}, s16[2,192,1280]{2,1,0:T(8,128)(2,1)}) custom-call(s32[5]{0:T(128)} %stack.221.core.sides, f32[2,384,768]{2,1,0:T(8,128)} %get-tuple-element.193.in_keep, f32[2,384,768]{2,1,0:T(8,128)} %collective-permute-done.16.in_other, f32[2,384,384]{2,1,0:T(8,128)} %get-tuple-element.195.out_keep, f32[2,384,384]{2,1,0:T(8,128)} %copy-done.20), custom_call_target="tpu_custom_call" | custom-call | flops 5289999872 | tf_op jit(solution)/shard_map/pallas_call | solution.py:1600
  197.1 4.1 %shard_map.586 = s16[384,1280]{1,0:T(8,128)(2,1)} custom-call(f32[384,1152]{1,0:T(8,128)} %get-tuple-element.192.keep, s16[384,1280]{1,0:T(8,128)(2,1)} %copy-done.23), custom_call_target="tpu_custom_call" | custom-call | flops 5059999744 | tf_op jit(solution)/shard_map/pallas_call | solution.py:847
  201.3 4.3 %all-to-all-done.5 = bf16[4,2,256,384]{3,2,1,0:T(8,128)(2,1)S(1)} async-done(((bf16[4,2,256,384]{3,2,1,0:T(8,128)(2,1)}), bf16[4,2,256,384]{3,2,1,0:T(8,128)(2,1)S(1)}, u32[]{:S(2)}, u32[]{:S(2)}) %all-to-all-start.5) | async-done | bytes 1572896 | tf_op jit(solution)/shard_map/all_to_all | solution.py:935
  205.6 3.9 %all-to-all-start.6 = ((s16[4,2,48,1280]{3,2,1,0:T(8,128)(2,1)}), s16[4,2,48,1280]{3,2,1,0:T(8,128)(2,1)S(1)}, u32[]{:S(2)}, u32[]{:S(2)}) async-start(s16[4,2,48,1280]{3,2,1,0:T(8,128)(2,1)} %bitcast.103), calls=%async_computation.6 | async-start | bytes 1966080 | tf_op jit(solution)/shard_map/all_to_all | solution.py:935
  209.6 5.9 %shard_map.588 = (f32[512,384]{1,0:T(8,128)}, bf16[512,384]{1,0:T(8,128)(2,1)}, f32[384,384]{1,0:T(8,128)}, f32[1,384]{1,0:T(1,128)}, f32[384,128]{1,0:T(8,128)}) custom-call(bf16[2048,384]{1,0:T(8,128)(2,1)} %bitcast.99, f32[512,128]{1,0:T(8,128)} %get-tuple-element.154.known, f32[512,384]{1,0:T(8,128)} %get-tuple-element.182.second_slope, ...), custom_call_target="tpu_custom_call" | custom-call | flops 6899999744 | tf_op jit(solution)/shard_map/pallas_call | solution.py:847
  215.4 4.3 %collective-permute-done.18.codes = s16[2,192,1280]{2,1,0:T(8,128)(2,1)S(1)} collective-permute-done((s16[2,192,1280]{2,1,0:T(8,128)(2,1)}, s16[2,192,1280]{2,1,0:T(8,128)(2,1)S(1)}, u32[]{:S(2)}, u32[]{:S(2)}) %collective-permute-start.18) | collective-permute-done | bytes 983072 | tf_op jit(solution)/shard_map/ppermute | solution.py:865
  220.7 3.4 shard_map.589
  224.1 5.4 %collective-permute-start.19 = (s16[192,1280]{1,0:T(8,128)(2,1)}, s16[192,1280]{1,0:T(8,128)(2,1)S(1)}, u32[]{:S(2)}, u32[]{:S(2)}) collective-permute-start(s16[192,1280]{1,0:T(8,128)(2,1)} %get-tuple-element.205), channel_id=1, source_target_pairs={{0,4},{1,5},{2,6},{3,7},{4,0},{5,1},{6,2},{7,3},{8,12},{9,13},{10,... | collective-permute-start | bytes 1474568 | tf_op jit(solution)/shard_map/ppermute | solution.py:865
  229.6 18.3 %shard_map.590 = (f32[384,896]{1,0:T(8,128)}, f32[384,896]{1,0:T(8,128)}) custom-call(s32[5]{0:T(128)} %stack.221.core.sides, bf16[512,384]{1,0:T(8,128)(2,1)} %get-tuple-element.206.mixed_slope, bf16[512,1152]{1,0:T(8,128)(2,1)} %get-tuple-element.207.qkv, f32[512,128]{1,0:T(8,128)} %get-tuple-element.208.log_total, f32[512,128]{1,0:T(8,128)} %get-tuple-element.154.known, ...), custom_call_target="tpu_custom_call" | custom-call | flops 21159999488 | tf_op jit(solution)/shard_map/pallas_call | solution.py:847
  250.1 2.7 shard_map.591
  254.5 3.3 shard_map.592
  257.8 4.9 %collective-permute-start.23 = (s16[96,1024]{1,0:T(8,128)(2,1)}, s16[96,1024]{1,0:T(8,128)(2,1)S(1)}, u32[]{:S(2)}, u32[]{:S(2)}) collective-permute-start(s16[96,1024]{1,0:T(8,128)(2,1)} %get-tuple-element.229), channel_id=1, source_target_pairs={{0,3},{1,2},{2,1},{3,0},{4,7},{5,6},{6,5},{7,4},{8,11},{9,10},{10,... | collective-permute-start | bytes 589832 | tf_op jit(solution)/shard_map/ppermute | solution.py:865
  263.2 2.8 shard_map.596.refs_2_.refs_37_
  268.6 3.0 collective-permute-done.22.refs_2_
  273.0 2.7 shard_map.593
  279.9 3.6 %collective-permute-done.24.code = s16[48,1024]{1,0:T(8,128)(2,1)S(1)} collective-permute-done((s16[48,1024]{1,0:T(8,128)(2,1)}, s16[48,1024]{1,0:T(8,128)(2,1)S(1)}, u32[]{:S(2)}, u32[]{:S(2)}) %collective-permute-start.24) | collective-permute-done | bytes 98336 | tf_op jit(solution)/shard_map/ppermute | solution.py:865
  287.6 4.1 %collective-permute-done.25.last_other = f32[48,896]{1,0:T(8,128)S(1)} collective-permute-done((f32[48,896]{1,0:T(8,128)}, f32[48,896]{1,0:T(8,128)S(1)}, u32[]{:S(2)}, u32[]{:S(2)}) %collective-permute-start.25) | collective-permute-done | bytes 172064 | tf_op jit(solution)/shard_map/ppermute | solution.py:865
  292.3 3.2 shard_map.597
  298.7 2.4 collective-permute-done.30
  308.6 14.5 %shard_map.598 = (f32[5,48]{1,0:T(8,128)}, f32[48,1152]{1,0:T(8,128)}, f32[48,384]{1,0:T(8,128)}, f32[9,48]{1,0:T(8,128)}, f32[48,3072]{1,0:T(8,128)}, /*index=5...) custom-call(s32[5]{0:T(128)} %stack.221.core.sides, ...), custom_call_target="tpu_custom_call" | custom-call | flops 19549999104 | tf_op jit(solution)/shard_map/pallas_call | solution.py:1757
  335.4 6.7 %shard_map.599 = (f32[5,48]{1,0:T(8,128)}, f32[48,1152]{1,0:T(8,128)}, f32[48,384]{1,0:T(8,128)}, f32[9,48]{1,0:T(8,128)}, f32[48,3072]{1,0:T(8,128)}, /*index=5...) custom-call(s32[5]{0:T(128)} %stack.221.core.sides, ...), custom_call_target="tpu_custom_call" | custom-call | flops 8049999872 | tf_op jit(solution)/shard_map/pallas_call | solution.py:1776
  (217 shorter events, 75.4 us)
Async XLA Ops:
  3.2 8.6 %collective-permute-start = (bf16[48,896]{1,0:T(8,128)(2,1)}, bf16[48,896]{1,0:T(8,128)(2,1)S(1)}, u32[]{:S(2)}, u32[]{:S(2)}) collective-permute-start(bf16[48,896]{1,0:T(8,128)(2,1)} %bitcast.176), channel_id=1, source_target_pairs={{0,4},{1,5},{2,6},{3,7},{4,0},{5,1},{6,2},{7,3},{8,12},{9,13},{10,... | collective-permute-start | bytes 258056 | tf_op jit(solution)/shard_map/ppermute | solution.py:865
  14.3 15.6 %all-to-all-start = ((bf16[4,2,48,896]{3,2,1,0:T(8,128)(2,1)}), bf16[4,2,48,896]{3,2,1,0:T(8,128)(2,1)S(1)}, u32[]{:S(2)}, u32[]{:S(2)}) async-start(bf16[4,2,48,896]{3,2,1,0:T(8,128)(2,1)} %shard_map.573), calls=%async_computation | async-start | bytes 1376256 | tf_op jit(solution)/shard_map/all_to_all | solution.py:935
  18.0 9.4 %collective-permute-start.1 = (bf16[48,1152]{1,0:T(8,128)(2,1)S(1)}, bf16[48,1152]{1,0:T(8,128)(2,1)S(1)}, u32[]{:S(2)}, u32[]{:S(2)}) collective-permute-start(bf16[48,1152]{1,0:T(8,128)(2,1)S(1)} %fusion.own), channel_id=1, source_target_pairs={{0,4},{1,5},{2,6},{3,7},{4,0},{5,1},{6,2},{7,3},{8,12},{9,13},{10,... | collective-permute-start | bytes 331784 | tf_op jit(solution)/shard_map/ppermute | solution.py:865
  30.0 7.9 %collective-permute-start.2 = (bf16[384,896]{1,0:T(8,128)(2,1)S(1)}, bf16[384,896]{1,0:T(8,128)(2,1)S(1)}, u32[]{:S(2)}, u32[]{:S(2)}) collective-permute-start(bf16[384,896]{1,0:T(8,128)(2,1)S(1)} %bitcast.105), channel_id=1, source_target_pairs={{0,8},{8,0},{16,24},{24,16},{1,9},{9,1},{17,25},{25,17},{2,10},{10... | collective-permute-start | bytes 2064392 | tf_op jit(solution)/shard_map/ppermute | solution.py:865
  30.0 24.0 %collective-permute-start.3 = (bf16[192,1152]{1,0:T(8,128)(2,1)}, bf16[192,1152]{1,0:T(8,128)(2,1)S(1)}, u32[]{:S(2)}, u32[]{:S(2)}) collective-permute-start(bf16[192,1152]{1,0:T(8,128)(2,1)} %shard_map.576), channel_id=1, source_target_pairs={{0,4},{1,5},{2,6},{3,7},{4,0},{5,1},{6,2},{7,3},{8,12},{9,13},{10,... | collective-permute-start | bytes 1327112 | tf_op jit(solution)/shard_map/ppermute | solution.py:865
  33.4 22.1 %all-to-all-start.1 = ((bf16[4,2,48,1152]{3,2,1,0:T(8,128)(2,1)}), bf16[4,2,48,1152]{3,2,1,0:T(8,128)(2,1)S(1)}, u32[]{:S(2)}, u32[]{:S(2)}) async-start(bf16[4,2,48,1152]{3,2,1,0:T(8,128)(2,1)} %shard_map.575), calls=%async_computation.1 | async-start | bytes 1769472 | tf_op jit(solution)/shard_map/all_to_all | solution.py:935
  55.5 26.4 %all-to-all-start.2 = ((bf16[4,2,256,384]{3,2,1,0:T(8,128)(2,1)}), bf16[4,2,256,384]{3,2,1,0:T(8,128)(2,1)S(1)}, u32[]{:S(2)}, u32[]{:S(2)}) async-start(bf16[4,2,256,384]{3,2,1,0:T(8,128)(2,1)} %bitcast.100), calls=%async_computation.2 | async-start | bytes 3145728 | tf_op jit(solution)/shard_map/all_to_all | solution.py:935
  59.5 11.5 %collective-permute-start.4 = (bf16[192,1152]{1,0:T(8,128)(2,1)S(1)}, bf16[192,1152]{1,0:T(8,128)(2,1)S(1)}, u32[]{:S(2)}, u32[]{:S(2)}) collective-permute-start(bf16[192,1152]{1,0:T(8,128)(2,1)S(1)} %collective-permute-done.3.refs_0_), channel_id=1, source_target_pairs={{0,16},{8,24},{16,0},{24,8},{1,17},{9,25},{17,1},{25,9},{2,18},{10... | collective-permute-start | bytes 1327112 | tf_op jit(solution)/shard_map/ppermute | solution.py:865
  61.1 16.5 %collective-permute-start.5 = (bf16[192,1152]{1,0:T(8,128)(2,1)S(1)}, bf16[192,1152]{1,0:T(8,128)(2,1)S(1)}, u32[]{:S(2)}, u32[]{:S(2)}) collective-permute-start(bf16[192,1152]{1,0:T(8,128)(2,1)S(1)} %collective-permute-done.3.refs_0_), channel_id=1, source_target_pairs={{0,8},{8,0},{16,24},{24,16},{1,9},{9,1},{17,25},{25,17},{2,10},{10... | collective-permute-start | bytes 1327112 | tf_op jit(solution)/shard_map/ppermute | solution.py:865
  71.0 6.5 %collective-permute-start.6 = (bf16[192,1152]{1,0:T(8,128)(2,1)S(1)}, bf16[192,1152]{1,0:T(8,128)(2,1)S(1)}, u32[]{:S(2)}, u32[]{:S(2)}) collective-permute-start(bf16[192,1152]{1,0:T(8,128)(2,1)S(1)} %collective-permute-done.4.refs_1_), channel_id=1, source_target_pairs={{0,8},{8,0},{16,24},{24,16},{1,9},{9,1},{17,25},{25,17},{2,10},{10... | collective-permute-start | bytes 1327112 | tf_op jit(solution)/shard_map/ppermute | solution.py:865
  76.0 22.1 %collective-permute-start.7 = (bf16[4,2,48,1152]{3,2,1,0:T(8,128)(2,1)S(1)}, bf16[4,2,48,1152]{3,2,1,0:T(8,128)(2,1)}, u32[]{:S(2)}, u32[]{:S(2)}) collective-permute-start(bf16[4,2,48,1152]{3,2,1,0:T(8,128)(2,1)S(1)} %all-to-all-done.1), channel_id=1, source_target_pairs={{0,16},{8,24},{16,0},{24,8},{1,17},{9,25},{17,1},{25,9},{2,18},{10... | collective-permute-start | bytes 2654216 | tf_op jit(solution)/shard_map/ppermute | solution.py:865
  92.8 24.6 %all-to-all-start.3 = ((s16[4,2,272,384]{3,2,1,0:T(8,128)(2,1)}), s16[4,2,272,384]{3,2,1,0:T(8,128)(2,1)S(1)}, u32[]{:S(2)}, u32[]{:S(2)}) async-start(s16[4,2,272,384]{3,2,1,0:T(8,128)(2,1)} %shard_map.579), calls=%async_computation.3 | async-start | bytes 3342336 | tf_op jit(solution)/shard_map/all_to_all | solution.py:935
  98.1 5.1 %collective-permute-start.9 = (bf16[4,2,48,1152]{3,2,1,0:T(8,128)(2,1)}, bf16[4,2,48,1152]{3,2,1,0:T(8,128)(2,1)}, u32[]{:S(2)}, u32[]{:S(2)}) collective-permute-start(bf16[4,2,48,1152]{3,2,1,0:T(8,128)(2,1)} %collective-permute-done.7), channel_id=1, source_target_pairs={{0,8},{8,0},{16,24},{24,16},{1,9},{9,1},{17,25},{25,17},{2,10},{10... | collective-permute-start | bytes 2654216 | tf_op jit(solution)/shard_map/ppermute | solution.py:865
  98.1 5.1 %collective-permute-start.8 = (bf16[4,2,48,1152]{3,2,1,0:T(8,128)(2,1)S(1)}, bf16[4,2,48,1152]{3,2,1,0:T(8,128)(2,1)}, u32[]{:S(2)}, u32[]{:S(2)}) collective-permute-start(bf16[4,2,48,1152]{3,2,1,0:T(8,128)(2,1)S(1)} %all-to-all-done.1), channel_id=1, source_target_pairs={{0,8},{8,0},{16,24},{24,16},{1,9},{9,1},{17,25},{25,17},{2,10},{10... | collective-permute-start | bytes 2654216 | tf_op jit(solution)/shard_map/ppermute | solution.py:865
  98.9 3.6 %collective-permute-start.10 = (f32[1,128]{1,0:T(1,128)S(1)}, f32[1,128]{1,0:T(1,128)S(1)}, u32[]{:S(2)}, u32[]{:S(2)}) collective-permute-start(f32[1,128]{1,0:T(1,128)S(1)} %copy-done.15), channel_id=1, source_target_pairs={{0,16},{8,24},{16,0},{24,8},{1,17},{9,25},{17,1},{25,9},{2,18},{10... | collective-permute-start | bytes 1544 | tf_op jit(solution)/shard_map/ppermute | solution.py:865
  129.1 29.1 %all-to-all-start.4 = ((bf16[4,2,256,384]{3,2,1,0:T(8,128)(2,1)}), bf16[4,2,256,384]{3,2,1,0:T(8,128)(2,1)S(1)}, u32[]{:S(2)}, u32[]{:S(2)}) async-start(bf16[4,2,256,384]{3,2,1,0:T(8,128)(2,1)} %bitcast.101), calls=%async_computation.4 | async-start | bytes 3145728 | tf_op jit(solution)/shard_map/all_to_all | solution.py:935
  144.9 4.7 %collective-permute-start.13 = (f32[2,384,384]{2,1,0:T(8,128)}, f32[2,384,384]{2,1,0:T(8,128)S(1)}, u32[]{:S(2)}, u32[]{:S(2)}) collective-permute-start(f32[2,384,384]{2,1,0:T(8,128)} %get-tuple-element.185), channel_id=1, source_target_pairs={{0,8},{8,0},{16,24},{24,16},{1,9},{9,1},{17,25},{25,17},{2,10},{10... | collective-permute-start | bytes 3538952 | tf_op jit(solution)/shard_map/ppermute | solution.py:865
  145.4 5.9 %collective-permute-start.14 = (f32[2,384,384]{2,1,0:T(8,128)}, f32[2,384,384]{2,1,0:T(8,128)S(1)}, u32[]{:S(2)}, u32[]{:S(2)}) collective-permute-start(f32[2,384,384]{2,1,0:T(8,128)} %get-tuple-element.187), channel_id=1, source_target_pairs={{0,8},{8,0},{16,24},{24,16},{1,9},{9,1},{17,25},{25,17},{2,10},{10... | collective-permute-start | bytes 3538952 | tf_op jit(solution)/shard_map/ppermute | solution.py:865
  157.6 24.0 %collective-permute-start.15 = (s16[384,1280]{1,0:T(8,128)(2,1)}, s16[384,1280]{1,0:T(8,128)(2,1)S(1)}, u32[]{:S(2)}, u32[]{:S(2)}) collective-permute-start(s16[384,1280]{1,0:T(8,128)(2,1)} %get-tuple-element.188), channel_id=1, source_target_pairs={{0,16},{8,24},{16,0},{24,8},{1,17},{9,25},{17,1},{25,9},{2,18},{10... | collective-permute-start | bytes 2949128 | tf_op jit(solution)/shard_map/ppermute | solution.py:865
  178.9 12.2 %collective-permute-start.16 = (f32[2,384,768]{2,1,0:T(8,128)}, f32[2,384,768]{2,1,0:T(8,128)}, u32[]{:S(2)}, u32[]{:S(2)}) collective-permute-start(f32[2,384,768]{2,1,0:T(8,128)} %get-tuple-element.194), channel_id=1, source_target_pairs={{0,8},{8,0},{16,24},{24,16},{1,9},{9,1},{17,25},{25,17},{2,10},{10... | collective-permute-start | bytes 7077896 | tf_op jit(solution)/shard_map/ppermute | solution.py:865
  182.6 23.0 %all-to-all-start.5 = ((bf16[4,2,256,384]{3,2,1,0:T(8,128)(2,1)}), bf16[4,2,256,384]{3,2,1,0:T(8,128)(2,1)S(1)}, u32[]{:S(2)}, u32[]{:S(2)}) async-start(bf16[4,2,256,384]{3,2,1,0:T(8,128)(2,1)} %get-tuple-element.191), calls=%async_computation.5 | async-start | bytes 3145728 | tf_op jit(solution)/shard_map/all_to_all | solution.py:935
  186.9 4.1 %collective-permute-start.17 = (f32[2,384,384]{2,1,0:T(8,128)S(1)}, f32[2,384,384]{2,1,0:T(8,128)S(1)}, u32[]{:S(2)}, u32[]{:S(2)}) collective-permute-start(f32[2,384,384]{2,1,0:T(8,128)S(1)} %copy-done.18), channel_id=1, source_target_pairs={{0,8},{8,0},{16,24},{24,16},{1,9},{9,1},{17,25},{25,17},{2,10},{10... | collective-permute-start | bytes 3538952 | tf_op jit(solution)/shard_map/ppermute | solution.py:865
  186.9 3.6 %collective-permute-start.11 = (f32[1,128]{1,0:T(1,128)S(1)}, f32[1,128]{1,0:T(1,128)S(1)}, u32[]{:S(2)}, u32[]{:S(2)}) collective-permute-start(f32[1,128]{1,0:T(1,128)S(1)} %copy-done.54), channel_id=1, source_target_pairs={{0,16},{8,24},{16,0},{24,8},{1,17},{9,25},{17,1},{25,9},{2,18},{10... | collective-permute-start | bytes 1544 | tf_op jit(solution)/shard_map/ppermute | solution.py:865
  196.6 23.2 %collective-permute-start.18 = (s16[2,192,1280]{2,1,0:T(8,128)(2,1)}, s16[2,192,1280]{2,1,0:T(8,128)(2,1)S(1)}, u32[]{:S(2)}, u32[]{:S(2)}) collective-permute-start(s16[2,192,1280]{2,1,0:T(8,128)(2,1)} %get-tuple-element.197), channel_id=1, source_target_pairs={{0,16},{8,24},{16,0},{24,8},{1,17},{9,25},{17,1},{25,9},{2,18},{10... | collective-permute-start | bytes 2949128 | tf_op jit(solution)/shard_map/ppermute | solution.py:865
  205.6 42.3 %all-to-all-start.6 = ((s16[4,2,48,1280]{3,2,1,0:T(8,128)(2,1)}), s16[4,2,48,1280]{3,2,1,0:T(8,128)(2,1)S(1)}, u32[]{:S(2)}, u32[]{:S(2)}) async-start(s16[4,2,48,1280]{3,2,1,0:T(8,128)(2,1)} %bitcast.103), calls=%async_computation.6 | async-start | bytes 1966080 | tf_op jit(solution)/shard_map/all_to_all | solution.py:935
  224.1 25.9 %collective-permute-start.19 = (s16[192,1280]{1,0:T(8,128)(2,1)}, s16[192,1280]{1,0:T(8,128)(2,1)S(1)}, u32[]{:S(2)}, u32[]{:S(2)}) collective-permute-start(s16[192,1280]{1,0:T(8,128)(2,1)} %get-tuple-element.205), channel_id=1, source_target_pairs={{0,4},{1,5},{2,6},{3,7},{4,0},{5,1},{6,2},{7,3},{8,12},{9,13},{10,... | collective-permute-start | bytes 1474568 | tf_op jit(solution)/shard_map/ppermute | solution.py:865
  250.1 3.3 collective-permute-start.20
  252.8 24.1 %collective-permute-start.26 = (s16[48,1280]{1,0:T(8,128)(2,1)}, s16[48,1280]{1,0:T(8,128)(2,1)S(1)}, u32[]{:S(2)}, u32[]{:S(2)}) collective-permute-start(s16[48,1280]{1,0:T(8,128)(2,1)} %get-tuple-element.219), channel_id=1, source_target_pairs={{0,4},{1,5},{2,6},{3,7},{4,0},{5,1},{6,2},{7,3},{8,12},{9,13},{10,... | collective-permute-start | bytes 368648 | tf_op jit(solution)/shard_map/ppermute | solution.py:865
  257.8 10.9 %collective-permute-start.23 = (s16[96,1024]{1,0:T(8,128)(2,1)}, s16[96,1024]{1,0:T(8,128)(2,1)S(1)}, u32[]{:S(2)}, u32[]{:S(2)}) collective-permute-start(s16[96,1024]{1,0:T(8,128)(2,1)} %get-tuple-element.229), channel_id=1, source_target_pairs={{0,3},{1,2},{2,1},{3,0},{4,7},{5,6},{6,5},{7,4},{8,11},{9,10},{10,... | collective-permute-start | bytes 589832 | tf_op jit(solution)/shard_map/ppermute | solution.py:865
  262.7 8.9 %collective-permute-start.22 = (s16[96,1024]{1,0:T(8,128)(2,1)}, s16[96,1024]{1,0:T(8,128)(2,1)S(1)}, u32[]{:S(2)}, u32[]{:S(2)}) collective-permute-start(s16[96,1024]{1,0:T(8,128)(2,1)} %get-tuple-element.227), channel_id=1, source_target_pairs={{0,2},{1,3},{2,0},{3,1},{4,6},{5,7},{6,4},{7,5},{8,10},{9,11},{10,... | collective-permute-start | bytes 589832 | tf_op jit(solution)/shard_map/ppermute | solution.py:865
  262.7 9.5 %collective-permute-start.21 = (s16[96,1024]{1,0:T(8,128)(2,1)}, s16[96,1024]{1,0:T(8,128)(2,1)S(1)}, u32[]{:S(2)}, u32[]{:S(2)}) collective-permute-start(s16[96,1024]{1,0:T(8,128)(2,1)} %get-tuple-element.225), channel_id=1, source_target_pairs={{0,1},{1,0},{2,3},{3,2},{4,5},{5,4},{6,7},{7,6},{8,9},{9,8},{10,11... | collective-permute-start | bytes 589832 | tf_op jit(solution)/shard_map/ppermute | solution.py:865
  266.0 21.1 %collective-permute-start.28 = (s16[192,1280]{1,0:T(8,128)(2,1)}, s16[192,1280]{1,0:T(8,128)(2,1)S(1)}, u32[]{:S(2)}, u32[]{:S(2)}) collective-permute-start(s16[192,1280]{1,0:T(8,128)(2,1)} %shard_map.596.refs_2_.refs_37_), channel_id=1, source_target_pairs={{0,16},{8,24},{16,0},{24,8},{1,17},{9,25},{17,1},{25,9},{2,18},{10... | collective-permute-start | bytes 1474568 | tf_op jit(solution)/shard_map/ppermute | solution.py:865
  275.7 7.9 %collective-permute-start.24 = (s16[48,1024]{1,0:T(8,128)(2,1)}, s16[48,1024]{1,0:T(8,128)(2,1)S(1)}, u32[]{:S(2)}, u32[]{:S(2)}) collective-permute-start(s16[48,1024]{1,0:T(8,128)(2,1)} %get-tuple-element.231), channel_id=1, source_target_pairs={{0,4},{1,5},{2,6},{3,7},{4,0},{5,1},{6,2},{7,3},{8,12},{9,13},{10,... | collective-permute-start | bytes 294920 | tf_op jit(solution)/shard_map/ppermute | solution.py:865
  279.4 7.2 %collective-permute-start.27 = (f32[48,1152]{1,0:T(8,128)}, f32[48,1152]{1,0:T(8,128)S(1)}, u32[]{:S(2)}, u32[]{:S(2)}) collective-permute-start(f32[48,1152]{1,0:T(8,128)} %shard_map.595.refs_0_.refs_33_), channel_id=1, source_target_pairs={{0,16},{8,24},{16,0},{24,8},{1,17},{9,25},{17,1},{25,9},{2,18},{10... | collective-permute-start | bytes 663560 | tf_op jit(solution)/shard_map/ppermute | solution.py:865
  286.0 5.6 %collective-permute-start.25 = (f32[48,896]{1,0:T(8,128)}, f32[48,896]{1,0:T(8,128)S(1)}, u32[]{:S(2)}, u32[]{:S(2)}) collective-permute-start(f32[48,896]{1,0:T(8,128)} %shard_map.594.last), channel_id=1, source_target_pairs={{0,16},{8,24},{16,0},{24,8},{1,17},{9,25},{17,1},{25,9},{2,18},{10... | collective-permute-start | bytes 516104 | tf_op jit(solution)/shard_map/ppermute | solution.py:865
  286.5 14.6 %collective-permute-start.35 = (f32[48,1152]{1,0:T(8,128)S(1)}, f32[48,1152]{1,0:T(8,128)S(1)}, u32[]{:S(2)}, u32[]{:S(2)}) collective-permute-start(f32[48,1152]{1,0:T(8,128)S(1)} %copy-done.35), channel_id=1, source_target_pairs={{0,8},{8,0},{16,24},{24,16},{1,9},{9,1},{17,25},{25,17},{2,10},{10... | collective-permute-start | bytes 663560 | tf_op jit(solution)/shard_map/ppermute | solution.py:865
  286.6 16.7 %collective-permute-start.36 = (f32[48,1152]{1,0:T(8,128)S(1)}, f32[48,1152]{1,0:T(8,128)S(1)}, u32[]{:S(2)}, u32[]{:S(2)}) collective-permute-start(f32[48,1152]{1,0:T(8,128)S(1)} %collective-permute-done.27.refs_1_.refs_34_), channel_id=1, source_target_pairs={{0,8},{8,0},{16,24},{24,16},{1,9},{9,1},{17,25},{25,17},{2,10},{10... | collective-permute-start | bytes 663560 | tf_op jit(solution)/shard_map/ppermute | solution.py:865
  287.1 16.2 %collective-permute-start.37 = (s16[192,1280]{1,0:T(8,128)(2,1)S(1)}, s16[192,1280]{1,0:T(8,128)(2,1)S(1)}, u32[]{:S(2)}, u32[]{:S(2)}) collective-permute-start(s16[192,1280]{1,0:T(8,128)(2,1)S(1)} %copy-done.26), channel_id=1, source_target_pairs={{0,8},{8,0},{16,24},{24,16},{1,9},{9,1},{17,25},{25,17},{2,10},{10... | collective-permute-start | bytes 1474568 | tf_op jit(solution)/shard_map/ppermute | solution.py:865
  287.1 20.6 %collective-permute-start.38 = (s16[192,1280]{1,0:T(8,128)(2,1)S(1)}, s16[192,1280]{1,0:T(8,128)(2,1)S(1)}, u32[]{:S(2)}, u32[]{:S(2)}) collective-permute-start(s16[192,1280]{1,0:T(8,128)(2,1)S(1)} %collective-permute-done.28.refs_3_.refs_38_), channel_id=1, source_target_pairs={{0,8},{8,0},{16,24},{24,16},{1,9},{9,1},{17,25},{25,17},{2,10},{10... | collective-permute-start | bytes 1474568 | tf_op jit(solution)/shard_map/ppermute | solution.py:865
  297.6 3.6 %collective-permute-start.30 = (f32[2,128]{1,0:T(2,128)S(1)}, f32[2,128]{1,0:T(2,128)S(1)}, u32[]{:S(2)}, u32[]{:S(2)}) collective-permute-start(f32[2,128]{1,0:T(2,128)S(1)} %add.39), channel_id=1, source_target_pairs={{0,1},{1,0},{2,3},{3,2},{4,5},{5,4},{6,7},{7,6},{8,9},{9,8},{10,11... | collective-permute-start | bytes 3080 | tf_op jit(solution)/shard_map/ppermute | solution.py:865
  301.1 6.6 %collective-permute-start.34 = (f32[48,896]{1,0:T(8,128)}, f32[48,896]{1,0:T(8,128)S(1)}, u32[]{:S(2)}, u32[]{:S(2)}) collective-permute-start(f32[48,896]{1,0:T(8,128)} %get-tuple-element.236.refs_31_), channel_id=1, source_target_pairs={{0,8},{8,0},{16,24},{24,16},{1,9},{9,1},{17,25},{25,17},{2,10},{10... | collective-permute-start | bytes 516104 | tf_op jit(solution)/shard_map/ppermute | solution.py:865
  301.2 5.4 %collective-permute-start.33 = (f32[2,128]{1,0:T(2,128)S(1)}, f32[2,128]{1,0:T(2,128)S(1)}, u32[]{:S(2)}, u32[]{:S(2)}) collective-permute-start(f32[2,128]{1,0:T(2,128)S(1)} %add.40.refs_0_), channel_id=1, source_target_pairs={{0,6},{1,7},{2,4},{3,5},{4,2},{5,3},{6,0},{7,1},{8,14},{9,15},{10,... | collective-permute-start | bytes 3080 | tf_op jit(solution)/shard_map/ppermute | solution.py:865
  303.3 4.5 %collective-permute-start.32 = (f32[2,128]{1,0:T(2,128)S(1)}, f32[2,128]{1,0:T(2,128)S(1)}, u32[]{:S(2)}, u32[]{:S(2)}) collective-permute-start(f32[2,128]{1,0:T(2,128)S(1)} %add.40.refs_0_), channel_id=1, source_target_pairs={{0,4},{1,5},{2,6},{3,7},{4,0},{5,1},{6,2},{7,3},{8,12},{9,13},{10,... | collective-permute-start | bytes 3080 | tf_op jit(solution)/shard_map/ppermute | solution.py:865
  303.3 4.4 %collective-permute-start.31 = (f32[2,128]{1,0:T(2,128)S(1)}, f32[2,128]{1,0:T(2,128)S(1)}, u32[]{:S(2)}, u32[]{:S(2)}) collective-permute-start(f32[2,128]{1,0:T(2,128)S(1)} %add.40.refs_0_), channel_id=1, source_target_pairs={{0,2},{1,3},{2,0},{3,1},{4,6},{5,7},{6,4},{7,5},{8,10},{9,11},{10,... | collective-permute-start | bytes 3080 | tf_op jit(solution)/shard_map/ppermute | solution.py:865
  323.2 4.0 %collective-permute-start.39 = (f32[32,128]{1,0:T(8,128)}, f32[32,128]{1,0:T(8,128)S(1)}, u32[]{:S(2)}, u32[]{:S(2)}) collective-permute-start(f32[32,128]{1,0:T(8,128)} %get-tuple-element.237), channel_id=1, source_target_pairs={{0,1},{1,0},{2,3},{3,2},{4,5},{5,4},{6,7},{7,6},{8,9},{9,8},{10,11... | collective-permute-start | bytes 49160 | tf_op jit(solution)/shard_map/ppermute | solution.py:865
  327.9 6.8 %collective-permute-start.42 = (f32[32,128]{1,0:T(8,128)S(1)}, f32[32,128]{1,0:T(8,128)S(1)}, u32[]{:S(2)}, u32[]{:S(2)}) collective-permute-start(f32[32,128]{1,0:T(8,128)S(1)} %add.41.refs_0_), channel_id=1, source_target_pairs={{0,6},{1,7},{2,4},{3,5},{4,2},{5,3},{6,0},{7,1},{8,14},{9,15},{10,... | collective-permute-start | bytes 49160 | tf_op jit(solution)/shard_map/ppermute | solution.py:865
  329.7 5.0 %collective-permute-start.41 = (f32[32,128]{1,0:T(8,128)S(1)}, f32[32,128]{1,0:T(8,128)S(1)}, u32[]{:S(2)}, u32[]{:S(2)}) collective-permute-start(f32[32,128]{1,0:T(8,128)S(1)} %add.41.refs_0_), channel_id=1, source_target_pairs={{0,4},{1,5},{2,6},{3,7},{4,0},{5,1},{6,2},{7,3},{8,12},{9,13},{10,... | collective-permute-start | bytes 49160 | tf_op jit(solution)/shard_map/ppermute | solution.py:865
  330.8 3.9 %collective-permute-start.40 = (f32[32,128]{1,0:T(8,128)S(1)}, f32[32,128]{1,0:T(8,128)S(1)}, u32[]{:S(2)}, u32[]{:S(2)}) collective-permute-start(f32[32,128]{1,0:T(8,128)S(1)} %add.41.refs_0_), channel_id=1, source_target_pairs={{0,2},{1,3},{2,0},{3,1},{4,6},{5,7},{6,4},{7,5},{8,10},{9,11},{10,... | collective-permute-start | bytes 49160 | tf_op jit(solution)/shard_map/ppermute | solution.py:865
  (57 other events, 218.2 us)

commit v7 on v6

--- a/solution.py
+++ b/solution.py
@@ -42,6 +42,7 @@
 
 
 ROW_BLOCK = 256
+SCORE_SCALE = HD ** (-0.5) * 1.4426950408889634
 SMALL = 128
 HORIZON_AT = EXPERTS + 1
 VECTORS_AT = 120
@@ -252,15 +253,15 @@
             gathered = jnp.zeros((ROW_BLOCK, 128), F32)
             for head in range(128 // HD):
                 own = lane // HD == head
-                raw = mm_nt(jnp.where(own, query, jnp.zeros_like(query)), key) * HD ** (-0.5)
+                raw = mm_nt(jnp.where(own, query, jnp.zeros_like(query)), key) * SCORE_SCALE
                 raw = jnp.where(allowed, raw, -1e30)
                 top = jnp.max(raw, -1, keepdims=True)
-                exponent = jnp.exp(raw - top)
+                exponent = jnp.exp2(raw - top)
                 total = jnp.sum(exponent, -1, keepdims=True)
                 attention = (exponent * (1.0 / total)).astype(BF16)
                 gathered = jnp.where(own, mm(attention, held), gathered)
                 log_rows = jnp.where(
-                    lane == group * (128 // HD) + head, top + jnp.log(total), log_rows
+                    lane == group * (128 // HD) + head, top + jnp.log2(total), log_rows
                 )
             mixed_out[start : start + ROW_BLOCK, group * 128 : (group + 1) * 128] = (
                 gathered.astype(BF16)
@@ -759,8 +760,8 @@
                 own_slope = jnp.where(own, out_slope, jnp.zeros_like(out_slope))
                 own_key = jnp.where(lane_all[:keys] // HD == head, key, jnp.zeros_like(key))
                 at = group * (128 // HD) + head
-                raw = mm_nt(own_query, key) * HD ** (-0.5)
-                probs = jnp.exp(jnp.where(allowed, raw - log_total[here, at : at + 1], -1e30))
+                raw = mm_nt(own_query, key) * SCORE_SCALE
+                probs = jnp.exp2(jnp.where(allowed, raw - log_total[here, at : at + 1], -1e30))
                 held_sum = held_sum + mm_tn(probs.astype(BF16), own_slope)
                 probs_slope = mm_nt(own_slope, held)
                 inner = jnp.sum(probs_slope * probs, -1, keepdims=True)

time: 348 us -> 348 us (level)
  no operation moved by 1% of the time
where the time goes in v7:
time: 348 us; the launch traced here: 344 us
  Pallas kernels  177 us (51%)
  starting transfers between devices  72.4 us (21%)
  waiting for transfers between devices  66 us (19%)
  local copies, waits for them, and re-layouts  21.7 us (6%)
    pallas_call x15, Pallas kernels, simple_call(): pl.pallas_call(kernel, out_shape=outs, in_specs=[spec for a, spec in pair...  82.7 us
    ppermute x43, waiting for transfers between devices, flip(): return lax.ppermute(value, axis_name, [(i, i ^ bit) for i in range(count)])  55.8 us
    ppermute x43, starting transfers between devices, flip(): return lax.ppermute(value, axis_name, [(i, i ^ bit) for i in range(count)])  44.4 us
    all_to_all x7, starting transfers between devices, exchange_near(): lax.all_to_all(value, 'expert', split_axis=0, concat_axis=0, tiled=True,...  28 us
    pallas_call x1, Pallas kernels, shards(): pl.pallas_call(expert_back_split_kernel, out_shape=[out((4, 2, CAP, D), B...  19.5 us
    unnamed x111, local copies, waits for them, and re-layouts  16.3 us
    pallas_call x1, Pallas kernels, shards(): pl.pallas_call(functools.partial(moments_kernel, fast, count, part_count,...  14.5 us
    pallas_call x1, Pallas kernels, shards(): pl.pallas_call(shared_back_split_kernel, out_shape=[out((amount, D)), out...  12.1 us
  transfers between devices with their start and end apart: 50, of which 26 were waited for; matrix products, arithmetic and copies ran while one was open for 2% of the time, Pallas kernels for 41%

profile of v7, /device:TPU:0, one launch (start us, length us, event | category | flops | bytes accessed | tf_op | source)
XLA Modules:
  0.0 343.6 jit_solution(4819141035157781684)
XLA Ops:
  3.2 4.0 %collective-permute-start = (bf16[48,896]{1,0:T(8,128)(2,1)}, bf16[48,896]{1,0:T(8,128)(2,1)S(1)}, u32[]{:S(2)}, u32[]{:S(2)}) collective-permute-start(bf16[48,896]{1,0:T(8,128)(2,1)} %bitcast.176), channel_id=1, source_target_pairs={{0,4},{1,5},{2,6},{3,7},{4,0},{5,1},{6,2},{7,3},{8,12},{9,13},{10,... | collective-permute-start | bytes 258056 | tf_op jit(solution)/shard_map/ppermute | solution.py:866
  7.4 4.4 %collective-permute-done.far = bf16[48,896]{1,0:T(8,128)(2,1)S(1)} collective-permute-done((bf16[48,896]{1,0:T(8,128)(2,1)}, bf16[48,896]{1,0:T(8,128)(2,1)S(1)}, u32[]{:S(2)}, u32[]{:S(2)}) %collective-permute-start) | collective-permute-done | bytes 86048 | tf_op jit(solution)/shard_map/ppermute | solution.py:866
  14.3 3.5 %all-to-all-start = ((bf16[4,2,48,896]{3,2,1,0:T(8,128)(2,1)}), bf16[4,2,48,896]{3,2,1,0:T(8,128)(2,1)S(1)}, u32[]{:S(2)}, u32[]{:S(2)}) async-start(bf16[4,2,48,896]{3,2,1,0:T(8,128)(2,1)} %shard_map.573), calls=%async_computation | async-start | bytes 1376256 | tf_op jit(solution)/shard_map/all_to_all | solution.py:936
  18.0 2.9 collective-permute-start.1
  21.5 3.0 shard_map.574
  24.5 2.6 shard_map.576
  30.0 3.4 %collective-permute-start.3 = (bf16[192,1152]{1,0:T(8,128)(2,1)}, bf16[192,1152]{1,0:T(8,128)(2,1)S(1)}, u32[]{:S(2)}, u32[]{:S(2)}) collective-permute-start(bf16[192,1152]{1,0:T(8,128)(2,1)} %shard_map.576), channel_id=1, source_target_pairs={{0,4},{1,5},{2,6},{3,7},{4,0},{5,1},{6,2},{7,3},{8,12},{9,13},{10,... | collective-permute-start | bytes 1327112 | tf_op jit(solution)/shard_map/ppermute | solution.py:866
  33.4 4.6 %all-to-all-start.1 = ((bf16[4,2,48,1152]{3,2,1,0:T(8,128)(2,1)}), bf16[4,2,48,1152]{3,2,1,0:T(8,128)(2,1)S(1)}, u32[]{:S(2)}, u32[]{:S(2)}) async-start(bf16[4,2,48,1152]{3,2,1,0:T(8,128)(2,1)} %shard_map.575), calls=%async_computation.1 | async-start | bytes 1769472 | tf_op jit(solution)/shard_map/all_to_all | solution.py:936
  38.9 14.8 %shard_map.577 = (f32[512,384]{1,0:T(8,128)}, bf16[512,384]{1,0:T(8,128)(2,1)}, bf16[512,1152]{1,0:T(8,128)(2,1)}, f32[512,128]{1,0:T(8,128)}, bf16[512,384]{1,0...) custom-call(s32[5]{0:T(128)} %stack.221.core.sides, ...), custom_call_target="tpu_custom_call" | custom-call | flops 17250000896 | tf_op jit(solution)/shard_map/pallas_call | solution.py:848
  55.7 4.1 %all-to-all-start.2 = ((bf16[4,2,256,384]{3,2,1,0:T(8,128)(2,1)}), bf16[4,2,256,384]{3,2,1,0:T(8,128)(2,1)S(1)}, u32[]{:S(2)}, u32[]{:S(2)}) async-start(bf16[4,2,256,384]{3,2,1,0:T(8,128)(2,1)} %bitcast.100), calls=%async_computation.2 | async-start | bytes 3145728 | tf_op jit(solution)/shard_map/all_to_all | solution.py:936
  61.4 9.9 %collective-permute-done.4.refs_1_ = bf16[192,1152]{1,0:T(8,128)(2,1)S(1)} collective-permute-done((bf16[192,1152]{1,0:T(8,128)(2,1)S(1)}, bf16[192,1152]{1,0:T(8,128)(2,1)S(1)}, u32[]{:S(2)}, u32[]{:S(2)}) %collective-permute-start.4) | collective-permute-done | bytes 442400 | tf_op jit(solution)/shard_map/ppermute | solution.py:866
  71.3 5.0 %shard_map.571 = (bf16[2,384,768]{2,1,0:T(8,128)(2,1)}, bf16[768,384]{1,0:T(8,128)(2,1)}, f32[16,128]{1,0:T(8,128)}) custom-call(f32[5,48]{1,0:T(8,128)} %refs_4_.5, f32[48,1152]{1,0:T(8,128)} %refs_5_.5, f32[48,384]{1,0:T(8,128)} %refs_6_.5, f32[9,48]{1,0:T(8,128)} %bitcast.181, f32[48,3072]{1,0:T(8,128)} %refs_8_.5, f32[192,384]{1,0:T(8,128)} %refs_9_.3, ...), custom_call_target="tpu_custom_call" | custom-call | flops 5750000128 | tf_op jit(solution)/shard_map/pallas_call | solution.py:1272
  79.3 2.9 shard_map.578
  83.4 9.6 %shard_map.579 = s16[4,2,272,384]{3,2,1,0:T(8,128)(2,1)} custom-call(s32[5]{0:T(128)} %stack.221.core.sides, bf16[4,2,256,384]{3,2,1,0:T(8,128)(2,1)} %copy-done.1, bf16[2,384,768]{2,1,0:T(8,128)(2,1)} %get-tuple-element.162.gate_up, bf16[768,384]{1,0:T(8,128)(2,1)} %get-tuple-element.163.down, bf16[2,384,768]{2,1,0:T(8,128)(2,1)} %get-tuple-element.166.gate_up_far, ...), custom_call_target="tpu_custom_call" | custom-call | flops 11500000256 | tf_op jit(solution)/shard_map/pallas_call | solution.py:1391
  93.1 4.0 %all-to-all-start.3 = ((s16[4,2,272,384]{3,2,1,0:T(8,128)(2,1)}), s16[4,2,272,384]{3,2,1,0:T(8,128)(2,1)S(1)}, u32[]{:S(2)}, u32[]{:S(2)}) async-start(s16[4,2,272,384]{3,2,1,0:T(8,128)(2,1)} %shard_map.579), calls=%async_computation.3 | async-start | bytes 3342336 | tf_op jit(solution)/shard_map/all_to_all | solution.py:936
  103.4 4.3 %shard_map.580 = (bf16[384,3072]{1,0:T(8,128)(2,1)}, bf16[1536,384]{1,0:T(8,128)(2,1)}) custom-call(s32[5]{0:T(128)} %stack.221.core.sides, bf16[384,1152]{1,0:T(8,128)(2,1)} %bitcast.104, bf16[384,1152]{1,0:T(8,128)(2,1)} %bitcast.15.refs_1_, bf16[384,1152]{1,0:T(8,128)(2,1)} %bitcast.16.refs_2_, bf16[384,1152]{1,0:T(8,128)(2,1)} %bitcast.17.refs_3_), custom_call_target="tpu_custom_call" | custom-call | flops 4944999936 | tf_op jit(solution)/shard_map/pallas_call | solution.py:848
  107.7 5.7 %shard_map.581.shared = f32[512,384]{1,0:T(8,128)} custom-call(bf16[512,384]{1,0:T(8,128)(2,1)} %get-tuple-element.169.second, bf16[384,3072]{1,0:T(8,128)(2,1)} %get-tuple-element.172.gate_w.lift_w, bf16[384,3072]{1,0:T(8,128)(2,1)} %get-tuple-element.172.gate_w.lift_w, bf16[1536,384]{1,0:T(8,128)(2,1)} %get-tuple-element.173.down_w), custom_call_target="tpu_custom_call" | custom-call | flops 6670000128 | tf_op jit(solution)/shard_map/pallas_call | solution.py:1442
  113.5 4.2 %all-to-all-done.3 = s16[4,2,272,384]{3,2,1,0:T(8,128)(2,1)S(1)} async-done(((s16[4,2,272,384]{3,2,1,0:T(8,128)(2,1)}), s16[4,2,272,384]{3,2,1,0:T(8,128)(2,1)S(1)}, u32[]{:S(2)}, u32[]{:S(2)}) %all-to-all-start.3) | async-done | bytes 1671200 | tf_op jit(solution)/shard_map/all_to_all | solution.py:936
  118.8 10.5 %shard_map.582 = (f32[512,384]{1,0:T(8,128)}, bf16[512,384]{1,0:T(8,128)(2,1)}, bf16[2048,384]{1,0:T(8,128)(2,1)}, bf16[512,128]{1,0:T(8,128)(2,1)}, f32[384,128...) custom-call(s16[8,272,384]{2,1,0:T(8,128)(2,1)} %bitcast.98, f32[512,128]{1,0:T(8,128)} %get-tuple-element.154.known, ...), custom_call_target="tpu_custom_call" | custom-call | flops 13109999616 | tf_op jit(solution)/shard_map/pallas_call | solution.py:848
  129.3 3.7 %all-to-all-start.4 = ((bf16[4,2,256,384]{3,2,1,0:T(8,128)(2,1)}), bf16[4,2,256,384]{3,2,1,0:T(8,128)(2,1)S(1)}, u32[]{:S(2)}, u32[]{:S(2)}) async-start(bf16[4,2,256,384]{3,2,1,0:T(8,128)(2,1)} %bitcast.101), calls=%async_computation.4 | async-start | bytes 3145728 | tf_op jit(solution)/shard_map/all_to_all | solution.py:936
  133.1 12.1 %shard_map.583 = (f32[512,384]{1,0:T(8,128)}, f32[2,384,768]{2,1,0:T(8,128)}, f32[2,384,384]{2,1,0:T(8,128)}, f32[2,384,384]{2,1,0:T(8,128)}, f32[2,384,384]{2,1,0:T(8,128)}, /*index=5*/f32[2,384,384]{2,1,0:T(8,128)}) custom-call(s32[5]{0:T(128)} %stack.221.core.sides, bf16[512,384]{1,0:T(8,128)(2,1)} %get-tuple-element.169.second, ...), custom_call_target="tpu_custom_call" | custom-call | flops 16099999744 | tf_op jit(solution)/shard_map/pallas_call | solution.py:1500
  145.7 2.5 collective-permute-done.12.in_even
  152.6 5.3 %shard_map.584 = (f32[384,1152]{1,0:T(8,128)}, s16[384,1280]{1,0:T(8,128)(2,1)}) custom-call(f32[2,384,768]{2,1,0:T(8,128)} %get-tuple-element.183.in_keep, f32[2,384,384]{2,1,0:T(8,128)} %copy-done.19, f32[2,384,384]{2,1,0:T(8,128)} %copy-done.21, f32[2,384,384]{2,1,0:T(8,128)} %get-tuple-element.186.out_keep, f32[2,384,384]{2,1,0:T(8,128)} %copy-done.22), custom_call_target="tpu_custom_call" | custom-call | flops 6095000064 | tf_op jit(solution)/shard_map/pallas_call | solution.py:1536
  159.6 19.5 %shard_map.585 = (bf16[4,2,256,384]{3,2,1,0:T(8,128)(2,1)}, f32[2,384,768]{2,1,0:T(8,128)}, f32[2,384,768]{2,1,0:T(8,128)}, f32[2,384,384]{2,1,0:T(8,128)}, f32[2,384,384]{2,1,0:T(8,128)}) custom-call(s32[5]{0:T(128)} %stack.221.core.sides, bf16[4,2,256,384]{3,2,1,0:T(8,128)(2,1)} %copy-done.1, bf16[4,2,256,384]{3,2,1,0:T(8,128)(2,1)} %copy-done.2, ...), custom_call_target="tpu_custom_call" | custom-call | flops 22424999936 | tf_op jit(solution)/shard_map/pallas_call | solution.py:1554
  179.2 2.7 collective-permute-done.15.other
  182.9 4.3 %all-to-all-start.5 = ((bf16[4,2,256,384]{3,2,1,0:T(8,128)(2,1)}), bf16[4,2,256,384]{3,2,1,0:T(8,128)(2,1)S(1)}, u32[]{:S(2)}, u32[]{:S(2)}) async-start(bf16[4,2,256,384]{3,2,1,0:T(8,128)(2,1)} %get-tuple-element.191), calls=%async_computation.5 | async-start | bytes 3145728 | tf_op jit(solution)/shard_map/all_to_all | solution.py:936
  187.8 3.0 collective-permute-done.11
  192.3 4.6 %shard_map.587 = (f32[2,192,1152]{2,1,0:T(8,128)}, s16[2,192,1280]{2,1,0:T(8,128)(2,1)}) custom-call(s32[5]{0:T(128)} %stack.221.core.sides, f32[2,384,768]{2,1,0:T(8,128)} %get-tuple-element.193.in_keep, f32[2,384,768]{2,1,0:T(8,128)} %collective-permute-done.16.in_other, f32[2,384,384]{2,1,0:T(8,128)} %get-tuple-element.195.out_keep, f32[2,384,384]{2,1,0:T(8,128)} %copy-done.20), custom_call_target="tpu_custom_call" | custom-call | flops 5289999872 | tf_op jit(solution)/shard_map/pallas_call | solution.py:1601
  197.4 4.1 %shard_map.586 = s16[384,1280]{1,0:T(8,128)(2,1)} custom-call(f32[384,1152]{1,0:T(8,128)} %get-tuple-element.192.keep, s16[384,1280]{1,0:T(8,128)(2,1)} %copy-done.23), custom_call_target="tpu_custom_call" | custom-call | flops 5059999744 | tf_op jit(solution)/shard_map/pallas_call | solution.py:848
  201.6 4.3 %all-to-all-done.5 = bf16[4,2,256,384]{3,2,1,0:T(8,128)(2,1)S(1)} async-done(((bf16[4,2,256,384]{3,2,1,0:T(8,128)(2,1)}), bf16[4,2,256,384]{3,2,1,0:T(8,128)(2,1)S(1)}, u32[]{:S(2)}, u32[]{:S(2)}) %all-to-all-start.5) | async-done | bytes 1572896 | tf_op jit(solution)/shard_map/all_to_all | solution.py:936
  205.9 3.7 %all-to-all-start.6 = ((s16[4,2,48,1280]{3,2,1,0:T(8,128)(2,1)}), s16[4,2,48,1280]{3,2,1,0:T(8,128)(2,1)S(1)}, u32[]{:S(2)}, u32[]{:S(2)}) async-start(s16[4,2,48,1280]{3,2,1,0:T(8,128)(2,1)} %bitcast.103), calls=%async_computation.6 | async-start | bytes 1966080 | tf_op jit(solution)/shard_map/all_to_all | solution.py:936
  209.6 5.9 %shard_map.588 = (f32[512,384]{1,0:T(8,128)}, bf16[512,384]{1,0:T(8,128)(2,1)}, f32[384,384]{1,0:T(8,128)}, f32[1,384]{1,0:T(1,128)}, f32[384,128]{1,0:T(8,128)}) custom-call(bf16[2048,384]{1,0:T(8,128)(2,1)} %bitcast.99, f32[512,128]{1,0:T(8,128)} %get-tuple-element.154.known, f32[512,384]{1,0:T(8,128)} %get-tuple-element.182.second_slope, ...), custom_call_target="tpu_custom_call" | custom-call | flops 6899999744 | tf_op jit(solution)/shard_map/pallas_call | solution.py:848
  215.5 4.5 %collective-permute-done.18.codes = s16[2,192,1280]{2,1,0:T(8,128)(2,1)S(1)} collective-permute-done((s16[2,192,1280]{2,1,0:T(8,128)(2,1)}, s16[2,192,1280]{2,1,0:T(8,128)(2,1)S(1)}, u32[]{:S(2)}, u32[]{:S(2)}) %collective-permute-start.18) | collective-permute-done | bytes 983072 | tf_op jit(solution)/shard_map/ppermute | solution.py:866
  221.0 3.4 shard_map.589
  224.4 5.4 %collective-permute-start.19 = (s16[192,1280]{1,0:T(8,128)(2,1)}, s16[192,1280]{1,0:T(8,128)(2,1)S(1)}, u32[]{:S(2)}, u32[]{:S(2)}) collective-permute-start(s16[192,1280]{1,0:T(8,128)(2,1)} %get-tuple-element.205), channel_id=1, source_target_pairs={{0,4},{1,5},{2,6},{3,7},{4,0},{5,1},{6,2},{7,3},{8,12},{9,13},{10,... | collective-permute-start | bytes 1474568 | tf_op jit(solution)/shard_map/ppermute | solution.py:866
  229.9 18.4 %shard_map.590 = (f32[384,896]{1,0:T(8,128)}, f32[384,896]{1,0:T(8,128)}) custom-call(s32[5]{0:T(128)} %stack.221.core.sides, bf16[512,384]{1,0:T(8,128)(2,1)} %get-tuple-element.206.mixed_slope, bf16[512,1152]{1,0:T(8,128)(2,1)} %get-tuple-element.207.qkv, f32[512,128]{1,0:T(8,128)} %get-tuple-element.208.log_total, f32[512,128]{1,0:T(8,128)} %get-tuple-element.154.known, ...), custom_call_target="tpu_custom_call" | custom-call | flops 21159999488 | tf_op jit(solution)/shard_map/pallas_call | solution.py:848
  250.4 2.7 shard_map.591
  254.8 3.3 shard_map.592
  258.0 4.9 %collective-permute-start.23 = (s16[96,1024]{1,0:T(8,128)(2,1)}, s16[96,1024]{1,0:T(8,128)(2,1)S(1)}, u32[]{:S(2)}, u32[]{:S(2)}) collective-permute-start(s16[96,1024]{1,0:T(8,128)(2,1)} %get-tuple-element.229), channel_id=1, source_target_pairs={{0,3},{1,2},{2,1},{3,0},{4,7},{5,6},{6,5},{7,4},{8,11},{9,10},{10,... | collective-permute-start | bytes 589832 | tf_op jit(solution)/shard_map/ppermute | solution.py:866
  263.5 2.8 shard_map.596.refs_2_.refs_37_
  268.9 3.0 collective-permute-done.22.refs_2_
  273.3 2.7 shard_map.593
  280.2 3.6 %collective-permute-done.24.code = s16[48,1024]{1,0:T(8,128)(2,1)S(1)} collective-permute-done((s16[48,1024]{1,0:T(8,128)(2,1)}, s16[48,1024]{1,0:T(8,128)(2,1)S(1)}, u32[]{:S(2)}, u32[]{:S(2)}) %collective-permute-start.24) | collective-permute-done | bytes 98336 | tf_op jit(solution)/shard_map/ppermute | solution.py:866
  287.9 4.0 %collective-permute-done.25.last_other = f32[48,896]{1,0:T(8,128)S(1)} collective-permute-done((f32[48,896]{1,0:T(8,128)}, f32[48,896]{1,0:T(8,128)S(1)}, u32[]{:S(2)}, u32[]{:S(2)}) %collective-permute-start.25) | collective-permute-done | bytes 172064 | tf_op jit(solution)/shard_map/ppermute | solution.py:866
  292.6 3.2 shard_map.597
  299.0 2.4 collective-permute-done.30
  308.9 14.5 %shard_map.598 = (f32[5,48]{1,0:T(8,128)}, f32[48,1152]{1,0:T(8,128)}, f32[48,384]{1,0:T(8,128)}, f32[9,48]{1,0:T(8,128)}, f32[48,3072]{1,0:T(8,128)}, /*index=5...) custom-call(s32[5]{0:T(128)} %stack.221.core.sides, ...), custom_call_target="tpu_custom_call" | custom-call | flops 19549999104 | tf_op jit(solution)/shard_map/pallas_call | solution.py:1758
  335.6 6.7 %shard_map.599 = (f32[5,48]{1,0:T(8,128)}, f32[48,1152]{1,0:T(8,128)}, f32[48,384]{1,0:T(8,128)}, f32[9,48]{1,0:T(8,128)}, f32[48,3072]{1,0:T(8,128)}, /*index=5...) custom-call(s32[5]{0:T(128)} %stack.221.core.sides, ...), custom_call_target="tpu_custom_call" | custom-call | flops 8049999872 | tf_op jit(solution)/shard_map/pallas_call | solution.py:1777
  (217 shorter events, 75.4 us)
Async XLA Ops:
  3.2 8.6 %collective-permute-start = (bf16[48,896]{1,0:T(8,128)(2,1)}, bf16[48,896]{1,0:T(8,128)(2,1)S(1)}, u32[]{:S(2)}, u32[]{:S(2)}) collective-permute-start(bf16[48,896]{1,0:T(8,128)(2,1)} %bitcast.176), channel_id=1, source_target_pairs={{0,4},{1,5},{2,6},{3,7},{4,0},{5,1},{6,2},{7,3},{8,12},{9,13},{10,... | collective-permute-start | bytes 258056 | tf_op jit(solution)/shard_map/ppermute | solution.py:866
  14.3 15.6 %all-to-all-start = ((bf16[4,2,48,896]{3,2,1,0:T(8,128)(2,1)}), bf16[4,2,48,896]{3,2,1,0:T(8,128)(2,1)S(1)}, u32[]{:S(2)}, u32[]{:S(2)}) async-start(bf16[4,2,48,896]{3,2,1,0:T(8,128)(2,1)} %shard_map.573), calls=%async_computation | async-start | bytes 1376256 | tf_op jit(solution)/shard_map/all_to_all | solution.py:936
  18.0 9.4 %collective-permute-start.1 = (bf16[48,1152]{1,0:T(8,128)(2,1)S(1)}, bf16[48,1152]{1,0:T(8,128)(2,1)S(1)}, u32[]{:S(2)}, u32[]{:S(2)}) collective-permute-start(bf16[48,1152]{1,0:T(8,128)(2,1)S(1)} %fusion.own), channel_id=1, source_target_pairs={{0,4},{1,5},{2,6},{3,7},{4,0},{5,1},{6,2},{7,3},{8,12},{9,13},{10,... | collective-permute-start | bytes 331784 | tf_op jit(solution)/shard_map/ppermute | solution.py:866
  30.0 8.1 %collective-permute-start.2 = (bf16[384,896]{1,0:T(8,128)(2,1)S(1)}, bf16[384,896]{1,0:T(8,128)(2,1)S(1)}, u32[]{:S(2)}, u32[]{:S(2)}) collective-permute-start(bf16[384,896]{1,0:T(8,128)(2,1)S(1)} %bitcast.105), channel_id=1, source_target_pairs={{0,8},{8,0},{16,24},{24,16},{1,9},{9,1},{17,25},{25,17},{2,10},{10... | collective-permute-start | bytes 2064392 | tf_op jit(solution)/shard_map/ppermute | solution.py:866
  30.0 24.0 %collective-permute-start.3 = (bf16[192,1152]{1,0:T(8,128)(2,1)}, bf16[192,1152]{1,0:T(8,128)(2,1)S(1)}, u32[]{:S(2)}, u32[]{:S(2)}) collective-permute-start(bf16[192,1152]{1,0:T(8,128)(2,1)} %shard_map.576), channel_id=1, source_target_pairs={{0,4},{1,5},{2,6},{3,7},{4,0},{5,1},{6,2},{7,3},{8,12},{9,13},{10,... | collective-permute-start | bytes 1327112 | tf_op jit(solution)/shard_map/ppermute | solution.py:866
  33.4 22.3 %all-to-all-start.1 = ((bf16[4,2,48,1152]{3,2,1,0:T(8,128)(2,1)}), bf16[4,2,48,1152]{3,2,1,0:T(8,128)(2,1)S(1)}, u32[]{:S(2)}, u32[]{:S(2)}) async-start(bf16[4,2,48,1152]{3,2,1,0:T(8,128)(2,1)} %shard_map.575), calls=%async_computation.1 | async-start | bytes 1769472 | tf_op jit(solution)/shard_map/all_to_all | solution.py:936
  55.7 26.6 %all-to-all-start.2 = ((bf16[4,2,256,384]{3,2,1,0:T(8,128)(2,1)}), bf16[4,2,256,384]{3,2,1,0:T(8,128)(2,1)S(1)}, u32[]{:S(2)}, u32[]{:S(2)}) async-start(bf16[4,2,256,384]{3,2,1,0:T(8,128)(2,1)} %bitcast.100), calls=%async_computation.2 | async-start | bytes 3145728 | tf_op jit(solution)/shard_map/all_to_all | solution.py:936
  59.8 11.5 %collective-permute-start.4 = (bf16[192,1152]{1,0:T(8,128)(2,1)S(1)}, bf16[192,1152]{1,0:T(8,128)(2,1)S(1)}, u32[]{:S(2)}, u32[]{:S(2)}) collective-permute-start(bf16[192,1152]{1,0:T(8,128)(2,1)S(1)} %collective-permute-done.3.refs_0_), channel_id=1, source_target_pairs={{0,16},{8,24},{16,0},{24,8},{1,17},{9,25},{17,1},{25,9},{2,18},{10... | collective-permute-start | bytes 1327112 | tf_op jit(solution)/shard_map/ppermute | solution.py:866
  61.4 16.5 %collective-permute-start.5 = (bf16[192,1152]{1,0:T(8,128)(2,1)S(1)}, bf16[192,1152]{1,0:T(8,128)(2,1)S(1)}, u32[]{:S(2)}, u32[]{:S(2)}) collective-permute-start(bf16[192,1152]{1,0:T(8,128)(2,1)S(1)} %collective-permute-done.3.refs_0_), channel_id=1, source_target_pairs={{0,8},{8,0},{16,24},{24,16},{1,9},{9,1},{17,25},{25,17},{2,10},{10... | collective-permute-start | bytes 1327112 | tf_op jit(solution)/shard_map/ppermute | solution.py:866
  71.3 6.5 %collective-permute-start.6 = (bf16[192,1152]{1,0:T(8,128)(2,1)S(1)}, bf16[192,1152]{1,0:T(8,128)(2,1)S(1)}, u32[]{:S(2)}, u32[]{:S(2)}) collective-permute-start(bf16[192,1152]{1,0:T(8,128)(2,1)S(1)} %collective-permute-done.4.refs_1_), channel_id=1, source_target_pairs={{0,8},{8,0},{16,24},{24,16},{1,9},{9,1},{17,25},{25,17},{2,10},{10... | collective-permute-start | bytes 1327112 | tf_op jit(solution)/shard_map/ppermute | solution.py:866
  76.3 22.1 %collective-permute-start.7 = (bf16[4,2,48,1152]{3,2,1,0:T(8,128)(2,1)S(1)}, bf16[4,2,48,1152]{3,2,1,0:T(8,128)(2,1)}, u32[]{:S(2)}, u32[]{:S(2)}) collective-permute-start(bf16[4,2,48,1152]{3,2,1,0:T(8,128)(2,1)S(1)} %all-to-all-done.1), channel_id=1, source_target_pairs={{0,16},{8,24},{16,0},{24,8},{1,17},{9,25},{17,1},{25,9},{2,18},{10... | collective-permute-start | bytes 2654216 | tf_op jit(solution)/shard_map/ppermute | solution.py:866
  93.1 24.6 %all-to-all-start.3 = ((s16[4,2,272,384]{3,2,1,0:T(8,128)(2,1)}), s16[4,2,272,384]{3,2,1,0:T(8,128)(2,1)S(1)}, u32[]{:S(2)}, u32[]{:S(2)}) async-start(s16[4,2,272,384]{3,2,1,0:T(8,128)(2,1)} %shard_map.579), calls=%async_computation.3 | async-start | bytes 3342336 | tf_op jit(solution)/shard_map/all_to_all | solution.py:936
  98.3 5.1 %collective-permute-start.9 = (bf16[4,2,48,1152]{3,2,1,0:T(8,128)(2,1)}, bf16[4,2,48,1152]{3,2,1,0:T(8,128)(2,1)}, u32[]{:S(2)}, u32[]{:S(2)}) collective-permute-start(bf16[4,2,48,1152]{3,2,1,0:T(8,128)(2,1)} %collective-permute-done.7), channel_id=1, source_target_pairs={{0,8},{8,0},{16,24},{24,16},{1,9},{9,1},{17,25},{25,17},{2,10},{10... | collective-permute-start | bytes 2654216 | tf_op jit(solution)/shard_map/ppermute | solution.py:866
  98.3 5.1 %collective-permute-start.8 = (bf16[4,2,48,1152]{3,2,1,0:T(8,128)(2,1)S(1)}, bf16[4,2,48,1152]{3,2,1,0:T(8,128)(2,1)}, u32[]{:S(2)}, u32[]{:S(2)}) collective-permute-start(bf16[4,2,48,1152]{3,2,1,0:T(8,128)(2,1)S(1)} %all-to-all-done.1), channel_id=1, source_target_pairs={{0,8},{8,0},{16,24},{24,16},{1,9},{9,1},{17,25},{25,17},{2,10},{10... | collective-permute-start | bytes 2654216 | tf_op jit(solution)/shard_map/ppermute | solution.py:866
  99.2 3.6 %collective-permute-start.10 = (f32[1,128]{1,0:T(1,128)S(1)}, f32[1,128]{1,0:T(1,128)S(1)}, u32[]{:S(2)}, u32[]{:S(2)}) collective-permute-start(f32[1,128]{1,0:T(1,128)S(1)} %copy-done.15), channel_id=1, source_target_pairs={{0,16},{8,24},{16,0},{24,8},{1,17},{9,25},{17,1},{25,9},{2,18},{10... | collective-permute-start | bytes 1544 | tf_op jit(solution)/shard_map/ppermute | solution.py:866
  129.3 29.1 %all-to-all-start.4 = ((bf16[4,2,256,384]{3,2,1,0:T(8,128)(2,1)}), bf16[4,2,256,384]{3,2,1,0:T(8,128)(2,1)S(1)}, u32[]{:S(2)}, u32[]{:S(2)}) async-start(bf16[4,2,256,384]{3,2,1,0:T(8,128)(2,1)} %bitcast.101), calls=%async_computation.4 | async-start | bytes 3145728 | tf_op jit(solution)/shard_map/all_to_all | solution.py:936
  145.1 4.7 %collective-permute-start.13 = (f32[2,384,384]{2,1,0:T(8,128)}, f32[2,384,384]{2,1,0:T(8,128)S(1)}, u32[]{:S(2)}, u32[]{:S(2)}) collective-permute-start(f32[2,384,384]{2,1,0:T(8,128)} %get-tuple-element.185), channel_id=1, source_target_pairs={{0,8},{8,0},{16,24},{24,16},{1,9},{9,1},{17,25},{25,17},{2,10},{10... | collective-permute-start | bytes 3538952 | tf_op jit(solution)/shard_map/ppermute | solution.py:866
  145.6 5.9 %collective-permute-start.14 = (f32[2,384,384]{2,1,0:T(8,128)}, f32[2,384,384]{2,1,0:T(8,128)S(1)}, u32[]{:S(2)}, u32[]{:S(2)}) collective-permute-start(f32[2,384,384]{2,1,0:T(8,128)} %get-tuple-element.187), channel_id=1, source_target_pairs={{0,8},{8,0},{16,24},{24,16},{1,9},{9,1},{17,25},{25,17},{2,10},{10... | collective-permute-start | bytes 3538952 | tf_op jit(solution)/shard_map/ppermute | solution.py:866
  157.9 24.0 %collective-permute-start.15 = (s16[384,1280]{1,0:T(8,128)(2,1)}, s16[384,1280]{1,0:T(8,128)(2,1)S(1)}, u32[]{:S(2)}, u32[]{:S(2)}) collective-permute-start(s16[384,1280]{1,0:T(8,128)(2,1)} %get-tuple-element.188), channel_id=1, source_target_pairs={{0,16},{8,24},{16,0},{24,8},{1,17},{9,25},{17,1},{25,9},{2,18},{10... | collective-permute-start | bytes 2949128 | tf_op jit(solution)/shard_map/ppermute | solution.py:866
  179.2 12.1 %collective-permute-start.16 = (f32[2,384,768]{2,1,0:T(8,128)}, f32[2,384,768]{2,1,0:T(8,128)}, u32[]{:S(2)}, u32[]{:S(2)}) collective-permute-start(f32[2,384,768]{2,1,0:T(8,128)} %get-tuple-element.194), channel_id=1, source_target_pairs={{0,8},{8,0},{16,24},{24,16},{1,9},{9,1},{17,25},{25,17},{2,10},{10... | collective-permute-start | bytes 7077896 | tf_op jit(solution)/shard_map/ppermute | solution.py:866
  182.9 23.0 %all-to-all-start.5 = ((bf16[4,2,256,384]{3,2,1,0:T(8,128)(2,1)}), bf16[4,2,256,384]{3,2,1,0:T(8,128)(2,1)S(1)}, u32[]{:S(2)}, u32[]{:S(2)}) async-start(bf16[4,2,256,384]{3,2,1,0:T(8,128)(2,1)} %get-tuple-element.191), calls=%async_computation.5 | async-start | bytes 3145728 | tf_op jit(solution)/shard_map/all_to_all | solution.py:936
  187.2 4.1 %collective-permute-start.17 = (f32[2,384,384]{2,1,0:T(8,128)S(1)}, f32[2,384,384]{2,1,0:T(8,128)S(1)}, u32[]{:S(2)}, u32[]{:S(2)}) collective-permute-start(f32[2,384,384]{2,1,0:T(8,128)S(1)} %copy-done.18), channel_id=1, source_target_pairs={{0,8},{8,0},{16,24},{24,16},{1,9},{9,1},{17,25},{25,17},{2,10},{10... | collective-permute-start | bytes 3538952 | tf_op jit(solution)/shard_map/ppermute | solution.py:866
  187.2 3.6 %collective-permute-start.11 = (f32[1,128]{1,0:T(1,128)S(1)}, f32[1,128]{1,0:T(1,128)S(1)}, u32[]{:S(2)}, u32[]{:S(2)}) collective-permute-start(f32[1,128]{1,0:T(1,128)S(1)} %copy-done.54), channel_id=1, source_target_pairs={{0,16},{8,24},{16,0},{24,8},{1,17},{9,25},{17,1},{25,9},{2,18},{10... | collective-permute-start | bytes 1544 | tf_op jit(solution)/shard_map/ppermute | solution.py:866
  196.9 23.2 %collective-permute-start.18 = (s16[2,192,1280]{2,1,0:T(8,128)(2,1)}, s16[2,192,1280]{2,1,0:T(8,128)(2,1)S(1)}, u32[]{:S(2)}, u32[]{:S(2)}) collective-permute-start(s16[2,192,1280]{2,1,0:T(8,128)(2,1)} %get-tuple-element.197), channel_id=1, source_target_pairs={{0,16},{8,24},{16,0},{24,8},{1,17},{9,25},{17,1},{25,9},{2,18},{10... | collective-permute-start | bytes 2949128 | tf_op jit(solution)/shard_map/ppermute | solution.py:866
  205.9 42.3 %all-to-all-start.6 = ((s16[4,2,48,1280]{3,2,1,0:T(8,128)(2,1)}), s16[4,2,48,1280]{3,2,1,0:T(8,128)(2,1)S(1)}, u32[]{:S(2)}, u32[]{:S(2)}) async-start(s16[4,2,48,1280]{3,2,1,0:T(8,128)(2,1)} %bitcast.103), calls=%async_computation.6 | async-start | bytes 1966080 | tf_op jit(solution)/shard_map/all_to_all | solution.py:936
  224.4 25.9 %collective-permute-start.19 = (s16[192,1280]{1,0:T(8,128)(2,1)}, s16[192,1280]{1,0:T(8,128)(2,1)S(1)}, u32[]{:S(2)}, u32[]{:S(2)}) collective-permute-start(s16[192,1280]{1,0:T(8,128)(2,1)} %get-tuple-element.205), channel_id=1, source_target_pairs={{0,4},{1,5},{2,6},{3,7},{4,0},{5,1},{6,2},{7,3},{8,12},{9,13},{10,... | collective-permute-start | bytes 1474568 | tf_op jit(solution)/shard_map/ppermute | solution.py:866
  250.4 3.3 collective-permute-start.20
  253.1 24.1 %collective-permute-start.26 = (s16[48,1280]{1,0:T(8,128)(2,1)}, s16[48,1280]{1,0:T(8,128)(2,1)S(1)}, u32[]{:S(2)}, u32[]{:S(2)}) collective-permute-start(s16[48,1280]{1,0:T(8,128)(2,1)} %get-tuple-element.219), channel_id=1, source_target_pairs={{0,4},{1,5},{2,6},{3,7},{4,0},{5,1},{6,2},{7,3},{8,12},{9,13},{10,... | collective-permute-start | bytes 368648 | tf_op jit(solution)/shard_map/ppermute | solution.py:866
  258.0 10.9 %collective-permute-start.23 = (s16[96,1024]{1,0:T(8,128)(2,1)}, s16[96,1024]{1,0:T(8,128)(2,1)S(1)}, u32[]{:S(2)}, u32[]{:S(2)}) collective-permute-start(s16[96,1024]{1,0:T(8,128)(2,1)} %get-tuple-element.229), channel_id=1, source_target_pairs={{0,3},{1,2},{2,1},{3,0},{4,7},{5,6},{6,5},{7,4},{8,11},{9,10},{10,... | collective-permute-start | bytes 589832 | tf_op jit(solution)/shard_map/ppermute | solution.py:866
  263.0 8.9 %collective-permute-start.22 = (s16[96,1024]{1,0:T(8,128)(2,1)}, s16[96,1024]{1,0:T(8,128)(2,1)S(1)}, u32[]{:S(2)}, u32[]{:S(2)}) collective-permute-start(s16[96,1024]{1,0:T(8,128)(2,1)} %get-tuple-element.227), channel_id=1, source_target_pairs={{0,2},{1,3},{2,0},{3,1},{4,6},{5,7},{6,4},{7,5},{8,10},{9,11},{10,... | collective-permute-start | bytes 589832 | tf_op jit(solution)/shard_map/ppermute | solution.py:866
  263.0 9.5 %collective-permute-start.21 = (s16[96,1024]{1,0:T(8,128)(2,1)}, s16[96,1024]{1,0:T(8,128)(2,1)S(1)}, u32[]{:S(2)}, u32[]{:S(2)}) collective-permute-start(s16[96,1024]{1,0:T(8,128)(2,1)} %get-tuple-element.225), channel_id=1, source_target_pairs={{0,1},{1,0},{2,3},{3,2},{4,5},{5,4},{6,7},{7,6},{8,9},{9,8},{10,11... | collective-permute-start | bytes 589832 | tf_op jit(solution)/shard_map/ppermute | solution.py:866
  266.3 21.1 %collective-permute-start.28 = (s16[192,1280]{1,0:T(8,128)(2,1)}, s16[192,1280]{1,0:T(8,128)(2,1)S(1)}, u32[]{:S(2)}, u32[]{:S(2)}) collective-permute-start(s16[192,1280]{1,0:T(8,128)(2,1)} %shard_map.596.refs_2_.refs_37_), channel_id=1, source_target_pairs={{0,16},{8,24},{16,0},{24,8},{1,17},{9,25},{17,1},{25,9},{2,18},{10... | collective-permute-start | bytes 1474568 | tf_op jit(solution)/shard_map/ppermute | solution.py:866
  276.0 7.9 %collective-permute-start.24 = (s16[48,1024]{1,0:T(8,128)(2,1)}, s16[48,1024]{1,0:T(8,128)(2,1)S(1)}, u32[]{:S(2)}, u32[]{:S(2)}) collective-permute-start(s16[48,1024]{1,0:T(8,128)(2,1)} %get-tuple-element.231), channel_id=1, source_target_pairs={{0,4},{1,5},{2,6},{3,7},{4,0},{5,1},{6,2},{7,3},{8,12},{9,13},{10,... | collective-permute-start | bytes 294920 | tf_op jit(solution)/shard_map/ppermute | solution.py:866
  279.7 7.2 %collective-permute-start.27 = (f32[48,1152]{1,0:T(8,128)}, f32[48,1152]{1,0:T(8,128)S(1)}, u32[]{:S(2)}, u32[]{:S(2)}) collective-permute-start(f32[48,1152]{1,0:T(8,128)} %shard_map.595.refs_0_.refs_33_), channel_id=1, source_target_pairs={{0,16},{8,24},{16,0},{24,8},{1,17},{9,25},{17,1},{25,9},{2,18},{10... | collective-permute-start | bytes 663560 | tf_op jit(solution)/shard_map/ppermute | solution.py:866
  286.3 5.6 %collective-permute-start.25 = (f32[48,896]{1,0:T(8,128)}, f32[48,896]{1,0:T(8,128)S(1)}, u32[]{:S(2)}, u32[]{:S(2)}) collective-permute-start(f32[48,896]{1,0:T(8,128)} %shard_map.594.last), channel_id=1, source_target_pairs={{0,16},{8,24},{16,0},{24,8},{1,17},{9,25},{17,1},{25,9},{2,18},{10... | collective-permute-start | bytes 516104 | tf_op jit(solution)/shard_map/ppermute | solution.py:866
  286.8 14.6 %collective-permute-start.35 = (f32[48,1152]{1,0:T(8,128)S(1)}, f32[48,1152]{1,0:T(8,128)S(1)}, u32[]{:S(2)}, u32[]{:S(2)}) collective-permute-start(f32[48,1152]{1,0:T(8,128)S(1)} %copy-done.35), channel_id=1, source_target_pairs={{0,8},{8,0},{16,24},{24,16},{1,9},{9,1},{17,25},{25,17},{2,10},{10... | collective-permute-start | bytes 663560 | tf_op jit(solution)/shard_map/ppermute | solution.py:866
  286.9 16.7 %collective-permute-start.36 = (f32[48,1152]{1,0:T(8,128)S(1)}, f32[48,1152]{1,0:T(8,128)S(1)}, u32[]{:S(2)}, u32[]{:S(2)}) collective-permute-start(f32[48,1152]{1,0:T(8,128)S(1)} %collective-permute-done.27.refs_1_.refs_34_), channel_id=1, source_target_pairs={{0,8},{8,0},{16,24},{24,16},{1,9},{9,1},{17,25},{25,17},{2,10},{10... | collective-permute-start | bytes 663560 | tf_op jit(solution)/shard_map/ppermute | solution.py:866
  287.4 16.2 %collective-permute-start.37 = (s16[192,1280]{1,0:T(8,128)(2,1)S(1)}, s16[192,1280]{1,0:T(8,128)(2,1)S(1)}, u32[]{:S(2)}, u32[]{:S(2)}) collective-permute-start(s16[192,1280]{1,0:T(8,128)(2,1)S(1)} %copy-done.26), channel_id=1, source_target_pairs={{0,8},{8,0},{16,24},{24,16},{1,9},{9,1},{17,25},{25,17},{2,10},{10... | collective-permute-start | bytes 1474568 | tf_op jit(solution)/shard_map/ppermute | solution.py:866
  287.4 20.6 %collective-permute-start.38 = (s16[192,1280]{1,0:T(8,128)(2,1)S(1)}, s16[192,1280]{1,0:T(8,128)(2,1)S(1)}, u32[]{:S(2)}, u32[]{:S(2)}) collective-permute-start(s16[192,1280]{1,0:T(8,128)(2,1)S(1)} %collective-permute-done.28.refs_3_.refs_38_), channel_id=1, source_target_pairs={{0,8},{8,0},{16,24},{24,16},{1,9},{9,1},{17,25},{25,17},{2,10},{10... | collective-permute-start | bytes 1474568 | tf_op jit(solution)/shard_map/ppermute | solution.py:866
  297.8 3.6 %collective-permute-start.30 = (f32[2,128]{1,0:T(2,128)S(1)}, f32[2,128]{1,0:T(2,128)S(1)}, u32[]{:S(2)}, u32[]{:S(2)}) collective-permute-start(f32[2,128]{1,0:T(2,128)S(1)} %add.39), channel_id=1, source_target_pairs={{0,1},{1,0},{2,3},{3,2},{4,5},{5,4},{6,7},{7,6},{8,9},{9,8},{10,11... | collective-permute-start | bytes 3080 | tf_op jit(solution)/shard_map/ppermute | solution.py:866
  301.4 6.6 %collective-permute-start.34 = (f32[48,896]{1,0:T(8,128)}, f32[48,896]{1,0:T(8,128)S(1)}, u32[]{:S(2)}, u32[]{:S(2)}) collective-permute-start(f32[48,896]{1,0:T(8,128)} %get-tuple-element.236.refs_31_), channel_id=1, source_target_pairs={{0,8},{8,0},{16,24},{24,16},{1,9},{9,1},{17,25},{25,17},{2,10},{10... | collective-permute-start | bytes 516104 | tf_op jit(solution)/shard_map/ppermute | solution.py:866
  301.4 5.4 %collective-permute-start.33 = (f32[2,128]{1,0:T(2,128)S(1)}, f32[2,128]{1,0:T(2,128)S(1)}, u32[]{:S(2)}, u32[]{:S(2)}) collective-permute-start(f32[2,128]{1,0:T(2,128)S(1)} %add.40.refs_0_), channel_id=1, source_target_pairs={{0,6},{1,7},{2,4},{3,5},{4,2},{5,3},{6,0},{7,1},{8,14},{9,15},{10,... | collective-permute-start | bytes 3080 | tf_op jit(solution)/shard_map/ppermute | solution.py:866
  303.6 4.5 %collective-permute-start.32 = (f32[2,128]{1,0:T(2,128)S(1)}, f32[2,128]{1,0:T(2,128)S(1)}, u32[]{:S(2)}, u32[]{:S(2)}) collective-permute-start(f32[2,128]{1,0:T(2,128)S(1)} %add.40.refs_0_), channel_id=1, source_target_pairs={{0,4},{1,5},{2,6},{3,7},{4,0},{5,1},{6,2},{7,3},{8,12},{9,13},{10,... | collective-permute-start | bytes 3080 | tf_op jit(solution)/shard_map/ppermute | solution.py:866
  303.6 4.4 %collective-permute-start.31 = (f32[2,128]{1,0:T(2,128)S(1)}, f32[2,128]{1,0:T(2,128)S(1)}, u32[]{:S(2)}, u32[]{:S(2)}) collective-permute-start(f32[2,128]{1,0:T(2,128)S(1)} %add.40.refs_0_), channel_id=1, source_target_pairs={{0,2},{1,3},{2,0},{3,1},{4,6},{5,7},{6,4},{7,5},{8,10},{9,11},{10,... | collective-permute-start | bytes 3080 | tf_op jit(solution)/shard_map/ppermute | solution.py:866
  323.4 4.0 %collective-permute-start.39 = (f32[32,128]{1,0:T(8,128)}, f32[32,128]{1,0:T(8,128)S(1)}, u32[]{:S(2)}, u32[]{:S(2)}) collective-permute-start(f32[32,128]{1,0:T(8,128)} %get-tuple-element.237), channel_id=1, source_target_pairs={{0,1},{1,0},{2,3},{3,2},{4,5},{5,4},{6,7},{7,6},{8,9},{9,8},{10,11... | collective-permute-start | bytes 49160 | tf_op jit(solution)/shard_map/ppermute | solution.py:866
  328.2 6.8 %collective-permute-start.42 = (f32[32,128]{1,0:T(8,128)S(1)}, f32[32,128]{1,0:T(8,128)S(1)}, u32[]{:S(2)}, u32[]{:S(2)}) collective-permute-start(f32[32,128]{1,0:T(8,128)S(1)} %add.41.refs_0_), channel_id=1, source_target_pairs={{0,6},{1,7},{2,4},{3,5},{4,2},{5,3},{6,0},{7,1},{8,14},{9,15},{10,... | collective-permute-start | bytes 49160 | tf_op jit(solution)/shard_map/ppermute | solution.py:866
  329.9 5.0 %collective-permute-start.41 = (f32[32,128]{1,0:T(8,128)S(1)}, f32[32,128]{1,0:T(8,128)S(1)}, u32[]{:S(2)}, u32[]{:S(2)}) collective-permute-start(f32[32,128]{1,0:T(8,128)S(1)} %add.41.refs_0_), channel_id=1, source_target_pairs={{0,4},{1,5},{2,6},{3,7},{4,0},{5,1},{6,2},{7,3},{8,12},{9,13},{10,... | collective-permute-start | bytes 49160 | tf_op jit(solution)/shard_map/ppermute | solution.py:866
  331.1 3.9 %collective-permute-start.40 = (f32[32,128]{1,0:T(8,128)S(1)}, f32[32,128]{1,0:T(8,128)S(1)}, u32[]{:S(2)}, u32[]{:S(2)}) collective-permute-start(f32[32,128]{1,0:T(8,128)S(1)} %add.41.refs_0_), channel_id=1, source_target_pairs={{0,2},{1,3},{2,0},{3,1},{4,6},{5,7},{6,4},{7,5},{8,10},{9,11},{10,... | collective-permute-start | bytes 49160 | tf_op jit(solution)/shard_map/ppermute | solution.py:866
  (57 other events, 218.5 us)
